TPU v7x, 32 devices: a whole 2x2x4 slice. The times are simulated.
32 devices in a mesh: apa: 2 (over y), gz: 4 (over x, core), drift: 4 (over z).
Axes of the slice: x: 2, y: 2, z: 4, core: 2. Of those that a mesh axis runs over, the one named last changes fastest.
Arguments:
- charge: bfloat16 [16384, 384], P(('apa', 'gz', 'drift')), parts along dimension 0, may hold values from 0.049804688 to 2
- intersection: bfloat16 [128, 3, 2, 32, 128], P(('apa', 'gz', 'drift')), parts along dimension 0, may hold values from 0 to 0.03125
- ovl_block: int32 [128, 3, 2], P(('apa', 'gz', 'drift')), parts along dimension 0, may hold values from 0 to 15, as said below
- ovl_count: int32 [128, 3], P(('apa', 'gz', 'drift')), parts along dimension 0, may hold values from 1 to 2
- diff_class: int32 [768], P('apa'), parts along dimension 0, may hold values from 0 to 5
- response: bfloat16 [3, 21, 200], replicated, may hold values from -0.029907227 to 0.029907227
- cotangent: bfloat16 [6, 512, 3072], P('apa', 'gz', 'drift'), parts along dimension 0, may hold values from -120 to 120
Outputs:
- signal: bfloat16 [6, 512, 3072], P('apa', 'gz', 'drift'), parts along dimension 0
- charge_grad: bfloat16 [16384, 384], P(('apa', 'gz', 'drift')), parts along dimension 0
There are 2 independent parts, one for each index of `apa`. A program takes and returns all parts, laid end to end along the dimension named above; an argument that names none is the same for every part. Nothing has to cross between parts.
Inputs may be any that keep to these rules, and one draw needn't show every extreme that they name: `ovl_block`: planes are U, V, W in this order. Cell block b lies in z-block b // 16; its W entries name wire blocks of that z-block, z-block g owning wire blocks g * 4 to (g + 1) * 4 - 1 of every plane. Entry 0 of each list is live. Among the live U and V entries of one group of 4 consecutive cell blocks (starting at a multiple of 4), at most 8 name wire blocks of one z-block, and every such group reaches 8 for some z-block. `ovl_count`: entry k of a list is live where k < count; the others are ignored.
All inputs are finite; a program needn't handle non-finite values.
Results may differ from a plain program's by a relative error of at most 0.0058.
Values may be sent and summed in bfloat16 or wider, within the bound.
No kernel may reach another device: no remote copies, remote signals or barrier semaphores. Data moves between devices by JAX's collectives and lax.ppermute only.
A program may use at most 128 MiB of HBM per device.

v0:
```python
import math

import jax
import jax.numpy as jnp
from jax import lax
from jax.sharding import PartitionSpec as P

TPB = 8
HB = 2


def extended_2(cells, sides, width):
    for axis, dim in sides:
        count = lax.axis_size(axis)
        ends = count - 1
        head = lax.slice_in_dim(cells, 0, width, axis=dim)
        tail = lax.slice_in_dim(cells, cells.shape[dim] - width, cells.shape[dim], axis=dim)
        cells = jnp.concatenate(
            [
                lax.ppermute(tail, axis, [(i, (i + 1) % count) for i in range(ends)]),
                cells,
                lax.ppermute(head, axis, [((i + 1) % count, i) for i in range(ends)]),
            ],
            axis=dim,
        )
    return cells


def passed_along(block, axis, distance):
    devices = range(lax.axis_size(axis))
    route = [(i - distance, i) for i in devices if i - distance in devices]
    return lax.ppermute(block, axis, route)


def smear_weights(offset, classes):
    spread_width = TPB * (0.2 + 0.15 * classes)
    reach_ticks = HB * TPB
    samples = jnp.arange(-reach_ticks, reach_ticks).astype(jnp.float32) + 0.5
    normalizer = jnp.sum(
        jnp.exp(-(samples * samples) / (2.0 * spread_width[..., None] * spread_width[..., None])),
        axis=-1,
    )
    inside = jnp.abs(offset) < reach_ticks
    bump = jnp.exp(-(offset * offset) / (2.0 * spread_width * spread_width))
    return jnp.where(inside, bump, jnp.zeros_like(bump)) / normalizer


def windows(padded, count, block_bins):
    length = padded.shape[-1]
    lead = padded.shape[:-1]
    extra = (count + 1) * block_bins - length
    grown = jnp.pad(padded, [(0, 0)] * len(lead) + [(0, extra)])
    front = grown[..., : count * block_bins].reshape(lead + (count, block_bins))
    after = grown[..., block_bins:].reshape(lead + (count, block_bins))[..., : 2 * HB]
    return jnp.concatenate([front, after], axis=-1)


def unwindows(parts, count, block_bins):
    lead = parts.shape[:-2]
    length = count * block_bins + 2 * HB
    front = parts[..., :block_bins].reshape(lead + (count * block_bins,))
    after = jnp.pad(
        parts[..., block_bins:], [(0, 0)] * (len(lead) + 1) + [(0, block_bins - 2 * HB)]
    )
    after = after.reshape(lead + (count * block_bins,))
    front = jnp.pad(front, [(0, 0)] * len(lead) + [(0, 2 * HB)])
    after = jnp.pad(after[..., : length - block_bins], [(0, 0)] * len(lead) + [(block_bins, 0)])
    return front + after


def block_kernel(class_windows, block_bins):
    index_in = jnp.arange(block_bins + 2 * HB).astype(jnp.float32)[:, None]
    tick_in = jnp.arange(block_bins * TPB).astype(jnp.float32)[None, :]
    offset = tick_in - TPB * (index_in - HB) - (TPB - 1) / 2.0
    return smear_weights(offset[None], class_windows[:, :, None])


def drift_forward(framed, class_ext, count, block_bins):
    kernel = block_kernel(windows(class_ext, count, block_bins), block_bins)
    spread = jnp.einsum(
        "pwbi,bit->pwbt",
        windows(framed, count, block_bins),
        kernel,
        precision=lax.Precision.HIGHEST,
    )
    return spread.reshape(spread.shape[0], spread.shape[1], -1)


def drift_backward(tick_values, class_ext, count, block_bins):
    kernel = block_kernel(windows(class_ext, count, block_bins), block_bins)
    framed = tick_values.reshape(tick_values.shape[0], tick_values.shape[1], count, -1)
    parts = jnp.einsum(
        "pwbt,bit->pwbi", framed.astype(jnp.float32), kernel, precision=lax.Precision.HIGHEST
    )
    return unwindows(parts, count, block_bins)


def tick_table(taps, tick_block, forward):
    resp_length = taps.shape[2]
    inputs = jnp.arange(tick_block + resp_length - 1, dtype=jnp.int32)[:, None]
    outputs = jnp.arange(tick_block, dtype=jnp.int32)[None, :]
    if forward:
        lag = outputs + resp_length - 1 - inputs
    else:
        lag = inputs - outputs
    valid = (lag >= 0) & (lag < resp_length)
    picked = taps[:, :, jnp.clip(lag, 0, resp_length - 1)]
    return jnp.where(valid[None, None], picked, jnp.zeros((), taps.dtype))


def planes_apply(extended, taps, wires_here, ticks_here, forward):
    wire_taps, resp_length = (taps.shape[1], taps.shape[2])
    tick_block = math.gcd(ticks_here, 128)
    count = ticks_here // tick_block
    table = tick_table(taps, tick_block, forward)
    shifted = jnp.stack(
        [extended[:, offset : offset + wires_here] for offset in range(wire_taps)], 1
    )
    framed = jnp.stack(
        [
            shifted[..., start * tick_block : start * tick_block + tick_block + resp_length - 1]
            for start in range(count)
        ],
        3,
    )
    result = jnp.einsum("pjwbi,pjit->pwbt", framed, table, preferred_element_type=jnp.float32)
    return result.reshape(result.shape[0], wires_here, ticks_here)


def local(charge, intersection, ovl_block, ovl_count, diff_class, response, cotangent):
    block_count, plane_count, entry_count, wire_block, cell_block = intersection.shape
    bin_count = charge.shape[1]
    owners_total = lax.axis_size("gz")
    z_index = lax.axis_index("gz")
    slab_total = lax.axis_size("drift")
    slab_index = lax.axis_index("drift")
    wires_here = cotangent.shape[1]
    ticks_here = cotangent.shape[2]
    per_owner = wires_here // wire_block
    capacity = 8 * block_count // owners_total
    half_width = (response.shape[1] - 1) // 2
    resp_length = response.shape[2]
    bins_here = bin_count // slab_total
    block_bins = math.gcd(bins_here, 16)
    row_width = wire_block * bin_count
    entry_live = jnp.arange(entry_count, dtype=jnp.int32)[None, None, :] < ovl_count[:, :, None]
    pieces = jnp.einsum(
        "bmc,bcx->bmx",
        intersection.reshape(block_count, plane_count * entry_count * wire_block, cell_block),
        charge.reshape(block_count, cell_block, bin_count),
        preferred_element_type=jnp.float32,
    )
    pieces = pieces.astype(jnp.bfloat16).reshape(block_count, plane_count, entry_count, row_width)
    local_index = ovl_block[:, 2, :].reshape(-1) - z_index * per_owner
    local_pick = (
        (local_index[None, :] == jnp.arange(per_owner)[:, None])
        & entry_live[:, 2, :].reshape(-1)[None, :]
    ).astype(jnp.bfloat16)
    local_sum = jnp.dot(
        local_pick, pieces[:, 2].reshape(-1, row_width), preferred_element_type=jnp.float32
    )
    cross_ids = ovl_block[:, :2, :].reshape(-1)
    cross_live = entry_live[:, :2, :].reshape(-1)
    cross_owner = cross_ids // per_owner
    owner_match = (
        (cross_owner[:, None] == jnp.arange(owners_total)[None, :]) & cross_live[:, None]
    ).astype(jnp.int32)
    earlier_count = jnp.cumsum(owner_match, axis=0) - owner_match
    slot_index = jnp.where(
        cross_live, cross_owner * capacity + jnp.sum(earlier_count * owner_match, axis=1), -1
    )
    slot_pick = (jnp.arange(owners_total * capacity)[:, None] == slot_index[None, :]).astype(
        jnp.bfloat16
    )
    cross_plane = jnp.broadcast_to(
        jnp.arange(2)[None, :, None], (block_count, 2, entry_count)
    ).reshape(-1)
    labels = jnp.where(
        cross_live, cross_plane * per_owner + cross_ids - cross_owner * per_owner + 1, 0
    )
    payload = jnp.dot(
        slot_pick, pieces[:, :2].reshape(-1, row_width), preferred_element_type=jnp.float32
    ).astype(jnp.bfloat16)
    slot_labels = jnp.dot(
        slot_pick, labels.astype(jnp.bfloat16)[:, None], preferred_element_type=jnp.float32
    ).astype(jnp.bfloat16)
    received, received_labels = (
        lax.all_to_all(
            payload.reshape(owners_total, capacity, row_width),
            "gz",
            split_axis=0,
            concat_axis=0,
            tiled=True,
        ),
        lax.all_to_all(
            slot_labels.reshape(owners_total, capacity),
            "gz",
            split_axis=0,
            concat_axis=0,
            tiled=True,
        ),
    )
    arrival = received_labels.reshape(-1).astype(jnp.int32) - 1
    arrival_pick = (jnp.arange(2 * per_owner)[:, None] == arrival[None, :]).astype(jnp.bfloat16)
    cross_sum = jnp.dot(
        arrival_pick, received.reshape(-1, row_width), preferred_element_type=jnp.float32
    )
    currents = jnp.concatenate([cross_sum, local_sum], 0).reshape(
        plane_count, wires_here, bin_count
    )
    class_padded = jnp.pad(diff_class.astype(jnp.float32), (HB, HB), mode="edge")
    class_local = lax.dynamic_slice_in_dim(class_padded, slab_index * bins_here, bins_here + 2 * HB)
    own_bins = lax.psum_scatter(currents, "drift", scatter_dimension=2, tiled=True)
    framed = extended_2(own_bins, (("drift", 2),), HB)
    drifted = drift_forward(framed, class_local, bins_here // block_bins, block_bins).astype(
        jnp.bfloat16
    )
    earlier = passed_along(drifted[:, :, ticks_here - (resp_length - 1) :], "drift", 1)
    extended = extended_2(jnp.concatenate([earlier, drifted], 2), (("gz", 1),), half_width)
    signal = planes_apply(extended, response, wires_here, ticks_here, True).astype(jnp.bfloat16)
    later = passed_along(cotangent[:, :, : resp_length - 1], "drift", -1)
    extended_back = extended_2(jnp.concatenate([cotangent, later], 2), (("gz", 1),), half_width)
    back_ticks = planes_apply(
        extended_back, response[:, ::-1, :], wires_here, ticks_here, False
    ).astype(jnp.bfloat16)
    spread_back = drift_backward(back_ticks, class_local, bins_here // block_bins, block_bins)
    edges = jnp.concatenate([spread_back[:, :, :HB], spread_back[:, :, -HB:]], 2)
    beside_all = extended_2(edges, (("drift", 2),), HB)
    inner = spread_back[:, :, HB : HB + bins_here]
    inner = inner.at[:, :, :HB].add(beside_all[:, :, :HB])
    inner = inner.at[:, :, bins_here - HB :].add(beside_all[:, :, 3 * HB :])
    bin_grads = lax.all_gather(inner.astype(jnp.bfloat16), "drift", axis=2, tiled=True)
    every = lax.all_gather(bin_grads, "gz", axis=1, tiled=True)
    every_rows = every.reshape(plane_count * per_owner * owners_total, row_width)
    plane_base = jnp.arange(plane_count, dtype=jnp.int32)[None, :, None] * (
        per_owner * owners_total
    )
    chosen = jnp.take(every_rows, (plane_base + ovl_block).reshape(-1), axis=0)
    chosen = jnp.where(entry_live.reshape(-1)[:, None], chosen, jnp.zeros((), jnp.bfloat16))
    chosen = chosen.reshape(block_count, plane_count * entry_count * wire_block, bin_count)
    charge_grad = jnp.einsum(
        "bmc,bmx->bcx",
        intersection.reshape(block_count, plane_count * entry_count * wire_block, cell_block),
        chosen,
        preferred_element_type=jnp.float32,
    )
    return (signal, charge_grad.reshape(block_count * cell_block, bin_count).astype(jnp.bfloat16))


def solution(mesh):
    return jax.shard_map(
        local,
        mesh=mesh,
        in_specs=(
            P(("apa", "gz", "drift"), None),
            P(("apa", "gz", "drift"), None, None, None, None),
            P(("apa", "gz", "drift"), None, None),
            P(("apa", "gz", "drift"), None),
            P("apa"),
            P(),
            P("apa", "gz", "drift"),
        ),
        out_specs=(P("apa", "gz", "drift"), P(("apa", "gz", "drift"), None)),
        check_vma=False,
    )
```

profile of v0, /device:TPU:0, one launch (start us, length us, event | category | flops | bytes accessed | tf_op | source)
XLA Modules:
  0.0 490.6 jit_solution(2786146220478637108)
XLA Ops:
  8.0 1.4 copy.280
  13.9 4.2 all-to-all-start
  23.1 111.1 %gather_fusion.1 = bf16[41856,3,21]{2,1,0:T(4,128)(2,1)} fusion(bf16[3,21,200]{1,0,2:T(4,128)(2,1)S(1)} %rev.3, s32[41984]{0:T(1024)S(1)} %get-tuple-element.54), kind=kCustom, calls=%fused_computation.1 | custom fusion | bytes 10715136 | tf_op jit(solution)/shard_map/gather | solution.py:107
  134.2 40.2 %copy.306 = bf16[327,128,3,21]{1,0,3,2:T(8,128)(2,1)} copy(bf16[327,128,3,21]{3,2,1,0:T(4,128)(2,1)} %bitcast.397) | data formatting | bytes 10547712 | tf_op jit(solution)/shard_map/gather | solution.py:107
  179.9 111.1 %gather_fusion = bf16[41856,3,21]{2,1,0:T(4,128)(2,1)} fusion(bf16[3,21,200]{1,0,2:T(4,128)(2,1)S(1)} %copy.275, s32[41984]{0:T(1024)S(1)} %get-tuple-element.55), kind=kCustom, calls=%fused_computation | custom fusion | bytes 10715136 | tf_op jit(solution)/shard_map/gather | solution.py:107
  291.0 40.2 %copy.276 = bf16[327,128,3,21]{1,0,3,2:T(8,128)(2,1)} copy(bf16[327,128,3,21]{3,2,1,0:T(4,128)(2,1)} %bitcast.398) | data formatting | bytes 10547712 | tf_op jit(solution)/shard_map/gather | solution.py:107
  333.4 2.4 collective-permute-start.6
  337.5 5.2 %all-to-all-start.1 = ((bf16[4,8,12288]{2,1,0:T(8,128)(2,1)}), bf16[4,8,12288]{2,1,0:T(8,128)(2,1)S(1)}, u32[]{:S(2)}, u32[]{:S(2)}) async-start(bf16[4,8,12288]{2,1,0:T(8,128)(2,1)} %fusion), calls=%async_computation.1 | async-start | bytes 1572864 | tf_op jit(solution)/shard_map/all_to_all | solution.py:188
  352.6 2.7 fusion.6
  355.3 2.7 fusion.5
  358.0 2.7 fusion.4
  360.7 2.6 fusion.3
  363.3 2.7 fusion.2
  366.1 2.7 fusion.1
  370.9 17.9 %fusion.29 = bf16[3,128,6,128]{3,1,0,2:T(8,128)(2,1)S(1)} fusion(bf16[3,21,128,6,327]{2,4,1,0,3:T(8,128)(2,1)} %fusion.1, bf16[327,128,3,21]{1,0,3,2:T(8,128)(2,1)} %copy.306, pred[327,128]{1,0:T(8,128)(4,1)S(1)} %fusion.101), kind=kOutput, calls=%fused_computation.47 | convolution fusion | flops 4053253120 | bytes 37548672 | tf_op jit(solution)/shard_map/pjwbi,pjit->pwbt/dot_general | solution.py:126
  389.7 4.5 collective-permute-start.8
  394.3 1.7 reduce-scatter.2.cloned.1.call-done
  396.8 2.2 collective-permute-start
  399.0 1.3 collective-permute-start.1
  401.6 2.9 collective-permute-done.1
  406.9 3.5 collective-permute-start.2
  410.4 2.7 collective-permute-done.2
  416.9 16.3 %all_gather.6 = bf16[3,128,384]{1,2,0:T(8,128)(2,1)} all-gather(bf16[3,128,96]{1,2,0:T(8,128)(2,1)S(1)} %convert_element_type.119), channel_id=1, replica_groups=mesh['apa'=2,'gz'=4,'drift'=4] {'drift'}, dimensions={2}, use_global_device_ids=true | all-gather | bytes 368640 | tf_op jit(solution)/shard_map/all_gather | solution.py:232
  442.9 3.2 fusion.12
  446.1 3.2 fusion.11
  449.4 3.4 fusion.10
  452.7 3.5 fusion.9
  456.3 3.3 fusion.8
  459.6 3.2 fusion.7
  462.8 14.2 %fusion.32 = bf16[3,128,6,128]{1,3,2,0:T(8,128)(2,1)S(1)} fusion(bf16[3,21,128,6,327]{2,4,1,3,0:T(8,128)(2,1)} %fusion.7, bf16[327,128,3,21]{1,0,3,2:T(8,128)(2,1)} %copy.276, pred[327,128]{1,0:T(8,128)(4,1)S(1)} %fusion.100), kind=kOutput, calls=%fused_computation.48 | convolution fusion | flops 4053253120 | bytes 37548672 | tf_op jit(solution)/shard_map/pjwbi,pjit->pwbt/dot_general | solution.py:126
  478.1 1.7 copy.309
  481.6 1.3 convolution_convert_fusion.3
  (183 shorter events, 51.8 us)
Async XLA Ops:
  8.0 11.3 %copy-start = (bf16[512,384]{1,0:T(8,128)(2,1)S(1)}, bf16[512,384]{1,0:T(8,128)(2,1)}, u32[]{:S(2)}) copy-start(bf16[512,384]{1,0:T(8,128)(2,1)} %param.11) | copy-start | bytes 1179652
  9.5 323.3 %collective-permute-start.5 = (bf16[3,128,199]{1,2,0:T(8,128)(2,1)S(1)}, bf16[3,128,199]{1,2,0:T(8,128)(2,1)S(1)}, u32[]{:S(2)}, u32[]{:S(2)}) collective-permute-start(bf16[3,128,199]{1,2,0:T(8,128)(2,1)S(1)} %slice.477), channel_id=1, source_target_pairs={{1,0},{2,1},{3,2},{5,4},{6,5},{7,6},{9,8},{10,9},{11,10},{13,12},{... | collective-permute-start | bytes 458504 | tf_op jit(solution)/shard_map/ppermute | solution.py:32
  13.9 323.7 %all-to-all-start = ((bf16[4,1,8]{2,1,0:T(2,128)(2,1)}), bf16[4,1,8]{2,1,0:T(2,128)(2,1)S(1)}, u32[]{:S(2)}, u32[]{:S(2)}) async-start(bf16[4,1,8]{2,1,0:T(2,128)(2,1)} %all_to_all.12), calls=%async_computation | async-start | bytes 4096 | tf_op jit(solution)/shard_map/all_to_all | solution.py:195
  134.2 40.2 %copy-start.4 = (s32[384]{0:T(512)S(1)}, s32[384]{0:T(512)}, u32[]{:S(2)}) copy-start(s32[384]{0:T(512)} %param.15) | copy-start | bytes 4612
  333.4 9.7 %collective-permute-start.6 = (bf16[3,10,967]{2,0,1:T(4,128)(2,1)S(1)}, bf16[3,10,967]{2,0,1:T(4,128)(2,1)S(1)}, u32[]{:S(2)}, u32[]{:S(2)}) collective-permute-start(bf16[3,10,967]{2,0,1:T(4,128)(2,1)S(1)} %copy.281), channel_id=1, source_target_pairs={{0,4},{4,8},{8,12},{1,5},{5,9},{9,13},{2,6},{6,10},{10,14},{3,7},{... | collective-permute-start | bytes 174068 | tf_op jit(solution)/shard_map/ppermute | solution.py:20
  336.2 7.3 %collective-permute-start.7 = (bf16[3,10,967]{2,0,1:T(4,128)(2,1)S(1)}, bf16[3,10,967]{2,0,1:T(4,128)(2,1)S(1)}, u32[]{:S(2)}, u32[]{:S(2)}) collective-permute-start(bf16[3,10,967]{2,0,1:T(4,128)(2,1)S(1)} %copy.283), channel_id=1, source_target_pairs={{4,0},{8,4},{12,8},{5,1},{9,5},{13,9},{6,2},{10,6},{14,10},{7,3},{... | collective-permute-start | bytes 174068 | tf_op jit(solution)/shard_map/ppermute | solution.py:22
  337.5 31.3 %all-to-all-start.1 = ((bf16[4,8,12288]{2,1,0:T(8,128)(2,1)}), bf16[4,8,12288]{2,1,0:T(8,128)(2,1)S(1)}, u32[]{:S(2)}, u32[]{:S(2)}) async-start(bf16[4,8,12288]{2,1,0:T(8,128)(2,1)} %fusion), calls=%async_computation.1 | async-start | bytes 1572864 | tf_op jit(solution)/shard_map/all_to_all | solution.py:188
  342.7 53.3 %reduce-scatter.2.cloned.1.call-start = ((), (), s32[]{:S(2)}) async-start(), calls=%async_computation.3 | async-start | bytes 737280 | tf_op jit(solution)/shard_map/reduce_scatter | solution.py:213
  360.7 8.3 %copy-start.2 = (f32[4,12288]{1,0:T(4,128)S(1)}, f32[4,12288]{1,0:T(4,128)}, u32[]{:S(2)}) copy-start(f32[4,12288]{1,0:T(4,128)} %fusion.133) | copy-start | bytes 589828
  370.3 107.8 %all-gather.2.cloned.1.call-start = ((), (), s32[]{:S(2)}) async-start(), calls=%async_computation.4 | async-start | bytes 1474560 | tf_op jit(solution)/shard_map/all_gather | solution.py:233
  389.7 10.6 %collective-permute-start.8 = (f32[3,128,2]{1,2,0:T(2,128)S(1)}, f32[3,128,2]{1,2,0:T(2,128)S(1)}, u32[]{:S(2)}, u32[]{:S(2)}) collective-permute-start(f32[3,128,2]{1,2,0:T(2,128)S(1)} %fusion.126), channel_id=1, source_target_pairs={{0,1},{1,2},{2,3},{4,5},{5,6},{6,7},{8,9},{9,10},{10,11},{12,13},{... | collective-permute-start | bytes 9224 | tf_op jit(solution)/shard_map/ppermute | solution.py:20
  396.8 4.9 collective-permute-start
  399.0 5.5 %collective-permute-start.1 = (f32[3,128,2]{1,2,0:T(2,128)S(1)}, f32[3,128,2]{1,2,0:T(2,128)S(1)}, u32[]{:S(2)}, u32[]{:S(2)}) collective-permute-start(f32[3,128,2]{1,2,0:T(2,128)S(1)} %get-tuple-element.49), channel_id=1, source_target_pairs={{1,0},{2,1},{3,2},{5,4},{6,5},{7,6},{9,8},{10,9},{11,10},{13,12},{... | collective-permute-start | bytes 9224 | tf_op jit(solution)/shard_map/ppermute | solution.py:22
  400.3 10.1 %collective-permute-start.9 = (f32[3,128,2]{1,2,0:T(2,128)S(1)}, f32[3,128,2]{1,2,0:T(2,128)S(1)}, u32[]{:S(2)}, u32[]{:S(2)}) collective-permute-start(f32[3,128,2]{1,2,0:T(2,128)S(1)} %get-tuple-element.44), channel_id=1, source_target_pairs={{1,0},{2,1},{3,2},{5,4},{6,5},{7,6},{9,8},{10,9},{11,10},{13,12},{... | collective-permute-start | bytes 9224 | tf_op jit(solution)/shard_map/ppermute | solution.py:22
  406.9 6.2 %collective-permute-start.2 = (bf16[3,128,199]{1,2,0:T(8,128)(2,1)S(1)}, bf16[3,128,199]{1,2,0:T(8,128)(2,1)S(1)}, u32[]{:S(2)}, u32[]{:S(2)}) collective-permute-start(bf16[3,128,199]{1,2,0:T(8,128)(2,1)S(1)} %slice.446), channel_id=1, source_target_pairs={{0,1},{1,2},{2,3},{4,5},{5,6},{6,7},{8,9},{9,10},{10,11},{12,13},{... | collective-permute-start | bytes 458504 | tf_op jit(solution)/shard_map/ppermute | solution.py:32
  413.9 19.3 %collective-permute-start.3 = (bf16[3,10,967]{2,0,1:T(4,128)(2,1)S(1)}, bf16[3,10,967]{2,0,1:T(4,128)(2,1)S(1)}, u32[]{:S(2)}, u32[]{:S(2)}) collective-permute-start(bf16[3,10,967]{2,0,1:T(4,128)(2,1)S(1)} %copy.246), channel_id=1, source_target_pairs={{0,4},{4,8},{8,12},{1,5},{5,9},{9,13},{2,6},{6,10},{10,14},{3,7},{... | collective-permute-start | bytes 174068 | tf_op jit(solution)/shard_map/ppermute | solution.py:20
  415.6 18.0 %collective-permute-start.4 = (bf16[3,10,967]{2,0,1:T(4,128)(2,1)S(1)}, bf16[3,10,967]{2,0,1:T(4,128)(2,1)S(1)}, u32[]{:S(2)}, u32[]{:S(2)}) collective-permute-start(bf16[3,10,967]{2,0,1:T(4,128)(2,1)S(1)} %copy.248), channel_id=1, source_target_pairs={{4,0},{8,4},{12,8},{5,1},{9,5},{13,9},{6,2},{10,6},{14,10},{7,3},{... | collective-permute-start | bytes 174068 | tf_op jit(solution)/shard_map/ppermute | solution.py:22
  462.8 18.8 %copy-start.3 = (bf16[4,3,2,32,128]{4,3,2,1,0:T(8,128)(2,1)S(1)}, bf16[4,3,2,32,128]{4,3,2,1,0:T(8,128)(2,1)}, u32[]{:S(2)}) copy-start(bf16[4,3,2,32,128]{4,3,2,1,0:T(8,128)(2,1)} %param.12) | copy-start | bytes 589828
  462.8 20.1 %copy-start.1 = (bf16[512,384]{1,0:T(8,128)(2,1)S(1)}, bf16[512,384]{1,0:T(8,128)(2,1)}, u32[]{:S(2)}) copy-start(bf16[512,384]{1,0:T(8,128)(2,1)} %param.11) | copy-start | bytes 1179652
Sparse Core Ops, SparseCore 0:
  370.5 25.5 reduce-scatter.1
Sparse Core Ops, SparseCore 1:
  433.3 21.5 all-gather.1
where the time goes:
time: 500 us; the launch traced here: 491 us
  local copies, waits for them, and re-layouts  374 us (75%)
  matrix products  39.2 us (8%)
  starting transfers between devices  30.6 us (6%)
  between operations  16.5 us (3%)
  blocking collectives  16.3 us (3%)
  waiting for transfers between devices  7.29 us (1%)
  other arithmetic  7.02 us (1%)
    gather x4, local copies, waits for them, and re-layouts, tick_table(): picked = taps[:, :, jnp.clip(lag, 0, resp_length - 1)]  303 us
    unnamed x63, local copies, waits for them, and re-layouts  48.5 us
    dot_general x2, matrix products, planes_apply(): jnp.einsum('pjwbi,pjit->pwbt', framed, table, preferred_element_type=jnp....  32.1 us
    all_gather x1, blocking collectives, local(): lax.all_gather(inner.astype(jnp.bfloat16), 'drift', axis=2, tiled=True)  16.3 us
    ppermute x4, starting transfers between devices, extended_2(): lax.ppermute(tail, axis, [(i, (i + 1) % count) for i in range(ends)])  10.5 us
  transfers between devices with their start and end apart: 14, of which 3 were waited for; matrix products, arithmetic and copies ran while one was open for 84% of the time, Pallas kernels for 0%

commit v1 on v0

v1 whole, which is shorter than its diff:
```python
import functools
import math

import jax
import jax.numpy as jnp
from jax import lax
from jax.experimental import pallas as pl
from jax.experimental.pallas import tpu as pltpu
from jax.sharding import PartitionSpec as P

TPB = 8
HB = 2
CLASSES = 6
LANES = 128
EDGE = 16
GROUP = 8
WINDOW = 64
LEAD = HB * TPB - TPB // 2
VMEM_LIMIT = 48 * 1024 * 1024
BF16 = jnp.bfloat16
F32 = jnp.float32


def params(semantics=None):
    return pltpu.CompilerParams(vmem_limit_bytes=VMEM_LIMIT, dimension_semantics=semantics)


def vmem():
    return pl.BlockSpec(memory_space=pltpu.VMEM)


def smem():
    return pl.BlockSpec(memory_space=pltpu.SMEM)


def cost(flops, moved):
    return pl.CostEstimate(flops=int(flops), bytes_accessed=int(moved), transcendentals=0)


def swap(block, axis, distance):
    count = lax.axis_size(axis)
    return lax.ppermute(block, axis, [(i, i ^ distance) for i in range(count)])


def widths(number):
    spread = TPB * (0.2 + 0.15 * number)
    half = HB * TPB
    total = sum(math.exp(-((j + 0.5) ** 2) / (2.0 * spread * spread)) for j in range(-half, half))
    return 1.0 / (2.0 * spread * spread), 1.0 / total


def shared_lanes(left, right, shift, lane):
    if shift == 0:
        return left
    back = LANES - shift
    return jnp.where(lane < back, pltpu.roll(left, back, 1), pltpu.roll(right, back, 1))


def table_kernel(class_ref, response_ref, table_ref, taps_ref, smeared_ref, *, tiles, blocks, bins):
    planes, wire_taps, length = response_ref.shape
    plane = pl.program_id(0)
    reach = taps_ref.shape[1]
    rows = taps_ref.shape[0] // planes
    first = lax.axis_index("drift") * bins - (WINDOW // 2 - HB)

    @pl.when(plane == 0)
    def _():
        taps_ref[...] = jnp.zeros(taps_ref.shape, F32)
        for p in range(planes):
            taps_ref[p * rows : p * rows + wire_taps, :length] = response_ref[p].astype(F32)
        taps = taps_ref[...].astype(BF16)
        tap = lax.broadcasted_iota(jnp.int32, (reach, reach), 0)
        tick = lax.broadcasted_iota(jnp.int32, (reach, reach), 1)
        step = tick - tap - LEAD
        offset = step.astype(F32) - (TPB - 1) / 2.0
        squared = offset * offset
        inside = jnp.abs(offset) < HB * TPB
        for kind in range(CLASSES + HB):
            keep = inside
            if kind < CLASSES:
                narrow, scale = widths(kind)
            else:
                edge = kind - CLASSES
                narrow, scale = widths(0)
                for number in range(1, CLASSES):
                    chosen = class_ref[edge] == number
                    narrow = jnp.where(chosen, widths(number)[0], narrow)
                    scale = jnp.where(chosen, widths(number)[1], scale)
                keep = inside & (step >= -TPB * edge)
            smear = jnp.where(keep, jnp.exp(-(squared * narrow)) * scale, 0.0)
            high = smear.astype(BF16)
            low = (smear - high.astype(F32)).astype(BF16)
            smeared_ref[kind] = jnp.dot(taps, high, preferred_element_type=F32) + jnp.dot(
                taps, low, preferred_element_type=F32
            )

    lane = lax.broadcasted_iota(jnp.int32, (GROUP, LANES), 1)
    row = lax.broadcasted_iota(jnp.int32, (GROUP, LANES), 0)
    groups = (bins + WINDOW // 2) // GROUP
    last = class_ref.shape[0] - 1
    kinds = []
    for m in range(groups):
        kind = jnp.zeros((GROUP, LANES), jnp.int32)
        for i in range(GROUP):
            x = first + m * GROUP + i
            number = class_ref[jnp.clip(x, 0, last)]
            number = jnp.where((x >= 0) & (x < HB), CLASSES + x, number)
            kind = jnp.where(row == i, number, kind)
        kinds.append(kind)
    edge_group = (WINDOW // 2 - HB) // GROUP
    starts = [LEAD_SHIFT + odd * (LANES // 2) + TPB * row for odd in range(2)]
    after = [lane >= start for start in starts]
    zero = jnp.zeros((GROUP, LANES), F32)
    empty = jnp.zeros((2 * GROUP, LANES), BF16)

    def body(a, _):
        line = plane * rows + a
        levels = []
        for kind in range(CLASSES + HB):
            values = smeared_ref[kind, pl.ds(line, 1), :]
            levels.append(
                [
                    jnp.broadcast_to(values[:, part * LANES : (part + 1) * LANES], (GROUP, LANES))
                    for part in range(2)
                ]
            )
        pieces = {}
        for m in range(groups):
            odd = m % 2
            parts = []
            for part in range(2):
                picked = levels[0][part]
                for kind in range(1, CLASSES + (HB if m == edge_group else 0)):
                    picked = jnp.where(kinds[m] == kind, levels[kind][part], picked)
                parts.append(
                    pltpu.roll(
                        picked, LEAD_SHIFT + odd * (LANES // 2), 1, stride=TPB, stride_axis=0
                    )
                )
            pieces[m] = (
                jnp.where(after[odd], parts[0], zero),
                jnp.where(after[odd], parts[1], parts[0]),
                jnp.where(after[odd], zero, parts[1]),
            )
        for block in range(blocks):
            for quarter in range(WINDOW // (2 * GROUP)):
                m = 2 * (tiles * block + quarter)
                at = pl.ds(pl.multiple_of(a * WINDOW + quarter * 2 * GROUP, 2 * GROUP), 2 * GROUP)
                for tile in range(tiles):
                    third = tile - quarter + 2
                    if 0 <= third <= 2 and m + 1 < groups:
                        value = jnp.concatenate(
                            [pieces[m][third], pieces[m + 1][third]], axis=0
                        ).astype(BF16)
                    else:
                        value = empty
                    table_ref[0, block, at, tile * LANES : (tile + 1) * LANES] = value
        return 0

    lax.fori_loop(0, wire_taps, body, 0)
    spare = table_ref.shape[2] - wire_taps * WINDOW
    for block in range(blocks):
        table_ref[0, block, wire_taps * WINDOW :, :] = jnp.zeros(
            (spare, tiles * LANES), BF16
        )


LEAD_SHIFT = (TPB * HB - LEAD) % LANES


def build_table(diff_class, response, ticks_here, bins):
    planes, wire_taps, length = response.shape
    tiles = math.gcd(ticks_here, 2 * LANES) // LANES
    blocks = ticks_here // (tiles * LANES)
    reach = 2 * LANES
    rows = -(-wire_taps // 8) * 8
    depth = (wire_taps + wire_taps % 2) * WINDOW
    shape = (planes, blocks, depth, tiles * LANES)
    return pl.pallas_call(
        functools.partial(table_kernel, tiles=tiles, blocks=blocks, bins=bins),
        grid=(planes,),
        out_shape=jax.ShapeDtypeStruct(shape, BF16),
        in_specs=[smem(), pl.BlockSpec(response.shape, lambda p: (0, 0, 0))],
        out_specs=pl.BlockSpec((1,) + shape[1:], lambda p: (p, 0, 0, 0)),
        scratch_shapes=[
            pltpu.VMEM((planes * rows, reach), F32),
            pltpu.VMEM((CLASSES + HB, planes * rows, reach), F32),
        ],
        compiler_params=params(("arbitrary",)),
        cost_estimate=cost(4e9, 2 * math.prod(shape)),
        name="table",
    )(diff_class, response)


def back_kernel(table_ref, own_ref, low_ref, high_ref, out_ref, cot_ref, wide_ref, sum_ref, *, wire_taps):
    blocks, span = table_ref.shape[1], table_ref.shape[3]
    wires = own_ref.shape[1]
    half = (wire_taps - 1) // 2
    cot_ref[:EDGE] = low_ref[0]
    cot_ref[EDGE : EDGE + wires] = own_ref[0]
    cot_ref[EDGE + wires :] = high_ref[0]
    sum_ref[...] = jnp.zeros(sum_ref.shape, F32)
    depth = wire_taps * WINDOW
    extent = cot_ref.shape[0]
    lane = lax.broadcasted_iota(jnp.int32, (WINDOW, LANES), 1)
    step = span * 16 // LANES
    for block in range(blocks):
        wide_ref[:, :extent] = lax.dot_general(
            table_ref[0, block, :depth],
            cot_ref[:, block * span : (block + 1) * span],
            (((1,), (1,)), ((), ())),
            preferred_element_type=F32,
        )
        total = sum_ref[block * step : block * step + WINDOW]
        for a in range(wire_taps):
            part = wide_ref[a * WINDOW : (a + 1) * WINDOW, :]
            total += shared_lanes(
                part[:, :LANES], part[:, LANES:], EDGE + half - a, lane
            )
        sum_ref[block * step : block * step + WINDOW] = total
    out_ref[0] = sum_ref[: out_ref.shape[1], :wires].astype(BF16)


def backward(table, cotangent, low, high, wire_taps, bins):
    planes, blocks, depth, span = table.shape
    _, wires, ticks = cotangent.shape
    extent = wires + 2 * EDGE
    window = bins + WINDOW // 2
    sums = (blocks - 1) * (span * 16 // LANES) + WINDOW
    edge = pl.BlockSpec((1, EDGE, ticks), lambda p: (p, 0, 0))
    return pl.pallas_call(
        functools.partial(back_kernel, wire_taps=wire_taps),
        grid=(planes,),
        out_shape=jax.ShapeDtypeStruct((planes, window, wires), BF16),
        in_specs=[
            pl.BlockSpec((1, blocks, depth, span), lambda p: (p, 0, 0, 0)),
            pl.BlockSpec((1, wires, ticks), lambda p: (p, 0, 0)),
            edge,
            edge,
        ],
        out_specs=pl.BlockSpec((1, window, wires), lambda p: (p, 0, 0)),
        scratch_shapes=[
            pltpu.VMEM((extent, ticks), BF16),
            pltpu.VMEM((wire_taps * WINDOW, 2 * LANES), F32),
            pltpu.VMEM((sums, LANES), F32),
        ],
        compiler_params=params(("arbitrary",)),
        cost_estimate=cost(4e9, 2 * math.prod(table.shape)),
        name="bin_gradients",
    )(table, cotangent, low, high)


def merge_kernel(*refs, bins, lead):
    parts, (cross_ref, local_ref, sum_ref) = refs[:-3], refs[-3:]
    planes, window, wires = parts[0].shape
    total = local_ref.shape[1]
    slab = lax.axis_index("drift")
    sum_ref[...] = jnp.zeros(sum_ref.shape, F32)
    for k, part in enumerate(parts):
        at = pl.ds(pl.multiple_of((slab ^ k) * bins, 8), window)
        for p in range(planes):
            sum_ref[p, at, :wires] += part[p].astype(F32)
    for p in range(planes):
        for tile in range(total // LANES):
            turned = sum_ref[p, lead + tile * LANES : lead + (tile + 1) * LANES, :].T
            here = slice(tile * LANES, (tile + 1) * LANES)
            if p < planes - 1:
                cross_ref[p, :, here] = turned[:wires].astype(BF16)
            else:
                local_ref[:, here] = turned[:wires].astype(BF16)


def merge(parts, bins, total):
    planes, window, wires = parts[0].shape
    lead = WINDOW // 2 - HB
    return pl.pallas_call(
        functools.partial(merge_kernel, bins=bins, lead=lead),
        out_shape=(
            jax.ShapeDtypeStruct((planes - 1, wires, total), BF16),
            jax.ShapeDtypeStruct((wires, total), BF16),
        ),
        in_specs=[vmem()] * len(parts),
        out_specs=(vmem(), vmem()),
        scratch_shapes=[pltpu.VMEM((planes, total + WINDOW // 2, LANES), F32)],
        compiler_params=params(),
        cost_estimate=cost(1e8, 4 * planes * wires * total),
        name="merge_bins",
    )(*parts)


def charge_kernel(block_ref, count_ref, cross_ref, local_ref, share_ref, out_ref, chosen_ref):
    cells, planes, entries, wire_block, width = share_ref.shape
    per_owner = cross_ref.shape[2] // wire_block
    owners = cross_ref.shape[0]
    z = lax.axis_index("gz")
    empty = jnp.zeros((wire_block, out_ref.shape[1]), BF16)
    for b in range(cells):
        for p in range(planes):
            for k in range(entries):
                name = block_ref[b, p, k]
                if p < planes - 1:
                    name = jnp.clip(name, 0, owners * per_owner - 1)
                    owner = name // per_owner
                    start = pl.multiple_of((name - owner * per_owner) * wire_block, wire_block)
                    rows = cross_ref[owner, p, pl.ds(start, wire_block), :]
                else:
                    name = jnp.clip(name - z * per_owner, 0, per_owner - 1)
                    start = pl.multiple_of(name * wire_block, wire_block)
                    rows = local_ref[pl.ds(start, wire_block), :]
                at = ((b * planes + p) * entries + k) * wire_block
                chosen_ref[at : at + wire_block] = jnp.where(k < count_ref[b, p], rows, empty)
    depth = planes * entries * wire_block
    for b in range(cells):
        out_ref[b * width : (b + 1) * width] = lax.dot_general(
            share_ref[b].reshape(depth, width),
            chosen_ref[b * depth : (b + 1) * depth],
            (((0,), (0,)), ((), ())),
            preferred_element_type=F32,
        ).astype(BF16)


def charge_gradient(ovl_block, ovl_count, cross, local, intersection):
    cells, planes, entries, wire_block, width = intersection.shape
    total = local.shape[1]
    return pl.pallas_call(
        charge_kernel,
        out_shape=jax.ShapeDtypeStruct((cells * width, total), BF16),
        in_specs=[smem(), smem(), vmem(), vmem(), vmem()],
        out_specs=vmem(),
        scratch_shapes=[pltpu.VMEM((cells * planes * entries * wire_block, total), BF16)],
        compiler_params=params(),
        cost_estimate=cost(1e8, 2 * math.prod(cross.shape)),
        name="charge_gradient",
    )(ovl_block, ovl_count, cross, local, intersection)


def pieces_kernel(block_ref, count_ref, charge_ref, share_ref, keep_ref, give_ref, local_ref, cross_ref):
    cells, planes, entries, wire_block, width = share_ref.shape
    wires, total = local_ref.shape
    per_owner = wires // wire_block
    owners = 2 * keep_ref.shape[0]
    z = lax.axis_index("gz")
    cross_ref[...] = jnp.zeros(cross_ref.shape, F32)
    local_ref[...] = jnp.zeros(local_ref.shape, F32)
    depth = planes * entries * wire_block
    for b in range(cells):
        pieces = (
            jnp.dot(
                share_ref[b].reshape(depth, width),
                charge_ref[b * width : (b + 1) * width],
                preferred_element_type=F32,
            )
            .astype(BF16)
            .astype(F32)
        )
        for p in range(planes):
            for k in range(entries):
                at = (p * entries + k) * wire_block
                piece = pieces[at : at + wire_block]
                piece = jnp.where(k < count_ref[b, p], piece, jnp.zeros_like(piece))
                name = block_ref[b, p, k]
                if p < planes - 1:
                    name = jnp.clip(name, 0, owners * per_owner - 1)
                    start = pl.multiple_of(EDGE + name * wire_block, EDGE)
                    cross_ref[p, pl.ds(start, wire_block)] += piece
                else:
                    name = jnp.clip(name - z * per_owner, 0, per_owner - 1)
                    start = pl.multiple_of(name * wire_block, wire_block)
                    local_ref[pl.ds(start, wire_block)] += piece
    extent = wires + 2 * EDGE
    edge = (planes - 1) * extent
    none = jnp.zeros((EDGE, total), F32)
    for k in range(owners):
        to = z ^ k
        out = (give_ref if k % 2 else keep_ref).at[k // 2]
        for p in range(planes - 1):
            rows = cross_ref[p, pl.ds(pl.multiple_of(to * wires, EDGE), extent)]
            out[p * extent : (p + 1) * extent] = rows.astype(BF16)
        below = jnp.where(to == z + 1, local_ref[wires - EDGE :], none)
        above = jnp.where(to == z - 1, local_ref[:EDGE], none)
        out[edge : edge + EDGE] = below.astype(BF16)
        out[edge + EDGE : edge + 2 * EDGE] = above.astype(BF16)


def cut_pieces(ovl_block, ovl_count, charge, intersection, wires, owners):
    cells, planes, entries, wire_block, width = intersection.shape
    total = charge.shape[1]
    rows = (planes - 1) * (wires + 2 * EDGE) + 2 * EDGE
    cut = jax.ShapeDtypeStruct((owners // 2, rows, total), BF16)
    return pl.pallas_call(
        pieces_kernel,
        out_shape=(cut, cut, jax.ShapeDtypeStruct((wires, total), F32)),
        in_specs=[smem(), smem(), vmem(), vmem()],
        out_specs=(vmem(), vmem(), vmem()),
        scratch_shapes=[pltpu.VMEM((planes - 1, owners * wires + 2 * EDGE, total), F32)],
        compiler_params=params(),
        cost_estimate=cost(1e8, 4 * owners * rows * total),
        name="pieces",
    )(ovl_block, ovl_count, charge, intersection)


def slabs_kernel(*refs, bins, lead, slabs):
    count = len(refs) - slabs - 1
    parts, local_ref = refs[: count - 1], refs[count - 1]
    outs, cut_ref = refs[count:-1], refs[-1]
    wires, total = local_ref.shape
    extent = wires + 2 * EDGE
    summed = parts[0][...].astype(F32)
    for part in parts[1:]:
        summed += part[...].astype(F32)
    summed = summed.reshape(summed.shape[-2:])
    edge = summed.shape[0] - 2 * EDGE
    rows = jnp.concatenate(
        [summed[:edge], summed[edge : edge + EDGE], local_ref[...], summed[edge + EDGE :]], axis=0
    )
    none = jnp.zeros((rows.shape[0], LANES), F32)
    lane = lax.broadcasted_iota(jnp.int32, none.shape, 1)
    tiles = [rows[:, t * LANES : (t + 1) * LANES] for t in range(total // LANES)]
    for to in range(slabs):
        at = to * bins - lead
        tile, shift = at // LANES, at % LANES
        pair = [tiles[t] if 0 <= t < len(tiles) else none for t in (tile, tile + 1)]
        cut_ref[to] = shared_lanes(pair[0], pair[1], shift, lane).astype(BF16)
    slab = lax.axis_index("drift")
    for k, out in enumerate(outs):
        out[...] = cut_ref[slab ^ k]


def cut_slabs(keep, received, others, local, bins, slabs):
    wires, total = local.shape
    rows = keep.shape[1] + wires
    lead = WINDOW // 2 - HB
    block = pl.BlockSpec((1,) + keep.shape[1:], lambda i: (0, 0, 0))
    cut = jax.ShapeDtypeStruct((rows, LANES), BF16)
    return pl.pallas_call(
        functools.partial(slabs_kernel, bins=bins, lead=lead, slabs=slabs),
        grid=(1,),
        out_shape=(cut,) * slabs,
        in_specs=[block, block]
        + [pl.BlockSpec(other.shape, lambda i: (0, 0)) for other in others]
        + [pl.BlockSpec(local.shape, lambda i: (0, 0))],
        out_specs=(pl.BlockSpec(cut.shape, lambda i: (0, 0)),) * slabs,
        scratch_shapes=[pltpu.VMEM((slabs, rows, LANES), BF16)],
        compiler_params=params(("arbitrary",)),
        cost_estimate=cost(1e8, 4 * rows * total),
        name="slab_currents",
    )(keep, received, *others, local)


def signal_kernel(*refs, wire_taps):
    parts, (table_ref, out_ref, even_ref, odd_ref, lines_ref) = refs[:-5], refs[-5:]
    blocks, span = table_ref.shape[1], table_ref.shape[3]
    wires = out_ref.shape[1]
    half = (wire_taps - 1) // 2
    step = span * 16 // LANES
    currents = parts[0][...].astype(F32)
    for part in parts[1:]:
        currents += part[...].astype(F32)
    lane = lax.broadcasted_iota(jnp.int32, (wires, LANES), 1)
    for block in range(blocks):
        even_ref[...] = pltpu.roll(currents, (-step * block) % LANES, 1)
        odd_ref[...] = pltpu.roll(currents, (WINDOW - step * block) % LANES, 1)
        for pair in range((wire_taps + 1) // 2):
            at = EDGE - half + 2 * pair
            line = jnp.where(
                lane < WINDOW, even_ref[at : at + wires], odd_ref[at + 1 : at + 1 + wires]
            )
            lines_ref[:, pair * LANES : (pair + 1) * LANES] = line.astype(BF16)
        out_ref[0, :, block * span : (block + 1) * span] = jnp.dot(
            lines_ref[...], table_ref[0, block], preferred_element_type=F32
        ).astype(BF16)


def forward(parts, table, wires, wire_taps):
    planes, blocks, depth, span = table.shape
    extent = wires + 2 * EDGE
    part = pl.BlockSpec((extent, LANES), lambda p: (p, 0))
    return pl.pallas_call(
        functools.partial(signal_kernel, wire_taps=wire_taps),
        grid=(planes,),
        out_shape=jax.ShapeDtypeStruct((planes, wires, blocks * span), BF16),
        in_specs=[part] * len(parts)
        + [pl.BlockSpec((1, blocks, depth, span), lambda p: (p, 0, 0, 0))],
        out_specs=pl.BlockSpec((1, wires, blocks * span), lambda p: (p, 0, 0)),
        scratch_shapes=[
            pltpu.VMEM((extent, LANES), F32),
            pltpu.VMEM((extent, LANES), F32),
            pltpu.VMEM((wires, depth), BF16),
        ],
        compiler_params=params(("arbitrary",)),
        cost_estimate=cost(4e9, 2 * math.prod(table.shape)),
        name="signal",
    )(*parts, table)


def local(charge, intersection, ovl_block, ovl_count, diff_class, response, cotangent):
    total = charge.shape[1]
    owners = lax.axis_size("gz")
    slabs = lax.axis_size("drift")
    _, wires, ticks = cotangent.shape
    wire_taps = response.shape[1]
    bins = total // slabs

    up = [(i, i + 1) for i in range(owners - 1)]
    down = [(i + 1, i) for i in range(owners - 1)]
    low = lax.ppermute(cotangent[:, wires - EDGE :], "gz", up)
    high = lax.ppermute(cotangent[:, :EDGE], "gz", down)

    keep, give, local_currents = cut_pieces(
        ovl_block, ovl_count, charge, intersection, wires, owners
    )
    received = swap(give, "gz", 1)

    table = build_table(diff_class, response, ticks, bins)
    partial = backward(table, cotangent, low, high, wire_taps, bins)

    others = []
    if owners > 2:
        sums = (keep[1:].astype(F32) + received[1:].astype(F32)).astype(BF16)
        others = [swap(sums[j - 1], "gz", 2 * j) for j in range(1, owners // 2)]

    spread = [partial] + [swap(partial, "drift", k) for k in range(1, slabs)]
    cross, own = merge(spread, bins, total)
    every = lax.all_gather(cross, "gz", axis=0)
    charge_grad = charge_gradient(ovl_block, ovl_count, every, own, intersection)

    cuts = cut_slabs(keep, received, others, local_currents, bins, slabs)
    windows = [cuts[0]] + [swap(cuts[k], "drift", k) for k in range(1, slabs)]
    signal = forward(windows, table, wires, wire_taps)
    return signal, charge_grad


def solution(mesh):
    return jax.shard_map(
        local,
        mesh=mesh,
        in_specs=(
            P(("apa", "gz", "drift"), None),
            P(("apa", "gz", "drift"), None, None, None, None),
            P(("apa", "gz", "drift"), None, None),
            P(("apa", "gz", "drift"), None),
            P("apa"),
            P(),
            P("apa", "gz", "drift"),
        ),
        out_specs=(P("apa", "gz", "drift"), P(("apa", "gz", "drift"), None)),
        check_vma=False,
    )
```

time: 500 us -> 65.7 us (0.13); the launches traced: 491 us -> 65.2 us
  local copies, waits for them, and re-layouts: 374 us -> 5.79 us
  matrix products: 39.2 us -> 0 us
  Pallas kernels: 0 us -> 25.9 us
  between operations: 16.5 us -> 0.74 us
  starting transfers between devices: 30.6 us -> 17.7 us
  blocking collectives: 16.3 us -> 8.24 us
  other arithmetic: 7.02 us -> 0.07 us
    gather x6 -> x0, local copies, waits for them, and re-layouts: 304 us -> none  [the longest x4 303 us: tick_table(): picked = taps[:, :, jnp.clip(lag, 0, resp_length - 1)]]
    unnamed x63 -> x17, local copies, waits for them, and re-layouts: 48.5 us -> 4.85 us
    dot_general x10 -> x0, matrix products: 39.2 us -> none  [the longest x2 32.1 us: planes_apply(): jnp.einsum('pjwbi,pjit->pwbt', framed, table, preferred_element_type=jnp....]
    pallas_call x0 -> x7, Pallas kernels: none -> 25.9 us  [the longest x1 10.8 us: build_table(): pl.pallas_call(functools.partial(table_kernel, tiles=tiles, blocks=blocks...]
    all_to_all x2 -> x0, starting transfers between devices: 9.36 us -> none  [the longest x1 5.16 us: local(): lax.all_to_all(payload.reshape(owners_total, capacity, row_width), 'gz',...]
    all_gather x1, blocking collectives: 16.3 us -> 8.24 us  [local(): every = lax.all_gather(cross, 'gz', axis=0)]
    another operation x5 -> x0, local copies, waits for them, and re-layouts: 6.81 us -> none  [the longest x2 5.97 us: planes_apply(): jnp.stack([shifted[..., start * tick_block:start * tick_block + tick_bloc...]
  transfers between devices with their start and end apart: 14 -> 10, of which waited for: 3 -> 2; matrix products, arithmetic and copies ran while one was open for 84% -> 2% of each run, Pallas kernels for 0% -> 29%
where the time goes in v1:
time: 65.7 us; the launch traced here: 65.2 us
  Pallas kernels  25.9 us (39%)
  starting transfers between devices  17.7 us (27%)
  blocking collectives  8.24 us (13%)
  waiting for transfers between devices  6.77 us (10%)
  local copies, waits for them, and re-layouts  5.79 us (9%)
  between operations  0.74 us (1%)
    ppermute x8, starting transfers between devices, swap(): return lax.ppermute(block, axis, [(i, i ^ distance) for i in range(count)])  14.3 us
    pallas_call x1, Pallas kernels, build_table(): pl.pallas_call(functools.partial(table_kernel, tiles=tiles, blocks=blocks...  10.8 us
    all_gather x1, blocking collectives, local(): every = lax.all_gather(cross, 'gz', axis=0)  8.24 us
    ppermute x8, waiting for transfers between devices, swap(): return lax.ppermute(block, axis, [(i, i ^ distance) for i in range(count)])  6.77 us
    pallas_call x1, Pallas kernels, backward(): pl.pallas_call(functools.partial(back_kernel, wire_taps=wire_taps), grid=...  6 us
    pallas_call x1, Pallas kernels, forward(): pl.pallas_call(functools.partial(signal_kernel, wire_taps=wire_taps), gri...  5.38 us
    unnamed x17, local copies, waits for them, and re-layouts  4.85 us
    ppermute x1, starting transfers between devices, local(): low = lax.ppermute(cotangent[:, wires - EDGE:], 'gz', up)  1.96 us
  transfers between devices with their start and end apart: 10, of which 2 were waited for; matrix products, arithmetic and copies ran while one was open for 2% of the time, Pallas kernels for 29%

profile of v1, /device:TPU:0, one launch (start us, length us, event | category | flops | bytes accessed | tf_op | source)
XLA Modules:
  0.0 65.2 jit_solution(12032475840815983957)
XLA Ops:
  0.6 0.8 %copy.11.block_ref = s32[4,3,2]{2,1,0:T(4,128)S(1)} copy(s32[4,3,2]{0,2,1:T(2,128)} %param.9) | data formatting | bytes 192 | tf_op args[2]
  1.4 0.9 %copy-done = bf16[4,3,2,32,128]{4,3,2,1,0:T(8,128)(2,1)S(1)} copy-done((bf16[4,3,2,32,128]{4,3,2,1,0:T(8,128)(2,1)S(1)}, bf16[4,3,2,32,128]{4,3,2,1,0:T(8,128)(2,1)}, u32[]{:S(2)}) %copy-start) | copy-done | bytes 196632
  2.3 1.0 %copy-done.2 = bf16[512,384]{1,0:T(8,128)(2,1)S(1)} copy-done((bf16[512,384]{1,0:T(8,128)(2,1)S(1)}, bf16[512,384]{1,0:T(8,128)(2,1)}, u32[]{:S(2)}) %copy-start.2) | copy-done | bytes 393240
  3.3 0.7 %copy-done.4 = s32[4,3]{1,0:T(4,128)S(1)} copy-done((s32[4,3]{1,0:T(4,128)S(1)}, s32[4,3]{1,0:T(4,128)}, u32[]{:S(2)}) %copy-start.4) | copy-done | bytes 72
  4.0 1.1 %pieces.1 = (bf16[2,352,384]{2,1,0:T(8,128)(2,1)S(1)}, bf16[2,352,384]{2,1,0:T(8,128)(2,1)S(1)}, f32[128,384]{1,0:T(8,128)S(1)}) custom-call(s32[4,3,2]{2,1,0:T(4,128)S(1)} %copy.11.block_ref, s32[4,3]{1,0:T(4,128)S(1)} %copy-done.4, bf16[512,384]{1,0:T(8,128)(2,1)S(1)} %copy-done.2, bf16[4,3,2,32,128]{4,3,2,1,0:T(8,128)(2,1)S(1)} %copy-done), custom_call_target="tpu_custom_call" | custom-call | flops 100000000 | bytes 2162688 | tf_op jit(solution)/shard_map/pieces/pallas_call | solution.py:390
  5.2 0.5 collective-permute-start
  5.7 0.9 %fusion.1 = (bf16[3,16,768]{2,1,0:T(8,128)(2,1)S(1)}, bf16[3,16,768]{2,1,0:T(8,128)(2,1)S(1)}) fusion(bf16[3,128,768]{2,1,0:T(8,128)(2,1)} %own_ref.1), kind=kLoop, calls=%fused_computation.2 | loop fusion | bytes 294912 | tf_op jit(solution)/shard_map/slice | solution.py:507
  6.6 2.0 %collective-permute-start.5 = (bf16[3,16,768]{2,1,0:T(8,128)(2,1)S(1)}, bf16[3,16,768]{2,1,0:T(8,128)(2,1)S(1)}, u32[]{:S(2)}, u32[]{:S(2)}) collective-permute-start(bf16[3,16,768]{2,1,0:T(8,128)(2,1)S(1)} %get-tuple-element.21), channel_id=1, source_target_pairs={{0,4},{4,8},{8,12},{1,5},{5,9},{9,13},{2,6},{6,10},{10,14},{3,7},{... | collective-permute-start | bytes 221192 | tf_op jit(solution)/shard_map/ppermute | solution.py:506
  8.6 0.0 copy-start.3
  8.6 1.4 %collective-permute-start.6 = (bf16[3,16,768]{2,1,0:T(8,128)(2,1)S(1)}, bf16[3,16,768]{2,1,0:T(8,128)(2,1)S(1)}, u32[]{:S(2)}, u32[]{:S(2)}) collective-permute-start(bf16[3,16,768]{2,1,0:T(8,128)(2,1)S(1)} %get-tuple-element.20), channel_id=1, source_target_pairs={{4,0},{8,4},{12,8},{5,1},{9,5},{13,9},{6,2},{10,6},{14,10},{7,3},{... | collective-permute-start | bytes 221192 | tf_op jit(solution)/shard_map/ppermute | solution.py:507
  10.0 0.0 copy-start.6
  10.1 0.8 %copy-done.6 = bf16[3,21,200]{2,1,0:T(8,128)(2,1)S(1)} copy-done((bf16[3,21,200]{2,1,0:T(8,128)(2,1)S(1)}, bf16[3,21,200]{2,1,0:T(8,128)(2,1)}, u32[]{:S(2)}) %copy-start.6) | copy-done | bytes 25224
  10.8 0.7 %copy-done.7 = s32[384]{0:T(512)S(1)} copy-done((s32[384]{0:T(512)S(1)}, s32[384]{0:T(512)}, u32[]{:S(2)}) %copy-start.7) | copy-done | bytes 1560
  11.5 10.8 %table.1.refs_4_.table_ref = bf16[3,3,1408,256]{3,2,1,0:T(8,128)(2,1)} custom-call(s32[384]{0:T(512)S(1)} %copy-done.7, bf16[3,21,200]{2,1,0:T(8,128)(2,1)S(1)} %copy-done.6), custom_call_target="tpu_custom_call" | custom-call | flops 4000000000 | bytes 6488064 | tf_op jit(solution)/shard_map/table/pallas_call | solution.py:179
  22.3 0.1 fusion
  22.4 0.0 copy-start.1
  22.4 0.0 copy-start.5
  22.4 4.9 %collective-permute-start.1 = (bf16[352,384]{1,0:T(8,128)(2,1)S(1)}, bf16[352,384]{1,0:T(8,128)(2,1)S(1)}, u32[]{:S(2)}, u32[]{:S(2)}) collective-permute-start(bf16[352,384]{1,0:T(8,128)(2,1)S(1)} %fusion), channel_id=1, source_target_pairs={{0,8},{4,12},{8,0},{12,4},{1,9},{5,13},{9,1},{13,5},{2,10},{6,14},... | collective-permute-start | bytes 811016 | tf_op jit(solution)/shard_map/ppermute | solution.py:42
  27.3 6.0 %bin_gradients.1.refs_0_ = bf16[3,128,128]{2,1,0:T(8,128)(2,1)S(1)} custom-call(bf16[3,3,1408,256]{3,2,1,0:T(8,128)(2,1)} %table.1.refs_4_.table_ref, bf16[3,128,768]{2,1,0:T(8,128)(2,1)S(1)} %copy-done.3, bf16[3,16,768]{2,1,0:T(8,128)(2,1)S(1)} %collective-permute-done.5.low_ref, bf16[3,16,768]{2,1,0:T(8,128)(2,1)S(1)} %collective-permute-done.6.high_ref), custom_call_target="tpu_custom_call" | custom-call | flops 4000000000 | bytes 6488064 | tf_op jit(solution)/shard_map/bin_gradients/pallas_call | solution.py:231
  33.3 1.6 %collective-permute-start.7 = (bf16[3,128,128]{2,1,0:T(8,128)(2,1)S(1)}, bf16[3,128,128]{2,1,0:T(8,128)(2,1)S(1)}, u32[]{:S(2)}, u32[]{:S(2)}) collective-permute-start(bf16[3,128,128]{2,1,0:T(8,128)(2,1)S(1)} %bin_gradients.1.refs_0_), channel_id=1, source_target_pairs={{0,1},{1,0},{2,3},{3,2},{4,5},{5,4},{6,7},{7,6},{8,9},{9,8},{10,11... | collective-permute-start | bytes 294920 | tf_op jit(solution)/shard_map/ppermute | solution.py:42
  35.0 2.6 %collective-permute-start.8 = (bf16[3,128,128]{2,1,0:T(8,128)(2,1)S(1)}, bf16[3,128,128]{2,1,0:T(8,128)(2,1)S(1)}, u32[]{:S(2)}, u32[]{:S(2)}) collective-permute-start(bf16[3,128,128]{2,1,0:T(8,128)(2,1)S(1)} %bin_gradients.1.refs_0_), channel_id=1, source_target_pairs={{0,2},{1,3},{2,0},{3,1},{4,6},{5,7},{6,4},{7,5},{8,10},{9,11},{10,... | collective-permute-start | bytes 294920 | tf_op jit(solution)/shard_map/ppermute | solution.py:42
  37.5 0.2 collective-permute-start.9
  37.8 1.2 %collective-permute-done.7.refs_1_ = bf16[3,128,128]{2,1,0:T(8,128)(2,1)S(1)} collective-permute-done((bf16[3,128,128]{2,1,0:T(8,128)(2,1)S(1)}, bf16[3,128,128]{2,1,0:T(8,128)(2,1)S(1)}, u32[]{:S(2)}, u32[]{:S(2)}) %collective-permute-start.7) | collective-permute-done | bytes 98336 | tf_op jit(solution)/shard_map/ppermute | solution.py:42
  39.0 5.5 %collective-permute-done.8.refs_2_ = bf16[3,128,128]{2,1,0:T(8,128)(2,1)S(1)} collective-permute-done((bf16[3,128,128]{2,1,0:T(8,128)(2,1)S(1)}, bf16[3,128,128]{2,1,0:T(8,128)(2,1)S(1)}, u32[]{:S(2)}, u32[]{:S(2)}) %collective-permute-start.8) | collective-permute-done | bytes 98336 | tf_op jit(solution)/shard_map/ppermute | solution.py:42
  44.5 0.3 merge_bins.1
  44.8 0.3 slab_currents.1
  45.2 1.7 %collective-permute-start.2 = (bf16[480,128]{1,0:T(8,128)(2,1)S(1)}, bf16[480,128]{1,0:T(8,128)(2,1)S(1)}, u32[]{:S(2)}, u32[]{:S(2)}) collective-permute-start(bf16[480,128]{1,0:T(8,128)(2,1)S(1)} %get-tuple-element.15), channel_id=1, source_target_pairs={{0,1},{1,0},{2,3},{3,2},{4,5},{5,4},{6,7},{7,6},{8,9},{9,8},{10,11... | collective-permute-start | bytes 368648 | tf_op jit(solution)/shard_map/ppermute | solution.py:42
  46.9 1.4 %collective-permute-start.3 = (bf16[480,128]{1,0:T(8,128)(2,1)S(1)}, bf16[480,128]{1,0:T(8,128)(2,1)S(1)}, u32[]{:S(2)}, u32[]{:S(2)}) collective-permute-start(bf16[480,128]{1,0:T(8,128)(2,1)S(1)} %get-tuple-element.16), channel_id=1, source_target_pairs={{0,2},{1,3},{2,0},{3,1},{4,6},{5,7},{6,4},{7,5},{8,10},{9,11},{10,... | collective-permute-start | bytes 368648 | tf_op jit(solution)/shard_map/ppermute | solution.py:42
  48.3 1.3 %collective-permute-start.4 = (bf16[480,128]{1,0:T(8,128)(2,1)S(1)}, bf16[480,128]{1,0:T(8,128)(2,1)S(1)}, u32[]{:S(2)}, u32[]{:S(2)}) collective-permute-start(bf16[480,128]{1,0:T(8,128)(2,1)S(1)} %get-tuple-element.17), channel_id=1, source_target_pairs={{0,3},{1,2},{2,1},{3,0},{4,7},{5,6},{6,5},{7,4},{8,11},{9,10},{10,... | collective-permute-start | bytes 368648 | tf_op jit(solution)/shard_map/ppermute | solution.py:42
  49.6 8.2 %all-gather = bf16[8,128,384]{2,1,0:T(8,128)(2,1)S(1)} all-gather(bf16[2,128,384]{2,1,0:T(8,128)(2,1)S(1)} %get-tuple-element.18), channel_id=2, replica_groups=mesh['apa'=2,'gz'=4,'drift'=4] {'gz'}, dimensions={0}, use_global_device_ids=true | all-gather | bytes 983040 | tf_op jit(solution)/shard_map/all_gather | solution.py:524
  57.9 1.9 %charge_gradient.1 = bf16[512,384]{1,0:T(8,128)(2,1)} custom-call(s32[4,3,2]{2,1,0:T(4,128)S(1)} %copy.11.block_ref, s32[4,3]{1,0:T(4,128)S(1)} %copy-done.5, bf16[4,2,128,384]{3,2,1,0:T(8,128)(2,1)S(1)} %bitcast.3, bf16[128,384]{1,0:T(8,128)(2,1)S(1)} %get-tuple-element.19.local_ref, bf16[4,3,2,32,128]{4,3,2,1,0:T(8,128)(2,1)S(1)} %copy-done.1), custom_call_target="tpu_custom_call" | custom-call | flops 100000000 | bytes 786432 | tf_op jit(solution)/shard_map/charge_gradient/pallas_call | solution.py:325
  59.8 5.4 %signal.1 = bf16[3,128,768]{2,1,0:T(8,128)(2,1)} custom-call(bf16[480,128]{1,0:T(8,128)(2,1)S(1)} %get-tuple-element.14.refs_0_, bf16[480,128]{1,0:T(8,128)(2,1)S(1)} %collective-permute-done.2.refs_1_, bf16[480,128]{1,0:T(8,128)(2,1)S(1)} %collective-permute-done.3.refs_2_, bf16[480,128]{1,0:T(8,128)(2,1)S(1)} %collective-permute-done.4.refs_3_, ...), custom_call_target="tpu_custom_call" | custom-call | flops 4000000000 | bytes 6488064 | tf_op jit(solution)/shard_map/signal/pallas_call | solution.py:478
  (15 shorter events, 0.0 us)
Async XLA Ops:
  1.4 0.9 %copy-start = (bf16[4,3,2,32,128]{4,3,2,1,0:T(8,128)(2,1)S(1)}, bf16[4,3,2,32,128]{4,3,2,1,0:T(8,128)(2,1)}, u32[]{:S(2)}) copy-start(bf16[4,3,2,32,128]{4,3,2,1,0:T(8,128)(2,1)} %share_ref.3) | copy-start | bytes 589828
  2.3 1.0 %copy-start.2 = (bf16[512,384]{1,0:T(8,128)(2,1)S(1)}, bf16[512,384]{1,0:T(8,128)(2,1)}, u32[]{:S(2)}) copy-start(bf16[512,384]{1,0:T(8,128)(2,1)} %charge_ref.1) | copy-start | bytes 1179652
  3.3 0.7 %copy-start.4 = (s32[4,3]{1,0:T(4,128)S(1)}, s32[4,3]{1,0:T(4,128)}, u32[]{:S(2)}) copy-start(s32[4,3]{1,0:T(4,128)} %count_ref.3) | copy-start | bytes 148
  5.2 17.2 %collective-permute-start = (bf16[2,352,384]{2,1,0:T(8,128)(2,1)S(1)}, bf16[2,352,384]{2,1,0:T(8,128)(2,1)S(1)}, u32[]{:S(2)}, u32[]{:S(2)}) collective-permute-start(bf16[2,352,384]{2,1,0:T(8,128)(2,1)S(1)} %get-tuple-element.12), channel_id=1, source_target_pairs={{0,4},{4,0},{8,12},{12,8},{1,5},{5,1},{9,13},{13,9},{2,6},{6,2},{1... | collective-permute-start | bytes 1622024 | tf_op jit(solution)/shard_map/ppermute | solution.py:42
  6.6 20.7 %collective-permute-start.5 = (bf16[3,16,768]{2,1,0:T(8,128)(2,1)S(1)}, bf16[3,16,768]{2,1,0:T(8,128)(2,1)S(1)}, u32[]{:S(2)}, u32[]{:S(2)}) collective-permute-start(bf16[3,16,768]{2,1,0:T(8,128)(2,1)S(1)} %get-tuple-element.21), channel_id=1, source_target_pairs={{0,4},{4,8},{8,12},{1,5},{5,9},{9,13},{2,6},{6,10},{10,14},{3,7},{... | collective-permute-start | bytes 221192 | tf_op jit(solution)/shard_map/ppermute | solution.py:506
  8.6 18.7 %copy-start.3 = (bf16[3,128,768]{2,1,0:T(8,128)(2,1)S(1)}, bf16[3,128,768]{2,1,0:T(8,128)(2,1)}, u32[]{:S(2)}) copy-start(bf16[3,128,768]{2,1,0:T(8,128)(2,1)} %own_ref.1) | copy-start | bytes 1769476
  8.6 18.7 %collective-permute-start.6 = (bf16[3,16,768]{2,1,0:T(8,128)(2,1)S(1)}, bf16[3,16,768]{2,1,0:T(8,128)(2,1)S(1)}, u32[]{:S(2)}, u32[]{:S(2)}) collective-permute-start(bf16[3,16,768]{2,1,0:T(8,128)(2,1)S(1)} %get-tuple-element.20), channel_id=1, source_target_pairs={{4,0},{8,4},{12,8},{5,1},{9,5},{13,9},{6,2},{10,6},{14,10},{7,3},{... | collective-permute-start | bytes 221192 | tf_op jit(solution)/shard_map/ppermute | solution.py:507
  10.0 0.8 %copy-start.6 = (bf16[3,21,200]{2,1,0:T(8,128)(2,1)S(1)}, bf16[3,21,200]{2,1,0:T(8,128)(2,1)}, u32[]{:S(2)}) copy-start(bf16[3,21,200]{2,1,0:T(8,128)(2,1)} %response_ref.1) | copy-start | bytes 75604
  10.8 0.7 %copy-start.7 = (s32[384]{0:T(512)S(1)}, s32[384]{0:T(512)}, u32[]{:S(2)}) copy-start(s32[384]{0:T(512)} %class_ref.1) | copy-start | bytes 4612
  22.4 35.5 %copy-start.1 = (bf16[4,3,2,32,128]{4,3,2,1,0:T(8,128)(2,1)S(1)}, bf16[4,3,2,32,128]{4,3,2,1,0:T(8,128)(2,1)}, u32[]{:S(2)}) copy-start(bf16[4,3,2,32,128]{4,3,2,1,0:T(8,128)(2,1)} %share_ref.3) | copy-start | bytes 589828
  22.4 35.5 %copy-start.5 = (s32[4,3]{1,0:T(4,128)S(1)}, s32[4,3]{1,0:T(4,128)}, u32[]{:S(2)}) copy-start(s32[4,3]{1,0:T(4,128)} %count_ref.3) | copy-start | bytes 148
  22.4 22.4 %collective-permute-start.1 = (bf16[352,384]{1,0:T(8,128)(2,1)S(1)}, bf16[352,384]{1,0:T(8,128)(2,1)S(1)}, u32[]{:S(2)}, u32[]{:S(2)}) collective-permute-start(bf16[352,384]{1,0:T(8,128)(2,1)S(1)} %fusion), channel_id=1, source_target_pairs={{0,8},{4,12},{8,0},{12,4},{1,9},{5,13},{9,1},{13,5},{2,10},{6,14},... | collective-permute-start | bytes 811016 | tf_op jit(solution)/shard_map/ppermute | solution.py:42
  33.3 5.7 %collective-permute-start.7 = (bf16[3,128,128]{2,1,0:T(8,128)(2,1)S(1)}, bf16[3,128,128]{2,1,0:T(8,128)(2,1)S(1)}, u32[]{:S(2)}, u32[]{:S(2)}) collective-permute-start(bf16[3,128,128]{2,1,0:T(8,128)(2,1)S(1)} %bin_gradients.1.refs_0_), channel_id=1, source_target_pairs={{0,1},{1,0},{2,3},{3,2},{4,5},{5,4},{6,7},{7,6},{8,9},{9,8},{10,11... | collective-permute-start | bytes 294920 | tf_op jit(solution)/shard_map/ppermute | solution.py:42
  35.0 9.6 %collective-permute-start.8 = (bf16[3,128,128]{2,1,0:T(8,128)(2,1)S(1)}, bf16[3,128,128]{2,1,0:T(8,128)(2,1)S(1)}, u32[]{:S(2)}, u32[]{:S(2)}) collective-permute-start(bf16[3,128,128]{2,1,0:T(8,128)(2,1)S(1)} %bin_gradients.1.refs_0_), channel_id=1, source_target_pairs={{0,2},{1,3},{2,0},{3,1},{4,6},{5,7},{6,4},{7,5},{8,10},{9,11},{10,... | collective-permute-start | bytes 294920 | tf_op jit(solution)/shard_map/ppermute | solution.py:42
  37.5 7.0 %collective-permute-start.9 = (bf16[3,128,128]{2,1,0:T(8,128)(2,1)S(1)}, bf16[3,128,128]{2,1,0:T(8,128)(2,1)S(1)}, u32[]{:S(2)}, u32[]{:S(2)}) collective-permute-start(bf16[3,128,128]{2,1,0:T(8,128)(2,1)S(1)} %bin_gradients.1.refs_0_), channel_id=1, source_target_pairs={{0,3},{1,2},{2,1},{3,0},{4,7},{5,6},{6,5},{7,4},{8,11},{9,10},{10,... | collective-permute-start | bytes 294920 | tf_op jit(solution)/shard_map/ppermute | solution.py:42
  45.2 14.6 %collective-permute-start.2 = (bf16[480,128]{1,0:T(8,128)(2,1)S(1)}, bf16[480,128]{1,0:T(8,128)(2,1)S(1)}, u32[]{:S(2)}, u32[]{:S(2)}) collective-permute-start(bf16[480,128]{1,0:T(8,128)(2,1)S(1)} %get-tuple-element.15), channel_id=1, source_target_pairs={{0,1},{1,0},{2,3},{3,2},{4,5},{5,4},{6,7},{7,6},{8,9},{9,8},{10,11... | collective-permute-start | bytes 368648 | tf_op jit(solution)/shard_map/ppermute | solution.py:42
  46.9 13.0 %collective-permute-start.3 = (bf16[480,128]{1,0:T(8,128)(2,1)S(1)}, bf16[480,128]{1,0:T(8,128)(2,1)S(1)}, u32[]{:S(2)}, u32[]{:S(2)}) collective-permute-start(bf16[480,128]{1,0:T(8,128)(2,1)S(1)} %get-tuple-element.16), channel_id=1, source_target_pairs={{0,2},{1,3},{2,0},{3,1},{4,6},{5,7},{6,4},{7,5},{8,10},{9,11},{10,... | collective-permute-start | bytes 368648 | tf_op jit(solution)/shard_map/ppermute | solution.py:42
  48.3 11.5 %collective-permute-start.4 = (bf16[480,128]{1,0:T(8,128)(2,1)S(1)}, bf16[480,128]{1,0:T(8,128)(2,1)S(1)}, u32[]{:S(2)}, u32[]{:S(2)}) collective-permute-start(bf16[480,128]{1,0:T(8,128)(2,1)S(1)} %get-tuple-element.17), channel_id=1, source_target_pairs={{0,3},{1,2},{2,1},{3,0},{4,7},{5,6},{6,5},{7,4},{8,11},{9,10},{10,... | collective-permute-start | bytes 368648 | tf_op jit(solution)/shard_map/ppermute | solution.py:42

commit v2 on v1

v2 whole, which is shorter than its diff:
```python
import functools
import math

import jax
import jax.numpy as jnp
from jax import lax
from jax.experimental import pallas as pl
from jax.experimental.pallas import tpu as pltpu
from jax.sharding import PartitionSpec as P

TPB = 8
HB = 2
CLASSES = 6
LANES = 128
EDGE = 16
GROUP = 8
WINDOW = 64
LEAD = HB * TPB - TPB // 2
VMEM_LIMIT = 24 * 1024 * 1024
WHOLE_VMEM = 61 * 1024 * 1024
BF16 = jnp.bfloat16
F32 = jnp.float32


def params(semantics=None, limit=VMEM_LIMIT):
    return pltpu.CompilerParams(vmem_limit_bytes=limit, dimension_semantics=semantics)


def vmem():
    return pl.BlockSpec(memory_space=pltpu.VMEM)


def smem():
    return pl.BlockSpec(memory_space=pltpu.SMEM)


def anywhere():
    return pl.BlockSpec(memory_space=pl.ANY)


def cost(flops, moved):
    return pl.CostEstimate(flops=int(flops), bytes_accessed=int(moved), transcendentals=0)


def swap(block, axis, distance):
    count = lax.axis_size(axis)
    return lax.ppermute(block, axis, [(i, i ^ distance) for i in range(count)])


def widths(number):
    spread = TPB * (0.2 + 0.15 * number)
    half = HB * TPB
    total = sum(math.exp(-((j + 0.5) ** 2) / (2.0 * spread * spread)) for j in range(-half, half))
    return 1.0 / (2.0 * spread * spread), 1.0 / total


def shared_lanes(left, right, shift, lane):
    if shift == 0:
        return left
    back = LANES - shift
    return jnp.where(lane < back, pltpu.roll(left, back, 1), pltpu.roll(right, back, 1))


def coded(rows, column):
    lane = lax.broadcasted_iota(jnp.int32, rows.shape, 1)
    level = jnp.broadcast_to(rows[:, column : column + 1].astype(BF16).astype(F32), rows.shape)
    return jnp.where(lane == 0, level, rows - level).astype(BF16)


def plain(rows, first):
    rows = rows.astype(F32)
    lane = lax.broadcasted_iota(jnp.int32, rows.shape, 1)
    level = jnp.broadcast_to(rows[:, :1], rows.shape)
    return jnp.where(lane == 0, level if first else jnp.zeros_like(rows), rows + level)


def levels_kernel(class_ref, response_ref, _, level_ref, kind_ref, flat_ref, *, bins):
    planes, wire_taps, length = response_ref.shape
    rows = level_ref.shape[0] // planes
    groups = kind_ref.shape[0]
    row = lax.broadcasted_iota(jnp.int32, (GROUP, LANES), 0)
    first = lax.axis_index("drift") * bins - (WINDOW // 2 - HB)
    last = class_ref.shape[0] - 1
    for m in range(groups):
        kind = jnp.zeros((GROUP, LANES), jnp.int32)
        for i in range(GROUP):
            x = first + m * GROUP + i
            number = class_ref[jnp.clip(x, 0, last)]
            number = jnp.where((x >= 0) & (x < HB), CLASSES + x, number)
            kind = jnp.where(row == i, number, kind)
        kind_ref[m] = kind
    flat_ref[...] = jnp.zeros(flat_ref.shape, F32)
    for p in range(planes):
        flat_ref[p * rows : p * rows + wire_taps, :length] = response_ref[p].astype(F32)
    taps = flat_ref[...].astype(BF16)
    tap = lax.broadcasted_iota(jnp.int32, (LANES, 2 * LANES), 0)
    tick = lax.broadcasted_iota(jnp.int32, (LANES, 2 * LANES), 1)
    step = tick - tap - LEAD
    offset = step.astype(F32) - (TPB - 1) / 2.0
    squared = offset * offset
    inside = jnp.abs(offset) < HB * TPB
    for kind in range(CLASSES + HB):
        keep = inside
        if kind < CLASSES:
            narrow, scale = widths(kind)
        else:
            edge = kind - CLASSES
            narrow, scale = widths(0)
            for number in range(1, CLASSES):
                chosen = class_ref[edge] == number
                narrow = jnp.where(chosen, widths(number)[0], narrow)
                scale = jnp.where(chosen, widths(number)[1], scale)
            keep = inside & (step >= -TPB * edge)
        smear = jnp.where(keep, jnp.exp(-(squared * narrow)) * scale, 0.0)
        high = smear.astype(BF16)
        low = (smear - high.astype(F32)).astype(BF16)
        near = jnp.dot(taps[:, :LANES], high, preferred_element_type=F32) + jnp.dot(
            taps[:, :LANES], low, preferred_element_type=F32
        )
        far = jnp.dot(taps[:, LANES:], high[:, :LANES], preferred_element_type=F32) + jnp.dot(
            taps[:, LANES:], low[:, :LANES], preferred_element_type=F32
        )
        level_ref[:, kind, :LANES] = near[:, :LANES]
        level_ref[:, kind, LANES:] = near[:, LANES:] + far


def smeared_levels(diff_class, response, bins, before):
    planes, wire_taps, _ = response.shape
    rows = -(-wire_taps // 8) * 8
    groups = (bins + WINDOW // 2) // GROUP
    return pl.pallas_call(
        functools.partial(levels_kernel, bins=bins),
        out_shape=(
            jax.ShapeDtypeStruct((planes * rows, CLASSES + HB, 2 * LANES), F32),
            jax.ShapeDtypeStruct((groups, GROUP, LANES), jnp.int32),
        ),
        in_specs=[smem(), vmem(), anywhere()],
        out_specs=(vmem(), vmem()),
        scratch_shapes=[pltpu.VMEM((planes * rows, 2 * LANES), F32)],
        compiler_params=params(),
        cost_estimate=cost(1e8, 1e6),
        name="levels",
    )(diff_class, response, before)


def table_kernel(level_ref, kind_ref, table_ref, sum_ref, *, wire_taps):
    planes, blocks, depth, span = table_ref.shape
    rows = level_ref.shape[0] // planes
    groups = kind_ref.shape[0]
    tiles = span // LANES
    lane = lax.broadcasted_iota(jnp.int32, (GROUP, LANES), 1)
    row = lax.broadcasted_iota(jnp.int32, (GROUP, LANES), 0)
    starts = [LEAD_SHIFT + odd * (LANES // 2) + TPB * row for odd in range(2)]
    after = [lane >= start for start in starts]
    zero = jnp.zeros((GROUP, LANES), F32)
    empty = jnp.zeros((2 * GROUP, LANES), BF16)

    def body(a, plane):
        levels = level_ref[plane * rows + a]
        halves = [levels[:, :LANES], levels[:, LANES:]]
        pieces = []
        for m in range(groups):
            odd = m % 2
            parts = [
                pltpu.roll(
                    jnp.take_along_axis(half, kind_ref[m], axis=0),
                    LEAD_SHIFT + odd * (LANES // 2),
                    1,
                    stride=TPB,
                    stride_axis=0,
                )
                for half in halves
            ]
            pieces.append(
                (
                    jnp.where(after[odd], parts[0], zero),
                    jnp.where(after[odd], parts[1], parts[0]),
                    jnp.where(after[odd], zero, parts[1]),
                )
            )
        for block in range(blocks):
            for tile in range(tiles):
                here = slice(tile * LANES, (tile + 1) * LANES)
                total = zero
                for quarter in range(WINDOW // (2 * GROUP)):
                    m = 2 * (tiles * block + quarter)
                    at = a * WINDOW + quarter * 2 * GROUP
                    at = pl.ds(pl.multiple_of(at, 2 * GROUP), 2 * GROUP)
                    third = tile - quarter + 2
                    value = empty
                    if 0 <= third <= 2 and m + 1 < groups:
                        value = jnp.concatenate(
                            [pieces[m][third], pieces[m + 1][third]], axis=0
                        ).astype(BF16)
                        total = total + pieces[m][third] + pieces[m + 1][third]
                    table_ref[plane, block, at, here] = value
                sum_ref[a, block, :, here] = total
        return plane

    def whole_plane(plane, _):
        lax.fori_loop(0, wire_taps, body, plane, unroll=UNROLL)
        for block in range(blocks):
            total = jnp.sum(sum_ref[:, block], axis=1)
            high = total.astype(BF16).astype(F32)
            spare = jnp.zeros((depth - (WINDOW + 2) * wire_taps, span), F32)
            table_ref[plane, block, wire_taps * WINDOW :, :] = jnp.concatenate(
                [high, total - high, spare], axis=0
            ).astype(BF16)
        return 0

    lax.fori_loop(0, planes, whole_plane, 0)


UNROLL = 7
LEAD_SHIFT = (TPB * HB - LEAD) % LANES


def build_table(levels, kinds, planes, wire_taps, ticks_here):
    tiles = math.gcd(ticks_here, 2 * LANES) // LANES
    blocks = ticks_here // (tiles * LANES)
    shape = (planes, blocks, (wire_taps + 1) * WINDOW, tiles * LANES)
    return pl.pallas_call(
        functools.partial(table_kernel, wire_taps=wire_taps),
        out_shape=jax.ShapeDtypeStruct(shape, BF16),
        in_specs=[vmem(), vmem()],
        out_specs=vmem(),
        scratch_shapes=[pltpu.VMEM((wire_taps, blocks, GROUP, tiles * LANES), F32)],
        compiler_params=params(),
        cost_estimate=cost(4e9, 2 * math.prod(shape)),
        name="table",
    )(levels, kinds)


def back_kernel(table_ref, own_ref, received_ref, next_ref, out_ref, cot_ref, wide_ref, *, wire_taps, rows):
    blocks, span = table_ref.shape[1], table_ref.shape[3]
    _, wires, ticks = own_ref.shape
    total = received_ref.shape[1]
    half = (wire_taps - 1) // 2
    parts = ticks // total
    plane = pl.program_id(0)
    even = lax.rem(lax.axis_index("gz"), 2) == 0
    cot_ref[EDGE : EDGE + wires] = own_ref[0]
    for part in range(parts):
        here = slice(part * total, (part + 1) * total)
        at = rows + (plane * parts + part) * EDGE
        near = received_ref[pl.ds(pl.multiple_of(at, EDGE), EDGE)]
        far = next_ref[0, :, here]
        cot_ref[:EDGE, here] = jnp.where(even, far, near)
        cot_ref[EDGE + wires :, here] = jnp.where(even, near, far)
    lane = lax.broadcasted_iota(jnp.int32, (wires, LANES), 1)
    none = jnp.zeros((wires, LANES), F32)
    step = span * 16 // LANES
    columns = (wire_taps + 1) // 2
    result = none
    for block in range(blocks):
        wide = lax.dot_general(
            cot_ref[:, block * span : (block + 1) * span],
            table_ref[plane, block, : columns * LANES],
            (((1,), (1,)), ((), ())),
            preferred_element_type=F32,
        )
        for column in range(columns):
            wide_ref[column] = wide[:, column * LANES : (column + 1) * LANES]
        left, right = none, none
        for column in range(columns):
            at = EDGE + half - 2 * column
            left += wide_ref[column, at : at + wires]
            if 2 * column + 1 < wire_taps:
                right += wide_ref[column, at - 1 : at - 1 + wires]
        both = jnp.where(lane < WINDOW, left + pltpu.roll(right, WINDOW, 1), none)
        result += pltpu.roll(both, block * step, 1) if block else both
    out_ref[0] = result.astype(BF16)


def backward(table, cotangent, received, beyond, wire_taps, rows):
    planes, blocks, depth, span = table.shape
    _, wires, ticks = cotangent.shape
    extent = wires + 2 * EDGE
    columns = (wire_taps + 1) // 2
    return pl.pallas_call(
        functools.partial(back_kernel, wire_taps=wire_taps, rows=rows),
        grid=(planes,),
        out_shape=jax.ShapeDtypeStruct((planes, wires, LANES), BF16),
        in_specs=[
            vmem(),
            pl.BlockSpec((1, wires, ticks), lambda p: (p, 0, 0)),
            vmem(),
            pl.BlockSpec((1, EDGE, ticks), lambda p: (p, 0, 0)),
        ],
        out_specs=pl.BlockSpec((1, wires, LANES), lambda p: (p, 0, 0)),
        scratch_shapes=[
            pltpu.VMEM((extent, ticks), BF16),
            pltpu.VMEM((columns, extent, LANES), F32),
        ],
        compiler_params=params(("arbitrary",)),
        cost_estimate=cost(4e9, 2 * math.prod(table.shape)),
        name="bin_gradients",
    )(table, cotangent, received, beyond)


def merge_kernel(*refs, bins, lead):
    parts, (cross_ref, local_ref, slab_ref) = refs[:-4], refs[-3:]
    planes, wires, _ = parts[0].shape
    total = local_ref.shape[1]
    slab = lax.axis_index("drift")
    for k, part in enumerate(parts):
        slab_ref[slab ^ k] = part[...]
    lane = lax.broadcasted_iota(jnp.int32, (wires, LANES), 1)
    none = jnp.zeros((wires, LANES), F32)
    for p in range(planes):
        tiles = [none] * (total // LANES)
        for source in range(len(parts)):
            values = slab_ref[source, p].astype(F32)
            tile, shift = (source * bins - lead) // LANES, (source * bins - lead) % LANES
            if shift:
                values = pltpu.roll(values, shift, 1)
            for t, inside in ((tile, lane >= shift), (tile + 1, lane < shift)):
                if 0 <= t < len(tiles):
                    tiles[t] += jnp.where(inside, values, none)
        for t, values in enumerate(tiles):
            here = slice(t * LANES, (t + 1) * LANES)
            if p < planes - 1:
                cross_ref[p, :, here] = values.astype(BF16)
            else:
                local_ref[:, here] = values.astype(BF16)


def merge(parts, bins, total, before):
    planes, wires, _ = parts[0].shape
    return pl.pallas_call(
        functools.partial(merge_kernel, bins=bins, lead=WINDOW // 2 - HB),
        out_shape=(
            jax.ShapeDtypeStruct((planes - 1, wires, total), BF16),
            jax.ShapeDtypeStruct((wires, total), BF16),
        ),
        in_specs=[vmem()] * len(parts) + [anywhere()],
        out_specs=(vmem(), vmem()),
        scratch_shapes=[pltpu.VMEM((len(parts), planes, wires, LANES), BF16)],
        compiler_params=params(),
        cost_estimate=cost(1e8, 4 * planes * wires * total),
        name="merge_bins",
    )(*parts, before)


def charge_kernel(block_ref, count_ref, *refs):
    sources, (local_ref, share_ref, out_ref, all_ref, chosen_ref) = refs[:-5], refs[-5:]
    _, planes, entries, wire_block, width = share_ref.shape
    owners, _, wires, total = all_ref.shape
    per_owner = wires // wire_block
    z = lax.axis_index("gz")
    b = pl.program_id(0)

    @pl.when(b == 0)
    def _():
        if len(sources) == 1:
            all_ref[...] = sources[0][...]
        else:
            for k, source in enumerate(sources):
                all_ref[z ^ k] = source[...]

    empty = jnp.zeros((wire_block, total), BF16)
    for p in range(planes):
        for k in range(entries):
            name = block_ref[p, k, b]
            if p < planes - 1:
                name = jnp.clip(name, 0, owners * per_owner - 1)
                owner = name // per_owner
                start = pl.multiple_of((name - owner * per_owner) * wire_block, wire_block)
                rows = all_ref[owner, p, pl.ds(start, wire_block), :]
            else:
                name = jnp.clip(name - z * per_owner, 0, per_owner - 1)
                start = pl.multiple_of(name * wire_block, wire_block)
                rows = local_ref[pl.ds(start, wire_block), :]
            at = (p * entries + k) * wire_block
            chosen_ref[at : at + wire_block] = jnp.where(k < count_ref[b, p], rows, empty)
    out_ref[...] = lax.dot_general(
        share_ref[0].reshape(planes * entries * wire_block, width),
        chosen_ref[...],
        (((0,), (0,)), ((), ())),
        preferred_element_type=F32,
    ).astype(BF16)


def charge_gradient(ovl_block, ovl_count, sources, local, intersection, owners):
    cells, planes, entries, wire_block, width = intersection.shape
    wires, total = local.shape
    shape = (owners, planes - 1, wires, total)
    return pl.pallas_call(
        charge_kernel,
        grid=(cells,),
        out_shape=jax.ShapeDtypeStruct((cells * width, total), BF16),
        in_specs=[smem(), smem()]
        + [vmem()] * (len(sources) + 1)
        + [pl.BlockSpec((1, planes, entries, wire_block, width), lambda b: (b, 0, 0, 0, 0))],
        out_specs=pl.BlockSpec((width, total), lambda b: (b, 0)),
        scratch_shapes=[
            pltpu.VMEM(shape, BF16),
            pltpu.VMEM((planes * entries * wire_block, total), BF16),
        ],
        compiler_params=params(("arbitrary",)),
        cost_estimate=cost(1e8, 2 * math.prod(shape)),
        name="charge_gradient",
    )(jnp.transpose(ovl_block, (1, 2, 0)), ovl_count, *sources, local, intersection)


def pieces_kernel(
    block_hbm, count_hbm, charge_hbm, share_hbm, cot_hbm, keep_ref, give_ref, local_ref, next_ref,
    block_ref, count_ref, charge_ref, share_ref, edge_ref, cross_ref, sems,
):
    cells, planes, entries, wire_block, width = share_ref.shape
    wires, total = local_ref.shape
    ticks = edge_ref.shape[2]
    per_owner = wires // wire_block
    halves = keep_ref.shape[0]
    owners = 2 * halves
    z = lax.axis_index("gz")
    even = lax.rem(z, 2) == 0
    upper = pl.ds(pl.multiple_of(jnp.where(even, wires - EDGE, 0), EDGE), EDGE)
    lower = pl.ds(pl.multiple_of(jnp.where(even, 0, wires - EDGE), EDGE), EDGE)
    loads = [
        pltpu.make_async_copy(source, target, sems.at[i])
        for i, (source, target) in enumerate(
            (
                (block_hbm, block_ref),
                (count_hbm, count_ref),
                (charge_hbm, charge_ref),
                (share_hbm, share_ref),
                (cot_hbm.at[:, upper], edge_ref),
                (cot_hbm.at[:, lower], next_ref),
            )
        )
    ]
    for load in loads:
        load.start()
    cross_ref[...] = jnp.zeros(cross_ref.shape, F32)
    local_ref[...] = jnp.zeros(local_ref.shape, F32)
    for load in loads:
        load.wait()
    for b in range(cells):
        pieces = (
            jnp.dot(
                share_ref[b].reshape(planes * entries * wire_block, width),
                charge_ref[b * width : (b + 1) * width],
                preferred_element_type=F32,
            )
            .astype(BF16)
            .astype(F32)
        )
        for p in range(planes):
            for k in range(entries):
                at = (p * entries + k) * wire_block
                piece = pieces[at : at + wire_block]
                piece = jnp.where(k < count_ref[b, p], piece, jnp.zeros_like(piece))
                name = block_ref[p, k, b]
                if p < planes - 1:
                    name = jnp.clip(name, 0, owners * per_owner - 1)
                    start = pl.multiple_of(EDGE + name * wire_block, EDGE)
                    cross_ref[p, pl.ds(start, wire_block)] += piece
                else:
                    name = jnp.clip(name - z * per_owner, 0, per_owner - 1)
                    start = pl.multiple_of(name * wire_block, wire_block)
                    local_ref[pl.ds(start, wire_block)] += piece
    extent = wires + 2 * EDGE
    cut = keep_ref.shape[1]
    none = jnp.zeros((EDGE, total), F32)
    for k in range(owners):
        to = z ^ k
        blocks = [
            cross_ref[p, pl.ds(pl.multiple_of(to * wires, EDGE), extent)] for p in range(planes - 1)
        ]
        blocks.append(jnp.where(to == z + 1, local_ref[wires - EDGE :], none))
        blocks.append(jnp.where(to == z - 1, local_ref[:EDGE], none))
        at = 0
        for rows in blocks:
            here = slice(at, at + rows.shape[0])
            at += rows.shape[0]
            if k % 2:
                give_ref[k // 2 * cut + here.start : k // 2 * cut + here.stop] = coded(rows, 0)
            else:
                keep_ref[k // 2, here] = rows
    at = halves * cut
    for p in range(planes):
        for part in range(ticks // total):
            give_ref[at : at + EDGE] = edge_ref[p, :, part * total : (part + 1) * total]
            at += EDGE


def cut_pieces(ovl_block, ovl_count, charge, intersection, cotangent, owners):
    cells, planes, entries, wire_block, width = intersection.shape
    total = charge.shape[1]
    _, wires, ticks = cotangent.shape
    rows = (planes - 1) * (wires + 2 * EDGE) + 2 * EDGE
    cut = (owners // 2, rows, total)
    edges = planes * EDGE * ticks // total
    hbm = pl.BlockSpec(memory_space=pltpu.HBM)
    blocks = jnp.transpose(ovl_block, (1, 2, 0))
    return pl.pallas_call(
        pieces_kernel,
        out_shape=(
            jax.ShapeDtypeStruct(cut, F32),
            jax.ShapeDtypeStruct((owners // 2 * rows + edges, total), BF16),
            jax.ShapeDtypeStruct((wires, total), F32),
            jax.ShapeDtypeStruct((planes, EDGE, ticks), BF16),
        ),
        in_specs=[hbm] * 5,
        out_specs=(vmem(), vmem(), vmem(), vmem()),
        scratch_shapes=[
            pltpu.SMEM(blocks.shape, jnp.int32),
            pltpu.SMEM(ovl_count.shape, jnp.int32),
            pltpu.VMEM(charge.shape, BF16),
            pltpu.VMEM(intersection.shape, BF16),
            pltpu.VMEM((planes, EDGE, ticks), BF16),
            pltpu.VMEM((planes - 1, owners * wires + 2 * EDGE, total), F32),
            pltpu.SemaphoreType.DMA((6,)),
        ],
        compiler_params=params(limit=WHOLE_VMEM),
        cost_estimate=cost(1e8, 4 * owners * rows * total),
        name="pieces",
    )(blocks, ovl_count, charge, intersection, cotangent)


def relay_kernel(keep_ref, received_ref, *outs):
    rows = keep_ref.shape[1]
    for j, out in enumerate(outs, 1):
        summed = keep_ref[j] + plain(received_ref[j * rows : (j + 1) * rows], True)
        out[...] = coded(summed, 0)


def relay(keep, received):
    halves, rows, total = keep.shape
    return pl.pallas_call(
        relay_kernel,
        out_shape=(jax.ShapeDtypeStruct((rows, total), BF16),) * (halves - 1),
        in_specs=[vmem(), vmem()],
        out_specs=(vmem(),) * (halves - 1),
        compiler_params=params(),
        cost_estimate=cost(1e7, 6 * halves * rows * total),
        name="relay",
    )(keep, received)


def slabs_kernel(*refs, bins, lead, slabs):
    count = len(refs) - slabs - 1
    keep_ref, received_ref, others, local_ref = refs[0], refs[1], refs[2 : count - 2], refs[count - 2]
    outs, cut_ref = refs[count:-1], refs[-1]
    total = local_ref.shape[1]
    cut = keep_ref.shape[1]
    summed = keep_ref[0] + plain(received_ref[:cut], True)
    for other in others:
        summed += plain(other[...], True)
    edge = cut - 2 * EDGE
    rows = jnp.concatenate(
        [summed[:edge], summed[edge : edge + EDGE], local_ref[...], summed[edge + EDGE :]], axis=0
    )
    none = jnp.zeros((rows.shape[0], LANES), F32)
    lane = lax.broadcasted_iota(jnp.int32, none.shape, 1)
    level = jnp.broadcast_to(rows[:, :1].astype(BF16).astype(F32), none.shape)
    tiles = [rows[:, t * LANES : (t + 1) * LANES] - level for t in range(total // LANES)]
    for to in range(slabs):
        at = to * bins - lead
        tile, shift = at // LANES, at % LANES
        pair = [tiles[t] if 0 <= t < len(tiles) else -level for t in (tile, tile + 1)]
        value = shared_lanes(pair[0], pair[1], shift, lane)
        cut_ref[to] = jnp.where(lane == 0, level, value).astype(BF16)
    slab = lax.axis_index("drift")
    for k, out in enumerate(outs):
        out[...] = cut_ref[slab ^ k]


def cut_slabs(keep, received, others, local, bins, slabs, before):
    wires, total = local.shape
    rows = keep.shape[1] + wires
    cut = jax.ShapeDtypeStruct((rows, LANES), BF16)
    first = pl.BlockSpec((1,) + keep.shape[1:], lambda i: (0, 0, 0))
    return pl.pallas_call(
        functools.partial(slabs_kernel, bins=bins, lead=WINDOW // 2 - HB, slabs=slabs),
        grid=(1,),
        out_shape=(cut,) * slabs,
        in_specs=[first] + [vmem()] * (2 + len(others)) + [anywhere()],
        out_specs=(vmem(),) * slabs,
        scratch_shapes=[pltpu.VMEM((slabs, rows, LANES), BF16)],
        compiler_params=params(("arbitrary",)),
        cost_estimate=cost(1e8, 4 * rows * total),
        name="slab_currents",
    )(keep, received, *others, local, before)


def signal_kernel(*refs, wire_taps):
    parts, (table_ref, out_ref, even_ref, odd_ref, level_ref, lines_ref) = refs[:-6], refs[-6:]
    blocks, span = table_ref.shape[1], table_ref.shape[3]
    wires = out_ref.shape[1]
    half = (wire_taps - 1) // 2
    step = span * 16 // LANES
    currents = plain(parts[0][...], False)
    for part in parts[1:]:
        currents += plain(part[...], False)
    middle = WINDOW // 2
    level = currents[:, middle : middle + 1].astype(BF16).astype(F32)
    level = jnp.broadcast_to(level, currents.shape)
    level_ref[...] = level
    currents = currents - level
    lane = lax.broadcasted_iota(jnp.int32, (wires, LANES), 1)
    levels = jnp.zeros((wires, LANES), F32)
    for a in range(wire_taps):
        at = EDGE - half + a
        here = (lane == WINDOW + a) | (lane == WINDOW + wire_taps + a)
        levels = jnp.where(here, level_ref[at : at + wires], levels)
    for block in range(blocks):
        even_ref[...] = pltpu.roll(currents, (-step * block) % LANES, 1)
        odd_ref[...] = pltpu.roll(currents, (WINDOW - step * block) % LANES, 1)
        for pair in range((wire_taps + 1) // 2):
            at = EDGE - half + 2 * pair
            right = levels
            if 2 * pair + 1 < wire_taps:
                right = odd_ref[at + 1 : at + 1 + wires]
            line = jnp.where(lane < WINDOW, even_ref[at : at + wires], right)
            lines_ref[:, pair * LANES : (pair + 1) * LANES] = line.astype(BF16)
        out_ref[0, :, block * span : (block + 1) * span] = jnp.dot(
            lines_ref[...], table_ref[pl.program_id(0), block], preferred_element_type=F32
        ).astype(BF16)


def forward(parts, table, wires, wire_taps):
    planes, blocks, depth, span = table.shape
    extent = wires + 2 * EDGE
    part = pl.BlockSpec((extent, LANES), lambda p: (p, 0))
    return pl.pallas_call(
        functools.partial(signal_kernel, wire_taps=wire_taps),
        grid=(planes,),
        out_shape=jax.ShapeDtypeStruct((planes, wires, blocks * span), BF16),
        in_specs=[part] * len(parts)
        + [vmem()],
        out_specs=pl.BlockSpec((1, wires, blocks * span), lambda p: (p, 0, 0)),
        scratch_shapes=[
            pltpu.VMEM((extent, LANES), F32),
            pltpu.VMEM((extent, LANES), F32),
            pltpu.VMEM((extent, LANES), F32),
            pltpu.VMEM((wires, depth), BF16),
        ],
        compiler_params=params(("arbitrary",)),
        cost_estimate=cost(4e9, 2 * math.prod(table.shape)),
        name="signal",
    )(*parts, table)


def local(charge, intersection, ovl_block, ovl_count, diff_class, response, cotangent):
    total = charge.shape[1]
    owners = lax.axis_size("gz")
    slabs = lax.axis_size("drift")
    planes, wires, ticks = cotangent.shape
    wire_taps = response.shape[1]
    bins = total // slabs

    keep, give, local_currents, edges = cut_pieces(
        ovl_block, ovl_count, charge, intersection, cotangent, owners
    )
    received = swap(give, "gz", 1)
    pairs = [(i, i + 1) for i in range(1, owners - 1, 2)]
    beyond = lax.ppermute(edges, "gz", pairs + [(j, i) for i, j in pairs])
    sums = relay(keep, received) if owners > 2 else ()
    others = [swap(block, "gz", 2 * j) for j, block in enumerate(sums, 1)]

    levels, kinds = smeared_levels(diff_class, response, bins, sums[0] if sums else received)
    table = build_table(levels, kinds, planes, wire_taps, ticks)
    rows = keep.shape[0] * keep.shape[1]
    partial = backward(table, cotangent, received, beyond, wire_taps, rows)
    spread = [partial] + [swap(partial, "drift", k) for k in range(1, slabs)]

    cuts = cut_slabs(keep, received, others, local_currents, bins, slabs, partial)
    windows = [cuts[0]] + [swap(cuts[k], "drift", k) for k in range(1, slabs)]
    signal = forward(windows, table, wires, wire_taps)

    cross, own = merge(spread, bins, total, cuts[0])
    if owners == 4:
        across = swap(cross, "gz", 2)
        sources = [cross, swap(cross, "gz", 1), across, swap(across, "gz", 1)]
    else:
        sources = [lax.all_gather(cross, "gz", axis=0)]
    charge_grad = charge_gradient(ovl_block, ovl_count, sources, own, intersection, owners)
    return signal, charge_grad


def solution(mesh):
    return jax.shard_map(
        local,
        mesh=mesh,
        in_specs=(
            P(("apa", "gz", "drift"), None),
            P(("apa", "gz", "drift"), None, None, None, None),
            P(("apa", "gz", "drift"), None, None),
            P(("apa", "gz", "drift"), None),
            P("apa"),
            P(),
            P("apa", "gz", "drift"),
        ),
        out_specs=(P("apa", "gz", "drift"), P(("apa", "gz", "drift"), None)),
        check_vma=False,
    )
```

time: 65.7 us -> 52.4 us (0.80)
  waiting for transfers between devices: 6.77 us -> 16.4 us
  Pallas kernels: 25.9 us -> 17.5 us
  blocking collectives: 8.24 us -> 0 us
  local copies, waits for them, and re-layouts: 5.79 us -> 2.71 us
  starting transfers between devices: 17.7 us -> 14.8 us
    ppermute x8 -> x11, waiting for transfers between devices: 6.77 us -> 16.4 us  [swap(): return lax.ppermute(block, axis, [(i, i ^ distance) for i in range(count)])]
    all_gather x1 -> x0, blocking collectives: 8.24 us -> none  [local(): every = lax.all_gather(cross, 'gz', axis=0)]
    pallas_call x6 -> x8, Pallas kernels: 20.5 us -> 14.3 us  [the longest x1 3.07 us: build_table(): pl.pallas_call(functools.partial(table_kernel, wire_taps=wire_taps), out_...]
    ppermute x2 -> x1, starting transfers between devices: 3.39 us -> 0.65 us  [local(): beyond = lax.ppermute(edges, 'gz', pairs + [(j, i) for i, j in pairs])]
    pallas_call x1, Pallas kernels: 5.38 us -> 3.18 us  [forward(): pl.pallas_call(functools.partial(signal_kernel, wire_taps=wire_taps), gri...]
    unnamed x17 -> x18, local copies, waits for them, and re-layouts: 4.85 us -> 2.71 us
    slice x1 -> x0, local copies, waits for them, and re-layouts: 0.93 us -> none  [local(): high = lax.ppermute(cotangent[:, :EDGE], 'gz', down)]
    ppermute x8 -> x11, starting transfers between devices: 14.3 us -> 14.1 us  [swap(): return lax.ppermute(block, axis, [(i, i ^ distance) for i in range(count)])]
  transfers between devices with their start and end apart: 10 -> 12, of which waited for: 2 -> 6; matrix products, arithmetic and copies ran while one was open for 2% -> 0% of each run, Pallas kernels for 29% -> 22%
where the time goes in v2:
time: 52.4 us; the launch traced here: 52.1 us
  Pallas kernels  17.5 us (33%)
  waiting for transfers between devices  16.4 us (31%)
  starting transfers between devices  14.8 us (28%)
  local copies, waits for them, and re-layouts  2.71 us (5%)
  between operations  0.77 us (1%)
    ppermute x11, waiting for transfers between devices, swap(): return lax.ppermute(block, axis, [(i, i ^ distance) for i in range(count)])  16.4 us
    ppermute x11, starting transfers between devices, swap(): return lax.ppermute(block, axis, [(i, i ^ distance) for i in range(count)])  14.1 us
    pallas_call x1, Pallas kernels, forward(): pl.pallas_call(functools.partial(signal_kernel, wire_taps=wire_taps), gri...  3.18 us
    pallas_call x1, Pallas kernels, build_table(): pl.pallas_call(functools.partial(table_kernel, wire_taps=wire_taps), out_...  3.07 us
    pallas_call x1, Pallas kernels, backward(): pl.pallas_call(functools.partial(back_kernel, wire_taps=wire_taps, rows=r...  3.06 us
    pallas_call x1, Pallas kernels, cut_pieces(): pl.pallas_call(pieces_kernel, out_shape=(jax.ShapeDtypeStruct(cut, F32),...  2.85 us
    pallas_call x1, Pallas kernels, charge_gradient(): pl.pallas_call(charge_kernel, grid=(cells,), out_shape=jax.ShapeDtypeStru...  2.76 us
    unnamed x18, local copies, waits for them, and re-layouts  2.71 us
  transfers between devices with their start and end apart: 12, of which 6 were waited for; matrix products, arithmetic and copies ran while one was open for 0% of the time, Pallas kernels for 22%

profile of v2, /device:TPU:0, one launch (start us, length us, event | category | flops | bytes accessed | tf_op | source)
XLA Modules:
  0.0 52.1 jit_solution(17284141512078497895)
XLA Ops:
  0.6 2.8 %pieces.1 = (f32[2,352,384]{2,1,0:T(8,128)}, bf16[800,384]{1,0:T(8,128)(2,1)}, f32[128,384]{1,0:T(8,128)}, bf16[3,16,768]{2,1,0:T(8,128)(2,1)}) custom-call(s32[3,2,4]{2,1,0:T(2,128)} %bitcast.1, s32[4,3]{1,0:T(4,128)} %count_ref.1, bf16[512,384]{1,0:T(8,128)(2,1)} %charge_hbm.1, bf16[4,3,2,32,128]{4,3,2,1,0:T(8,128)(2,1)} %refs_5_.1, ...), custom_call_target="tpu_custom_call" | custom-call | flops 100000000 | bytes 2162688 | tf_op jit(solution)/shard_map/pieces/pallas_call | solution.py:497
  3.5 0.5 collective-permute-start
  4.0 0.7 %collective-permute-start.2 = (bf16[3,16,768]{2,1,0:T(8,128)(2,1)}, bf16[3,16,768]{2,1,0:T(8,128)(2,1)S(1)}, u32[]{:S(2)}, u32[]{:S(2)}) collective-permute-start(bf16[3,16,768]{2,1,0:T(8,128)(2,1)} %get-tuple-element.19), channel_id=1, source_target_pairs={{4,8},{8,4},{5,9},{9,5},{6,10},{10,6},{7,11},{11,7},{20,24},{24,20... | collective-permute-start | bytes 221192 | tf_op jit(solution)/shard_map/ppermute | solution.py:659
  4.7 1.2 %collective-permute-done.received_ref.refs_1_ = bf16[800,384]{1,0:T(8,128)(2,1)S(1)} collective-permute-done((bf16[800,384]{1,0:T(8,128)(2,1)}, bf16[800,384]{1,0:T(8,128)(2,1)S(1)}, u32[]{:S(2)}, u32[]{:S(2)}) %collective-permute-start) | collective-permute-done | bytes 614432 | tf_op jit(solution)/shard_map/ppermute | solution.py:47
  5.9 1.2 %copy-done = f32[2,352,384]{2,1,0:T(8,128)S(1)} copy-done((f32[2,352,384]{2,1,0:T(8,128)S(1)}, f32[2,352,384]{2,1,0:T(8,128)}, u32[]{:S(2)}) %copy-start) | copy-done | bytes 1081368
  7.1 0.2 relay.1._
  7.3 2.9 %collective-permute-start.1 = (bf16[352,384]{1,0:T(8,128)(2,1)S(1)}, bf16[352,384]{1,0:T(8,128)(2,1)S(1)}, u32[]{:S(2)}, u32[]{:S(2)}) collective-permute-start(bf16[352,384]{1,0:T(8,128)(2,1)S(1)} %relay.1._), channel_id=1, source_target_pairs={{0,8},{4,12},{8,0},{12,4},{1,9},{5,13},{9,1},{13,5},{2,10},{6,14},... | collective-permute-start | bytes 811016 | tf_op jit(solution)/shard_map/ppermute | solution.py:47
  10.2 0.8 %copy-done.7 = bf16[3,21,200]{2,1,0:T(8,128)(2,1)S(1)} copy-done((bf16[3,21,200]{2,1,0:T(8,128)(2,1)S(1)}, bf16[3,21,200]{2,1,0:T(8,128)(2,1)}, u32[]{:S(2)}) %copy-start.7) | copy-done | bytes 25224
  11.0 0.7 %copy-done.8 = s32[384]{0:T(512)S(1)} copy-done((s32[384]{0:T(512)S(1)}, s32[384]{0:T(512)}, u32[]{:S(2)}) %copy-start.8) | copy-done | bytes 1560
  11.7 1.5 %levels.1 = (f32[72,8,256]{2,1,0:T(8,128)S(1)}, s32[16,8,128]{2,1,0:T(8,128)S(1)}) custom-call(s32[384]{0:T(512)S(1)} %copy-done.8, bf16[3,21,200]{2,1,0:T(8,128)(2,1)S(1)} %copy-done.7, bf16[352,384]{1,0:T(8,128)(2,1)S(1)} %relay.1._), custom_call_target="tpu_custom_call" | custom-call | flops 100000000 | bytes 1000000 | tf_op jit(solution)/shard_map/levels/pallas_call | solution.py:131
  13.2 0.0 copy-start.3
  13.3 3.1 %table.1.table_ref.refs_4_ = bf16[3,3,1408,256]{3,2,1,0:T(8,128)(2,1)S(1)} custom-call(f32[72,8,256]{2,1,0:T(8,128)S(1)} %get-tuple-element.17.level_ref, s32[16,8,128]{2,1,0:T(8,128)S(1)} %get-tuple-element.18.kind_ref), custom_call_target="tpu_custom_call" | custom-call | flops 4000000000 | bytes 6488064 | tf_op jit(solution)/shard_map/table/pallas_call | solution.py:222
  16.3 0.0 copy-start.4
  16.4 0.0 collective-permute-done.2.next_ref
  16.4 3.1 %bin_gradients.1.refs_4_.refs_0_ = bf16[3,128,128]{2,1,0:T(8,128)(2,1)S(1)} custom-call(bf16[3,3,1408,256]{3,2,1,0:T(8,128)(2,1)S(1)} %table.1.table_ref.refs_4_, bf16[3,128,768]{2,1,0:T(8,128)(2,1)S(1)} %copy-done.3, bf16[800,384]{1,0:T(8,128)(2,1)S(1)} %collective-permute-done.received_ref.refs_1_, bf16[3,16,768]{2,1,0:T(8,128)(2,1)S(1)} %collective-permute-done.2.next_ref), custom_call_target="tpu_custom_call" | custom-call | flops 4000000000 | bytes 6488064 | tf_op jit(solution)/shard_map/bin_gradients/pallas_call | solution.py:280
  19.4 4.0 %collective-permute-start.8 = (bf16[3,128,128]{2,1,0:T(8,128)(2,1)S(1)}, bf16[3,128,128]{2,1,0:T(8,128)(2,1)S(1)}, u32[]{:S(2)}, u32[]{:S(2)}) collective-permute-start(bf16[3,128,128]{2,1,0:T(8,128)(2,1)S(1)} %bin_gradients.1.refs_4_.refs_0_), channel_id=1, source_target_pairs={{0,3},{1,2},{2,1},{3,0},{4,7},{5,6},{6,5},{7,4},{8,11},{9,10},{10,... | collective-permute-start | bytes 294920 | tf_op jit(solution)/shard_map/ppermute | solution.py:47
  23.4 0.0 collective-permute-start.7
  23.4 0.6 %collective-permute-start.6 = (bf16[3,128,128]{2,1,0:T(8,128)(2,1)S(1)}, bf16[3,128,128]{2,1,0:T(8,128)(2,1)S(1)}, u32[]{:S(2)}, u32[]{:S(2)}) collective-permute-start(bf16[3,128,128]{2,1,0:T(8,128)(2,1)S(1)} %bin_gradients.1.refs_4_.refs_0_), channel_id=1, source_target_pairs={{0,1},{1,0},{2,3},{3,2},{4,5},{5,4},{6,7},{7,6},{8,9},{9,8},{10,11... | collective-permute-start | bytes 294920 | tf_op jit(solution)/shard_map/ppermute | solution.py:47
  24.1 0.0 collective-permute-done.1.refs_2_
  24.1 0.6 %slab_currents.1 = (bf16[480,128]{1,0:T(8,128)(2,1)S(1)}, bf16[480,128]{1,0:T(8,128)(2,1)S(1)}, bf16[480,128]{1,0:T(8,128)(2,1)S(1)}, bf16[480,128]{1,0:T(8,128)(2,1)S(1)}) custom-call(f32[2,352,384]{2,1,0:T(8,128)S(1)} %copy-done.1, bf16[800,384]{1,0:T(8,128)(2,1)S(1)} %collective-permute-done.received_ref.refs_1_, ...), custom_call_target="tpu_custom_call" | custom-call | flops 100000000 | bytes 737280 | tf_op jit(solution)/shard_map/slab_currents/pallas_call | solution.py:575
  24.7 2.2 %collective-permute-done.8.refs_3_ = bf16[3,128,128]{2,1,0:T(8,128)(2,1)S(1)} collective-permute-done((bf16[3,128,128]{2,1,0:T(8,128)(2,1)S(1)}, bf16[3,128,128]{2,1,0:T(8,128)(2,1)S(1)}, u32[]{:S(2)}, u32[]{:S(2)}) %collective-permute-start.8) | collective-permute-done | bytes 98336 | tf_op jit(solution)/shard_map/ppermute | solution.py:47
  26.9 4.5 %collective-permute-done.7.refs_2_ = bf16[3,128,128]{2,1,0:T(8,128)(2,1)S(1)} collective-permute-done((bf16[3,128,128]{2,1,0:T(8,128)(2,1)S(1)}, bf16[3,128,128]{2,1,0:T(8,128)(2,1)S(1)}, u32[]{:S(2)}, u32[]{:S(2)}) %collective-permute-start.7) | collective-permute-done | bytes 98336 | tf_op jit(solution)/shard_map/ppermute | solution.py:47
  31.4 0.2 merge_bins.1
  31.6 1.7 %collective-permute-start.10 = (bf16[2,128,384]{2,1,0:T(8,128)(2,1)S(1)}, bf16[2,128,384]{2,1,0:T(8,128)(2,1)S(1)}, u32[]{:S(2)}, u32[]{:S(2)}) collective-permute-start(bf16[2,128,384]{2,1,0:T(8,128)(2,1)S(1)} %get-tuple-element.24.refs_0_), channel_id=1, source_target_pairs={{0,8},{4,12},{8,0},{12,4},{1,9},{5,13},{9,1},{13,5},{2,10},{6,14},... | collective-permute-start | bytes 589832 | tf_op jit(solution)/shard_map/ppermute | solution.py:47
  33.3 0.6 %collective-permute-start.3 = (bf16[480,128]{1,0:T(8,128)(2,1)S(1)}, bf16[480,128]{1,0:T(8,128)(2,1)S(1)}, u32[]{:S(2)}, u32[]{:S(2)}) collective-permute-start(bf16[480,128]{1,0:T(8,128)(2,1)S(1)} %get-tuple-element.21), channel_id=1, source_target_pairs={{0,1},{1,0},{2,3},{3,2},{4,5},{5,4},{6,7},{7,6},{8,9},{9,8},{10,11... | collective-permute-start | bytes 368648 | tf_op jit(solution)/shard_map/ppermute | solution.py:47
  33.8 2.5 %collective-permute-start.4 = (bf16[480,128]{1,0:T(8,128)(2,1)S(1)}, bf16[480,128]{1,0:T(8,128)(2,1)S(1)}, u32[]{:S(2)}, u32[]{:S(2)}) collective-permute-start(bf16[480,128]{1,0:T(8,128)(2,1)S(1)} %get-tuple-element.22), channel_id=1, source_target_pairs={{0,2},{1,3},{2,0},{3,1},{4,6},{5,7},{6,4},{7,5},{8,10},{9,11},{10,... | collective-permute-start | bytes 368648 | tf_op jit(solution)/shard_map/ppermute | solution.py:47
  36.3 1.4 %collective-permute-start.5 = (bf16[480,128]{1,0:T(8,128)(2,1)S(1)}, bf16[480,128]{1,0:T(8,128)(2,1)S(1)}, u32[]{:S(2)}, u32[]{:S(2)}) collective-permute-start(bf16[480,128]{1,0:T(8,128)(2,1)S(1)} %get-tuple-element.23), channel_id=1, source_target_pairs={{0,3},{1,2},{2,1},{3,0},{4,7},{5,6},{6,5},{7,4},{8,11},{9,10},{10,... | collective-permute-start | bytes 368648 | tf_op jit(solution)/shard_map/ppermute | solution.py:47
  37.7 0.8 %collective-permute-done.10.refs_2_ = bf16[2,128,384]{2,1,0:T(8,128)(2,1)S(1)} collective-permute-done((bf16[2,128,384]{2,1,0:T(8,128)(2,1)S(1)}, bf16[2,128,384]{2,1,0:T(8,128)(2,1)S(1)}, u32[]{:S(2)}, u32[]{:S(2)}) %collective-permute-start.10) | collective-permute-done | bytes 196640 | tf_op jit(solution)/shard_map/ppermute | solution.py:47
  38.5 1.6 %collective-permute-done.3.refs_1_ = bf16[480,128]{1,0:T(8,128)(2,1)S(1)} collective-permute-done((bf16[480,128]{1,0:T(8,128)(2,1)S(1)}, bf16[480,128]{1,0:T(8,128)(2,1)S(1)}, u32[]{:S(2)}, u32[]{:S(2)}) %collective-permute-start.3) | collective-permute-done | bytes 122912 | tf_op jit(solution)/shard_map/ppermute | solution.py:47
  40.1 6.1 %collective-permute-done.4.refs_2_ = bf16[480,128]{1,0:T(8,128)(2,1)S(1)} collective-permute-done((bf16[480,128]{1,0:T(8,128)(2,1)S(1)}, bf16[480,128]{1,0:T(8,128)(2,1)S(1)}, u32[]{:S(2)}, u32[]{:S(2)}) %collective-permute-start.4) | collective-permute-done | bytes 122912 | tf_op jit(solution)/shard_map/ppermute | solution.py:47
  46.2 3.2 %signal.1 = bf16[3,128,768]{2,1,0:T(8,128)(2,1)} custom-call(bf16[480,128]{1,0:T(8,128)(2,1)S(1)} %get-tuple-element.20.refs_0_.refs_4_, bf16[480,128]{1,0:T(8,128)(2,1)S(1)} %collective-permute-done.3.refs_1_, bf16[480,128]{1,0:T(8,128)(2,1)S(1)} %collective-permute-done.4.refs_2_, bf16[480,128]{1,0:T(8,128)(2,1)S(1)} %collective-permute-done.5.refs_3_, ...), custom_call_target="tpu_custom_call" | custom-call | flops 4000000000 | bytes 6488064 | tf_op jit(solution)/shard_map/signal/pallas_call | solution.py:627
  49.4 2.8 %charge_gradient.1 = bf16[512,384]{1,0:T(8,128)(2,1)} custom-call(s32[3,2,4]{2,1,0:T(2,128)S(1)} %bitcast.2, s32[4,3]{1,0:T(4,128)S(1)} %copy-done.6, bf16[2,128,384]{2,1,0:T(8,128)(2,1)S(1)} %get-tuple-element.24.refs_0_, bf16[2,128,384]{2,1,0:T(8,128)(2,1)S(1)} %collective-permute-done.9.refs_1_, bf16[2,128,384]{2,1,0:T(8,128)(2,1)S(1)} %collective-permute-done.10.refs_2_, ...), custom_call_target="tpu_custom_call" | custom-call | flops 100000000 | bytes 786432 | tf_op jit(solution)/shard_map/charge_gradient/pallas_call | solution.py:388
  (19 shorter events, 0.0 us)
Async XLA Ops:
  3.5 2.4 %collective-permute-start = (bf16[800,384]{1,0:T(8,128)(2,1)}, bf16[800,384]{1,0:T(8,128)(2,1)S(1)}, u32[]{:S(2)}, u32[]{:S(2)}) collective-permute-start(bf16[800,384]{1,0:T(8,128)(2,1)} %get-tuple-element.15), channel_id=1, source_target_pairs={{0,4},{4,0},{8,12},{12,8},{1,5},{5,1},{9,13},{13,9},{2,6},{6,2},{1... | collective-permute-start | bytes 1843208 | tf_op jit(solution)/shard_map/ppermute | solution.py:47
  4.0 12.4 %collective-permute-start.2 = (bf16[3,16,768]{2,1,0:T(8,128)(2,1)}, bf16[3,16,768]{2,1,0:T(8,128)(2,1)S(1)}, u32[]{:S(2)}, u32[]{:S(2)}) collective-permute-start(bf16[3,16,768]{2,1,0:T(8,128)(2,1)} %get-tuple-element.19), channel_id=1, source_target_pairs={{4,8},{8,4},{5,9},{9,5},{6,10},{10,6},{7,11},{11,7},{20,24},{24,20... | collective-permute-start | bytes 221192 | tf_op jit(solution)/shard_map/ppermute | solution.py:659
  5.9 1.2 %copy-start = (f32[2,352,384]{2,1,0:T(8,128)S(1)}, f32[2,352,384]{2,1,0:T(8,128)}, u32[]{:S(2)}) copy-start(f32[2,352,384]{2,1,0:T(8,128)} %get-tuple-element.14.keep_ref.refs_0_) | copy-start | bytes 3244036
  7.3 16.7 %collective-permute-start.1 = (bf16[352,384]{1,0:T(8,128)(2,1)S(1)}, bf16[352,384]{1,0:T(8,128)(2,1)S(1)}, u32[]{:S(2)}, u32[]{:S(2)}) collective-permute-start(bf16[352,384]{1,0:T(8,128)(2,1)S(1)} %relay.1._), channel_id=1, source_target_pairs={{0,8},{4,12},{8,0},{12,4},{1,9},{5,13},{9,1},{13,5},{2,10},{6,14},... | collective-permute-start | bytes 811016 | tf_op jit(solution)/shard_map/ppermute | solution.py:47
  10.2 0.8 %copy-start.7 = (bf16[3,21,200]{2,1,0:T(8,128)(2,1)S(1)}, bf16[3,21,200]{2,1,0:T(8,128)(2,1)}, u32[]{:S(2)}) copy-start(bf16[3,21,200]{2,1,0:T(8,128)(2,1)} %response_ref.1) | copy-start | bytes 75604
  11.0 0.7 %copy-start.8 = (s32[384]{0:T(512)S(1)}, s32[384]{0:T(512)}, u32[]{:S(2)}) copy-start(s32[384]{0:T(512)} %class_ref.1) | copy-start | bytes 4612
  13.2 3.1 %copy-start.3 = (bf16[3,128,768]{2,1,0:T(8,128)(2,1)S(1)}, bf16[3,128,768]{2,1,0:T(8,128)(2,1)}, u32[]{:S(2)}) copy-start(bf16[3,128,768]{2,1,0:T(8,128)(2,1)} %own_ref.1) | copy-start | bytes 1769476
  16.3 7.7 %copy-start.1 = (f32[2,352,384]{2,1,0:T(8,128)S(1)}, f32[2,352,384]{2,1,0:T(8,128)}, u32[]{:S(2)}) copy-start(f32[2,352,384]{2,1,0:T(8,128)} %get-tuple-element.14.keep_ref.refs_0_) | copy-start | bytes 3244036
  16.3 7.7 %copy-start.4 = (f32[128,384]{1,0:T(8,128)S(1)}, f32[128,384]{1,0:T(8,128)}, u32[]{:S(2)}) copy-start(f32[128,384]{1,0:T(8,128)} %get-tuple-element.16.refs_3_) | copy-start | bytes 589828
  19.4 7.5 %collective-permute-start.8 = (bf16[3,128,128]{2,1,0:T(8,128)(2,1)S(1)}, bf16[3,128,128]{2,1,0:T(8,128)(2,1)S(1)}, u32[]{:S(2)}, u32[]{:S(2)}) collective-permute-start(bf16[3,128,128]{2,1,0:T(8,128)(2,1)S(1)} %bin_gradients.1.refs_4_.refs_0_), channel_id=1, source_target_pairs={{0,3},{1,2},{2,1},{3,0},{4,7},{5,6},{6,5},{7,4},{8,11},{9,10},{10,... | collective-permute-start | bytes 294920 | tf_op jit(solution)/shard_map/ppermute | solution.py:47
  23.4 8.0 %collective-permute-start.7 = (bf16[3,128,128]{2,1,0:T(8,128)(2,1)S(1)}, bf16[3,128,128]{2,1,0:T(8,128)(2,1)S(1)}, u32[]{:S(2)}, u32[]{:S(2)}) collective-permute-start(bf16[3,128,128]{2,1,0:T(8,128)(2,1)S(1)} %bin_gradients.1.refs_4_.refs_0_), channel_id=1, source_target_pairs={{0,2},{1,3},{2,0},{3,1},{4,6},{5,7},{6,4},{7,5},{8,10},{9,11},{10,... | collective-permute-start | bytes 294920 | tf_op jit(solution)/shard_map/ppermute | solution.py:47
  23.4 8.0 %collective-permute-start.6 = (bf16[3,128,128]{2,1,0:T(8,128)(2,1)S(1)}, bf16[3,128,128]{2,1,0:T(8,128)(2,1)S(1)}, u32[]{:S(2)}, u32[]{:S(2)}) collective-permute-start(bf16[3,128,128]{2,1,0:T(8,128)(2,1)S(1)} %bin_gradients.1.refs_4_.refs_0_), channel_id=1, source_target_pairs={{0,1},{1,0},{2,3},{3,2},{4,5},{5,4},{6,7},{7,6},{8,9},{9,8},{10,11... | collective-permute-start | bytes 294920 | tf_op jit(solution)/shard_map/ppermute | solution.py:47
  31.6 6.9 %collective-permute-start.10 = (bf16[2,128,384]{2,1,0:T(8,128)(2,1)S(1)}, bf16[2,128,384]{2,1,0:T(8,128)(2,1)S(1)}, u32[]{:S(2)}, u32[]{:S(2)}) collective-permute-start(bf16[2,128,384]{2,1,0:T(8,128)(2,1)S(1)} %get-tuple-element.24.refs_0_), channel_id=1, source_target_pairs={{0,8},{4,12},{8,0},{12,4},{1,9},{5,13},{9,1},{13,5},{2,10},{6,14},... | collective-permute-start | bytes 589832 | tf_op jit(solution)/shard_map/ppermute | solution.py:47
  33.3 6.8 %collective-permute-start.3 = (bf16[480,128]{1,0:T(8,128)(2,1)S(1)}, bf16[480,128]{1,0:T(8,128)(2,1)S(1)}, u32[]{:S(2)}, u32[]{:S(2)}) collective-permute-start(bf16[480,128]{1,0:T(8,128)(2,1)S(1)} %get-tuple-element.21), channel_id=1, source_target_pairs={{0,1},{1,0},{2,3},{3,2},{4,5},{5,4},{6,7},{7,6},{8,9},{9,8},{10,11... | collective-permute-start | bytes 368648 | tf_op jit(solution)/shard_map/ppermute | solution.py:47
  33.8 12.3 %collective-permute-start.4 = (bf16[480,128]{1,0:T(8,128)(2,1)S(1)}, bf16[480,128]{1,0:T(8,128)(2,1)S(1)}, u32[]{:S(2)}, u32[]{:S(2)}) collective-permute-start(bf16[480,128]{1,0:T(8,128)(2,1)S(1)} %get-tuple-element.22), channel_id=1, source_target_pairs={{0,2},{1,3},{2,0},{3,1},{4,6},{5,7},{6,4},{7,5},{8,10},{9,11},{10,... | collective-permute-start | bytes 368648 | tf_op jit(solution)/shard_map/ppermute | solution.py:47
  36.3 13.0 %copy-start.2 = (bf16[4,3,2,32,128]{4,3,2,1,0:T(8,128)(2,1)S(1)}, bf16[4,3,2,32,128]{4,3,2,1,0:T(8,128)(2,1)}, u32[]{:S(2)}) copy-start(bf16[4,3,2,32,128]{4,3,2,1,0:T(8,128)(2,1)} %refs_5_.1) | copy-start | bytes 589828
  36.3 13.0 %copy-start.5 = (s32[4,3,2]{0,2,1:T(2,128)S(1)}, s32[4,3,2]{0,2,1:T(2,128)}, u32[]{:S(2)}) copy-start(s32[4,3,2]{0,2,1:T(2,128)} %param.9) | copy-start | bytes 292
  36.3 13.0 %copy-start.6 = (s32[4,3]{1,0:T(4,128)S(1)}, s32[4,3]{1,0:T(4,128)}, u32[]{:S(2)}) copy-start(s32[4,3]{1,0:T(4,128)} %count_ref.1) | copy-start | bytes 148
  36.3 9.8 %collective-permute-start.5 = (bf16[480,128]{1,0:T(8,128)(2,1)S(1)}, bf16[480,128]{1,0:T(8,128)(2,1)S(1)}, u32[]{:S(2)}, u32[]{:S(2)}) collective-permute-start(bf16[480,128]{1,0:T(8,128)(2,1)S(1)} %get-tuple-element.23), channel_id=1, source_target_pairs={{0,3},{1,2},{2,1},{3,0},{4,7},{5,6},{6,5},{7,4},{8,11},{9,10},{10,... | collective-permute-start | bytes 368648 | tf_op jit(solution)/shard_map/ppermute | solution.py:47
  37.7 11.7 %collective-permute-start.9 = (bf16[2,128,384]{2,1,0:T(8,128)(2,1)S(1)}, bf16[2,128,384]{2,1,0:T(8,128)(2,1)S(1)}, u32[]{:S(2)}, u32[]{:S(2)}) collective-permute-start(bf16[2,128,384]{2,1,0:T(8,128)(2,1)S(1)} %get-tuple-element.24.refs_0_), channel_id=1, source_target_pairs={{0,4},{4,0},{8,12},{12,8},{1,5},{5,1},{9,13},{13,9},{2,6},{6,2},{1... | collective-permute-start | bytes 589832 | tf_op jit(solution)/shard_map/ppermute | solution.py:47
  38.5 10.9 %collective-permute-start.11 = (bf16[2,128,384]{2,1,0:T(8,128)(2,1)S(1)}, bf16[2,128,384]{2,1,0:T(8,128)(2,1)S(1)}, u32[]{:S(2)}, u32[]{:S(2)}) collective-permute-start(bf16[2,128,384]{2,1,0:T(8,128)(2,1)S(1)} %collective-permute-done.10.refs_2_), channel_id=1, source_target_pairs={{0,4},{4,0},{8,12},{12,8},{1,5},{5,1},{9,13},{13,9},{2,6},{6,2},{1... | collective-permute-start | bytes 589832 | tf_op jit(solution)/shard_map/ppermute | solution.py:47

commit v3 on v2

--- a/solution.py
+++ b/solution.py
@@ -74,21 +74,26 @@
     return jnp.where(lane == 0, level if first else jnp.zeros_like(rows), rows + level)
 
 
-def levels_kernel(class_ref, response_ref, _, level_ref, kind_ref, flat_ref, *, bins):
+def levels_kernel(class_ref, response_ref, _, level_ref, kind_ref, flat_ref, *, bins, slabs):
     planes, wire_taps, length = response_ref.shape
     rows = level_ref.shape[0] // planes
     groups = kind_ref.shape[0]
-    row = lax.broadcasted_iota(jnp.int32, (GROUP, LANES), 0)
-    first = lax.axis_index("drift") * bins - (WINDOW // 2 - HB)
-    last = class_ref.shape[0] - 1
+    slab = lax.axis_index("drift")
+    lane = lax.broadcasted_iota(jnp.int32, (GROUP, LANES), 1)
+    classes = jnp.broadcast_to(class_ref[...].astype(F32), (GROUP, class_ref.shape[1]))
+    tiles = [classes[:, t : t + LANES] for t in range(0, class_ref.shape[1], LANES)]
+    none = jnp.zeros((GROUP, LANES), F32)
+    numbers = none
+    for source in range(slabs):
+        at = source * bins - (WINDOW // 2 - HB)
+        tile, shift = at // LANES, at % LANES
+        pair = [tiles[t] if 0 <= t < len(tiles) else none for t in (tile, tile + 1)]
+        numbers = jnp.where(slab == source, shared_lanes(pair[0], pair[1], shift, lane), numbers)
+    x = slab * bins - (WINDOW // 2 - HB) + lane
+    numbers = jnp.where((x >= 0) & (x < HB), (CLASSES + x).astype(F32), numbers)
+    column = jnp.broadcast_to(numbers[:1], (LANES, LANES)).T.astype(jnp.int32)
     for m in range(groups):
-        kind = jnp.zeros((GROUP, LANES), jnp.int32)
-        for i in range(GROUP):
-            x = first + m * GROUP + i
-            number = class_ref[jnp.clip(x, 0, last)]
-            number = jnp.where((x >= 0) & (x < HB), CLASSES + x, number)
-            kind = jnp.where(row == i, number, kind)
-        kind_ref[m] = kind
+        kind_ref[m] = column[m * GROUP : (m + 1) * GROUP]
     flat_ref[...] = jnp.zeros(flat_ref.shape, F32)
     for p in range(planes):
         flat_ref[p * rows : p * rows + wire_taps, :length] = response_ref[p].astype(F32)
@@ -107,7 +112,7 @@
             edge = kind - CLASSES
             narrow, scale = widths(0)
             for number in range(1, CLASSES):
-                chosen = class_ref[edge] == number
+                chosen = classes[:1, edge : edge + 1] == number
                 narrow = jnp.where(chosen, widths(number)[0], narrow)
                 scale = jnp.where(chosen, widths(number)[1], scale)
             keep = inside & (step >= -TPB * edge)
@@ -124,23 +129,23 @@
         level_ref[:, kind, LANES:] = near[:, LANES:] + far
 
 
-def smeared_levels(diff_class, response, bins, before):
+def smeared_levels(diff_class, response, bins, slabs, before):
     planes, wire_taps, _ = response.shape
     rows = -(-wire_taps // 8) * 8
     groups = (bins + WINDOW // 2) // GROUP
     return pl.pallas_call(
-        functools.partial(levels_kernel, bins=bins),
+        functools.partial(levels_kernel, bins=bins, slabs=slabs),
         out_shape=(
             jax.ShapeDtypeStruct((planes * rows, CLASSES + HB, 2 * LANES), F32),
             jax.ShapeDtypeStruct((groups, GROUP, LANES), jnp.int32),
         ),
-        in_specs=[smem(), vmem(), anywhere()],
+        in_specs=[vmem(), vmem(), anywhere()],
         out_specs=(vmem(), vmem()),
         scratch_shapes=[pltpu.VMEM((planes * rows, 2 * LANES), F32)],
         compiler_params=params(),
         cost_estimate=cost(1e8, 1e6),
         name="levels",
-    )(diff_class, response, before)
+    )(diff_class[None], response, before)
 
 
 def table_kernel(level_ref, kind_ref, table_ref, sum_ref, *, wire_taps):
@@ -231,20 +236,28 @@
     )(levels, kinds)
 
 
-def back_kernel(table_ref, own_ref, received_ref, next_ref, out_ref, cot_ref, wide_ref, *, wire_taps, rows):
+def back_kernel(table_ref, own_ref, received_ref, *refs, wire_taps):
+    others, (out_ref, cot_ref, wide_ref) = refs[:-3], refs[-3:]
     blocks, span = table_ref.shape[1], table_ref.shape[3]
+    planes = table_ref.shape[0]
     _, wires, ticks = own_ref.shape
     total = received_ref.shape[1]
     half = (wire_taps - 1) // 2
     parts = ticks // total
+    side = planes * parts * EDGE
+    lows = received_ref.shape[0] - 2 * side
     plane = pl.program_id(0)
     even = lax.rem(lax.axis_index("gz"), 2) == 0
     cot_ref[EDGE : EDGE + wires] = own_ref[0]
     for part in range(parts):
         here = slice(part * total, (part + 1) * total)
-        at = rows + (plane * parts + part) * EDGE
-        near = received_ref[pl.ds(pl.multiple_of(at, EDGE), EDGE)]
-        far = next_ref[0, :, here]
+        at = (plane * parts + part) * EDGE
+        low = received_ref[pl.ds(pl.multiple_of(lows + at, EDGE), EDGE)]
+        high = received_ref[pl.ds(pl.multiple_of(lows + side + at, EDGE), EDGE)]
+        near = jnp.where(even, low, high)
+        far = jnp.zeros((EDGE, total), BF16)
+        for other in others:
+            far += other[pl.ds(pl.multiple_of(at, EDGE), EDGE)]
         cot_ref[:EDGE, here] = jnp.where(even, far, near)
         cot_ref[EDGE + wires :, here] = jnp.where(even, near, far)
     lane = lax.broadcasted_iota(jnp.int32, (wires, LANES), 1)
@@ -272,21 +285,20 @@
     out_ref[0] = result.astype(BF16)
 
 
-def backward(table, cotangent, received, beyond, wire_taps, rows):
+def backward(table, cotangent, received, others, wire_taps):
     planes, blocks, depth, span = table.shape
     _, wires, ticks = cotangent.shape
     extent = wires + 2 * EDGE
     columns = (wire_taps + 1) // 2
     return pl.pallas_call(
-        functools.partial(back_kernel, wire_taps=wire_taps, rows=rows),
+        functools.partial(back_kernel, wire_taps=wire_taps),
         grid=(planes,),
         out_shape=jax.ShapeDtypeStruct((planes, wires, LANES), BF16),
         in_specs=[
             vmem(),
             pl.BlockSpec((1, wires, ticks), lambda p: (p, 0, 0)),
-            vmem(),
-            pl.BlockSpec((1, EDGE, ticks), lambda p: (p, 0, 0)),
-        ],
+        ]
+        + [vmem()] * (1 + len(others)),
         out_specs=pl.BlockSpec((1, wires, LANES), lambda p: (p, 0, 0)),
         scratch_shapes=[
             pltpu.VMEM((extent, ticks), BF16),
@@ -295,7 +307,7 @@
         compiler_params=params(("arbitrary",)),
         cost_estimate=cost(4e9, 2 * math.prod(table.shape)),
         name="bin_gradients",
-    )(table, cotangent, received, beyond)
+    )(table, cotangent, received, *others)
 
 
 def merge_kernel(*refs, bins, lead):
@@ -343,80 +355,81 @@
 
 
 def charge_kernel(block_ref, count_ref, *refs):
-    sources, (local_ref, share_ref, out_ref, all_ref, chosen_ref) = refs[:-5], refs[-5:]
-    _, planes, entries, wire_block, width = share_ref.shape
+    sources, (local_ref, share_ref, _, out_hbm) = refs[:-8], refs[-8:-4]
+    all_ref, chosen_ref, out_ref, sems = refs[-4:]
+    cells, planes, entries, wire_block, width = share_ref.shape
     owners, _, wires, total = all_ref.shape
     per_owner = wires // wire_block
     z = lax.axis_index("gz")
-    b = pl.program_id(0)
-
-    @pl.when(b == 0)
-    def _():
-        if len(sources) == 1:
-            all_ref[...] = sources[0][...]
-        else:
-            for k, source in enumerate(sources):
-                all_ref[z ^ k] = source[...]
-
+    if len(sources) == 1:
+        all_ref[...] = sources[0][...]
+    else:
+        for k, source in enumerate(sources):
+            all_ref[z ^ k] = source[...]
     empty = jnp.zeros((wire_block, total), BF16)
-    for p in range(planes):
-        for k in range(entries):
-            name = block_ref[p, k, b]
-            if p < planes - 1:
-                name = jnp.clip(name, 0, owners * per_owner - 1)
-                owner = name // per_owner
-                start = pl.multiple_of((name - owner * per_owner) * wire_block, wire_block)
-                rows = all_ref[owner, p, pl.ds(start, wire_block), :]
-            else:
-                name = jnp.clip(name - z * per_owner, 0, per_owner - 1)
-                start = pl.multiple_of(name * wire_block, wire_block)
-                rows = local_ref[pl.ds(start, wire_block), :]
-            at = (p * entries + k) * wire_block
-            chosen_ref[at : at + wire_block] = jnp.where(k < count_ref[b, p], rows, empty)
-    out_ref[...] = lax.dot_general(
-        share_ref[0].reshape(planes * entries * wire_block, width),
-        chosen_ref[...],
-        (((0,), (0,)), ((), ())),
-        preferred_element_type=F32,
-    ).astype(BF16)
-
-
-def charge_gradient(ovl_block, ovl_count, sources, local, intersection, owners):
+    stores = []
+    for b in range(cells):
+        for p in range(planes):
+            for k in range(entries):
+                name = block_ref[p, k, b]
+                if p < planes - 1:
+                    name = jnp.clip(name, 0, owners * per_owner - 1)
+                    owner = name // per_owner
+                    start = pl.multiple_of((name - owner * per_owner) * wire_block, wire_block)
+                    rows = all_ref[owner, p, pl.ds(start, wire_block), :]
+                else:
+                    name = jnp.clip(name - z * per_owner, 0, per_owner - 1)
+                    start = pl.multiple_of(name * wire_block, wire_block)
+                    rows = local_ref[pl.ds(start, wire_block), :]
+                at = (p * entries + k) * wire_block
+                chosen_ref[b, at : at + wire_block] = jnp.where(k < count_ref[b, p], rows, empty)
+        here = slice(b * width, (b + 1) * width)
+        out_ref[here] = lax.dot_general(
+            share_ref[b].reshape(planes * entries * wire_block, width),
+            chosen_ref[b],
+            (((0,), (0,)), ((), ())),
+            preferred_element_type=F32,
+        ).astype(BF16)
+        store = pltpu.make_async_copy(out_ref.at[here], out_hbm.at[here], sems.at[b])
+        store.start()
+        stores.append(store)
+    for store in stores:
+        store.wait()
+
+
+def charge_gradient(ovl_block, ovl_count, sources, local, intersection, owners, before):
     cells, planes, entries, wire_block, width = intersection.shape
     wires, total = local.shape
     shape = (owners, planes - 1, wires, total)
     return pl.pallas_call(
         charge_kernel,
-        grid=(cells,),
         out_shape=jax.ShapeDtypeStruct((cells * width, total), BF16),
-        in_specs=[smem(), smem()]
-        + [vmem()] * (len(sources) + 1)
-        + [pl.BlockSpec((1, planes, entries, wire_block, width), lambda b: (b, 0, 0, 0, 0))],
-        out_specs=pl.BlockSpec((width, total), lambda b: (b, 0)),
+        in_specs=[smem(), smem()] + [vmem()] * (len(sources) + 3),
+        out_specs=anywhere(),
         scratch_shapes=[
             pltpu.VMEM(shape, BF16),
-            pltpu.VMEM((planes * entries * wire_block, total), BF16),
+            pltpu.VMEM((cells, planes * entries * wire_block, total), BF16),
+            pltpu.VMEM((cells * width, total), BF16),
+            pltpu.SemaphoreType.DMA((cells,)),
         ],
-        compiler_params=params(("arbitrary",)),
+        compiler_params=params(),
         cost_estimate=cost(1e8, 2 * math.prod(shape)),
         name="charge_gradient",
-    )(jnp.transpose(ovl_block, (1, 2, 0)), ovl_count, *sources, local, intersection)
+    )(jnp.transpose(ovl_block, (1, 2, 0)), ovl_count, *sources, local, intersection, before)
 
 
 def pieces_kernel(
-    block_hbm, count_hbm, charge_hbm, share_hbm, cot_hbm, keep_ref, give_ref, local_ref, next_ref,
+    block_hbm, count_hbm, charge_hbm, share_hbm, cot_hbm, own_ref, keep_ref, give_ref, local_ref,
     block_ref, count_ref, charge_ref, share_ref, edge_ref, cross_ref, sems,
 ):
     cells, planes, entries, wire_block, width = share_ref.shape
     wires, total = local_ref.shape
-    ticks = edge_ref.shape[2]
+    ticks = edge_ref.shape[3]
     per_owner = wires // wire_block
-    halves = keep_ref.shape[0]
+    cut = own_ref.shape[0]
+    halves = 1 + keep_ref.shape[0]
     owners = 2 * halves
     z = lax.axis_index("gz")
-    even = lax.rem(z, 2) == 0
-    upper = pl.ds(pl.multiple_of(jnp.where(even, wires - EDGE, 0), EDGE), EDGE)
-    lower = pl.ds(pl.multiple_of(jnp.where(even, 0, wires - EDGE), EDGE), EDGE)
     loads = [
         pltpu.make_async_copy(source, target, sems.at[i])
         for i, (source, target) in enumerate(
@@ -425,8 +438,8 @@
                 (count_hbm, count_ref),
                 (charge_hbm, charge_ref),
                 (share_hbm, share_ref),
-                (cot_hbm.at[:, upper], edge_ref),
-                (cot_hbm.at[:, lower], next_ref),
+                (cot_hbm.at[:, :EDGE], edge_ref.at[0]),
+                (cot_hbm.at[:, wires - EDGE :], edge_ref.at[1]),
             )
         )
     ]
@@ -461,7 +474,6 @@
                     start = pl.multiple_of(name * wire_block, wire_block)
                     local_ref[pl.ds(start, wire_block)] += piece
     extent = wires + 2 * EDGE
-    cut = keep_ref.shape[1]
     none = jnp.zeros((EDGE, total), F32)
     for k in range(owners):
         to = z ^ k
@@ -476,13 +488,16 @@
             at += rows.shape[0]
             if k % 2:
                 give_ref[k // 2 * cut + here.start : k // 2 * cut + here.stop] = coded(rows, 0)
+            elif k:
+                keep_ref[k // 2 - 1, here] = coded(rows, 0)
             else:
-                keep_ref[k // 2, here] = rows
+                own_ref[here] = rows
     at = halves * cut
-    for p in range(planes):
-        for part in range(ticks // total):
-            give_ref[at : at + EDGE] = edge_ref[p, :, part * total : (part + 1) * total]
-            at += EDGE
+    for side in range(2):
+        for p in range(planes):
+            for part in range(ticks // total):
+                give_ref[at : at + EDGE] = edge_ref[side, p, :, part * total : (part + 1) * total]
+                at += EDGE
 
 
 def cut_pieces(ovl_block, ovl_count, charge, intersection, cotangent, owners):
@@ -490,17 +505,16 @@
     total = charge.shape[1]
     _, wires, ticks = cotangent.shape
     rows = (planes - 1) * (wires + 2 * EDGE) + 2 * EDGE
-    cut = (owners // 2, rows, total)
-    edges = planes * EDGE * ticks // total
+    edges = 2 * planes * EDGE * ticks // total
     hbm = pl.BlockSpec(memory_space=pltpu.HBM)
     blocks = jnp.transpose(ovl_block, (1, 2, 0))
     return pl.pallas_call(
         pieces_kernel,
         out_shape=(
-            jax.ShapeDtypeStruct(cut, F32),
+            jax.ShapeDtypeStruct((rows, total), F32),
+            jax.ShapeDtypeStruct((owners // 2 - 1, rows, total), BF16),
             jax.ShapeDtypeStruct((owners // 2 * rows + edges, total), BF16),
             jax.ShapeDtypeStruct((wires, total), F32),
-            jax.ShapeDtypeStruct((planes, EDGE, ticks), BF16),
         ),
         in_specs=[hbm] * 5,
         out_specs=(vmem(), vmem(), vmem(), vmem()),
@@ -509,7 +523,7 @@
             pltpu.SMEM(ovl_count.shape, jnp.int32),
             pltpu.VMEM(charge.shape, BF16),
             pltpu.VMEM(intersection.shape, BF16),
-            pltpu.VMEM((planes, EDGE, ticks), BF16),
+            pltpu.VMEM((2, planes, EDGE, ticks), BF16),
             pltpu.VMEM((planes - 1, owners * wires + 2 * EDGE, total), F32),
             pltpu.SemaphoreType.DMA((6,)),
         ],
@@ -520,32 +534,46 @@
 
 
 def relay_kernel(keep_ref, received_ref, *outs):
-    rows = keep_ref.shape[1]
-    for j, out in enumerate(outs, 1):
-        summed = keep_ref[j] + plain(received_ref[j * rows : (j + 1) * rows], True)
-        out[...] = coded(summed, 0)
+    others, rows, _ = keep_ref.shape
+    edges = (received_ref.shape[0] - (others + 1) * rows) // 2
+    z = lax.axis_index("gz")
+    even = lax.rem(z, 2) == 0
+    low = received_ref[(others + 1) * rows : (others + 1) * rows + edges]
+    high = received_ref[(others + 1) * rows + edges :]
+    for j in range(others):
+        to = z ^ (2 * (j + 1))
+        summed = plain(keep_ref[j], True)
+        summed += plain(received_ref[(j + 1) * rows : (j + 2) * rows], True)
+        outs[j][...] = coded(summed, 0)
+        upward, downward = even & (to == z + 2), jnp.logical_not(even) & (to == z - 2)
+        outs[others + j][...] = jnp.where(
+            upward, high, jnp.where(downward, low, jnp.zeros_like(low))
+        )
 
 
 def relay(keep, received):
-    halves, rows, total = keep.shape
-    return pl.pallas_call(
+    others, rows, total = keep.shape
+    edges = (received.shape[0] - (others + 1) * rows) // 2
+    outs = pl.pallas_call(
         relay_kernel,
-        out_shape=(jax.ShapeDtypeStruct((rows, total), BF16),) * (halves - 1),
+        out_shape=(jax.ShapeDtypeStruct((rows, total), BF16),) * others
+        + (jax.ShapeDtypeStruct((edges, total), BF16),) * others,
         in_specs=[vmem(), vmem()],
-        out_specs=(vmem(),) * (halves - 1),
+        out_specs=(vmem(),) * (2 * others),
         compiler_params=params(),
-        cost_estimate=cost(1e7, 6 * halves * rows * total),
+        cost_estimate=cost(1e7, 6 * others * rows * total),
         name="relay",
     )(keep, received)
+    return outs[:others], outs[others:]
 
 
 def slabs_kernel(*refs, bins, lead, slabs):
-    count = len(refs) - slabs - 1
+    count = len(refs) - slabs.bit_length() - 1
     keep_ref, received_ref, others, local_ref = refs[0], refs[1], refs[2 : count - 2], refs[count - 2]
     outs, cut_ref = refs[count:-1], refs[-1]
     total = local_ref.shape[1]
-    cut = keep_ref.shape[1]
-    summed = keep_ref[0] + plain(received_ref[:cut], True)
+    cut = keep_ref.shape[0]
+    summed = keep_ref[...] + plain(received_ref[:cut], True)
     for other in others:
         summed += plain(other[...], True)
     edge = cut - 2 * EDGE
@@ -563,30 +591,56 @@
         value = shared_lanes(pair[0], pair[1], shift, lane)
         cut_ref[to] = jnp.where(lane == 0, level, value).astype(BF16)
     slab = lax.axis_index("drift")
-    for k, out in enumerate(outs):
-        out[...] = cut_ref[slab ^ k]
+    outs[0][...] = cut_ref[slab]
+    size = rows.shape[0]
+    for s, out in enumerate(outs[1:]):
+        for i in range(slabs >> (s + 1)):
+            out[i * size : (i + 1) * size] = cut_ref[slab ^ ((2 * i + 1) << s)]
 
 
 def cut_slabs(keep, received, others, local, bins, slabs, before):
     wires, total = local.shape
-    rows = keep.shape[1] + wires
-    cut = jax.ShapeDtypeStruct((rows, LANES), BF16)
-    first = pl.BlockSpec((1,) + keep.shape[1:], lambda i: (0, 0, 0))
+    rows = keep.shape[0] + wires
+    steps = slabs.bit_length() - 1
+    counts = [1] + [slabs >> (s + 1) for s in range(steps)]
     return pl.pallas_call(
         functools.partial(slabs_kernel, bins=bins, lead=WINDOW // 2 - HB, slabs=slabs),
-        grid=(1,),
-        out_shape=(cut,) * slabs,
-        in_specs=[first] + [vmem()] * (2 + len(others)) + [anywhere()],
-        out_specs=(vmem(),) * slabs,
+        out_shape=tuple(jax.ShapeDtypeStruct((n * rows, LANES), BF16) for n in counts),
+        in_specs=[vmem()] * (3 + len(others)) + [anywhere()],
+        out_specs=(vmem(),) * len(counts),
         scratch_shapes=[pltpu.VMEM((slabs, rows, LANES), BF16)],
-        compiler_params=params(("arbitrary",)),
+        compiler_params=params(),
         cost_estimate=cost(1e8, 4 * rows * total),
         name="slab_currents",
     )(keep, received, *others, local, before)
 
 
+def pass_kernel(*refs, step, size):
+    own_ref, arrived, out_ref = refs[0], refs[1:-1], refs[-1]
+    for i in range(own_ref.shape[0] // size):
+        here = slice(i * size, (i + 1) * size)
+        total = plain(own_ref[here], False)
+        for r, other in enumerate(arrived):
+            at = ((2 * i + 1) << step) >> (r + 1)
+            total += plain(other[at * size : (at + 1) * size], False)
+        out_ref[here] = coded(total, WINDOW // 2)
+
+
+def pass_on(own, arrived, step, size):
+    return pl.pallas_call(
+        functools.partial(pass_kernel, step=step, size=size),
+        out_shape=jax.ShapeDtypeStruct(own.shape, BF16),
+        in_specs=[vmem()] * (1 + len(arrived)),
+        out_specs=vmem(),
+        compiler_params=params(),
+        cost_estimate=cost(1e6, 4 * math.prod(own.shape)),
+        name="pass_on",
+    )(own, *arrived)
+
+
 def signal_kernel(*refs, wire_taps):
-    parts, (table_ref, out_ref, even_ref, odd_ref, level_ref, lines_ref) = refs[:-6], refs[-6:]
+    parts, (table_ref, out_ref, token_ref, even_ref, odd_ref, level_ref, lines_ref) = refs[:-7], refs[-7:]
+    token_ref[...] = jnp.zeros(token_ref.shape, F32)
     blocks, span = table_ref.shape[1], table_ref.shape[3]
     wires = out_ref.shape[1]
     half = (wire_taps - 1) // 2
@@ -627,10 +681,15 @@
     return pl.pallas_call(
         functools.partial(signal_kernel, wire_taps=wire_taps),
         grid=(planes,),
-        out_shape=jax.ShapeDtypeStruct((planes, wires, blocks * span), BF16),
-        in_specs=[part] * len(parts)
-        + [vmem()],
-        out_specs=pl.BlockSpec((1, wires, blocks * span), lambda p: (p, 0, 0)),
+        out_shape=(
+            jax.ShapeDtypeStruct((planes, wires, blocks * span), BF16),
+            jax.ShapeDtypeStruct((8, LANES), F32),
+        ),
+        in_specs=[part] * len(parts) + [vmem()],
+        out_specs=(
+            pl.BlockSpec((1, wires, blocks * span), lambda p: (p, 0, 0)),
+            pl.BlockSpec((8, LANES), lambda p: (0, 0)),
+        ),
         scratch_shapes=[
             pltpu.VMEM((extent, LANES), F32),
             pltpu.VMEM((extent, LANES), F32),
@@ -651,32 +710,37 @@
     wire_taps = response.shape[1]
     bins = total // slabs
 
-    keep, give, local_currents, edges = cut_pieces(
+    currents, keep, give, local_currents = cut_pieces(
         ovl_block, ovl_count, charge, intersection, cotangent, owners
     )
     received = swap(give, "gz", 1)
-    pairs = [(i, i + 1) for i in range(1, owners - 1, 2)]
-    beyond = lax.ppermute(edges, "gz", pairs + [(j, i) for i, j in pairs])
-    sums = relay(keep, received) if owners > 2 else ()
+    sums, edges = relay(keep, received) if owners > 2 else ((), ())
+    beyond = [swap(block, "gz", 2 * j) for j, block in enumerate(edges, 1)]
     others = [swap(block, "gz", 2 * j) for j, block in enumerate(sums, 1)]
 
-    levels, kinds = smeared_levels(diff_class, response, bins, sums[0] if sums else received)
+    before = sums[0] if sums else received
+    levels, kinds = smeared_levels(diff_class, response, bins, slabs, before)
     table = build_table(levels, kinds, planes, wire_taps, ticks)
-    rows = keep.shape[0] * keep.shape[1]
-    partial = backward(table, cotangent, received, beyond, wire_taps, rows)
+    partial = backward(table, cotangent, received, beyond, wire_taps)
     spread = [partial] + [swap(partial, "drift", k) for k in range(1, slabs)]
 
-    cuts = cut_slabs(keep, received, others, local_currents, bins, slabs, partial)
-    windows = [cuts[0]] + [swap(cuts[k], "drift", k) for k in range(1, slabs)]
-    signal = forward(windows, table, wires, wire_taps)
-
-    cross, own = merge(spread, bins, total, cuts[0])
+    cuts = cut_slabs(currents, received, others, local_currents, bins, slabs, partial)
+    windows, ready = [cuts[0]], cuts[0]
+    for step, block in enumerate(cuts[1:]):
+        if step:
+            block = ready = pass_on(block, windows[1:], step, cuts[0].shape[0])
+        windows.append(swap(block, "drift", 1 << step))
+
+    cross, own = merge(spread, bins, total, ready)
     if owners == 4:
         across = swap(cross, "gz", 2)
         sources = [cross, swap(cross, "gz", 1), across, swap(across, "gz", 1)]
     else:
         sources = [lax.all_gather(cross, "gz", axis=0)]
-    charge_grad = charge_gradient(ovl_block, ovl_count, sources, own, intersection, owners)
+    signal, done = forward(windows, table, wires, wire_taps)
+    charge_grad = charge_gradient(
+        ovl_block, ovl_count, sources, own, intersection, owners, done
+    )
     return signal, charge_grad
 
 

time: 52.4 us -> 47.3 us (0.903)
  waiting for transfers between devices: 16.4 us -> 13.4 us
  Pallas kernels: 17.5 us -> 16.3 us
  starting transfers between devices: 14.8 us -> 14.2 us
    ppermute x11, waiting for transfers between devices: 16.4 us -> 13.4 us  [swap(): return lax.ppermute(block, axis, [(i, i ^ distance) for i in range(count)])]
    pallas_call x4 -> x5, Pallas kernels: 10.2 us -> 8.87 us  [the longest x1 3.07 us: backward(): pl.pallas_call(functools.partial(back_kernel, wire_taps=wire_taps), grid=...]
    unnamed x18 -> x16, local copies, waits for them, and re-layouts: 2.71 us -> 1.75 us
    broadcast_in_dim x0 -> x1, local copies, waits for them, and re-layouts: none -> 0.68 us  [smeared_levels(): diff_class[None]]
    ppermute x1 -> x0, starting transfers between devices: 0.65 us -> none  [local(): beyond = lax.ppermute(edges, 'gz', pairs + [(j, i) for i, j in pairs])]
  transfers between devices with their start and end apart: 12 -> 11, of which waited for: 6 -> 7; matrix products, arithmetic and copies ran while one was open for 0% -> 1% of each run, Pallas kernels for 22% -> 22%
where the time goes in v3:
time: 47.3 us; the launch traced here: 47 us
  Pallas kernels  16.3 us (34%)
  starting transfers between devices  14.2 us (30%)
  waiting for transfers between devices  13.4 us (28%)
  local copies, waits for them, and re-layouts  2.43 us (5%)
  between operations  0.76 us (2%)
    ppermute x11, starting transfers between devices, swap(): return lax.ppermute(block, axis, [(i, i ^ distance) for i in range(count)])  14.2 us
    ppermute x11, waiting for transfers between devices, swap(): return lax.ppermute(block, axis, [(i, i ^ distance) for i in range(count)])  13.4 us
    pallas_call x1, Pallas kernels, forward(): pl.pallas_call(functools.partial(signal_kernel, wire_taps=wire_taps), gri...  3.25 us
    pallas_call x1, Pallas kernels, build_table(): pl.pallas_call(functools.partial(table_kernel, wire_taps=wire_taps), out_...  3.07 us
    pallas_call x1, Pallas kernels, backward(): pl.pallas_call(functools.partial(back_kernel, wire_taps=wire_taps), grid=...  3.07 us
    pallas_call x1, Pallas kernels, cut_pieces(): pl.pallas_call(pieces_kernel, out_shape=(jax.ShapeDtypeStruct((rows, tota...  2.84 us
    pallas_call x1, Pallas kernels, charge_gradient(): pl.pallas_call(charge_kernel, out_shape=jax.ShapeDtypeStruct((cells * wid...  1.84 us
    unnamed x16, local copies, waits for them, and re-layouts  1.75 us
  transfers between devices with their start and end apart: 11, of which 7 were waited for; matrix products, arithmetic and copies ran while one was open for 1% of the time, Pallas kernels for 22%

profile of v3, /device:TPU:0, one launch (start us, length us, event | category | flops | bytes accessed | tf_op | source)
XLA Modules:
  0.0 47.0 jit_solution(5335239229528274372)
XLA Ops:
  0.6 2.8 %pieces.1 = (f32[352,384]{1,0:T(8,128)}, bf16[1,352,384]{2,1,0:T(8,128)(2,1)}, bf16[896,384]{1,0:T(8,128)(2,1)}, f32[128,384]{1,0:T(8,128)}) custom-call(s32[3,2,4]{2,1,0:T(2,128)} %bitcast.1, s32[4,3]{1,0:T(4,128)} %count_ref.1, bf16[512,384]{1,0:T(8,128)(2,1)} %charge_hbm.1, bf16[4,3,2,32,128]{4,3,2,1,0:T(8,128)(2,1)} %refs_5_.1, bf16[3,128,768]{2,1,0:T(8,128)(2,1)} %own_ref.1), custom_call_target="tpu_custom_call" | custom-call | flops 100000000 | bytes 2162688 | tf_op jit(solution)/shard_map/pieces/pallas_call | solution.py:511
  3.5 0.5 %collective-permute-start = (bf16[896,384]{1,0:T(8,128)(2,1)}, bf16[896,384]{1,0:T(8,128)(2,1)S(1)}, u32[]{:S(2)}, u32[]{:S(2)}) collective-permute-start(bf16[896,384]{1,0:T(8,128)(2,1)} %get-tuple-element.18), channel_id=1, source_target_pairs={{0,4},{4,0},{8,12},{12,8},{1,5},{5,1},{9,13},{13,9},{2,6},{6,2},{1... | collective-permute-start | bytes 2064392 | tf_op jit(solution)/shard_map/ppermute | solution.py:47
  4.0 0.7 %broadcast_in_dim.3.class_ref = s32[1,384]{1,0:T(1,128)S(1)} reshape(s32[384]{0:T(512)} %param.11) | data formatting | bytes 3072 | tf_op jit(solution)/shard_map/broadcast_in_dim | solution.py:148
  4.7 1.3 %collective-permute-done.received_ref.refs_1_ = bf16[896,384]{1,0:T(8,128)(2,1)S(1)} collective-permute-done((bf16[896,384]{1,0:T(8,128)(2,1)}, bf16[896,384]{1,0:T(8,128)(2,1)S(1)}, u32[]{:S(2)}, u32[]{:S(2)}) %collective-permute-start) | collective-permute-done | bytes 688160 | tf_op jit(solution)/shard_map/ppermute | solution.py:47
  6.0 1.0 %copy-done.3 = bf16[1,352,384]{2,1,0:T(8,128)(2,1)S(1)} copy-done((bf16[1,352,384]{2,1,0:T(8,128)(2,1)S(1)}, bf16[1,352,384]{2,1,0:T(8,128)(2,1)}, u32[]{:S(2)}) %copy-start.3) | copy-done | bytes 270360
  6.9 0.3 relay.1
  7.2 2.9 %collective-permute-start.2 = (bf16[96,384]{1,0:T(8,128)(2,1)S(1)}, bf16[96,384]{1,0:T(8,128)(2,1)S(1)}, u32[]{:S(2)}, u32[]{:S(2)}) collective-permute-start(bf16[96,384]{1,0:T(8,128)(2,1)S(1)} %get-tuple-element.24), channel_id=1, source_target_pairs={{0,8},{4,12},{8,0},{12,4},{1,9},{5,13},{9,1},{13,5},{2,10},{6,14},... | collective-permute-start | bytes 221192 | tf_op jit(solution)/shard_map/ppermute | solution.py:47
  10.1 0.1 collective-permute-start.1
  10.2 0.8 %copy-done.7 = bf16[3,21,200]{2,1,0:T(8,128)(2,1)S(1)} copy-done((bf16[3,21,200]{2,1,0:T(8,128)(2,1)S(1)}, bf16[3,21,200]{2,1,0:T(8,128)(2,1)}, u32[]{:S(2)}) %copy-start.7) | copy-done | bytes 25224
  11.0 0.9 %levels.1 = (f32[72,8,256]{2,1,0:T(8,128)S(1)}, s32[16,8,128]{2,1,0:T(8,128)S(1)}) custom-call(s32[1,384]{1,0:T(1,128)S(1)} %broadcast_in_dim.3.class_ref, bf16[3,21,200]{2,1,0:T(8,128)(2,1)S(1)} %copy-done.7, bf16[352,384]{1,0:T(8,128)(2,1)S(1)} %get-tuple-element.20._), custom_call_target="tpu_custom_call" | custom-call | flops 100000000 | bytes 1000000 | tf_op jit(solution)/shard_map/levels/pallas_call | solution.py:136
  11.9 0.0 copy-start.1
  11.9 3.1 %table.1.table_ref.refs_3_ = bf16[3,3,1408,256]{3,2,1,0:T(8,128)(2,1)S(1)} custom-call(f32[72,8,256]{2,1,0:T(8,128)S(1)} %get-tuple-element.22.level_ref, s32[16,8,128]{2,1,0:T(8,128)S(1)} %get-tuple-element.23.kind_ref), custom_call_target="tpu_custom_call" | custom-call | flops 4000000000 | bytes 6488064 | tf_op jit(solution)/shard_map/table/pallas_call | solution.py:227
  15.0 0.0 copy-start.2
  15.0 3.1 %bin_gradients.1.refs_4_.refs_0_ = bf16[3,128,128]{2,1,0:T(8,128)(2,1)S(1)} custom-call(bf16[3,3,1408,256]{3,2,1,0:T(8,128)(2,1)S(1)} %table.1.table_ref.refs_3_, bf16[3,128,768]{2,1,0:T(8,128)(2,1)S(1)} %copy-done.1, bf16[896,384]{1,0:T(8,128)(2,1)S(1)} %collective-permute-done.received_ref.refs_1_, bf16[96,384]{1,0:T(8,128)(2,1)S(1)} %collective-permute-done.2.refs_0_), custom_call_target="tpu_custom_call" | custom-call | flops 4000000000 | bytes 6488064 | tf_op jit(solution)/shard_map/bin_gradients/pallas_call | solution.py:293
  18.1 0.4 collective-permute-done.1.refs_2_
  18.5 0.6 %slab_currents.1 = (bf16[480,128]{1,0:T(8,128)(2,1)S(1)}, bf16[960,128]{1,0:T(8,128)(2,1)S(1)}, bf16[480,128]{1,0:T(8,128)(2,1)S(1)}) custom-call(f32[352,384]{1,0:T(8,128)S(1)} %copy-done.2, bf16[896,384]{1,0:T(8,128)(2,1)S(1)} %collective-permute-done.received_ref.refs_1_, bf16[352,384]{1,0:T(8,128)(2,1)S(1)} %collective-permute-done.1.refs_2_, ...), custom_call_target="tpu_custom_call" | custom-call | flops 100000000 | bytes 737280 | tf_op jit(solution)/shard_map/slab_currents/pallas_call | solution.py:606
  19.1 1.9 %collective-permute-start.3 = (bf16[960,128]{1,0:T(8,128)(2,1)S(1)}, bf16[960,128]{1,0:T(8,128)(2,1)S(1)}, u32[]{:S(2)}, u32[]{:S(2)}) collective-permute-start(bf16[960,128]{1,0:T(8,128)(2,1)S(1)} %get-tuple-element.26), channel_id=1, source_target_pairs={{0,1},{1,0},{2,3},{3,2},{4,5},{5,4},{6,7},{7,6},{8,9},{9,8},{10,11... | collective-permute-start | bytes 737288 | tf_op jit(solution)/shard_map/ppermute | solution.py:47
  21.0 2.5 %collective-permute-start.7 = (bf16[3,128,128]{2,1,0:T(8,128)(2,1)S(1)}, bf16[3,128,128]{2,1,0:T(8,128)(2,1)S(1)}, u32[]{:S(2)}, u32[]{:S(2)}) collective-permute-start(bf16[3,128,128]{2,1,0:T(8,128)(2,1)S(1)} %bin_gradients.1.refs_4_.refs_0_), channel_id=1, source_target_pairs={{0,3},{1,2},{2,1},{3,0},{4,7},{5,6},{6,5},{7,4},{8,11},{9,10},{10,... | collective-permute-start | bytes 294920 | tf_op jit(solution)/shard_map/ppermute | solution.py:47
  23.5 0.1 collective-permute-start.6
  23.7 1.8 %collective-permute-start.5 = (bf16[3,128,128]{2,1,0:T(8,128)(2,1)S(1)}, bf16[3,128,128]{2,1,0:T(8,128)(2,1)S(1)}, u32[]{:S(2)}, u32[]{:S(2)}) collective-permute-start(bf16[3,128,128]{2,1,0:T(8,128)(2,1)S(1)} %bin_gradients.1.refs_4_.refs_0_), channel_id=1, source_target_pairs={{0,1},{1,0},{2,3},{3,2},{4,5},{5,4},{6,7},{7,6},{8,9},{9,8},{10,11... | collective-permute-start | bytes 294920 | tf_op jit(solution)/shard_map/ppermute | solution.py:47
  25.4 5.7 %collective-permute-done.3.refs_1_ = bf16[960,128]{1,0:T(8,128)(2,1)S(1)} collective-permute-done((bf16[960,128]{1,0:T(8,128)(2,1)S(1)}, bf16[960,128]{1,0:T(8,128)(2,1)S(1)}, u32[]{:S(2)}, u32[]{:S(2)}) %collective-permute-start.3) | collective-permute-done | bytes 245792 | tf_op jit(solution)/shard_map/ppermute | solution.py:47
  31.1 0.2 pass_on.1.refs_4_
  31.3 1.2 %collective-permute-done.7.refs_3_ = bf16[3,128,128]{2,1,0:T(8,128)(2,1)S(1)} collective-permute-done((bf16[3,128,128]{2,1,0:T(8,128)(2,1)S(1)}, bf16[3,128,128]{2,1,0:T(8,128)(2,1)S(1)}, u32[]{:S(2)}, u32[]{:S(2)}) %collective-permute-start.7) | collective-permute-done | bytes 98336 | tf_op jit(solution)/shard_map/ppermute | solution.py:47
  32.5 0.4 collective-permute-done.5.refs_1_
  32.9 0.2 merge_bins.1
  33.1 1.7 %collective-permute-start.9 = (bf16[2,128,384]{2,1,0:T(8,128)(2,1)S(1)}, bf16[2,128,384]{2,1,0:T(8,128)(2,1)S(1)}, u32[]{:S(2)}, u32[]{:S(2)}) collective-permute-start(bf16[2,128,384]{2,1,0:T(8,128)(2,1)S(1)} %get-tuple-element.29.refs_0_), channel_id=1, source_target_pairs={{0,8},{4,12},{8,0},{12,4},{1,9},{5,13},{9,1},{13,5},{2,10},{6,14},... | collective-permute-start | bytes 589832 | tf_op jit(solution)/shard_map/ppermute | solution.py:47
  34.8 2.6 %collective-permute-start.4 = (bf16[480,128]{1,0:T(8,128)(2,1)S(1)}, bf16[480,128]{1,0:T(8,128)(2,1)S(1)}, u32[]{:S(2)}, u32[]{:S(2)}) collective-permute-start(bf16[480,128]{1,0:T(8,128)(2,1)S(1)} %pass_on.1.refs_4_), channel_id=1, source_target_pairs={{0,2},{1,3},{2,0},{3,1},{4,6},{5,7},{6,4},{7,5},{8,10},{9,11},{10,... | collective-permute-start | bytes 368648 | tf_op jit(solution)/shard_map/ppermute | solution.py:47
  37.4 0.0 collective-permute-start.8
  37.4 1.4 %collective-permute-done.9.refs_2_ = bf16[2,128,384]{2,1,0:T(8,128)(2,1)S(1)} collective-permute-done((bf16[2,128,384]{2,1,0:T(8,128)(2,1)S(1)}, bf16[2,128,384]{2,1,0:T(8,128)(2,1)S(1)}, u32[]{:S(2)}, u32[]{:S(2)}) %collective-permute-start.9) | collective-permute-done | bytes 196640 | tf_op jit(solution)/shard_map/ppermute | solution.py:47
  38.8 3.1 %collective-permute-done.4.refs_2_ = bf16[480,128]{1,0:T(8,128)(2,1)S(1)} collective-permute-done((bf16[480,128]{1,0:T(8,128)(2,1)S(1)}, bf16[480,128]{1,0:T(8,128)(2,1)S(1)}, u32[]{:S(2)}, u32[]{:S(2)}) %collective-permute-start.4) | collective-permute-done | bytes 122912 | tf_op jit(solution)/shard_map/ppermute | solution.py:47
  41.9 3.3 %signal.1 = (bf16[3,128,768]{2,1,0:T(8,128)(2,1)}, f32[8,128]{1,0:T(8,128)S(1)}) custom-call(bf16[480,128]{1,0:T(8,128)(2,1)S(1)} %get-tuple-element.25.refs_0_, bf16[960,128]{1,0:T(8,128)(2,1)S(1)} %collective-permute-done.3.refs_1_, bf16[480,128]{1,0:T(8,128)(2,1)S(1)} %collective-permute-done.4.refs_2_, bf16[3,3,1408,256]{3,2,1,0:T(8,128)(2,1)S(1)} %table.1.table_ref.refs_3_), custom_call_target="tpu_custom_call" | custom-call | flops 4000000000 | bytes 6488064 | tf_op jit(solution)/shard_map/signal/pallas_call | solution.py:681
  45.2 1.8 %charge_gradient.1 = bf16[512,384]{1,0:T(8,128)(2,1)} custom-call(s32[3,2,4]{2,1,0:T(2,128)S(1)} %bitcast.2, s32[4,3]{1,0:T(4,128)S(1)} %copy-done.6, bf16[2,128,384]{2,1,0:T(8,128)(2,1)S(1)} %get-tuple-element.29.refs_0_, bf16[2,128,384]{2,1,0:T(8,128)(2,1)S(1)} %collective-permute-done.8.refs_1_, bf16[2,128,384]{2,1,0:T(8,128)(2,1)S(1)} %collective-permute-done.9.refs_2_, ...), custom_call_target="tpu_custom_call" | custom-call | flops 100000000 | bytes 786432 | tf_op jit(solution)/shard_map/charge_gradient/pallas_call | solution.py:404
  (17 shorter events, 0.0 us)
Async XLA Ops:
  3.5 2.5 %collective-permute-start = (bf16[896,384]{1,0:T(8,128)(2,1)}, bf16[896,384]{1,0:T(8,128)(2,1)S(1)}, u32[]{:S(2)}, u32[]{:S(2)}) collective-permute-start(bf16[896,384]{1,0:T(8,128)(2,1)} %get-tuple-element.18), channel_id=1, source_target_pairs={{0,4},{4,0},{8,12},{12,8},{1,5},{5,1},{9,13},{13,9},{2,6},{6,2},{1... | collective-permute-start | bytes 2064392 | tf_op jit(solution)/shard_map/ppermute | solution.py:47
  6.0 1.0 %copy-start.3 = (bf16[1,352,384]{2,1,0:T(8,128)(2,1)S(1)}, bf16[1,352,384]{2,1,0:T(8,128)(2,1)}, u32[]{:S(2)}) copy-start(bf16[1,352,384]{2,1,0:T(8,128)(2,1)} %get-tuple-element.19.keep_ref) | copy-start | bytes 811012
  7.2 7.8 %collective-permute-start.2 = (bf16[96,384]{1,0:T(8,128)(2,1)S(1)}, bf16[96,384]{1,0:T(8,128)(2,1)S(1)}, u32[]{:S(2)}, u32[]{:S(2)}) collective-permute-start(bf16[96,384]{1,0:T(8,128)(2,1)S(1)} %get-tuple-element.24), channel_id=1, source_target_pairs={{0,8},{4,12},{8,0},{12,4},{1,9},{5,13},{9,1},{13,5},{2,10},{6,14},... | collective-permute-start | bytes 221192 | tf_op jit(solution)/shard_map/ppermute | solution.py:47
  10.1 8.4 %collective-permute-start.1 = (bf16[352,384]{1,0:T(8,128)(2,1)S(1)}, bf16[352,384]{1,0:T(8,128)(2,1)S(1)}, u32[]{:S(2)}, u32[]{:S(2)}) collective-permute-start(bf16[352,384]{1,0:T(8,128)(2,1)S(1)} %get-tuple-element.20._), channel_id=1, source_target_pairs={{0,8},{4,12},{8,0},{12,4},{1,9},{5,13},{9,1},{13,5},{2,10},{6,14},... | collective-permute-start | bytes 811016 | tf_op jit(solution)/shard_map/ppermute | solution.py:47
  10.2 0.8 %copy-start.7 = (bf16[3,21,200]{2,1,0:T(8,128)(2,1)S(1)}, bf16[3,21,200]{2,1,0:T(8,128)(2,1)}, u32[]{:S(2)}) copy-start(bf16[3,21,200]{2,1,0:T(8,128)(2,1)} %response_ref.1) | copy-start | bytes 75604
  11.9 3.1 %copy-start.1 = (bf16[3,128,768]{2,1,0:T(8,128)(2,1)S(1)}, bf16[3,128,768]{2,1,0:T(8,128)(2,1)}, u32[]{:S(2)}) copy-start(bf16[3,128,768]{2,1,0:T(8,128)(2,1)} %own_ref.1) | copy-start | bytes 1769476
  15.0 3.5 %copy-start.2 = (f32[352,384]{1,0:T(8,128)S(1)}, f32[352,384]{1,0:T(8,128)}, u32[]{:S(2)}) copy-start(f32[352,384]{1,0:T(8,128)} %get-tuple-element.17.refs_0_) | copy-start | bytes 1622020
  15.0 3.5 %copy-start.4 = (f32[128,384]{1,0:T(8,128)S(1)}, f32[128,384]{1,0:T(8,128)}, u32[]{:S(2)}) copy-start(f32[128,384]{1,0:T(8,128)} %get-tuple-element.21.refs_3_) | copy-start | bytes 589828
  19.1 12.0 %collective-permute-start.3 = (bf16[960,128]{1,0:T(8,128)(2,1)S(1)}, bf16[960,128]{1,0:T(8,128)(2,1)S(1)}, u32[]{:S(2)}, u32[]{:S(2)}) collective-permute-start(bf16[960,128]{1,0:T(8,128)(2,1)S(1)} %get-tuple-element.26), channel_id=1, source_target_pairs={{0,1},{1,0},{2,3},{3,2},{4,5},{5,4},{6,7},{7,6},{8,9},{9,8},{10,11... | collective-permute-start | bytes 737288 | tf_op jit(solution)/shard_map/ppermute | solution.py:47
  21.0 11.4 %collective-permute-start.7 = (bf16[3,128,128]{2,1,0:T(8,128)(2,1)S(1)}, bf16[3,128,128]{2,1,0:T(8,128)(2,1)S(1)}, u32[]{:S(2)}, u32[]{:S(2)}) collective-permute-start(bf16[3,128,128]{2,1,0:T(8,128)(2,1)S(1)} %bin_gradients.1.refs_4_.refs_0_), channel_id=1, source_target_pairs={{0,3},{1,2},{2,1},{3,0},{4,7},{5,6},{6,5},{7,4},{8,11},{9,10},{10,... | collective-permute-start | bytes 294920 | tf_op jit(solution)/shard_map/ppermute | solution.py:47
  23.5 9.0 %collective-permute-start.6 = (bf16[3,128,128]{2,1,0:T(8,128)(2,1)S(1)}, bf16[3,128,128]{2,1,0:T(8,128)(2,1)S(1)}, u32[]{:S(2)}, u32[]{:S(2)}) collective-permute-start(bf16[3,128,128]{2,1,0:T(8,128)(2,1)S(1)} %bin_gradients.1.refs_4_.refs_0_), channel_id=1, source_target_pairs={{0,2},{1,3},{2,0},{3,1},{4,6},{5,7},{6,4},{7,5},{8,10},{9,11},{10,... | collective-permute-start | bytes 294920 | tf_op jit(solution)/shard_map/ppermute | solution.py:47
  23.7 9.2 %collective-permute-start.5 = (bf16[3,128,128]{2,1,0:T(8,128)(2,1)S(1)}, bf16[3,128,128]{2,1,0:T(8,128)(2,1)S(1)}, u32[]{:S(2)}, u32[]{:S(2)}) collective-permute-start(bf16[3,128,128]{2,1,0:T(8,128)(2,1)S(1)} %bin_gradients.1.refs_4_.refs_0_), channel_id=1, source_target_pairs={{0,1},{1,0},{2,3},{3,2},{4,5},{5,4},{6,7},{7,6},{8,9},{9,8},{10,11... | collective-permute-start | bytes 294920 | tf_op jit(solution)/shard_map/ppermute | solution.py:47
  33.1 5.7 %collective-permute-start.9 = (bf16[2,128,384]{2,1,0:T(8,128)(2,1)S(1)}, bf16[2,128,384]{2,1,0:T(8,128)(2,1)S(1)}, u32[]{:S(2)}, u32[]{:S(2)}) collective-permute-start(bf16[2,128,384]{2,1,0:T(8,128)(2,1)S(1)} %get-tuple-element.29.refs_0_), channel_id=1, source_target_pairs={{0,8},{4,12},{8,0},{12,4},{1,9},{5,13},{9,1},{13,5},{2,10},{6,14},... | collective-permute-start | bytes 589832 | tf_op jit(solution)/shard_map/ppermute | solution.py:47
  34.8 7.1 %collective-permute-start.4 = (bf16[480,128]{1,0:T(8,128)(2,1)S(1)}, bf16[480,128]{1,0:T(8,128)(2,1)S(1)}, u32[]{:S(2)}, u32[]{:S(2)}) collective-permute-start(bf16[480,128]{1,0:T(8,128)(2,1)S(1)} %pass_on.1.refs_4_), channel_id=1, source_target_pairs={{0,2},{1,3},{2,0},{3,1},{4,6},{5,7},{6,4},{7,5},{8,10},{9,11},{10,... | collective-permute-start | bytes 368648 | tf_op jit(solution)/shard_map/ppermute | solution.py:47
  37.4 7.8 %collective-permute-start.8 = (bf16[2,128,384]{2,1,0:T(8,128)(2,1)S(1)}, bf16[2,128,384]{2,1,0:T(8,128)(2,1)S(1)}, u32[]{:S(2)}, u32[]{:S(2)}) collective-permute-start(bf16[2,128,384]{2,1,0:T(8,128)(2,1)S(1)} %get-tuple-element.29.refs_0_), channel_id=1, source_target_pairs={{0,4},{4,0},{8,12},{12,8},{1,5},{5,1},{9,13},{13,9},{2,6},{6,2},{1... | collective-permute-start | bytes 589832 | tf_op jit(solution)/shard_map/ppermute | solution.py:47
  38.8 6.4 %collective-permute-start.10 = (bf16[2,128,384]{2,1,0:T(8,128)(2,1)S(1)}, bf16[2,128,384]{2,1,0:T(8,128)(2,1)S(1)}, u32[]{:S(2)}, u32[]{:S(2)}) collective-permute-start(bf16[2,128,384]{2,1,0:T(8,128)(2,1)S(1)} %collective-permute-done.9.refs_2_), channel_id=1, source_target_pairs={{0,4},{4,0},{8,12},{12,8},{1,5},{5,1},{9,13},{13,9},{2,6},{6,2},{1... | collective-permute-start | bytes 589832 | tf_op jit(solution)/shard_map/ppermute | solution.py:47
  41.9 3.3 %copy-start = (bf16[4,3,2,32,128]{4,3,2,1,0:T(8,128)(2,1)S(1)}, bf16[4,3,2,32,128]{4,3,2,1,0:T(8,128)(2,1)}, u32[]{:S(2)}) copy-start(bf16[4,3,2,32,128]{4,3,2,1,0:T(8,128)(2,1)} %refs_5_.1) | copy-start | bytes 589828
  41.9 3.3 %copy-start.5 = (s32[4,3,2]{0,2,1:T(2,128)S(1)}, s32[4,3,2]{0,2,1:T(2,128)}, u32[]{:S(2)}) copy-start(s32[4,3,2]{0,2,1:T(2,128)} %param.9) | copy-start | bytes 292
  41.9 3.3 %copy-start.6 = (s32[4,3]{1,0:T(4,128)S(1)}, s32[4,3]{1,0:T(4,128)}, u32[]{:S(2)}) copy-start(s32[4,3]{1,0:T(4,128)} %count_ref.1) | copy-start | bytes 148

commit v4 on v3

--- a/solution.py
+++ b/solution.py
@@ -74,14 +74,17 @@
     return jnp.where(lane == 0, level if first else jnp.zeros_like(rows), rows + level)
 
 
-def levels_kernel(class_ref, response_ref, _, level_ref, kind_ref, flat_ref, *, bins, slabs):
-    planes, wire_taps, length = response_ref.shape
-    rows = level_ref.shape[0] // planes
+def levels_kernel(packed_ref, _, level_ref, kind_ref, *, bins, slabs, total):
+    rows = level_ref.shape[0]
     groups = kind_ref.shape[0]
     slab = lax.axis_index("drift")
     lane = lax.broadcasted_iota(jnp.int32, (GROUP, LANES), 1)
-    classes = jnp.broadcast_to(class_ref[...].astype(F32), (GROUP, class_ref.shape[1]))
-    tiles = [classes[:, t : t + LANES] for t in range(0, class_ref.shape[1], LANES)]
+    packed = packed_ref[rows:].astype(F32)
+    tiles = []
+    for t in range(total // LANES):
+        at = slice(t % 2 * LANES, (t % 2 + 1) * LANES)
+        tiles.append(jnp.broadcast_to(packed[t // 2 : t // 2 + 1, at], (GROUP, LANES)))
+    classes = tiles[0]
     none = jnp.zeros((GROUP, LANES), F32)
     numbers = none
     for source in range(slabs):
@@ -94,10 +97,7 @@
     column = jnp.broadcast_to(numbers[:1], (LANES, LANES)).T.astype(jnp.int32)
     for m in range(groups):
         kind_ref[m] = column[m * GROUP : (m + 1) * GROUP]
-    flat_ref[...] = jnp.zeros(flat_ref.shape, F32)
-    for p in range(planes):
-        flat_ref[p * rows : p * rows + wire_taps, :length] = response_ref[p].astype(F32)
-    taps = flat_ref[...].astype(BF16)
+    taps = packed_ref[:rows]
     tap = lax.broadcasted_iota(jnp.int32, (LANES, 2 * LANES), 0)
     tick = lax.broadcasted_iota(jnp.int32, (LANES, 2 * LANES), 1)
     step = tick - tap - LEAD
@@ -129,23 +129,30 @@
         level_ref[:, kind, LANES:] = near[:, LANES:] + far
 
 
-def smeared_levels(diff_class, response, bins, slabs, before):
-    planes, wire_taps, _ = response.shape
+def packed_inputs(diff_class, response):
+    planes, wire_taps, length = response.shape
+    reach = 2 * LANES
     rows = -(-wire_taps // 8) * 8
+    taps = jnp.pad(response, ((0, 0), (0, rows - wire_taps), (0, reach - length)))
+    classes = jnp.pad(diff_class.astype(BF16), (0, 8 * reach - diff_class.shape[0]))
+    return jnp.concatenate([taps.reshape(planes * rows, reach), classes.reshape(8, reach)], axis=0)
+
+
+def smeared_levels(packed, bins, slabs, total, before):
+    rows = packed.shape[0] - 8
     groups = (bins + WINDOW // 2) // GROUP
     return pl.pallas_call(
-        functools.partial(levels_kernel, bins=bins, slabs=slabs),
+        functools.partial(levels_kernel, bins=bins, slabs=slabs, total=total),
         out_shape=(
-            jax.ShapeDtypeStruct((planes * rows, CLASSES + HB, 2 * LANES), F32),
+            jax.ShapeDtypeStruct((rows, CLASSES + HB, 2 * LANES), F32),
             jax.ShapeDtypeStruct((groups, GROUP, LANES), jnp.int32),
         ),
-        in_specs=[vmem(), vmem(), anywhere()],
+        in_specs=[vmem(), anywhere()],
         out_specs=(vmem(), vmem()),
-        scratch_shapes=[pltpu.VMEM((planes * rows, 2 * LANES), F32)],
         compiler_params=params(),
         cost_estimate=cost(1e8, 1e6),
         name="levels",
-    )(diff_class[None], response, before)
+    )(packed, before)
 
 
 def table_kernel(level_ref, kind_ref, table_ref, sum_ref, *, wire_taps):
@@ -238,73 +245,73 @@
 
 def back_kernel(table_ref, own_ref, received_ref, *refs, wire_taps):
     others, (out_ref, cot_ref, wide_ref) = refs[:-3], refs[-3:]
-    blocks, span = table_ref.shape[1], table_ref.shape[3]
-    planes = table_ref.shape[0]
+    planes, blocks, _, span = table_ref.shape
     _, wires, ticks = own_ref.shape
     total = received_ref.shape[1]
     half = (wire_taps - 1) // 2
     parts = ticks // total
-    side = planes * parts * EDGE
+    size = packed_rows(planes, half)
+    side = parts * size
     lows = received_ref.shape[0] - 2 * side
-    plane = pl.program_id(0)
     even = lax.rem(lax.axis_index("gz"), 2) == 0
-    cot_ref[EDGE : EDGE + wires] = own_ref[0]
-    for part in range(parts):
-        here = slice(part * total, (part + 1) * total)
-        at = (plane * parts + part) * EDGE
-        low = received_ref[pl.ds(pl.multiple_of(lows + at, EDGE), EDGE)]
-        high = received_ref[pl.ds(pl.multiple_of(lows + side + at, EDGE), EDGE)]
-        near = jnp.where(even, low, high)
-        far = jnp.zeros((EDGE, total), BF16)
-        for other in others:
-            far += other[pl.ds(pl.multiple_of(at, EDGE), EDGE)]
-        cot_ref[:EDGE, here] = jnp.where(even, far, near)
-        cot_ref[EDGE + wires :, here] = jnp.where(even, near, far)
     lane = lax.broadcasted_iota(jnp.int32, (wires, LANES), 1)
     none = jnp.zeros((wires, LANES), F32)
+    gap = jnp.zeros((EDGE - half, total), F32)
     step = span * 16 // LANES
     columns = (wire_taps + 1) // 2
-    result = none
-    for block in range(blocks):
-        wide = lax.dot_general(
-            cot_ref[:, block * span : (block + 1) * span],
-            table_ref[plane, block, : columns * LANES],
-            (((1,), (1,)), ((), ())),
-            preferred_element_type=F32,
-        )
-        for column in range(columns):
-            wide_ref[column] = wide[:, column * LANES : (column + 1) * LANES]
-        left, right = none, none
-        for column in range(columns):
-            at = EDGE + half - 2 * column
-            left += wide_ref[column, at : at + wires]
-            if 2 * column + 1 < wire_taps:
-                right += wide_ref[column, at - 1 : at - 1 + wires]
-        both = jnp.where(lane < WINDOW, left + pltpu.roll(right, WINDOW, 1), none)
-        result += pltpu.roll(both, block * step, 1) if block else both
-    out_ref[0] = result.astype(BF16)
+    edges = []
+    for part in range(parts):
+        low = received_ref[lows + part * size : lows + (part + 1) * size].astype(F32)
+        high = received_ref[lows + side + part * size : lows + side + (part + 1) * size].astype(F32)
+        near = jnp.where(even, low, high)
+        far = jnp.zeros((size, total), F32)
+        for other in others:
+            far += other[part * size : (part + 1) * size].astype(F32)
+        edges.append((jnp.where(even, far, near), jnp.where(even, near, far)))
+    for plane in range(planes):
+        cot_ref[plane, EDGE : EDGE + wires] = own_ref[plane]
+        for part in range(parts):
+            here = slice(part * total, (part + 1) * total)
+            before, after = [edge[plane * half : (plane + 1) * half] for edge in edges[part]]
+            cot_ref[plane, :EDGE, here] = jnp.concatenate([gap, before], axis=0).astype(BF16)
+            cot_ref[plane, EDGE + wires :, here] = jnp.concatenate([after, gap], axis=0).astype(BF16)
+        result = none
+        for block in range(blocks):
+            i = (plane * blocks + block) % wide_ref.shape[0]
+            wide = lax.dot_general(
+                cot_ref[plane, :, block * span : (block + 1) * span],
+                table_ref[plane, block, : columns * LANES],
+                (((1,), (1,)), ((), ())),
+                preferred_element_type=F32,
+            )
+            for column in range(columns):
+                wide_ref[i, column] = wide[:, column * LANES : (column + 1) * LANES]
+            left, right = none, none
+            for column in range(columns):
+                at = EDGE + half - 2 * column
+                left += wide_ref[i, column, at : at + wires]
+                if 2 * column + 1 < wire_taps:
+                    right += wide_ref[i, column, at - 1 : at - 1 + wires]
+            both = jnp.where(lane < WINDOW, left + pltpu.roll(right, WINDOW, 1), none)
+            result += pltpu.roll(both, block * step, 1) if block else both
+        out_ref[plane] = result.astype(BF16)
 
 
 def backward(table, cotangent, received, others, wire_taps):
-    planes, blocks, depth, span = table.shape
+    planes, _, _, _ = table.shape
     _, wires, ticks = cotangent.shape
     extent = wires + 2 * EDGE
     columns = (wire_taps + 1) // 2
     return pl.pallas_call(
         functools.partial(back_kernel, wire_taps=wire_taps),
-        grid=(planes,),
         out_shape=jax.ShapeDtypeStruct((planes, wires, LANES), BF16),
-        in_specs=[
-            vmem(),
-            pl.BlockSpec((1, wires, ticks), lambda p: (p, 0, 0)),
-        ]
-        + [vmem()] * (1 + len(others)),
-        out_specs=pl.BlockSpec((1, wires, LANES), lambda p: (p, 0, 0)),
+        in_specs=[vmem()] * (3 + len(others)),
+        out_specs=vmem(),
         scratch_shapes=[
-            pltpu.VMEM((extent, ticks), BF16),
-            pltpu.VMEM((columns, extent, LANES), F32),
+            pltpu.VMEM((planes, extent, ticks), BF16),
+            pltpu.VMEM((2, columns, extent, LANES), F32),
         ],
-        compiler_params=params(("arbitrary",)),
+        compiler_params=params(),
         cost_estimate=cost(4e9, 2 * math.prod(table.shape)),
         name="bin_gradients",
     )(table, cotangent, received, *others)
@@ -419,8 +426,9 @@
 
 
 def pieces_kernel(
-    block_hbm, count_hbm, charge_hbm, share_hbm, cot_hbm, own_ref, keep_ref, give_ref, local_ref,
-    block_ref, count_ref, charge_ref, share_ref, edge_ref, cross_ref, sems,
+    block_hbm, count_hbm, charge_hbm, share_hbm, cot_hbm, own_hbm, keep_hbm, give_hbm, local_hbm,
+    block_ref, count_ref, charge_ref, share_ref, edge_ref, cross_ref, own_ref, keep_ref, give_ref, local_ref,
+    sems, out_sems, *, half,
 ):
     cells, planes, entries, wire_block, width = share_ref.shape
     wires, total = local_ref.shape
@@ -473,9 +481,29 @@
                     name = jnp.clip(name - z * per_owner, 0, per_owner - 1)
                     start = pl.multiple_of(name * wire_block, wire_block)
                     local_ref[pl.ds(start, wire_block)] += piece
+    at = halves * cut
+    gap = jnp.zeros((packed_rows(planes, half) - planes * half, ticks), F32)
+    for side, first in ((0, 0), (1, EDGE - half)):
+        rows = [edge_ref[side, p].astype(F32)[first : first + half] for p in range(planes)]
+        rows = jnp.concatenate(rows + [gap], axis=0).astype(BF16)
+        for part in range(ticks // total):
+            give_ref[at : at + rows.shape[0]] = rows[:, part * total : (part + 1) * total]
+            at += rows.shape[0]
     extent = wires + 2 * EDGE
     none = jnp.zeros((EDGE, total), F32)
-    for k in range(owners):
+    stores = [
+        pltpu.make_async_copy(source, target, out_sems.at[i])
+        for i, (source, target) in enumerate(
+            (
+                (give_ref, give_hbm),
+                (keep_ref, keep_hbm),
+                (own_ref, own_hbm),
+                (local_ref, local_hbm),
+            )
+        )
+    ]
+    stores[3].start()
+    for k in [*range(1, owners, 2), *range(2, owners, 2), 0]:
         to = z ^ k
         blocks = [
             cross_ref[p, pl.ds(pl.multiple_of(to * wires, EDGE), extent)] for p in range(planes - 1)
@@ -492,32 +520,40 @@
                 keep_ref[k // 2 - 1, here] = coded(rows, 0)
             else:
                 own_ref[here] = rows
-    at = halves * cut
-    for side in range(2):
-        for p in range(planes):
-            for part in range(ticks // total):
-                give_ref[at : at + EDGE] = edge_ref[side, p, :, part * total : (part + 1) * total]
-                at += EDGE
-
-
-def cut_pieces(ovl_block, ovl_count, charge, intersection, cotangent, owners):
+        if k == owners - 1:
+            stores[0].start()
+        if k == owners - 2 and k:
+            stores[1].start()
+    if owners == 2:
+        stores[1].start()
+    stores[2].start()
+    for store in stores:
+        store.wait()
+
+
+def packed_rows(planes, half):
+    return -(-planes * half // 16) * 16
+
+
+def cut_pieces(ovl_block, ovl_count, charge, intersection, cotangent, owners, half):
     cells, planes, entries, wire_block, width = intersection.shape
     total = charge.shape[1]
     _, wires, ticks = cotangent.shape
     rows = (planes - 1) * (wires + 2 * EDGE) + 2 * EDGE
-    edges = 2 * planes * EDGE * ticks // total
+    edges = 2 * packed_rows(planes, half) * ticks // total
     hbm = pl.BlockSpec(memory_space=pltpu.HBM)
     blocks = jnp.transpose(ovl_block, (1, 2, 0))
+    outs = (
+        jax.ShapeDtypeStruct((rows, total), F32),
+        jax.ShapeDtypeStruct((owners // 2 - 1, rows, total), BF16),
+        jax.ShapeDtypeStruct((owners // 2 * rows + edges, total), BF16),
+        jax.ShapeDtypeStruct((wires, total), F32),
+    )
     return pl.pallas_call(
-        pieces_kernel,
-        out_shape=(
-            jax.ShapeDtypeStruct((rows, total), F32),
-            jax.ShapeDtypeStruct((owners // 2 - 1, rows, total), BF16),
-            jax.ShapeDtypeStruct((owners // 2 * rows + edges, total), BF16),
-            jax.ShapeDtypeStruct((wires, total), F32),
-        ),
+        functools.partial(pieces_kernel, half=half),
+        out_shape=outs,
         in_specs=[hbm] * 5,
-        out_specs=(vmem(), vmem(), vmem(), vmem()),
+        out_specs=(hbm,) * 4,
         scratch_shapes=[
             pltpu.SMEM(blocks.shape, jnp.int32),
             pltpu.SMEM(ovl_count.shape, jnp.int32),
@@ -525,7 +561,9 @@
             pltpu.VMEM(intersection.shape, BF16),
             pltpu.VMEM((2, planes, EDGE, ticks), BF16),
             pltpu.VMEM((planes - 1, owners * wires + 2 * EDGE, total), F32),
+            *[pltpu.VMEM(out.shape, out.dtype) for out in outs],
             pltpu.SemaphoreType.DMA((6,)),
+            pltpu.SemaphoreType.DMA((4,)),
         ],
         compiler_params=params(limit=WHOLE_VMEM),
         cost_estimate=cost(1e8, 4 * owners * rows * total),
@@ -639,64 +677,73 @@
 
 
 def signal_kernel(*refs, wire_taps):
-    parts, (table_ref, out_ref, token_ref, even_ref, odd_ref, level_ref, lines_ref) = refs[:-7], refs[-7:]
-    token_ref[...] = jnp.zeros(token_ref.shape, F32)
-    blocks, span = table_ref.shape[1], table_ref.shape[3]
-    wires = out_ref.shape[1]
+    parts, (table_ref, out_hbm, token_ref) = refs[:-9], refs[-9:-6]
+    even_ref, odd_ref, level_ref, lines_ref, out_ref, sems = refs[-6:]
+    planes, blocks, _, span = table_ref.shape
+    _, wires, _ = out_ref.shape
+    extent = wires + 2 * EDGE
     half = (wire_taps - 1) // 2
     step = span * 16 // LANES
-    currents = plain(parts[0][...], False)
-    for part in parts[1:]:
-        currents += plain(part[...], False)
     middle = WINDOW // 2
-    level = currents[:, middle : middle + 1].astype(BF16).astype(F32)
-    level = jnp.broadcast_to(level, currents.shape)
-    level_ref[...] = level
-    currents = currents - level
+    token_ref[...] = jnp.zeros(token_ref.shape, F32)
     lane = lax.broadcasted_iota(jnp.int32, (wires, LANES), 1)
-    levels = jnp.zeros((wires, LANES), F32)
-    for a in range(wire_taps):
-        at = EDGE - half + a
-        here = (lane == WINDOW + a) | (lane == WINDOW + wire_taps + a)
-        levels = jnp.where(here, level_ref[at : at + wires], levels)
-    for block in range(blocks):
-        even_ref[...] = pltpu.roll(currents, (-step * block) % LANES, 1)
-        odd_ref[...] = pltpu.roll(currents, (WINDOW - step * block) % LANES, 1)
-        for pair in range((wire_taps + 1) // 2):
-            at = EDGE - half + 2 * pair
-            right = levels
-            if 2 * pair + 1 < wire_taps:
-                right = odd_ref[at + 1 : at + 1 + wires]
-            line = jnp.where(lane < WINDOW, even_ref[at : at + wires], right)
-            lines_ref[:, pair * LANES : (pair + 1) * LANES] = line.astype(BF16)
-        out_ref[0, :, block * span : (block + 1) * span] = jnp.dot(
-            lines_ref[...], table_ref[pl.program_id(0), block], preferred_element_type=F32
-        ).astype(BF16)
+    stores = []
+    for p in range(planes):
+        here = slice(p * extent, (p + 1) * extent)
+        currents = plain(parts[0][here], False)
+        for part in parts[1:]:
+            currents += plain(part[here], False)
+        level = currents[:, middle : middle + 1].astype(BF16).astype(F32)
+        level = jnp.broadcast_to(level, currents.shape)
+        level_ref[p] = level
+        currents = currents - level
+        levels = jnp.zeros((wires, LANES), F32)
+        for a in range(wire_taps):
+            at = EDGE - half + a
+            both = (lane == WINDOW + a) | (lane == WINDOW + wire_taps + a)
+            levels = jnp.where(both, level_ref[p, at : at + wires], levels)
+        for block in range(blocks):
+            i = p * blocks + block
+            even_ref[i] = pltpu.roll(currents, (-step * block) % LANES, 1)
+            odd_ref[i] = pltpu.roll(currents, (WINDOW - step * block) % LANES, 1)
+            for pair in range((wire_taps + 1) // 2):
+                at = EDGE - half + 2 * pair
+                right = levels
+                if 2 * pair + 1 < wire_taps:
+                    right = odd_ref[i, at + 1 : at + 1 + wires]
+                line = jnp.where(lane < WINDOW, even_ref[i, at : at + wires], right)
+                lines_ref[i % 2, :, pair * LANES : (pair + 1) * LANES] = line.astype(BF16)
+            out_ref[p, :, block * span : (block + 1) * span] = jnp.dot(
+                lines_ref[i % 2], table_ref[p, block], preferred_element_type=F32
+            ).astype(BF16)
+        store = pltpu.make_async_copy(out_ref.at[p], out_hbm.at[p], sems.at[p])
+        store.start()
+        stores.append(store)
+    for store in stores:
+        store.wait()
 
 
 def forward(parts, table, wires, wire_taps):
     planes, blocks, depth, span = table.shape
     extent = wires + 2 * EDGE
-    part = pl.BlockSpec((extent, LANES), lambda p: (p, 0))
+    shape = (planes, wires, blocks * span)
     return pl.pallas_call(
         functools.partial(signal_kernel, wire_taps=wire_taps),
-        grid=(planes,),
         out_shape=(
-            jax.ShapeDtypeStruct((planes, wires, blocks * span), BF16),
+            jax.ShapeDtypeStruct(shape, BF16),
             jax.ShapeDtypeStruct((8, LANES), F32),
         ),
-        in_specs=[part] * len(parts) + [vmem()],
-        out_specs=(
-            pl.BlockSpec((1, wires, blocks * span), lambda p: (p, 0, 0)),
-            pl.BlockSpec((8, LANES), lambda p: (0, 0)),
-        ),
+        in_specs=[vmem()] * (len(parts) + 1),
+        out_specs=(anywhere(), vmem()),
         scratch_shapes=[
-            pltpu.VMEM((extent, LANES), F32),
-            pltpu.VMEM((extent, LANES), F32),
-            pltpu.VMEM((extent, LANES), F32),
-            pltpu.VMEM((wires, depth), BF16),
+            pltpu.VMEM((planes * blocks, extent, LANES), F32),
+            pltpu.VMEM((planes * blocks, extent, LANES), F32),
+            pltpu.VMEM((planes, extent, LANES), F32),
+            pltpu.VMEM((2, wires, depth), BF16),
+            pltpu.VMEM(shape, BF16),
+            pltpu.SemaphoreType.DMA((planes,)),
         ],
-        compiler_params=params(("arbitrary",)),
+        compiler_params=params(),
         cost_estimate=cost(4e9, 2 * math.prod(table.shape)),
         name="signal",
     )(*parts, table)
@@ -711,15 +758,15 @@
     bins = total // slabs
 
     currents, keep, give, local_currents = cut_pieces(
-        ovl_block, ovl_count, charge, intersection, cotangent, owners
+        ovl_block, ovl_count, charge, intersection, cotangent, owners, (wire_taps - 1) // 2
     )
     received = swap(give, "gz", 1)
-    sums, edges = relay(keep, received) if owners > 2 else ((), ())
+    packed = packed_inputs(diff_class, response)
+    sums, edges = relay(keep.astype(F32), received) if owners > 2 else ((), ())
     beyond = [swap(block, "gz", 2 * j) for j, block in enumerate(edges, 1)]
     others = [swap(block, "gz", 2 * j) for j, block in enumerate(sums, 1)]
 
-    before = sums[0] if sums else received
-    levels, kinds = smeared_levels(diff_class, response, bins, slabs, before)
+    levels, kinds = smeared_levels(packed, bins, slabs, total, sums[0] if sums else received)
     table = build_table(levels, kinds, planes, wire_taps, ticks)
     partial = backward(table, cotangent, received, beyond, wire_taps)
     spread = [partial] + [swap(partial, "drift", k) for k in range(1, slabs)]

time: 47.3 us -> 46.3 us (0.979)
  other arithmetic: 0 us -> 1.68 us
  local copies, waits for them, and re-layouts: 2.43 us -> 0.83 us
  Pallas kernels: 16.3 us -> 15.1 us
  waiting for transfers between devices: 13.4 us -> 14.2 us
  starting transfers between devices: 14.2 us -> 13.5 us
    unnamed x16 -> x12, local copies, waits for them, and re-layouts: 1.75 us -> 0.03 us
    convert_element_type x0 -> x2, other arithmetic: none -> 1.68 us  [the longest x1 0.99 us: local(): sums, edges = relay(keep.astype(F32), received) if owners > 2 else ((), ())]
    pallas_call x4, Pallas kernels: 10.1 us -> 8.92 us  [the longest x1 2.87 us: cut_pieces(): pl.pallas_call(functools.partial(pieces_kernel, half=half), out_shape=out...]
    pad x0 -> x2, local copies, waits for them, and re-layouts: none -> 0.79 us  [the longest x1 0.78 us: packed_inputs(): jnp.pad(response, ((0, 0), (0, rows - wire_taps), (0, reach - length)))]
    ppermute x11, waiting for transfers between devices: 13.4 us -> 14.2 us  [swap(): return lax.ppermute(block, axis, [(i, i ^ distance) for i in range(count)])]
    ppermute x11, starting transfers between devices: 14.2 us -> 13.5 us  [swap(): return lax.ppermute(block, axis, [(i, i ^ distance) for i in range(count)])]
    broadcast_in_dim x1 -> x0, local copies, waits for them, and re-layouts: 0.68 us -> none  [smeared_levels(): diff_class[None]]
  transfers between devices with their start and end apart: 11 -> 11, of which waited for: 7 -> 6; matrix products, arithmetic and copies ran while one was open for 1% -> 5% of each run, Pallas kernels for 22% -> 20%
where the time goes in v4:
time: 46.3 us; the launch traced here: 46.1 us
  Pallas kernels  15.1 us (33%)
  waiting for transfers between devices  14.2 us (31%)
  starting transfers between devices  13.5 us (29%)
  other arithmetic  1.68 us (4%)
  local copies, waits for them, and re-layouts  0.83 us (2%)
  between operations  0.81 us (2%)
    ppermute x11, waiting for transfers between devices, swap(): return lax.ppermute(block, axis, [(i, i ^ distance) for i in range(count)])  14.2 us
    ppermute x11, starting transfers between devices, swap(): return lax.ppermute(block, axis, [(i, i ^ distance) for i in range(count)])  13.5 us
    pallas_call x1, Pallas kernels, build_table(): pl.pallas_call(functools.partial(table_kernel, wire_taps=wire_taps), out_...  3.07 us
    pallas_call x1, Pallas kernels, cut_pieces(): pl.pallas_call(functools.partial(pieces_kernel, half=half), out_shape=out...  2.87 us
    pallas_call x1, Pallas kernels, forward(): pl.pallas_call(functools.partial(signal_kernel, wire_taps=wire_taps), out...  2.74 us
    pallas_call x1, Pallas kernels, backward(): pl.pallas_call(functools.partial(back_kernel, wire_taps=wire_taps), out_s...  2.39 us
    pallas_call x1, Pallas kernels, charge_gradient(): pl.pallas_call(charge_kernel, out_shape=jax.ShapeDtypeStruct((cells * wid...  1.84 us
    convert_element_type x1, other arithmetic, local(): sums, edges = relay(keep.astype(F32), received) if owners > 2 else ((), ())  0.99 us
  transfers between devices with their start and end apart: 11, of which 6 were waited for; matrix products, arithmetic and copies ran while one was open for 5% of the time, Pallas kernels for 20%

profile of v4, /device:TPU:0, one launch (start us, length us, event | category | flops | bytes accessed | tf_op | source)
XLA Modules:
  0.0 46.1 jit_solution(8263037103232997685)
XLA Ops:
  0.6 2.9 %pieces.1 = (f32[352,384]{1,0:T(8,128)}, bf16[1,352,384]{2,1,0:T(8,128)(2,1)}, bf16[832,384]{1,0:T(8,128)(2,1)}, f32[128,384]{1,0:T(8,128)}) custom-call(s32[3,2,4]{2,1,0:T(2,128)} %bitcast.2, s32[4,3]{1,0:T(4,128)} %count_ref.1, bf16[512,384]{1,0:T(8,128)(2,1)} %charge_hbm.1, bf16[4,3,2,32,128]{4,3,2,1,0:T(8,128)(2,1)} %refs_5_.1, bf16[3,128,768]{2,1,0:T(8,128)(2,1)} %own_ref.1), custom_call_target="tpu_custom_call" | custom-call | flops 100000000 | bytes 2162688 | tf_op jit(solution)/shard_map/pieces/pallas_call | solution.py:552
  3.5 0.5 %collective-permute-start = (bf16[832,384]{1,0:T(8,128)(2,1)}, bf16[832,384]{1,0:T(8,128)(2,1)S(1)}, u32[]{:S(2)}, u32[]{:S(2)}) collective-permute-start(bf16[832,384]{1,0:T(8,128)(2,1)} %get-tuple-element.18), channel_id=1, source_target_pairs={{0,4},{4,0},{8,12},{12,8},{1,5},{5,1},{9,13},{13,9},{2,6},{6,2},{1... | collective-permute-start | bytes 1916936 | tf_op jit(solution)/shard_map/ppermute | solution.py:47
  4.0 0.7 %convert_element_type.11 = bf16[384]{0:T(512)(128)(2,1)S(1)} convert(s32[384]{0:T(512)} %param.11) | non-fusion elementwise | flops 384 | bytes 2304 | tf_op jit(solution)/shard_map/convert_element_type | solution.py:137
  4.7 0.8 %pad.8 = bf16[3,24,256]{2,1,0:T(8,128)(2,1)S(1)} pad(bf16[3,21,200]{2,1,0:T(8,128)(2,1)} %param.12, bf16[]{:T(256)} %constant.2.clone.1), padding=0_0x0_3x0_56 | pad | bytes 62066 | tf_op jit(solution)/shard_map/jit(_pad)/pad | solution.py:136
  5.5 1.0 %convert_element_type.10.keep_ref = f32[1,352,384]{2,1,0:T(8,128)S(1)} convert(bf16[1,352,384]{2,1,0:T(8,128)(2,1)} %get-tuple-element.19) | non-fusion elementwise | flops 135168 | bytes 811008 | tf_op jit(solution)/shard_map/convert_element_type | solution.py:765
  6.5 0.0 collective-permute-done.received_ref.refs_1_
  6.5 0.3 relay.1
  6.8 2.6 %collective-permute-start.2 = (bf16[64,384]{1,0:T(8,128)(2,1)S(1)}, bf16[64,384]{1,0:T(8,128)(2,1)S(1)}, u32[]{:S(2)}, u32[]{:S(2)}) collective-permute-start(bf16[64,384]{1,0:T(8,128)(2,1)S(1)} %get-tuple-element.24), channel_id=1, source_target_pairs={{0,8},{4,12},{8,0},{12,4},{1,9},{5,13},{9,1},{13,5},{2,10},{6,14},... | collective-permute-start | bytes 147464 | tf_op jit(solution)/shard_map/ppermute | solution.py:47
  9.4 0.1 collective-permute-start.1
  9.4 0.9 %levels.1 = (f32[72,8,256]{2,1,0:T(8,128)S(1)}, s32[16,8,128]{2,1,0:T(8,128)S(1)}) custom-call(bf16[80,256]{1,0:T(8,128)(2,1)S(1)} %pad_maximum_fusion.packed_ref, bf16[352,384]{1,0:T(8,128)(2,1)S(1)} %get-tuple-element.20._), custom_call_target="tpu_custom_call" | custom-call | flops 100000000 | bytes 1000000 | tf_op jit(solution)/shard_map/levels/pallas_call | solution.py:144
  10.4 0.0 copy-start.1
  10.4 3.1 %table.1.table_ref.refs_3_ = bf16[3,3,1408,256]{3,2,1,0:T(8,128)(2,1)S(1)} custom-call(f32[72,8,256]{2,1,0:T(8,128)S(1)} %get-tuple-element.22.level_ref, s32[16,8,128]{2,1,0:T(8,128)S(1)} %get-tuple-element.23.kind_ref), custom_call_target="tpu_custom_call" | custom-call | flops 4000000000 | bytes 6488064 | tf_op jit(solution)/shard_map/table/pallas_call | solution.py:234
  13.5 0.0 copy-start.2
  13.5 2.4 %bin_gradients.1.refs_4_.refs_0_ = bf16[3,128,128]{2,1,0:T(8,128)(2,1)S(1)} custom-call(bf16[3,3,1408,256]{3,2,1,0:T(8,128)(2,1)S(1)} %table.1.table_ref.refs_3_, bf16[3,128,768]{2,1,0:T(8,128)(2,1)S(1)} %copy-done.1, bf16[832,384]{1,0:T(8,128)(2,1)S(1)} %collective-permute-done.received_ref.refs_1_, bf16[64,384]{1,0:T(8,128)(2,1)S(1)} %collective-permute-done.2.refs_0_), custom_call_target="tpu_custom_call" | custom-call | flops 4000000000 | bytes 6488064 | tf_op jit(solution)/shard_map/bin_gradients/pallas_call | solution.py:305
  15.9 2.1 %collective-permute-done.1.refs_2_ = bf16[352,384]{1,0:T(8,128)(2,1)S(1)} collective-permute-done((bf16[352,384]{1,0:T(8,128)(2,1)S(1)}, bf16[352,384]{1,0:T(8,128)(2,1)S(1)}, u32[]{:S(2)}, u32[]{:S(2)}) %collective-permute-start.1) | collective-permute-done | bytes 270368 | tf_op jit(solution)/shard_map/ppermute | solution.py:47
  18.0 0.6 %slab_currents.1 = (bf16[480,128]{1,0:T(8,128)(2,1)S(1)}, bf16[960,128]{1,0:T(8,128)(2,1)S(1)}, bf16[480,128]{1,0:T(8,128)(2,1)S(1)}) custom-call(f32[352,384]{1,0:T(8,128)S(1)} %copy-done.2, bf16[832,384]{1,0:T(8,128)(2,1)S(1)} %collective-permute-done.received_ref.refs_1_, bf16[352,384]{1,0:T(8,128)(2,1)S(1)} %collective-permute-done.1.refs_2_, ...), custom_call_target="tpu_custom_call" | custom-call | flops 100000000 | bytes 737280 | tf_op jit(solution)/shard_map/slab_currents/pallas_call | solution.py:644
  18.6 1.6 %collective-permute-start.3 = (bf16[960,128]{1,0:T(8,128)(2,1)S(1)}, bf16[960,128]{1,0:T(8,128)(2,1)S(1)}, u32[]{:S(2)}, u32[]{:S(2)}) collective-permute-start(bf16[960,128]{1,0:T(8,128)(2,1)S(1)} %get-tuple-element.26), channel_id=1, source_target_pairs={{0,1},{1,0},{2,3},{3,2},{4,5},{5,4},{6,7},{7,6},{8,9},{9,8},{10,11... | collective-permute-start | bytes 737288 | tf_op jit(solution)/shard_map/ppermute | solution.py:47
  20.2 2.5 %collective-permute-start.7 = (bf16[3,128,128]{2,1,0:T(8,128)(2,1)S(1)}, bf16[3,128,128]{2,1,0:T(8,128)(2,1)S(1)}, u32[]{:S(2)}, u32[]{:S(2)}) collective-permute-start(bf16[3,128,128]{2,1,0:T(8,128)(2,1)S(1)} %bin_gradients.1.refs_4_.refs_0_), channel_id=1, source_target_pairs={{0,3},{1,2},{2,1},{3,0},{4,7},{5,6},{6,5},{7,4},{8,11},{9,10},{10,... | collective-permute-start | bytes 294920 | tf_op jit(solution)/shard_map/ppermute | solution.py:47
  22.7 0.1 collective-permute-start.6
  22.9 1.8 %collective-permute-start.5 = (bf16[3,128,128]{2,1,0:T(8,128)(2,1)S(1)}, bf16[3,128,128]{2,1,0:T(8,128)(2,1)S(1)}, u32[]{:S(2)}, u32[]{:S(2)}) collective-permute-start(bf16[3,128,128]{2,1,0:T(8,128)(2,1)S(1)} %bin_gradients.1.refs_4_.refs_0_), channel_id=1, source_target_pairs={{0,1},{1,0},{2,3},{3,2},{4,5},{5,4},{6,7},{7,6},{8,9},{9,8},{10,11... | collective-permute-start | bytes 294920 | tf_op jit(solution)/shard_map/ppermute | solution.py:47
  24.6 6.1 %collective-permute-done.3.refs_1_ = bf16[960,128]{1,0:T(8,128)(2,1)S(1)} collective-permute-done((bf16[960,128]{1,0:T(8,128)(2,1)S(1)}, bf16[960,128]{1,0:T(8,128)(2,1)S(1)}, u32[]{:S(2)}, u32[]{:S(2)}) %collective-permute-start.3) | collective-permute-done | bytes 245792 | tf_op jit(solution)/shard_map/ppermute | solution.py:47
  30.7 0.2 pass_on.1.refs_4_
  30.9 0.7 %collective-permute-done.7.refs_3_ = bf16[3,128,128]{2,1,0:T(8,128)(2,1)S(1)} collective-permute-done((bf16[3,128,128]{2,1,0:T(8,128)(2,1)S(1)}, bf16[3,128,128]{2,1,0:T(8,128)(2,1)S(1)}, u32[]{:S(2)}, u32[]{:S(2)}) %collective-permute-start.7) | collective-permute-done | bytes 98336 | tf_op jit(solution)/shard_map/ppermute | solution.py:47
  31.7 0.6 %collective-permute-done.5.refs_1_ = bf16[3,128,128]{2,1,0:T(8,128)(2,1)S(1)} collective-permute-done((bf16[3,128,128]{2,1,0:T(8,128)(2,1)S(1)}, bf16[3,128,128]{2,1,0:T(8,128)(2,1)S(1)}, u32[]{:S(2)}, u32[]{:S(2)}) %collective-permute-start.5) | collective-permute-done | bytes 98336 | tf_op jit(solution)/shard_map/ppermute | solution.py:47
  32.3 0.2 merge_bins.1
  32.5 1.7 %collective-permute-start.9 = (bf16[2,128,384]{2,1,0:T(8,128)(2,1)S(1)}, bf16[2,128,384]{2,1,0:T(8,128)(2,1)S(1)}, u32[]{:S(2)}, u32[]{:S(2)}) collective-permute-start(bf16[2,128,384]{2,1,0:T(8,128)(2,1)S(1)} %get-tuple-element.29.refs_0_), channel_id=1, source_target_pairs={{0,8},{4,12},{8,0},{12,4},{1,9},{5,13},{9,1},{13,5},{2,10},{6,14},... | collective-permute-start | bytes 589832 | tf_op jit(solution)/shard_map/ppermute | solution.py:47
  34.2 2.6 %collective-permute-start.4 = (bf16[480,128]{1,0:T(8,128)(2,1)S(1)}, bf16[480,128]{1,0:T(8,128)(2,1)S(1)}, u32[]{:S(2)}, u32[]{:S(2)}) collective-permute-start(bf16[480,128]{1,0:T(8,128)(2,1)S(1)} %pass_on.1.refs_4_), channel_id=1, source_target_pairs={{0,2},{1,3},{2,0},{3,1},{4,6},{5,7},{6,4},{7,5},{8,10},{9,11},{10,... | collective-permute-start | bytes 368648 | tf_op jit(solution)/shard_map/ppermute | solution.py:47
  36.8 0.0 collective-permute-start.8
  36.8 1.4 %collective-permute-done.9.refs_2_ = bf16[2,128,384]{2,1,0:T(8,128)(2,1)S(1)} collective-permute-done((bf16[2,128,384]{2,1,0:T(8,128)(2,1)S(1)}, bf16[2,128,384]{2,1,0:T(8,128)(2,1)S(1)}, u32[]{:S(2)}, u32[]{:S(2)}) %collective-permute-start.9) | collective-permute-done | bytes 196640 | tf_op jit(solution)/shard_map/ppermute | solution.py:47
  38.2 3.2 %collective-permute-done.4.refs_2_ = bf16[480,128]{1,0:T(8,128)(2,1)S(1)} collective-permute-done((bf16[480,128]{1,0:T(8,128)(2,1)S(1)}, bf16[480,128]{1,0:T(8,128)(2,1)S(1)}, u32[]{:S(2)}, u32[]{:S(2)}) %collective-permute-start.4) | collective-permute-done | bytes 122912 | tf_op jit(solution)/shard_map/ppermute | solution.py:47
  41.4 2.7 %signal.1 = (bf16[3,128,768]{2,1,0:T(8,128)(2,1)}, f32[8,128]{1,0:T(8,128)S(1)}) custom-call(bf16[480,128]{1,0:T(8,128)(2,1)S(1)} %get-tuple-element.25.refs_0_, bf16[960,128]{1,0:T(8,128)(2,1)S(1)} %collective-permute-done.3.refs_1_, bf16[480,128]{1,0:T(8,128)(2,1)S(1)} %collective-permute-done.4.refs_2_, bf16[3,3,1408,256]{3,2,1,0:T(8,128)(2,1)S(1)} %table.1.table_ref.refs_3_), custom_call_target="tpu_custom_call" | custom-call | flops 4000000000 | bytes 6488064 | tf_op jit(solution)/shard_map/signal/pallas_call | solution.py:730
  44.2 1.8 %charge_gradient.1 = bf16[512,384]{1,0:T(8,128)(2,1)} custom-call(s32[3,2,4]{2,1,0:T(2,128)S(1)} %bitcast.3, s32[4,3]{1,0:T(4,128)S(1)} %copy-done.5, bf16[2,128,384]{2,1,0:T(8,128)(2,1)S(1)} %get-tuple-element.29.refs_0_, bf16[2,128,384]{2,1,0:T(8,128)(2,1)S(1)} %collective-permute-done.8.refs_1_, bf16[2,128,384]{2,1,0:T(8,128)(2,1)S(1)} %collective-permute-done.9.refs_2_, ...), custom_call_target="tpu_custom_call" | custom-call | flops 100000000 | bytes 786432 | tf_op jit(solution)/shard_map/charge_gradient/pallas_call | solution.py:411
  (18 shorter events, 0.1 us)
Async XLA Ops:
  3.5 3.0 %collective-permute-start = (bf16[832,384]{1,0:T(8,128)(2,1)}, bf16[832,384]{1,0:T(8,128)(2,1)S(1)}, u32[]{:S(2)}, u32[]{:S(2)}) collective-permute-start(bf16[832,384]{1,0:T(8,128)(2,1)} %get-tuple-element.18), channel_id=1, source_target_pairs={{0,4},{4,0},{8,12},{12,8},{1,5},{5,1},{9,13},{13,9},{2,6},{6,2},{1... | collective-permute-start | bytes 1916936 | tf_op jit(solution)/shard_map/ppermute | solution.py:47
  6.8 6.7 %collective-permute-start.2 = (bf16[64,384]{1,0:T(8,128)(2,1)S(1)}, bf16[64,384]{1,0:T(8,128)(2,1)S(1)}, u32[]{:S(2)}, u32[]{:S(2)}) collective-permute-start(bf16[64,384]{1,0:T(8,128)(2,1)S(1)} %get-tuple-element.24), channel_id=1, source_target_pairs={{0,8},{4,12},{8,0},{12,4},{1,9},{5,13},{9,1},{13,5},{2,10},{6,14},... | collective-permute-start | bytes 147464 | tf_op jit(solution)/shard_map/ppermute | solution.py:47
  9.4 8.6 %collective-permute-start.1 = (bf16[352,384]{1,0:T(8,128)(2,1)S(1)}, bf16[352,384]{1,0:T(8,128)(2,1)S(1)}, u32[]{:S(2)}, u32[]{:S(2)}) collective-permute-start(bf16[352,384]{1,0:T(8,128)(2,1)S(1)} %get-tuple-element.20._), channel_id=1, source_target_pairs={{0,8},{4,12},{8,0},{12,4},{1,9},{5,13},{9,1},{13,5},{2,10},{6,14},... | collective-permute-start | bytes 811016 | tf_op jit(solution)/shard_map/ppermute | solution.py:47
  10.4 3.1 %copy-start.1 = (bf16[3,128,768]{2,1,0:T(8,128)(2,1)S(1)}, bf16[3,128,768]{2,1,0:T(8,128)(2,1)}, u32[]{:S(2)}) copy-start(bf16[3,128,768]{2,1,0:T(8,128)(2,1)} %own_ref.1) | copy-start | bytes 1769476
  13.5 4.5 %copy-start.2 = (f32[352,384]{1,0:T(8,128)S(1)}, f32[352,384]{1,0:T(8,128)}, u32[]{:S(2)}) copy-start(f32[352,384]{1,0:T(8,128)} %get-tuple-element.17.refs_0_) | copy-start | bytes 1622020
  13.5 4.5 %copy-start.3 = (f32[128,384]{1,0:T(8,128)S(1)}, f32[128,384]{1,0:T(8,128)}, u32[]{:S(2)}) copy-start(f32[128,384]{1,0:T(8,128)} %get-tuple-element.21.refs_3_) | copy-start | bytes 589828
  18.6 12.1 %collective-permute-start.3 = (bf16[960,128]{1,0:T(8,128)(2,1)S(1)}, bf16[960,128]{1,0:T(8,128)(2,1)S(1)}, u32[]{:S(2)}, u32[]{:S(2)}) collective-permute-start(bf16[960,128]{1,0:T(8,128)(2,1)S(1)} %get-tuple-element.26), channel_id=1, source_target_pairs={{0,1},{1,0},{2,3},{3,2},{4,5},{5,4},{6,7},{7,6},{8,9},{9,8},{10,11... | collective-permute-start | bytes 737288 | tf_op jit(solution)/shard_map/ppermute | solution.py:47
  20.2 11.5 %collective-permute-start.7 = (bf16[3,128,128]{2,1,0:T(8,128)(2,1)S(1)}, bf16[3,128,128]{2,1,0:T(8,128)(2,1)S(1)}, u32[]{:S(2)}, u32[]{:S(2)}) collective-permute-start(bf16[3,128,128]{2,1,0:T(8,128)(2,1)S(1)} %bin_gradients.1.refs_4_.refs_0_), channel_id=1, source_target_pairs={{0,3},{1,2},{2,1},{3,0},{4,7},{5,6},{6,5},{7,4},{8,11},{9,10},{10,... | collective-permute-start | bytes 294920 | tf_op jit(solution)/shard_map/ppermute | solution.py:47
  22.7 9.0 %collective-permute-start.6 = (bf16[3,128,128]{2,1,0:T(8,128)(2,1)S(1)}, bf16[3,128,128]{2,1,0:T(8,128)(2,1)S(1)}, u32[]{:S(2)}, u32[]{:S(2)}) collective-permute-start(bf16[3,128,128]{2,1,0:T(8,128)(2,1)S(1)} %bin_gradients.1.refs_4_.refs_0_), channel_id=1, source_target_pairs={{0,2},{1,3},{2,0},{3,1},{4,6},{5,7},{6,4},{7,5},{8,10},{9,11},{10,... | collective-permute-start | bytes 294920 | tf_op jit(solution)/shard_map/ppermute | solution.py:47
  22.9 9.4 %collective-permute-start.5 = (bf16[3,128,128]{2,1,0:T(8,128)(2,1)S(1)}, bf16[3,128,128]{2,1,0:T(8,128)(2,1)S(1)}, u32[]{:S(2)}, u32[]{:S(2)}) collective-permute-start(bf16[3,128,128]{2,1,0:T(8,128)(2,1)S(1)} %bin_gradients.1.refs_4_.refs_0_), channel_id=1, source_target_pairs={{0,1},{1,0},{2,3},{3,2},{4,5},{5,4},{6,7},{7,6},{8,9},{9,8},{10,11... | collective-permute-start | bytes 294920 | tf_op jit(solution)/shard_map/ppermute | solution.py:47
  32.5 5.7 %collective-permute-start.9 = (bf16[2,128,384]{2,1,0:T(8,128)(2,1)S(1)}, bf16[2,128,384]{2,1,0:T(8,128)(2,1)S(1)}, u32[]{:S(2)}, u32[]{:S(2)}) collective-permute-start(bf16[2,128,384]{2,1,0:T(8,128)(2,1)S(1)} %get-tuple-element.29.refs_0_), channel_id=1, source_target_pairs={{0,8},{4,12},{8,0},{12,4},{1,9},{5,13},{9,1},{13,5},{2,10},{6,14},... | collective-permute-start | bytes 589832 | tf_op jit(solution)/shard_map/ppermute | solution.py:47
  34.2 7.2 %collective-permute-start.4 = (bf16[480,128]{1,0:T(8,128)(2,1)S(1)}, bf16[480,128]{1,0:T(8,128)(2,1)S(1)}, u32[]{:S(2)}, u32[]{:S(2)}) collective-permute-start(bf16[480,128]{1,0:T(8,128)(2,1)S(1)} %pass_on.1.refs_4_), channel_id=1, source_target_pairs={{0,2},{1,3},{2,0},{3,1},{4,6},{5,7},{6,4},{7,5},{8,10},{9,11},{10,... | collective-permute-start | bytes 368648 | tf_op jit(solution)/shard_map/ppermute | solution.py:47
  36.8 7.4 %collective-permute-start.8 = (bf16[2,128,384]{2,1,0:T(8,128)(2,1)S(1)}, bf16[2,128,384]{2,1,0:T(8,128)(2,1)S(1)}, u32[]{:S(2)}, u32[]{:S(2)}) collective-permute-start(bf16[2,128,384]{2,1,0:T(8,128)(2,1)S(1)} %get-tuple-element.29.refs_0_), channel_id=1, source_target_pairs={{0,4},{4,0},{8,12},{12,8},{1,5},{5,1},{9,13},{13,9},{2,6},{6,2},{1... | collective-permute-start | bytes 589832 | tf_op jit(solution)/shard_map/ppermute | solution.py:47
  38.2 6.0 %collective-permute-start.10 = (bf16[2,128,384]{2,1,0:T(8,128)(2,1)S(1)}, bf16[2,128,384]{2,1,0:T(8,128)(2,1)S(1)}, u32[]{:S(2)}, u32[]{:S(2)}) collective-permute-start(bf16[2,128,384]{2,1,0:T(8,128)(2,1)S(1)} %collective-permute-done.9.refs_2_), channel_id=1, source_target_pairs={{0,4},{4,0},{8,12},{12,8},{1,5},{5,1},{9,13},{13,9},{2,6},{6,2},{1... | collective-permute-start | bytes 589832 | tf_op jit(solution)/shard_map/ppermute | solution.py:47
  41.4 2.8 %copy-start = (bf16[4,3,2,32,128]{4,3,2,1,0:T(8,128)(2,1)S(1)}, bf16[4,3,2,32,128]{4,3,2,1,0:T(8,128)(2,1)}, u32[]{:S(2)}) copy-start(bf16[4,3,2,32,128]{4,3,2,1,0:T(8,128)(2,1)} %refs_5_.1) | copy-start | bytes 589828
  41.4 2.8 %copy-start.4 = (s32[4,3,2]{0,2,1:T(2,128)S(1)}, s32[4,3,2]{0,2,1:T(2,128)}, u32[]{:S(2)}) copy-start(s32[4,3,2]{0,2,1:T(2,128)} %param.9) | copy-start | bytes 292
  41.4 2.8 %copy-start.5 = (s32[4,3]{1,0:T(4,128)S(1)}, s32[4,3]{1,0:T(4,128)}, u32[]{:S(2)}) copy-start(s32[4,3]{1,0:T(4,128)} %count_ref.1) | copy-start | bytes 148

commit v5 on v4

--- a/solution.py
+++ b/solution.py
@@ -74,12 +74,15 @@
     return jnp.where(lane == 0, level if first else jnp.zeros_like(rows), rows + level)
 
 
-def levels_kernel(packed_ref, _, level_ref, kind_ref, *, bins, slabs, total):
-    rows = level_ref.shape[0]
+def levels_kernel(
+    class_ref, response_ref, _, level_ref, kind_ref, flat_ref, *, bins, slabs, total
+):
+    planes, wire_taps, length = response_ref.shape
+    rows = level_ref.shape[0] // planes
     groups = kind_ref.shape[0]
     slab = lax.axis_index("drift")
     lane = lax.broadcasted_iota(jnp.int32, (GROUP, LANES), 1)
-    packed = packed_ref[rows:].astype(F32)
+    packed = class_ref[...].astype(F32)
     tiles = []
     for t in range(total // LANES):
         at = slice(t % 2 * LANES, (t % 2 + 1) * LANES)
@@ -97,7 +100,10 @@
     column = jnp.broadcast_to(numbers[:1], (LANES, LANES)).T.astype(jnp.int32)
     for m in range(groups):
         kind_ref[m] = column[m * GROUP : (m + 1) * GROUP]
-    taps = packed_ref[:rows]
+    flat_ref[...] = jnp.zeros(flat_ref.shape, F32)
+    for p in range(planes):
+        flat_ref[p * rows : p * rows + wire_taps, :length] = response_ref[p].astype(F32)
+    taps = flat_ref[...].astype(BF16)
     tap = lax.broadcasted_iota(jnp.int32, (LANES, 2 * LANES), 0)
     tick = lax.broadcasted_iota(jnp.int32, (LANES, 2 * LANES), 1)
     step = tick - tap - LEAD
@@ -129,30 +135,26 @@
         level_ref[:, kind, LANES:] = near[:, LANES:] + far
 
 
-def packed_inputs(diff_class, response):
-    planes, wire_taps, length = response.shape
+def smeared_levels(diff_class, response, bins, slabs, before):
+    planes, wire_taps, _ = response.shape
+    total = diff_class.shape[0]
     reach = 2 * LANES
     rows = -(-wire_taps // 8) * 8
-    taps = jnp.pad(response, ((0, 0), (0, rows - wire_taps), (0, reach - length)))
-    classes = jnp.pad(diff_class.astype(BF16), (0, 8 * reach - diff_class.shape[0]))
-    return jnp.concatenate([taps.reshape(planes * rows, reach), classes.reshape(8, reach)], axis=0)
-
-
-def smeared_levels(packed, bins, slabs, total, before):
-    rows = packed.shape[0] - 8
     groups = (bins + WINDOW // 2) // GROUP
+    classes = jnp.pad(diff_class.astype(BF16), (0, 8 * reach - total)).reshape(8, reach)
     return pl.pallas_call(
         functools.partial(levels_kernel, bins=bins, slabs=slabs, total=total),
         out_shape=(
-            jax.ShapeDtypeStruct((rows, CLASSES + HB, 2 * LANES), F32),
+            jax.ShapeDtypeStruct((planes * rows, CLASSES + HB, reach), F32),
             jax.ShapeDtypeStruct((groups, GROUP, LANES), jnp.int32),
         ),
-        in_specs=[vmem(), anywhere()],
+        in_specs=[vmem(), vmem(), anywhere()],
         out_specs=(vmem(), vmem()),
+        scratch_shapes=[pltpu.VMEM((planes * rows, reach), F32)],
         compiler_params=params(),
         cost_estimate=cost(1e8, 1e6),
         name="levels",
-    )(packed, before)
+    )(classes, response, before)
 
 
 def table_kernel(level_ref, kind_ref, table_ref, sum_ref, *, wire_taps):
@@ -318,9 +320,10 @@
 
 
 def merge_kernel(*refs, bins, lead):
-    parts, (cross_ref, local_ref, slab_ref) = refs[:-4], refs[-3:]
-    planes, wires, _ = parts[0].shape
-    total = local_ref.shape[1]
+    planes, wires, _ = refs[0].shape
+    outs, slab_ref = refs[-planes - 1 : -1], refs[-1]
+    parts = refs[: -planes - 2]
+    total = outs[0].shape[1]
     slab = lax.axis_index("drift")
     for k, part in enumerate(parts):
         slab_ref[slab ^ k] = part[...]
@@ -337,23 +340,16 @@
                 if 0 <= t < len(tiles):
                     tiles[t] += jnp.where(inside, values, none)
         for t, values in enumerate(tiles):
-            here = slice(t * LANES, (t + 1) * LANES)
-            if p < planes - 1:
-                cross_ref[p, :, here] = values.astype(BF16)
-            else:
-                local_ref[:, here] = values.astype(BF16)
+            outs[p][:, t * LANES : (t + 1) * LANES] = values.astype(BF16)
 
 
 def merge(parts, bins, total, before):
     planes, wires, _ = parts[0].shape
     return pl.pallas_call(
         functools.partial(merge_kernel, bins=bins, lead=WINDOW // 2 - HB),
-        out_shape=(
-            jax.ShapeDtypeStruct((planes - 1, wires, total), BF16),
-            jax.ShapeDtypeStruct((wires, total), BF16),
-        ),
+        out_shape=(jax.ShapeDtypeStruct((wires, total), BF16),) * planes,
         in_specs=[vmem()] * len(parts) + [anywhere()],
-        out_specs=(vmem(), vmem()),
+        out_specs=(vmem(),) * planes,
         scratch_shapes=[pltpu.VMEM((len(parts), planes, wires, LANES), BF16)],
         compiler_params=params(),
         cost_estimate=cost(1e8, 4 * planes * wires * total),
@@ -368,11 +364,11 @@
     owners, _, wires, total = all_ref.shape
     per_owner = wires // wire_block
     z = lax.axis_index("gz")
-    if len(sources) == 1:
-        all_ref[...] = sources[0][...]
-    else:
-        for k, source in enumerate(sources):
-            all_ref[z ^ k] = source[...]
+    for i, source in enumerate(sources):
+        if len(sources) == planes - 1:
+            all_ref[:, i] = source[...]
+        else:
+            all_ref[z ^ (i // (planes - 1)), i % (planes - 1)] = source[...]
     empty = jnp.zeros((wire_block, total), BF16)
     stores = []
     for b in range(cells):
@@ -455,7 +451,7 @@
         load.start()
     cross_ref[...] = jnp.zeros(cross_ref.shape, F32)
     local_ref[...] = jnp.zeros(local_ref.shape, F32)
-    for load in loads:
+    for load in loads[:4]:
         load.wait()
     for b in range(cells):
         pieces = (
@@ -481,6 +477,8 @@
                     name = jnp.clip(name - z * per_owner, 0, per_owner - 1)
                     start = pl.multiple_of(name * wire_block, wire_block)
                     local_ref[pl.ds(start, wire_block)] += piece
+    for load in loads[4:]:
+        load.wait()
     at = halves * cut
     gap = jnp.zeros((packed_rows(planes, half) - planes * half, ticks), F32)
     for side, first in ((0, 0), (1, EDGE - half)):
@@ -761,12 +759,13 @@
         ovl_block, ovl_count, charge, intersection, cotangent, owners, (wire_taps - 1) // 2
     )
     received = swap(give, "gz", 1)
-    packed = packed_inputs(diff_class, response)
     sums, edges = relay(keep.astype(F32), received) if owners > 2 else ((), ())
     beyond = [swap(block, "gz", 2 * j) for j, block in enumerate(edges, 1)]
     others = [swap(block, "gz", 2 * j) for j, block in enumerate(sums, 1)]
 
-    levels, kinds = smeared_levels(packed, bins, slabs, total, sums[0] if sums else received)
+    levels, kinds = smeared_levels(
+        diff_class, response, bins, slabs, sums[0] if sums else received
+    )
     table = build_table(levels, kinds, planes, wire_taps, ticks)
     partial = backward(table, cotangent, received, beyond, wire_taps)
     spread = [partial] + [swap(partial, "drift", k) for k in range(1, slabs)]
@@ -778,12 +777,13 @@
             block = ready = pass_on(block, windows[1:], step, cuts[0].shape[0])
         windows.append(swap(block, "drift", 1 << step))
 
-    cross, own = merge(spread, bins, total, ready)
+    *cross, own = merge(spread, bins, total, ready)
     if owners == 4:
-        across = swap(cross, "gz", 2)
-        sources = [cross, swap(cross, "gz", 1), across, swap(across, "gz", 1)]
+        across = [swap(block, "gz", 2) for block in cross]
+        sources = [*cross, *(swap(block, "gz", 1) for block in cross)]
+        sources += [*across, *(swap(block, "gz", 1) for block in across)]
     else:
-        sources = [lax.all_gather(cross, "gz", axis=0)]
+        sources = [lax.all_gather(block, "gz", axis=0) for block in cross]
     signal, done = forward(windows, table, wires, wire_taps)
     charge_grad = charge_gradient(
         ovl_block, ovl_count, sources, own, intersection, owners, done

time: 46.3 us -> 43.9 us (0.948)
  waiting for transfers between devices: 14.2 us -> 10.4 us
  starting transfers between devices: 13.5 us -> 14.9 us
    ppermute x11 -> x14, waiting for transfers between devices: 14.2 us -> 10.4 us  [swap(): return lax.ppermute(block, axis, [(i, i ^ distance) for i in range(count)])]
    ppermute x11 -> x14, starting transfers between devices: 13.5 us -> 14.9 us  [swap(): return lax.ppermute(block, axis, [(i, i ^ distance) for i in range(count)])]
    pad x2 -> x1, local copies, waits for them, and re-layouts: 0.79 us -> 0.01 us  [smeared_levels(): jnp.pad(diff_class.astype(BF16), (0, 8 * reach - total)).reshape(8, reach)]
    unnamed x12 -> x14, local copies, waits for them, and re-layouts: 0.03 us -> 0.8 us
  transfers between devices with their start and end apart: 11 -> 14, of which waited for: 6 -> 5; matrix products, arithmetic and copies ran while one was open for 5% -> 4% of each run, Pallas kernels for 20% -> 22%
where the time goes in v5:
time: 43.9 us; the launch traced here: 43.6 us
  Pallas kernels  15.1 us (34%)
  starting transfers between devices  14.9 us (34%)
  waiting for transfers between devices  10.4 us (24%)
  other arithmetic  1.67 us (4%)
  between operations  0.83 us (2%)
  local copies, waits for them, and re-layouts  0.82 us (2%)
    ppermute x14, starting transfers between devices, swap(): return lax.ppermute(block, axis, [(i, i ^ distance) for i in range(count)])  14.9 us
    ppermute x14, waiting for transfers between devices, swap(): return lax.ppermute(block, axis, [(i, i ^ distance) for i in range(count)])  10.4 us
    pallas_call x1, Pallas kernels, build_table(): pl.pallas_call(functools.partial(table_kernel, wire_taps=wire_taps), out_...  3.07 us
    pallas_call x1, Pallas kernels, cut_pieces(): pl.pallas_call(functools.partial(pieces_kernel, half=half), out_shape=out...  2.8 us
    pallas_call x1, Pallas kernels, forward(): pl.pallas_call(functools.partial(signal_kernel, wire_taps=wire_taps), out...  2.74 us
    pallas_call x1, Pallas kernels, backward(): pl.pallas_call(functools.partial(back_kernel, wire_taps=wire_taps), out_s...  2.39 us
    pallas_call x1, Pallas kernels, charge_gradient(): pl.pallas_call(charge_kernel, out_shape=jax.ShapeDtypeStruct((cells * wid...  1.84 us
    convert_element_type x1, other arithmetic, local(): sums, edges = relay(keep.astype(F32), received) if owners > 2 else ((), ())  0.99 us
  transfers between devices with their start and end apart: 14, of which 5 were waited for; matrix products, arithmetic and copies ran while one was open for 4% of the time, Pallas kernels for 22%

profile of v5, /device:TPU:0, one launch (start us, length us, event | category | flops | bytes accessed | tf_op | source)
XLA Modules:
  0.0 43.6 jit_solution(1616450687327826840)
XLA Ops:
  0.6 2.8 %pieces.1 = (f32[352,384]{1,0:T(8,128)}, bf16[1,352,384]{2,1,0:T(8,128)(2,1)}, bf16[832,384]{1,0:T(8,128)(2,1)}, f32[128,384]{1,0:T(8,128)}) custom-call(s32[3,2,4]{2,1,0:T(2,128)} %bitcast.1, s32[4,3]{1,0:T(4,128)} %count_ref.1, bf16[512,384]{1,0:T(8,128)(2,1)} %charge_hbm.1, bf16[4,3,2,32,128]{4,3,2,1,0:T(8,128)(2,1)} %refs_9_.1, bf16[3,128,768]{2,1,0:T(8,128)(2,1)} %own_ref.1), custom_call_target="tpu_custom_call" | custom-call | flops 100000000 | bytes 2162688 | tf_op jit(solution)/shard_map/pieces/pallas_call | solution.py:550
  3.4 0.5 %collective-permute-start = (bf16[832,384]{1,0:T(8,128)(2,1)}, bf16[832,384]{1,0:T(8,128)(2,1)S(1)}, u32[]{:S(2)}, u32[]{:S(2)}) collective-permute-start(bf16[832,384]{1,0:T(8,128)(2,1)} %get-tuple-element.19), channel_id=1, source_target_pairs={{0,4},{4,0},{8,12},{12,8},{1,5},{5,1},{9,13},{13,9},{2,6},{6,2},{1... | collective-permute-start | bytes 1916936 | tf_op jit(solution)/shard_map/ppermute | solution.py:47
  4.0 0.7 %convert_element_type.9 = bf16[384]{0:T(512)(128)(2,1)S(1)} convert(s32[384]{0:T(512)} %param.11) | non-fusion elementwise | flops 384 | bytes 2304 | tf_op jit(solution)/shard_map/convert_element_type | solution.py:144
  4.7 1.0 %convert_element_type.8.keep_ref = f32[1,352,384]{2,1,0:T(8,128)S(1)} convert(bf16[1,352,384]{2,1,0:T(8,128)(2,1)} %get-tuple-element.20) | non-fusion elementwise | flops 135168 | bytes 811008 | tf_op jit(solution)/shard_map/convert_element_type | solution.py:762
  5.7 0.2 collective-permute-done.received_ref.refs_1_
  5.9 0.3 relay.1
  6.1 2.9 %collective-permute-start.2 = (bf16[64,384]{1,0:T(8,128)(2,1)S(1)}, bf16[64,384]{1,0:T(8,128)(2,1)S(1)}, u32[]{:S(2)}, u32[]{:S(2)}) collective-permute-start(bf16[64,384]{1,0:T(8,128)(2,1)S(1)} %get-tuple-element.25), channel_id=1, source_target_pairs={{0,8},{4,12},{8,0},{12,4},{1,9},{5,13},{9,1},{13,5},{2,10},{6,14},... | collective-permute-start | bytes 147464 | tf_op jit(solution)/shard_map/ppermute | solution.py:47
  9.1 0.1 collective-permute-start.1
  9.1 0.8 %copy-done.6 = bf16[3,21,200]{2,1,0:T(8,128)(2,1)S(1)} copy-done((bf16[3,21,200]{2,1,0:T(8,128)(2,1)S(1)}, bf16[3,21,200]{2,1,0:T(8,128)(2,1)}, u32[]{:S(2)}) %copy-start.6) | copy-done | bytes 25224
  9.9 0.9 %levels.1 = (f32[72,8,256]{2,1,0:T(8,128)S(1)}, s32[16,8,128]{2,1,0:T(8,128)S(1)}) custom-call(bf16[8,256]{1,0:T(8,128)(2,1)S(1)} %reshape.7.class_ref, bf16[3,21,200]{2,1,0:T(8,128)(2,1)S(1)} %copy-done.6, bf16[352,384]{1,0:T(8,128)(2,1)S(1)} %get-tuple-element.21._), custom_call_target="tpu_custom_call" | custom-call | flops 100000000 | bytes 1000000 | tf_op jit(solution)/shard_map/levels/pallas_call | solution.py:145
  10.8 0.0 copy-start.1
  10.8 3.1 %table.1.table_ref.refs_3_ = bf16[3,3,1408,256]{3,2,1,0:T(8,128)(2,1)S(1)} custom-call(f32[72,8,256]{2,1,0:T(8,128)S(1)} %get-tuple-element.23.level_ref, s32[16,8,128]{2,1,0:T(8,128)S(1)} %get-tuple-element.24.kind_ref), custom_call_target="tpu_custom_call" | custom-call | flops 4000000000 | bytes 6488064 | tf_op jit(solution)/shard_map/table/pallas_call | solution.py:236
  13.9 0.0 copy-start.2
  14.0 2.4 %bin_gradients.1.refs_4_.refs_0_ = bf16[3,128,128]{2,1,0:T(8,128)(2,1)S(1)} custom-call(bf16[3,3,1408,256]{3,2,1,0:T(8,128)(2,1)S(1)} %table.1.table_ref.refs_3_, bf16[3,128,768]{2,1,0:T(8,128)(2,1)S(1)} %copy-done.1, bf16[832,384]{1,0:T(8,128)(2,1)S(1)} %collective-permute-done.received_ref.refs_1_, bf16[64,384]{1,0:T(8,128)(2,1)S(1)} %collective-permute-done.2.refs_0_), custom_call_target="tpu_custom_call" | custom-call | flops 4000000000 | bytes 6488064 | tf_op jit(solution)/shard_map/bin_gradients/pallas_call | solution.py:307
  16.4 0.9 %collective-permute-done.1.refs_2_ = bf16[352,384]{1,0:T(8,128)(2,1)S(1)} collective-permute-done((bf16[352,384]{1,0:T(8,128)(2,1)S(1)}, bf16[352,384]{1,0:T(8,128)(2,1)S(1)}, u32[]{:S(2)}, u32[]{:S(2)}) %collective-permute-start.1) | collective-permute-done | bytes 270368 | tf_op jit(solution)/shard_map/ppermute | solution.py:47
  17.3 0.6 %slab_currents.1 = (bf16[480,128]{1,0:T(8,128)(2,1)S(1)}, bf16[960,128]{1,0:T(8,128)(2,1)S(1)}, bf16[480,128]{1,0:T(8,128)(2,1)S(1)}) custom-call(f32[352,384]{1,0:T(8,128)S(1)} %copy-done.2, bf16[832,384]{1,0:T(8,128)(2,1)S(1)} %collective-permute-done.received_ref.refs_1_, bf16[352,384]{1,0:T(8,128)(2,1)S(1)} %collective-permute-done.1.refs_2_, ...), custom_call_target="tpu_custom_call" | custom-call | flops 100000000 | bytes 737280 | tf_op jit(solution)/shard_map/slab_currents/pallas_call | solution.py:642
  17.9 1.8 %collective-permute-start.3 = (bf16[960,128]{1,0:T(8,128)(2,1)S(1)}, bf16[960,128]{1,0:T(8,128)(2,1)S(1)}, u32[]{:S(2)}, u32[]{:S(2)}) collective-permute-start(bf16[960,128]{1,0:T(8,128)(2,1)S(1)} %get-tuple-element.27), channel_id=1, source_target_pairs={{0,1},{1,0},{2,3},{3,2},{4,5},{5,4},{6,7},{7,6},{8,9},{9,8},{10,11... | collective-permute-start | bytes 737288 | tf_op jit(solution)/shard_map/ppermute | solution.py:47
  19.7 2.5 %collective-permute-start.7 = (bf16[3,128,128]{2,1,0:T(8,128)(2,1)S(1)}, bf16[3,128,128]{2,1,0:T(8,128)(2,1)S(1)}, u32[]{:S(2)}, u32[]{:S(2)}) collective-permute-start(bf16[3,128,128]{2,1,0:T(8,128)(2,1)S(1)} %bin_gradients.1.refs_4_.refs_0_), channel_id=1, source_target_pairs={{0,3},{1,2},{2,1},{3,0},{4,7},{5,6},{6,5},{7,4},{8,11},{9,10},{10,... | collective-permute-start | bytes 294920 | tf_op jit(solution)/shard_map/ppermute | solution.py:47
  22.2 0.1 collective-permute-start.6
  22.3 1.8 %collective-permute-start.5 = (bf16[3,128,128]{2,1,0:T(8,128)(2,1)S(1)}, bf16[3,128,128]{2,1,0:T(8,128)(2,1)S(1)}, u32[]{:S(2)}, u32[]{:S(2)}) collective-permute-start(bf16[3,128,128]{2,1,0:T(8,128)(2,1)S(1)} %bin_gradients.1.refs_4_.refs_0_), channel_id=1, source_target_pairs={{0,1},{1,0},{2,3},{3,2},{4,5},{5,4},{6,7},{7,6},{8,9},{9,8},{10,11... | collective-permute-start | bytes 294920 | tf_op jit(solution)/shard_map/ppermute | solution.py:47
  24.1 5.5 %collective-permute-done.3.refs_1_ = bf16[960,128]{1,0:T(8,128)(2,1)S(1)} collective-permute-done((bf16[960,128]{1,0:T(8,128)(2,1)S(1)}, bf16[960,128]{1,0:T(8,128)(2,1)S(1)}, u32[]{:S(2)}, u32[]{:S(2)}) %collective-permute-start.3) | collective-permute-done | bytes 245792 | tf_op jit(solution)/shard_map/ppermute | solution.py:47
  29.6 0.2 pass_on.1.refs_4_
  29.8 2.6 %collective-permute-start.4 = (bf16[480,128]{1,0:T(8,128)(2,1)S(1)}, bf16[480,128]{1,0:T(8,128)(2,1)S(1)}, u32[]{:S(2)}, u32[]{:S(2)}) collective-permute-start(bf16[480,128]{1,0:T(8,128)(2,1)S(1)} %pass_on.1.refs_4_), channel_id=1, source_target_pairs={{0,2},{1,3},{2,0},{3,1},{4,6},{5,7},{6,4},{7,5},{8,10},{9,11},{10,... | collective-permute-start | bytes 368648 | tf_op jit(solution)/shard_map/ppermute | solution.py:47
  32.4 0.2 merge_bins.1
  32.6 1.7 %collective-permute-start.10 = (bf16[128,384]{1,0:T(8,128)(2,1)S(1)}, bf16[128,384]{1,0:T(8,128)(2,1)S(1)}, u32[]{:S(2)}, u32[]{:S(2)}) collective-permute-start(bf16[128,384]{1,0:T(8,128)(2,1)S(1)} %get-tuple-element.30.refs_0_), channel_id=1, source_target_pairs={{0,8},{4,12},{8,0},{12,4},{1,9},{5,13},{9,1},{13,5},{2,10},{6,14},... | collective-permute-start | bytes 294920 | tf_op jit(solution)/shard_map/ppermute | solution.py:47
  34.3 0.4 collective-permute-start.11
  34.7 0.5 %collective-permute-start.9 = (bf16[128,384]{1,0:T(8,128)(2,1)S(1)}, bf16[128,384]{1,0:T(8,128)(2,1)S(1)}, u32[]{:S(2)}, u32[]{:S(2)}) collective-permute-start(bf16[128,384]{1,0:T(8,128)(2,1)S(1)} %get-tuple-element.31.refs_1_), channel_id=1, source_target_pairs={{0,4},{4,0},{8,12},{12,8},{1,5},{5,1},{9,13},{13,9},{2,6},{6,2},{1... | collective-permute-start | bytes 294920 | tf_op jit(solution)/shard_map/ppermute | solution.py:47
  35.2 2.1 %collective-permute-done.10.refs_4_ = bf16[128,384]{1,0:T(8,128)(2,1)S(1)} collective-permute-done((bf16[128,384]{1,0:T(8,128)(2,1)S(1)}, bf16[128,384]{1,0:T(8,128)(2,1)S(1)}, u32[]{:S(2)}, u32[]{:S(2)}) %collective-permute-start.10) | collective-permute-done | bytes 98336 | tf_op jit(solution)/shard_map/ppermute | solution.py:47
  37.3 1.6 %collective-permute-done.11.refs_5_ = bf16[128,384]{1,0:T(8,128)(2,1)S(1)} collective-permute-done((bf16[128,384]{1,0:T(8,128)(2,1)S(1)}, bf16[128,384]{1,0:T(8,128)(2,1)S(1)}, u32[]{:S(2)}, u32[]{:S(2)}) %collective-permute-start.11) | collective-permute-done | bytes 98336 | tf_op jit(solution)/shard_map/ppermute | solution.py:47
  38.9 0.0 copy-start.4
  39.0 2.7 %signal.1 = (bf16[3,128,768]{2,1,0:T(8,128)(2,1)}, f32[8,128]{1,0:T(8,128)S(1)}) custom-call(bf16[480,128]{1,0:T(8,128)(2,1)S(1)} %get-tuple-element.26.refs_0_, bf16[960,128]{1,0:T(8,128)(2,1)S(1)} %collective-permute-done.3.refs_1_, bf16[480,128]{1,0:T(8,128)(2,1)S(1)} %collective-permute-done.4.refs_2_, bf16[3,3,1408,256]{3,2,1,0:T(8,128)(2,1)S(1)} %table.1.table_ref.refs_3_), custom_call_target="tpu_custom_call" | custom-call | flops 4000000000 | bytes 6488064 | tf_op jit(solution)/shard_map/signal/pallas_call | solution.py:728
  41.8 1.8 %charge_gradient.1 = bf16[512,384]{1,0:T(8,128)(2,1)} custom-call(s32[3,2,4]{2,1,0:T(2,128)S(1)} %bitcast.2, s32[4,3]{1,0:T(4,128)S(1)} %copy-done.5, bf16[128,384]{1,0:T(8,128)(2,1)S(1)} %get-tuple-element.30.refs_0_, bf16[128,384]{1,0:T(8,128)(2,1)S(1)} %get-tuple-element.31.refs_1_, bf16[128,384]{1,0:T(8,128)(2,1)S(1)} %collective-permute-done.8.refs_2_, ...), custom_call_target="tpu_custom_call" | custom-call | flops 100000000 | bytes 786432 | tf_op jit(solution)/shard_map/charge_gradient/pallas_call | solution.py:407
  (24 shorter events, 0.1 us)
Async XLA Ops:
  3.4 2.4 %collective-permute-start = (bf16[832,384]{1,0:T(8,128)(2,1)}, bf16[832,384]{1,0:T(8,128)(2,1)S(1)}, u32[]{:S(2)}, u32[]{:S(2)}) collective-permute-start(bf16[832,384]{1,0:T(8,128)(2,1)} %get-tuple-element.19), channel_id=1, source_target_pairs={{0,4},{4,0},{8,12},{12,8},{1,5},{5,1},{9,13},{13,9},{2,6},{6,2},{1... | collective-permute-start | bytes 1916936 | tf_op jit(solution)/shard_map/ppermute | solution.py:47
  6.1 7.8 %collective-permute-start.2 = (bf16[64,384]{1,0:T(8,128)(2,1)S(1)}, bf16[64,384]{1,0:T(8,128)(2,1)S(1)}, u32[]{:S(2)}, u32[]{:S(2)}) collective-permute-start(bf16[64,384]{1,0:T(8,128)(2,1)S(1)} %get-tuple-element.25), channel_id=1, source_target_pairs={{0,8},{4,12},{8,0},{12,4},{1,9},{5,13},{9,1},{13,5},{2,10},{6,14},... | collective-permute-start | bytes 147464 | tf_op jit(solution)/shard_map/ppermute | solution.py:47
  9.1 8.2 %collective-permute-start.1 = (bf16[352,384]{1,0:T(8,128)(2,1)S(1)}, bf16[352,384]{1,0:T(8,128)(2,1)S(1)}, u32[]{:S(2)}, u32[]{:S(2)}) collective-permute-start(bf16[352,384]{1,0:T(8,128)(2,1)S(1)} %get-tuple-element.21._), channel_id=1, source_target_pairs={{0,8},{4,12},{8,0},{12,4},{1,9},{5,13},{9,1},{13,5},{2,10},{6,14},... | collective-permute-start | bytes 811016 | tf_op jit(solution)/shard_map/ppermute | solution.py:47
  9.1 0.8 %copy-start.6 = (bf16[3,21,200]{2,1,0:T(8,128)(2,1)S(1)}, bf16[3,21,200]{2,1,0:T(8,128)(2,1)}, u32[]{:S(2)}) copy-start(bf16[3,21,200]{2,1,0:T(8,128)(2,1)} %response_ref.1) | copy-start | bytes 75604
  10.8 3.1 %copy-start.1 = (bf16[3,128,768]{2,1,0:T(8,128)(2,1)S(1)}, bf16[3,128,768]{2,1,0:T(8,128)(2,1)}, u32[]{:S(2)}) copy-start(bf16[3,128,768]{2,1,0:T(8,128)(2,1)} %own_ref.1) | copy-start | bytes 1769476
  13.9 3.4 %copy-start.2 = (f32[352,384]{1,0:T(8,128)S(1)}, f32[352,384]{1,0:T(8,128)}, u32[]{:S(2)}) copy-start(f32[352,384]{1,0:T(8,128)} %get-tuple-element.18.refs_0_) | copy-start | bytes 1622020
  13.9 3.4 %copy-start.3 = (f32[128,384]{1,0:T(8,128)S(1)}, f32[128,384]{1,0:T(8,128)}, u32[]{:S(2)}) copy-start(f32[128,384]{1,0:T(8,128)} %get-tuple-element.22.refs_3_) | copy-start | bytes 589828
  17.9 11.7 %collective-permute-start.3 = (bf16[960,128]{1,0:T(8,128)(2,1)S(1)}, bf16[960,128]{1,0:T(8,128)(2,1)S(1)}, u32[]{:S(2)}, u32[]{:S(2)}) collective-permute-start(bf16[960,128]{1,0:T(8,128)(2,1)S(1)} %get-tuple-element.27), channel_id=1, source_target_pairs={{0,1},{1,0},{2,3},{3,2},{4,5},{5,4},{6,7},{7,6},{8,9},{9,8},{10,11... | collective-permute-start | bytes 737288 | tf_op jit(solution)/shard_map/ppermute | solution.py:47
  19.7 12.7 %collective-permute-start.7 = (bf16[3,128,128]{2,1,0:T(8,128)(2,1)S(1)}, bf16[3,128,128]{2,1,0:T(8,128)(2,1)S(1)}, u32[]{:S(2)}, u32[]{:S(2)}) collective-permute-start(bf16[3,128,128]{2,1,0:T(8,128)(2,1)S(1)} %bin_gradients.1.refs_4_.refs_0_), channel_id=1, source_target_pairs={{0,3},{1,2},{2,1},{3,0},{4,7},{5,6},{6,5},{7,4},{8,11},{9,10},{10,... | collective-permute-start | bytes 294920 | tf_op jit(solution)/shard_map/ppermute | solution.py:47
  22.2 10.2 %collective-permute-start.6 = (bf16[3,128,128]{2,1,0:T(8,128)(2,1)S(1)}, bf16[3,128,128]{2,1,0:T(8,128)(2,1)S(1)}, u32[]{:S(2)}, u32[]{:S(2)}) collective-permute-start(bf16[3,128,128]{2,1,0:T(8,128)(2,1)S(1)} %bin_gradients.1.refs_4_.refs_0_), channel_id=1, source_target_pairs={{0,2},{1,3},{2,0},{3,1},{4,6},{5,7},{6,4},{7,5},{8,10},{9,11},{10,... | collective-permute-start | bytes 294920 | tf_op jit(solution)/shard_map/ppermute | solution.py:47
  22.3 10.1 %collective-permute-start.5 = (bf16[3,128,128]{2,1,0:T(8,128)(2,1)S(1)}, bf16[3,128,128]{2,1,0:T(8,128)(2,1)S(1)}, u32[]{:S(2)}, u32[]{:S(2)}) collective-permute-start(bf16[3,128,128]{2,1,0:T(8,128)(2,1)S(1)} %bin_gradients.1.refs_4_.refs_0_), channel_id=1, source_target_pairs={{0,1},{1,0},{2,3},{3,2},{4,5},{5,4},{6,7},{7,6},{8,9},{9,8},{10,11... | collective-permute-start | bytes 294920 | tf_op jit(solution)/shard_map/ppermute | solution.py:47
  29.8 9.1 %collective-permute-start.4 = (bf16[480,128]{1,0:T(8,128)(2,1)S(1)}, bf16[480,128]{1,0:T(8,128)(2,1)S(1)}, u32[]{:S(2)}, u32[]{:S(2)}) collective-permute-start(bf16[480,128]{1,0:T(8,128)(2,1)S(1)} %pass_on.1.refs_4_), channel_id=1, source_target_pairs={{0,2},{1,3},{2,0},{3,1},{4,6},{5,7},{6,4},{7,5},{8,10},{9,11},{10,... | collective-permute-start | bytes 368648 | tf_op jit(solution)/shard_map/ppermute | solution.py:47
  32.6 4.7 %collective-permute-start.10 = (bf16[128,384]{1,0:T(8,128)(2,1)S(1)}, bf16[128,384]{1,0:T(8,128)(2,1)S(1)}, u32[]{:S(2)}, u32[]{:S(2)}) collective-permute-start(bf16[128,384]{1,0:T(8,128)(2,1)S(1)} %get-tuple-element.30.refs_0_), channel_id=1, source_target_pairs={{0,8},{4,12},{8,0},{12,4},{1,9},{5,13},{9,1},{13,5},{2,10},{6,14},... | collective-permute-start | bytes 294920 | tf_op jit(solution)/shard_map/ppermute | solution.py:47
  34.3 4.6 %collective-permute-start.11 = (bf16[128,384]{1,0:T(8,128)(2,1)S(1)}, bf16[128,384]{1,0:T(8,128)(2,1)S(1)}, u32[]{:S(2)}, u32[]{:S(2)}) collective-permute-start(bf16[128,384]{1,0:T(8,128)(2,1)S(1)} %get-tuple-element.31.refs_1_), channel_id=1, source_target_pairs={{0,8},{4,12},{8,0},{12,4},{1,9},{5,13},{9,1},{13,5},{2,10},{6,14},... | collective-permute-start | bytes 294920 | tf_op jit(solution)/shard_map/ppermute | solution.py:47
  34.7 7.0 %collective-permute-start.8 = (bf16[128,384]{1,0:T(8,128)(2,1)S(1)}, bf16[128,384]{1,0:T(8,128)(2,1)S(1)}, u32[]{:S(2)}, u32[]{:S(2)}) collective-permute-start(bf16[128,384]{1,0:T(8,128)(2,1)S(1)} %get-tuple-element.30.refs_0_), channel_id=1, source_target_pairs={{0,4},{4,0},{8,12},{12,8},{1,5},{5,1},{9,13},{13,9},{2,6},{6,2},{1... | collective-permute-start | bytes 294920 | tf_op jit(solution)/shard_map/ppermute | solution.py:47
  34.7 7.0 %collective-permute-start.9 = (bf16[128,384]{1,0:T(8,128)(2,1)S(1)}, bf16[128,384]{1,0:T(8,128)(2,1)S(1)}, u32[]{:S(2)}, u32[]{:S(2)}) collective-permute-start(bf16[128,384]{1,0:T(8,128)(2,1)S(1)} %get-tuple-element.31.refs_1_), channel_id=1, source_target_pairs={{0,4},{4,0},{8,12},{12,8},{1,5},{5,1},{9,13},{13,9},{2,6},{6,2},{1... | collective-permute-start | bytes 294920 | tf_op jit(solution)/shard_map/ppermute | solution.py:47
  37.3 4.4 %collective-permute-start.12 = (bf16[128,384]{1,0:T(8,128)(2,1)S(1)}, bf16[128,384]{1,0:T(8,128)(2,1)S(1)}, u32[]{:S(2)}, u32[]{:S(2)}) collective-permute-start(bf16[128,384]{1,0:T(8,128)(2,1)S(1)} %collective-permute-done.10.refs_4_), channel_id=1, source_target_pairs={{0,4},{4,0},{8,12},{12,8},{1,5},{5,1},{9,13},{13,9},{2,6},{6,2},{1... | collective-permute-start | bytes 294920 | tf_op jit(solution)/shard_map/ppermute | solution.py:47
  38.9 2.8 %collective-permute-start.13 = (bf16[128,384]{1,0:T(8,128)(2,1)S(1)}, bf16[128,384]{1,0:T(8,128)(2,1)S(1)}, u32[]{:S(2)}, u32[]{:S(2)}) collective-permute-start(bf16[128,384]{1,0:T(8,128)(2,1)S(1)} %collective-permute-done.11.refs_5_), channel_id=1, source_target_pairs={{0,4},{4,0},{8,12},{12,8},{1,5},{5,1},{9,13},{13,9},{2,6},{6,2},{1... | collective-permute-start | bytes 294920 | tf_op jit(solution)/shard_map/ppermute | solution.py:47
  38.9 2.8 %copy-start = (bf16[4,3,2,32,128]{4,3,2,1,0:T(8,128)(2,1)S(1)}, bf16[4,3,2,32,128]{4,3,2,1,0:T(8,128)(2,1)}, u32[]{:S(2)}) copy-start(bf16[4,3,2,32,128]{4,3,2,1,0:T(8,128)(2,1)} %refs_9_.1) | copy-start | bytes 589828
  38.9 2.8 %copy-start.4 = (s32[4,3,2]{0,2,1:T(2,128)S(1)}, s32[4,3,2]{0,2,1:T(2,128)}, u32[]{:S(2)}) copy-start(s32[4,3,2]{0,2,1:T(2,128)} %param.9) | copy-start | bytes 292
  38.9 2.8 %copy-start.5 = (s32[4,3]{1,0:T(4,128)S(1)}, s32[4,3]{1,0:T(4,128)}, u32[]{:S(2)}) copy-start(s32[4,3]{1,0:T(4,128)} %count_ref.1) | copy-start | bytes 148

commit v6 on v5

--- a/solution.py
+++ b/solution.py
@@ -252,7 +252,7 @@
     total = received_ref.shape[1]
     half = (wire_taps - 1) // 2
     parts = ticks // total
-    size = packed_rows(planes, half)
+    size = sixteens(planes * half)
     side = parts * size
     lows = received_ref.shape[0] - 2 * side
     even = lax.rem(lax.axis_index("gz"), 2) == 0
@@ -480,7 +480,7 @@
     for load in loads[4:]:
         load.wait()
     at = halves * cut
-    gap = jnp.zeros((packed_rows(planes, half) - planes * half, ticks), F32)
+    gap = jnp.zeros((sixteens(planes * half) - planes * half, ticks), F32)
     for side, first in ((0, 0), (1, EDGE - half)):
         rows = [edge_ref[side, p].astype(F32)[first : first + half] for p in range(planes)]
         rows = jnp.concatenate(rows + [gap], axis=0).astype(BF16)
@@ -488,7 +488,7 @@
             give_ref[at : at + rows.shape[0]] = rows[:, part * total : (part + 1) * total]
             at += rows.shape[0]
     extent = wires + 2 * EDGE
-    none = jnp.zeros((EDGE, total), F32)
+    none = jnp.zeros((half, total), F32)
     stores = [
         pltpu.make_async_copy(source, target, out_sems.at[i])
         for i, (source, target) in enumerate(
@@ -503,21 +503,19 @@
     stores[3].start()
     for k in [*range(1, owners, 2), *range(2, owners, 2), 0]:
         to = z ^ k
-        blocks = [
-            cross_ref[p, pl.ds(pl.multiple_of(to * wires, EDGE), extent)] for p in range(planes - 1)
-        ]
-        blocks.append(jnp.where(to == z + 1, local_ref[wires - EDGE :], none))
-        blocks.append(jnp.where(to == z - 1, local_ref[:EDGE], none))
-        at = 0
-        for rows in blocks:
-            here = slice(at, at + rows.shape[0])
-            at += rows.shape[0]
-            if k % 2:
-                give_ref[k // 2 * cut + here.start : k // 2 * cut + here.stop] = coded(rows, 0)
-            elif k:
-                keep_ref[k // 2 - 1, here] = coded(rows, 0)
-            else:
-                own_ref[here] = rows
+        blocks = []
+        for p in range(planes - 1):
+            rows = cross_ref[p, pl.ds(pl.multiple_of(to * wires, EDGE), extent)]
+            blocks.append(rows[EDGE - half : extent - EDGE + half])
+        blocks.append(jnp.where(to == z + 1, local_ref[wires - half :], none))
+        blocks.append(jnp.where(to == z - 1, local_ref[:half], none))
+        rows = padded(blocks)
+        if k % 2:
+            give_ref[k // 2 * cut : (k // 2 + 1) * cut] = coded(rows, 0)
+        elif k:
+            keep_ref[k // 2 - 1] = coded(rows, 0)
+        else:
+            own_ref[...] = rows
         if k == owners - 1:
             stores[0].start()
         if k == owners - 2 and k:
@@ -529,16 +527,23 @@
         store.wait()
 
 
-def packed_rows(planes, half):
-    return -(-planes * half // 16) * 16
+def sixteens(rows):
+    return -(-rows // 16) * 16
+
+
+def padded(blocks):
+    count = sum(block.shape[0] for block in blocks)
+    if count % 16:
+        blocks = blocks + [jnp.zeros((sixteens(count) - count, blocks[0].shape[1]), F32)]
+    return jnp.concatenate(blocks, axis=0)
 
 
 def cut_pieces(ovl_block, ovl_count, charge, intersection, cotangent, owners, half):
     cells, planes, entries, wire_block, width = intersection.shape
     total = charge.shape[1]
     _, wires, ticks = cotangent.shape
-    rows = (planes - 1) * (wires + 2 * EDGE) + 2 * EDGE
-    edges = 2 * packed_rows(planes, half) * ticks // total
+    rows = sixteens((planes - 1) * (wires + 2 * half) + 2 * half)
+    edges = 2 * sixteens(planes * half) * ticks // total
     hbm = pl.BlockSpec(memory_space=pltpu.HBM)
     blocks = jnp.transpose(ovl_block, (1, 2, 0))
     outs = (
@@ -603,7 +608,7 @@
     return outs[:others], outs[others:]
 
 
-def slabs_kernel(*refs, bins, lead, slabs):
+def slabs_kernel(*refs, bins, lead, slabs, cross, half):
     count = len(refs) - slabs.bit_length() - 1
     keep_ref, received_ref, others, local_ref = refs[0], refs[1], refs[2 : count - 2], refs[count - 2]
     outs, cut_ref = refs[count:-1], refs[-1]
@@ -612,10 +617,9 @@
     summed = keep_ref[...] + plain(received_ref[:cut], True)
     for other in others:
         summed += plain(other[...], True)
-    edge = cut - 2 * EDGE
-    rows = jnp.concatenate(
-        [summed[:edge], summed[edge : edge + EDGE], local_ref[...], summed[edge + EDGE :]], axis=0
-    )
+    wires = local_ref.shape[0]
+    edge = cross * (wires + 2 * half)
+    rows = padded([summed[: edge + half], local_ref[...], summed[edge + half : edge + 2 * half]])
     none = jnp.zeros((rows.shape[0], LANES), F32)
     lane = lax.broadcasted_iota(jnp.int32, none.shape, 1)
     level = jnp.broadcast_to(rows[:, :1].astype(BF16).astype(F32), none.shape)
@@ -634,13 +638,15 @@
             out[i * size : (i + 1) * size] = cut_ref[slab ^ ((2 * i + 1) << s)]
 
 
-def cut_slabs(keep, received, others, local, bins, slabs, before):
+def cut_slabs(keep, received, others, local, bins, slabs, cross, half, before):
     wires, total = local.shape
-    rows = keep.shape[0] + wires
+    rows = sixteens((cross + 1) * (wires + 2 * half))
     steps = slabs.bit_length() - 1
     counts = [1] + [slabs >> (s + 1) for s in range(steps)]
     return pl.pallas_call(
-        functools.partial(slabs_kernel, bins=bins, lead=WINDOW // 2 - HB, slabs=slabs),
+        functools.partial(
+            slabs_kernel, bins=bins, lead=WINDOW // 2 - HB, slabs=slabs, cross=cross, half=half
+        ),
         out_shape=tuple(jax.ShapeDtypeStruct((n * rows, LANES), BF16) for n in counts),
         in_specs=[vmem()] * (3 + len(others)) + [anywhere()],
         out_specs=(vmem(),) * len(counts),
@@ -679,25 +685,26 @@
     even_ref, odd_ref, level_ref, lines_ref, out_ref, sems = refs[-6:]
     planes, blocks, _, span = table_ref.shape
     _, wires, _ = out_ref.shape
-    extent = wires + 2 * EDGE
     half = (wire_taps - 1) // 2
+    extent = wires + 2 * half
     step = span * 16 // LANES
     middle = WINDOW // 2
     token_ref[...] = jnp.zeros(token_ref.shape, F32)
     lane = lax.broadcasted_iota(jnp.int32, (wires, LANES), 1)
     stores = []
+    size = parts[0].shape[0]
+    summed = plain(parts[0][...], False)
+    for part in parts[1:]:
+        summed += plain(part[:size], False)
     for p in range(planes):
-        here = slice(p * extent, (p + 1) * extent)
-        currents = plain(parts[0][here], False)
-        for part in parts[1:]:
-            currents += plain(part[here], False)
+        currents = summed[p * extent : (p + 1) * extent]
         level = currents[:, middle : middle + 1].astype(BF16).astype(F32)
         level = jnp.broadcast_to(level, currents.shape)
         level_ref[p] = level
         currents = currents - level
         levels = jnp.zeros((wires, LANES), F32)
         for a in range(wire_taps):
-            at = EDGE - half + a
+            at = a
             both = (lane == WINDOW + a) | (lane == WINDOW + wire_taps + a)
             levels = jnp.where(both, level_ref[p, at : at + wires], levels)
         for block in range(blocks):
@@ -705,7 +712,7 @@
             even_ref[i] = pltpu.roll(currents, (-step * block) % LANES, 1)
             odd_ref[i] = pltpu.roll(currents, (WINDOW - step * block) % LANES, 1)
             for pair in range((wire_taps + 1) // 2):
-                at = EDGE - half + 2 * pair
+                at = 2 * pair
                 right = levels
                 if 2 * pair + 1 < wire_taps:
                     right = odd_ref[i, at + 1 : at + 1 + wires]
@@ -723,7 +730,7 @@
 
 def forward(parts, table, wires, wire_taps):
     planes, blocks, depth, span = table.shape
-    extent = wires + 2 * EDGE
+    extent = wires + wire_taps - 1
     shape = (planes, wires, blocks * span)
     return pl.pallas_call(
         functools.partial(signal_kernel, wire_taps=wire_taps),
@@ -753,10 +760,11 @@
     slabs = lax.axis_size("drift")
     planes, wires, ticks = cotangent.shape
     wire_taps = response.shape[1]
+    half = (wire_taps - 1) // 2
     bins = total // slabs
 
     currents, keep, give, local_currents = cut_pieces(
-        ovl_block, ovl_count, charge, intersection, cotangent, owners, (wire_taps - 1) // 2
+        ovl_block, ovl_count, charge, intersection, cotangent, owners, half
     )
     received = swap(give, "gz", 1)
     sums, edges = relay(keep.astype(F32), received) if owners > 2 else ((), ())
@@ -770,7 +778,9 @@
     partial = backward(table, cotangent, received, beyond, wire_taps)
     spread = [partial] + [swap(partial, "drift", k) for k in range(1, slabs)]
 
-    cuts = cut_slabs(currents, received, others, local_currents, bins, slabs, partial)
+    cuts = cut_slabs(
+        currents, received, others, local_currents, bins, slabs, planes - 1, half, partial
+    )
     windows, ready = [cuts[0]], cuts[0]
     for step, block in enumerate(cuts[1:]):
         if step:

time: 43.9 us -> 43.2 us (0.984)
  waiting for transfers between devices: 10.4 us -> 9.84 us
    ppermute x14, waiting for transfers between devices: 10.4 us -> 9.84 us  [swap(): return lax.ppermute(block, axis, [(i, i ^ distance) for i in range(count)])]
where the time goes in v6:
time: 43.2 us; the launch traced here: 42.9 us
  Pallas kernels  15 us (35%)
  starting transfers between devices  14.8 us (34%)
  waiting for transfers between devices  9.84 us (23%)
  other arithmetic  1.66 us (4%)
  between operations  0.83 us (2%)
  local copies, waits for them, and re-layouts  0.82 us (2%)
    ppermute x14, starting transfers between devices, swap(): return lax.ppermute(block, axis, [(i, i ^ distance) for i in range(count)])  14.8 us
    ppermute x14, waiting for transfers between devices, swap(): return lax.ppermute(block, axis, [(i, i ^ distance) for i in range(count)])  9.84 us
    pallas_call x1, Pallas kernels, build_table(): pl.pallas_call(functools.partial(table_kernel, wire_taps=wire_taps), out_...  3.07 us
    pallas_call x1, Pallas kernels, cut_pieces(): pl.pallas_call(functools.partial(pieces_kernel, half=half), out_shape=out...  2.82 us
    pallas_call x1, Pallas kernels, forward(): pl.pallas_call(functools.partial(signal_kernel, wire_taps=wire_taps), out...  2.69 us
    pallas_call x1, Pallas kernels, backward(): pl.pallas_call(functools.partial(back_kernel, wire_taps=wire_taps), out_s...  2.38 us
    pallas_call x1, Pallas kernels, charge_gradient(): pl.pallas_call(charge_kernel, out_shape=jax.ShapeDtypeStruct((cells * wid...  1.84 us
    convert_element_type x1, other arithmetic, local(): sums, edges = relay(keep.astype(F32), received) if owners > 2 else ((), ())  0.98 us
  transfers between devices with their start and end apart: 14, of which 5 were waited for; matrix products, arithmetic and copies ran while one was open for 4% of the time, Pallas kernels for 22%

profile of v6, /device:TPU:0, one launch (start us, length us, event | category | flops | bytes accessed | tf_op | source)
XLA Modules:
  0.0 42.9 jit_solution(7578945548680532043)
XLA Ops:
  0.6 2.8 %pieces.1 = (f32[320,384]{1,0:T(8,128)}, bf16[1,320,384]{2,1,0:T(8,128)(2,1)}, bf16[768,384]{1,0:T(8,128)(2,1)}, f32[128,384]{1,0:T(8,128)}) custom-call(s32[3,2,4]{2,1,0:T(2,128)} %bitcast.1, s32[4,3]{1,0:T(4,128)} %count_ref.1, bf16[512,384]{1,0:T(8,128)(2,1)} %charge_hbm.1, bf16[4,3,2,32,128]{4,3,2,1,0:T(8,128)(2,1)} %refs_9_.1, bf16[3,128,768]{2,1,0:T(8,128)(2,1)} %own_ref.1), custom_call_target="tpu_custom_call" | custom-call | flops 100000000 | bytes 1966080 | tf_op jit(solution)/shard_map/pieces/pallas_call | solution.py:555
  3.5 0.5 %collective-permute-start = (bf16[768,384]{1,0:T(8,128)(2,1)}, bf16[768,384]{1,0:T(8,128)(2,1)S(1)}, u32[]{:S(2)}, u32[]{:S(2)}) collective-permute-start(bf16[768,384]{1,0:T(8,128)(2,1)} %get-tuple-element.19), channel_id=1, source_target_pairs={{0,4},{4,0},{8,12},{12,8},{1,5},{5,1},{9,13},{13,9},{2,6},{6,2},{1... | collective-permute-start | bytes 1769480 | tf_op jit(solution)/shard_map/ppermute | solution.py:47
  4.0 0.7 %convert_element_type.9 = bf16[384]{0:T(512)(128)(2,1)S(1)} convert(s32[384]{0:T(512)} %param.11) | non-fusion elementwise | flops 384 | bytes 2304 | tf_op jit(solution)/shard_map/convert_element_type | solution.py:144
  4.7 1.0 %convert_element_type.8.keep_ref = f32[1,320,384]{2,1,0:T(8,128)S(1)} convert(bf16[1,320,384]{2,1,0:T(8,128)(2,1)} %get-tuple-element.20) | non-fusion elementwise | flops 122880 | bytes 737280 | tf_op jit(solution)/shard_map/convert_element_type | solution.py:770
  5.7 0.2 collective-permute-done.received_ref.refs_1_
  5.8 0.2 relay.1
  6.1 2.9 %collective-permute-start.2 = (bf16[64,384]{1,0:T(8,128)(2,1)S(1)}, bf16[64,384]{1,0:T(8,128)(2,1)S(1)}, u32[]{:S(2)}, u32[]{:S(2)}) collective-permute-start(bf16[64,384]{1,0:T(8,128)(2,1)S(1)} %get-tuple-element.25), channel_id=1, source_target_pairs={{0,8},{4,12},{8,0},{12,4},{1,9},{5,13},{9,1},{13,5},{2,10},{6,14},... | collective-permute-start | bytes 147464 | tf_op jit(solution)/shard_map/ppermute | solution.py:47
  9.0 0.1 collective-permute-start.1
  9.1 0.8 %copy-done.6 = bf16[3,21,200]{2,1,0:T(8,128)(2,1)S(1)} copy-done((bf16[3,21,200]{2,1,0:T(8,128)(2,1)S(1)}, bf16[3,21,200]{2,1,0:T(8,128)(2,1)}, u32[]{:S(2)}) %copy-start.6) | copy-done | bytes 25224
  9.8 0.9 %levels.1 = (f32[72,8,256]{2,1,0:T(8,128)S(1)}, s32[16,8,128]{2,1,0:T(8,128)S(1)}) custom-call(bf16[8,256]{1,0:T(8,128)(2,1)S(1)} %reshape.7.class_ref, bf16[3,21,200]{2,1,0:T(8,128)(2,1)S(1)} %copy-done.6, bf16[320,384]{1,0:T(8,128)(2,1)S(1)} %get-tuple-element.21._), custom_call_target="tpu_custom_call" | custom-call | flops 100000000 | bytes 1000000 | tf_op jit(solution)/shard_map/levels/pallas_call | solution.py:145
  10.8 0.0 copy-start.1
  10.8 3.1 %table.1.table_ref.refs_3_ = bf16[3,3,1408,256]{3,2,1,0:T(8,128)(2,1)S(1)} custom-call(f32[72,8,256]{2,1,0:T(8,128)S(1)} %get-tuple-element.23.level_ref, s32[16,8,128]{2,1,0:T(8,128)S(1)} %get-tuple-element.24.kind_ref), custom_call_target="tpu_custom_call" | custom-call | flops 4000000000 | bytes 6488064 | tf_op jit(solution)/shard_map/table/pallas_call | solution.py:236
  13.9 2.4 %bin_gradients.1.refs_4_.refs_0_ = bf16[3,128,128]{2,1,0:T(8,128)(2,1)S(1)} custom-call(bf16[3,3,1408,256]{3,2,1,0:T(8,128)(2,1)S(1)} %table.1.table_ref.refs_3_, bf16[3,128,768]{2,1,0:T(8,128)(2,1)S(1)} %copy-done.1, bf16[768,384]{1,0:T(8,128)(2,1)S(1)} %collective-permute-done.received_ref.refs_1_, bf16[64,384]{1,0:T(8,128)(2,1)S(1)} %collective-permute-done.2.refs_0_), custom_call_target="tpu_custom_call" | custom-call | flops 4000000000 | bytes 6488064 | tf_op jit(solution)/shard_map/bin_gradients/pallas_call | solution.py:307
  16.3 0.4 %collective-permute-done.1.refs_2_ = bf16[320,384]{1,0:T(8,128)(2,1)S(1)} collective-permute-done((bf16[320,384]{1,0:T(8,128)(2,1)S(1)}, bf16[320,384]{1,0:T(8,128)(2,1)S(1)}, u32[]{:S(2)}, u32[]{:S(2)}) %collective-permute-start.1) | collective-permute-done | bytes 245792 | tf_op jit(solution)/shard_map/ppermute | solution.py:47
  16.7 0.6 %slab_currents.1 = (bf16[448,128]{1,0:T(8,128)(2,1)S(1)}, bf16[896,128]{1,0:T(8,128)(2,1)S(1)}, bf16[448,128]{1,0:T(8,128)(2,1)S(1)}) custom-call(f32[320,384]{1,0:T(8,128)S(1)} %copy-done.2, bf16[768,384]{1,0:T(8,128)(2,1)S(1)} %collective-permute-done.received_ref.refs_1_, bf16[320,384]{1,0:T(8,128)(2,1)S(1)} %collective-permute-done.1.refs_2_, ...), custom_call_target="tpu_custom_call" | custom-call | flops 100000000 | bytes 688128 | tf_op jit(solution)/shard_map/slab_currents/pallas_call | solution.py:646
  17.3 1.8 %collective-permute-start.3 = (bf16[896,128]{1,0:T(8,128)(2,1)S(1)}, bf16[896,128]{1,0:T(8,128)(2,1)S(1)}, u32[]{:S(2)}, u32[]{:S(2)}) collective-permute-start(bf16[896,128]{1,0:T(8,128)(2,1)S(1)} %get-tuple-element.27), channel_id=1, source_target_pairs={{0,1},{1,0},{2,3},{3,2},{4,5},{5,4},{6,7},{7,6},{8,9},{9,8},{10,11... | collective-permute-start | bytes 688136 | tf_op jit(solution)/shard_map/ppermute | solution.py:47
  19.1 2.5 %collective-permute-start.7 = (bf16[3,128,128]{2,1,0:T(8,128)(2,1)S(1)}, bf16[3,128,128]{2,1,0:T(8,128)(2,1)S(1)}, u32[]{:S(2)}, u32[]{:S(2)}) collective-permute-start(bf16[3,128,128]{2,1,0:T(8,128)(2,1)S(1)} %bin_gradients.1.refs_4_.refs_0_), channel_id=1, source_target_pairs={{0,3},{1,2},{2,1},{3,0},{4,7},{5,6},{6,5},{7,4},{8,11},{9,10},{10,... | collective-permute-start | bytes 294920 | tf_op jit(solution)/shard_map/ppermute | solution.py:47
  21.6 0.1 collective-permute-start.6
  21.7 1.8 %collective-permute-start.5 = (bf16[3,128,128]{2,1,0:T(8,128)(2,1)S(1)}, bf16[3,128,128]{2,1,0:T(8,128)(2,1)S(1)}, u32[]{:S(2)}, u32[]{:S(2)}) collective-permute-start(bf16[3,128,128]{2,1,0:T(8,128)(2,1)S(1)} %bin_gradients.1.refs_4_.refs_0_), channel_id=1, source_target_pairs={{0,1},{1,0},{2,3},{3,2},{4,5},{5,4},{6,7},{7,6},{8,9},{9,8},{10,11... | collective-permute-start | bytes 294920 | tf_op jit(solution)/shard_map/ppermute | solution.py:47
  23.5 5.6 %collective-permute-done.3.refs_1_ = bf16[896,128]{1,0:T(8,128)(2,1)S(1)} collective-permute-done((bf16[896,128]{1,0:T(8,128)(2,1)S(1)}, bf16[896,128]{1,0:T(8,128)(2,1)S(1)}, u32[]{:S(2)}, u32[]{:S(2)}) %collective-permute-start.3) | collective-permute-done | bytes 229408 | tf_op jit(solution)/shard_map/ppermute | solution.py:47
  29.1 0.2 pass_on.1.refs_4_
  29.3 2.5 %collective-permute-start.4 = (bf16[448,128]{1,0:T(8,128)(2,1)S(1)}, bf16[448,128]{1,0:T(8,128)(2,1)S(1)}, u32[]{:S(2)}, u32[]{:S(2)}) collective-permute-start(bf16[448,128]{1,0:T(8,128)(2,1)S(1)} %pass_on.1.refs_4_), channel_id=1, source_target_pairs={{0,2},{1,3},{2,0},{3,1},{4,6},{5,7},{6,4},{7,5},{8,10},{9,11},{10,... | collective-permute-start | bytes 344072 | tf_op jit(solution)/shard_map/ppermute | solution.py:47
  31.8 0.2 merge_bins.1
  32.1 1.6 %collective-permute-start.10 = (bf16[128,384]{1,0:T(8,128)(2,1)S(1)}, bf16[128,384]{1,0:T(8,128)(2,1)S(1)}, u32[]{:S(2)}, u32[]{:S(2)}) collective-permute-start(bf16[128,384]{1,0:T(8,128)(2,1)S(1)} %get-tuple-element.30.refs_0_), channel_id=1, source_target_pairs={{0,8},{4,12},{8,0},{12,4},{1,9},{5,13},{9,1},{13,5},{2,10},{6,14},... | collective-permute-start | bytes 294920 | tf_op jit(solution)/shard_map/ppermute | solution.py:47
  33.7 0.5 %collective-permute-start.11 = (bf16[128,384]{1,0:T(8,128)(2,1)S(1)}, bf16[128,384]{1,0:T(8,128)(2,1)S(1)}, u32[]{:S(2)}, u32[]{:S(2)}) collective-permute-start(bf16[128,384]{1,0:T(8,128)(2,1)S(1)} %get-tuple-element.31.refs_1_), channel_id=1, source_target_pairs={{0,8},{4,12},{8,0},{12,4},{1,9},{5,13},{9,1},{13,5},{2,10},{6,14},... | collective-permute-start | bytes 294920 | tf_op jit(solution)/shard_map/ppermute | solution.py:47
  34.2 0.5 %collective-permute-start.9 = (bf16[128,384]{1,0:T(8,128)(2,1)S(1)}, bf16[128,384]{1,0:T(8,128)(2,1)S(1)}, u32[]{:S(2)}, u32[]{:S(2)}) collective-permute-start(bf16[128,384]{1,0:T(8,128)(2,1)S(1)} %get-tuple-element.31.refs_1_), channel_id=1, source_target_pairs={{0,4},{4,0},{8,12},{12,8},{1,5},{5,1},{9,13},{13,9},{2,6},{6,2},{1... | collective-permute-start | bytes 294920 | tf_op jit(solution)/shard_map/ppermute | solution.py:47
  34.7 2.1 %collective-permute-done.10.refs_4_ = bf16[128,384]{1,0:T(8,128)(2,1)S(1)} collective-permute-done((bf16[128,384]{1,0:T(8,128)(2,1)S(1)}, bf16[128,384]{1,0:T(8,128)(2,1)S(1)}, u32[]{:S(2)}, u32[]{:S(2)}) %collective-permute-start.10) | collective-permute-done | bytes 98336 | tf_op jit(solution)/shard_map/ppermute | solution.py:47
  36.8 1.5 %collective-permute-done.11.refs_5_ = bf16[128,384]{1,0:T(8,128)(2,1)S(1)} collective-permute-done((bf16[128,384]{1,0:T(8,128)(2,1)S(1)}, bf16[128,384]{1,0:T(8,128)(2,1)S(1)}, u32[]{:S(2)}, u32[]{:S(2)}) %collective-permute-start.11) | collective-permute-done | bytes 98336 | tf_op jit(solution)/shard_map/ppermute | solution.py:47
  38.3 0.0 copy-start.4
  38.3 0.0 copy-start.5
  38.3 2.7 %signal.1 = (bf16[3,128,768]{2,1,0:T(8,128)(2,1)}, f32[8,128]{1,0:T(8,128)S(1)}) custom-call(bf16[448,128]{1,0:T(8,128)(2,1)S(1)} %get-tuple-element.26.refs_0_, bf16[896,128]{1,0:T(8,128)(2,1)S(1)} %collective-permute-done.3.refs_1_, bf16[448,128]{1,0:T(8,128)(2,1)S(1)} %collective-permute-done.4.refs_2_, bf16[3,3,1408,256]{3,2,1,0:T(8,128)(2,1)S(1)} %table.1.table_ref.refs_3_), custom_call_target="tpu_custom_call" | custom-call | flops 4000000000 | bytes 6488064 | tf_op jit(solution)/shard_map/signal/pallas_call | solution.py:735
  41.1 1.8 %charge_gradient.1 = bf16[512,384]{1,0:T(8,128)(2,1)} custom-call(s32[3,2,4]{2,1,0:T(2,128)S(1)} %bitcast.2, s32[4,3]{1,0:T(4,128)S(1)} %copy-done.5, bf16[128,384]{1,0:T(8,128)(2,1)S(1)} %get-tuple-element.30.refs_0_, bf16[128,384]{1,0:T(8,128)(2,1)S(1)} %get-tuple-element.31.refs_1_, bf16[128,384]{1,0:T(8,128)(2,1)S(1)} %collective-permute-done.8.refs_2_, ...), custom_call_target="tpu_custom_call" | custom-call | flops 100000000 | bytes 786432 | tf_op jit(solution)/shard_map/charge_gradient/pallas_call | solution.py:407
  (24 shorter events, 0.1 us)
Async XLA Ops:
  3.5 2.4 %collective-permute-start = (bf16[768,384]{1,0:T(8,128)(2,1)}, bf16[768,384]{1,0:T(8,128)(2,1)S(1)}, u32[]{:S(2)}, u32[]{:S(2)}) collective-permute-start(bf16[768,384]{1,0:T(8,128)(2,1)} %get-tuple-element.19), channel_id=1, source_target_pairs={{0,4},{4,0},{8,12},{12,8},{1,5},{5,1},{9,13},{13,9},{2,6},{6,2},{1... | collective-permute-start | bytes 1769480 | tf_op jit(solution)/shard_map/ppermute | solution.py:47
  6.1 7.8 %collective-permute-start.2 = (bf16[64,384]{1,0:T(8,128)(2,1)S(1)}, bf16[64,384]{1,0:T(8,128)(2,1)S(1)}, u32[]{:S(2)}, u32[]{:S(2)}) collective-permute-start(bf16[64,384]{1,0:T(8,128)(2,1)S(1)} %get-tuple-element.25), channel_id=1, source_target_pairs={{0,8},{4,12},{8,0},{12,4},{1,9},{5,13},{9,1},{13,5},{2,10},{6,14},... | collective-permute-start | bytes 147464 | tf_op jit(solution)/shard_map/ppermute | solution.py:47
  9.0 7.7 %collective-permute-start.1 = (bf16[320,384]{1,0:T(8,128)(2,1)S(1)}, bf16[320,384]{1,0:T(8,128)(2,1)S(1)}, u32[]{:S(2)}, u32[]{:S(2)}) collective-permute-start(bf16[320,384]{1,0:T(8,128)(2,1)S(1)} %get-tuple-element.21._), channel_id=1, source_target_pairs={{0,8},{4,12},{8,0},{12,4},{1,9},{5,13},{9,1},{13,5},{2,10},{6,14},... | collective-permute-start | bytes 737288 | tf_op jit(solution)/shard_map/ppermute | solution.py:47
  9.1 0.8 %copy-start.6 = (bf16[3,21,200]{2,1,0:T(8,128)(2,1)S(1)}, bf16[3,21,200]{2,1,0:T(8,128)(2,1)}, u32[]{:S(2)}) copy-start(bf16[3,21,200]{2,1,0:T(8,128)(2,1)} %response_ref.1) | copy-start | bytes 75604
  10.8 3.1 %copy-start.1 = (bf16[3,128,768]{2,1,0:T(8,128)(2,1)S(1)}, bf16[3,128,768]{2,1,0:T(8,128)(2,1)}, u32[]{:S(2)}) copy-start(bf16[3,128,768]{2,1,0:T(8,128)(2,1)} %own_ref.1) | copy-start | bytes 1769476
  13.9 2.9 %copy-start.2 = (f32[320,384]{1,0:T(8,128)S(1)}, f32[320,384]{1,0:T(8,128)}, u32[]{:S(2)}) copy-start(f32[320,384]{1,0:T(8,128)} %get-tuple-element.18.refs_0_) | copy-start | bytes 1474564
  13.9 2.8 %copy-start.3 = (f32[128,384]{1,0:T(8,128)S(1)}, f32[128,384]{1,0:T(8,128)}, u32[]{:S(2)}) copy-start(f32[128,384]{1,0:T(8,128)} %get-tuple-element.22.refs_3_) | copy-start | bytes 589828
  17.3 11.8 %collective-permute-start.3 = (bf16[896,128]{1,0:T(8,128)(2,1)S(1)}, bf16[896,128]{1,0:T(8,128)(2,1)S(1)}, u32[]{:S(2)}, u32[]{:S(2)}) collective-permute-start(bf16[896,128]{1,0:T(8,128)(2,1)S(1)} %get-tuple-element.27), channel_id=1, source_target_pairs={{0,1},{1,0},{2,3},{3,2},{4,5},{5,4},{6,7},{7,6},{8,9},{9,8},{10,11... | collective-permute-start | bytes 688136 | tf_op jit(solution)/shard_map/ppermute | solution.py:47
  19.1 12.7 %collective-permute-start.7 = (bf16[3,128,128]{2,1,0:T(8,128)(2,1)S(1)}, bf16[3,128,128]{2,1,0:T(8,128)(2,1)S(1)}, u32[]{:S(2)}, u32[]{:S(2)}) collective-permute-start(bf16[3,128,128]{2,1,0:T(8,128)(2,1)S(1)} %bin_gradients.1.refs_4_.refs_0_), channel_id=1, source_target_pairs={{0,3},{1,2},{2,1},{3,0},{4,7},{5,6},{6,5},{7,4},{8,11},{9,10},{10,... | collective-permute-start | bytes 294920 | tf_op jit(solution)/shard_map/ppermute | solution.py:47
  21.6 10.3 %collective-permute-start.6 = (bf16[3,128,128]{2,1,0:T(8,128)(2,1)S(1)}, bf16[3,128,128]{2,1,0:T(8,128)(2,1)S(1)}, u32[]{:S(2)}, u32[]{:S(2)}) collective-permute-start(bf16[3,128,128]{2,1,0:T(8,128)(2,1)S(1)} %bin_gradients.1.refs_4_.refs_0_), channel_id=1, source_target_pairs={{0,2},{1,3},{2,0},{3,1},{4,6},{5,7},{6,4},{7,5},{8,10},{9,11},{10,... | collective-permute-start | bytes 294920 | tf_op jit(solution)/shard_map/ppermute | solution.py:47
  21.7 10.1 %collective-permute-start.5 = (bf16[3,128,128]{2,1,0:T(8,128)(2,1)S(1)}, bf16[3,128,128]{2,1,0:T(8,128)(2,1)S(1)}, u32[]{:S(2)}, u32[]{:S(2)}) collective-permute-start(bf16[3,128,128]{2,1,0:T(8,128)(2,1)S(1)} %bin_gradients.1.refs_4_.refs_0_), channel_id=1, source_target_pairs={{0,1},{1,0},{2,3},{3,2},{4,5},{5,4},{6,7},{7,6},{8,9},{9,8},{10,11... | collective-permute-start | bytes 294920 | tf_op jit(solution)/shard_map/ppermute | solution.py:47
  29.3 9.0 %collective-permute-start.4 = (bf16[448,128]{1,0:T(8,128)(2,1)S(1)}, bf16[448,128]{1,0:T(8,128)(2,1)S(1)}, u32[]{:S(2)}, u32[]{:S(2)}) collective-permute-start(bf16[448,128]{1,0:T(8,128)(2,1)S(1)} %pass_on.1.refs_4_), channel_id=1, source_target_pairs={{0,2},{1,3},{2,0},{3,1},{4,6},{5,7},{6,4},{7,5},{8,10},{9,11},{10,... | collective-permute-start | bytes 344072 | tf_op jit(solution)/shard_map/ppermute | solution.py:47
  32.1 4.7 %collective-permute-start.10 = (bf16[128,384]{1,0:T(8,128)(2,1)S(1)}, bf16[128,384]{1,0:T(8,128)(2,1)S(1)}, u32[]{:S(2)}, u32[]{:S(2)}) collective-permute-start(bf16[128,384]{1,0:T(8,128)(2,1)S(1)} %get-tuple-element.30.refs_0_), channel_id=1, source_target_pairs={{0,8},{4,12},{8,0},{12,4},{1,9},{5,13},{9,1},{13,5},{2,10},{6,14},... | collective-permute-start | bytes 294920 | tf_op jit(solution)/shard_map/ppermute | solution.py:47
  33.7 4.6 %collective-permute-start.11 = (bf16[128,384]{1,0:T(8,128)(2,1)S(1)}, bf16[128,384]{1,0:T(8,128)(2,1)S(1)}, u32[]{:S(2)}, u32[]{:S(2)}) collective-permute-start(bf16[128,384]{1,0:T(8,128)(2,1)S(1)} %get-tuple-element.31.refs_1_), channel_id=1, source_target_pairs={{0,8},{4,12},{8,0},{12,4},{1,9},{5,13},{9,1},{13,5},{2,10},{6,14},... | collective-permute-start | bytes 294920 | tf_op jit(solution)/shard_map/ppermute | solution.py:47
  34.2 6.9 %collective-permute-start.8 = (bf16[128,384]{1,0:T(8,128)(2,1)S(1)}, bf16[128,384]{1,0:T(8,128)(2,1)S(1)}, u32[]{:S(2)}, u32[]{:S(2)}) collective-permute-start(bf16[128,384]{1,0:T(8,128)(2,1)S(1)} %get-tuple-element.30.refs_0_), channel_id=1, source_target_pairs={{0,4},{4,0},{8,12},{12,8},{1,5},{5,1},{9,13},{13,9},{2,6},{6,2},{1... | collective-permute-start | bytes 294920 | tf_op jit(solution)/shard_map/ppermute | solution.py:47
  34.2 6.9 %collective-permute-start.9 = (bf16[128,384]{1,0:T(8,128)(2,1)S(1)}, bf16[128,384]{1,0:T(8,128)(2,1)S(1)}, u32[]{:S(2)}, u32[]{:S(2)}) collective-permute-start(bf16[128,384]{1,0:T(8,128)(2,1)S(1)} %get-tuple-element.31.refs_1_), channel_id=1, source_target_pairs={{0,4},{4,0},{8,12},{12,8},{1,5},{5,1},{9,13},{13,9},{2,6},{6,2},{1... | collective-permute-start | bytes 294920 | tf_op jit(solution)/shard_map/ppermute | solution.py:47
  36.8 4.3 %collective-permute-start.12 = (bf16[128,384]{1,0:T(8,128)(2,1)S(1)}, bf16[128,384]{1,0:T(8,128)(2,1)S(1)}, u32[]{:S(2)}, u32[]{:S(2)}) collective-permute-start(bf16[128,384]{1,0:T(8,128)(2,1)S(1)} %collective-permute-done.10.refs_4_), channel_id=1, source_target_pairs={{0,4},{4,0},{8,12},{12,8},{1,5},{5,1},{9,13},{13,9},{2,6},{6,2},{1... | collective-permute-start | bytes 294920 | tf_op jit(solution)/shard_map/ppermute | solution.py:47
  38.3 2.8 %collective-permute-start.13 = (bf16[128,384]{1,0:T(8,128)(2,1)S(1)}, bf16[128,384]{1,0:T(8,128)(2,1)S(1)}, u32[]{:S(2)}, u32[]{:S(2)}) collective-permute-start(bf16[128,384]{1,0:T(8,128)(2,1)S(1)} %collective-permute-done.11.refs_5_), channel_id=1, source_target_pairs={{0,4},{4,0},{8,12},{12,8},{1,5},{5,1},{9,13},{13,9},{2,6},{6,2},{1... | collective-permute-start | bytes 294920 | tf_op jit(solution)/shard_map/ppermute | solution.py:47
  38.3 2.8 %copy-start = (bf16[4,3,2,32,128]{4,3,2,1,0:T(8,128)(2,1)S(1)}, bf16[4,3,2,32,128]{4,3,2,1,0:T(8,128)(2,1)}, u32[]{:S(2)}) copy-start(bf16[4,3,2,32,128]{4,3,2,1,0:T(8,128)(2,1)} %refs_9_.1) | copy-start | bytes 589828
  38.3 2.8 %copy-start.4 = (s32[4,3,2]{0,2,1:T(2,128)S(1)}, s32[4,3,2]{0,2,1:T(2,128)}, u32[]{:S(2)}) copy-start(s32[4,3,2]{0,2,1:T(2,128)} %param.9) | copy-start | bytes 292
  38.3 2.8 %copy-start.5 = (s32[4,3]{1,0:T(4,128)S(1)}, s32[4,3]{1,0:T(4,128)}, u32[]{:S(2)}) copy-start(s32[4,3]{1,0:T(4,128)} %count_ref.1) | copy-start | bytes 148

commit v7 on v6

--- a/solution.py
+++ b/solution.py
@@ -358,7 +358,7 @@
 
 
 def charge_kernel(block_ref, count_ref, *refs):
-    sources, (local_ref, share_ref, _, out_hbm) = refs[:-8], refs[-8:-4]
+    sources, (local_ref, share_ref, signal_ref, out_hbm, signal_hbm) = refs[:-9], refs[-9:-4]
     all_ref, chosen_ref, out_ref, sems = refs[-4:]
     cells, planes, entries, wire_block, width = share_ref.shape
     owners, _, wires, total = all_ref.shape
@@ -370,7 +370,8 @@
         else:
             all_ref[z ^ (i // (planes - 1)), i % (planes - 1)] = source[...]
     empty = jnp.zeros((wire_block, total), BF16)
-    stores = []
+    stores = [pltpu.make_async_copy(signal_ref, signal_hbm, sems.at[cells])]
+    stores[0].start()
     for b in range(cells):
         for p in range(planes):
             for k in range(entries):
@@ -400,25 +401,28 @@
         store.wait()
 
 
-def charge_gradient(ovl_block, ovl_count, sources, local, intersection, owners, before):
+def charge_gradient(ovl_block, ovl_count, sources, local, intersection, owners, signal):
     cells, planes, entries, wire_block, width = intersection.shape
     wires, total = local.shape
     shape = (owners, planes - 1, wires, total)
     return pl.pallas_call(
         charge_kernel,
-        out_shape=jax.ShapeDtypeStruct((cells * width, total), BF16),
+        out_shape=(
+            jax.ShapeDtypeStruct((cells * width, total), BF16),
+            jax.ShapeDtypeStruct(signal.shape, BF16),
+        ),
         in_specs=[smem(), smem()] + [vmem()] * (len(sources) + 3),
-        out_specs=anywhere(),
+        out_specs=(anywhere(), anywhere()),
         scratch_shapes=[
             pltpu.VMEM(shape, BF16),
             pltpu.VMEM((cells, planes * entries * wire_block, total), BF16),
             pltpu.VMEM((cells * width, total), BF16),
-            pltpu.SemaphoreType.DMA((cells,)),
+            pltpu.SemaphoreType.DMA((cells + 1,)),
         ],
         compiler_params=params(),
         cost_estimate=cost(1e8, 2 * math.prod(shape)),
         name="charge_gradient",
-    )(jnp.transpose(ovl_block, (1, 2, 0)), ovl_count, *sources, local, intersection, before)
+    )(jnp.transpose(ovl_block, (1, 2, 0)), ovl_count, *sources, local, intersection, signal)
 
 
 def pieces_kernel(
@@ -681,17 +685,14 @@
 
 
 def signal_kernel(*refs, wire_taps):
-    parts, (table_ref, out_hbm, token_ref) = refs[:-9], refs[-9:-6]
-    even_ref, odd_ref, level_ref, lines_ref, out_ref, sems = refs[-6:]
+    parts, (table_ref, out_ref, even_ref, odd_ref, level_ref, lines_ref) = refs[:-6], refs[-6:]
     planes, blocks, _, span = table_ref.shape
     _, wires, _ = out_ref.shape
     half = (wire_taps - 1) // 2
     extent = wires + 2 * half
     step = span * 16 // LANES
     middle = WINDOW // 2
-    token_ref[...] = jnp.zeros(token_ref.shape, F32)
     lane = lax.broadcasted_iota(jnp.int32, (wires, LANES), 1)
-    stores = []
     size = parts[0].shape[0]
     summed = plain(parts[0][...], False)
     for part in parts[1:]:
@@ -721,11 +722,6 @@
             out_ref[p, :, block * span : (block + 1) * span] = jnp.dot(
                 lines_ref[i % 2], table_ref[p, block], preferred_element_type=F32
             ).astype(BF16)
-        store = pltpu.make_async_copy(out_ref.at[p], out_hbm.at[p], sems.at[p])
-        store.start()
-        stores.append(store)
-    for store in stores:
-        store.wait()
 
 
 def forward(parts, table, wires, wire_taps):
@@ -734,19 +730,14 @@
     shape = (planes, wires, blocks * span)
     return pl.pallas_call(
         functools.partial(signal_kernel, wire_taps=wire_taps),
-        out_shape=(
-            jax.ShapeDtypeStruct(shape, BF16),
-            jax.ShapeDtypeStruct((8, LANES), F32),
-        ),
+        out_shape=jax.ShapeDtypeStruct(shape, BF16),
         in_specs=[vmem()] * (len(parts) + 1),
-        out_specs=(anywhere(), vmem()),
+        out_specs=vmem(),
         scratch_shapes=[
             pltpu.VMEM((planes * blocks, extent, LANES), F32),
             pltpu.VMEM((planes * blocks, extent, LANES), F32),
             pltpu.VMEM((planes, extent, LANES), F32),
             pltpu.VMEM((2, wires, depth), BF16),
-            pltpu.VMEM(shape, BF16),
-            pltpu.SemaphoreType.DMA((planes,)),
         ],
         compiler_params=params(),
         cost_estimate=cost(4e9, 2 * math.prod(table.shape)),
@@ -794,9 +785,9 @@
         sources += [*across, *(swap(block, "gz", 1) for block in across)]
     else:
         sources = [lax.all_gather(block, "gz", axis=0) for block in cross]
-    signal, done = forward(windows, table, wires, wire_taps)
-    charge_grad = charge_gradient(
-        ovl_block, ovl_count, sources, own, intersection, owners, done
+    signal = forward(windows, table, wires, wire_taps)
+    charge_grad, signal = charge_gradient(
+        ovl_block, ovl_count, sources, own, intersection, owners, signal
     )
     return signal, charge_grad
 

time: 43.2 us -> 42.6 us (0.986)
  Pallas kernels: 15 us -> 14.3 us
    pallas_call x1, Pallas kernels: 2.69 us -> 1.96 us  [forward(): pl.pallas_call(functools.partial(signal_kernel, wire_taps=wire_taps), out...]
  transfers between devices with their start and end apart: 14 -> 14, of which waited for: 5 -> 5; matrix products, arithmetic and copies ran while one was open for 4% -> 4% of each run, Pallas kernels for 22% -> 21%
where the time goes in v7:
time: 42.6 us; the launch traced here: 42.3 us
  starting transfers between devices  14.8 us (35%)
  Pallas kernels  14.3 us (34%)
  waiting for transfers between devices  9.83 us (23%)
  other arithmetic  1.66 us (4%)
  between operations  0.83 us (2%)
  local copies, waits for them, and re-layouts  0.82 us (2%)
    ppermute x14, starting transfers between devices, swap(): return lax.ppermute(block, axis, [(i, i ^ distance) for i in range(count)])  14.8 us
    ppermute x14, waiting for transfers between devices, swap(): return lax.ppermute(block, axis, [(i, i ^ distance) for i in range(count)])  9.83 us
    pallas_call x1, Pallas kernels, build_table(): pl.pallas_call(functools.partial(table_kernel, wire_taps=wire_taps), out_...  3.07 us
    pallas_call x1, Pallas kernels, cut_pieces(): pl.pallas_call(functools.partial(pieces_kernel, half=half), out_shape=out...  2.82 us
    pallas_call x1, Pallas kernels, backward(): pl.pallas_call(functools.partial(back_kernel, wire_taps=wire_taps), out_s...  2.38 us
    pallas_call x1, Pallas kernels, forward(): pl.pallas_call(functools.partial(signal_kernel, wire_taps=wire_taps), out...  1.96 us
    pallas_call x1, Pallas kernels, charge_gradient(): pl.pallas_call(charge_kernel, out_shape=(jax.ShapeDtypeStruct((cells * wi...  1.94 us
    convert_element_type x1, other arithmetic, local(): sums, edges = relay(keep.astype(F32), received) if owners > 2 else ((), ())  0.98 us
  transfers between devices with their start and end apart: 14, of which 5 were waited for; matrix products, arithmetic and copies ran while one was open for 4% of the time, Pallas kernels for 21%

profile of v7, /device:TPU:0, one launch (start us, length us, event | category | flops | bytes accessed | tf_op | source)
XLA Modules:
  0.0 42.3 jit_solution(11823731670444058853)
XLA Ops:
  0.6 2.8 %pieces.1 = (f32[320,384]{1,0:T(8,128)}, bf16[1,320,384]{2,1,0:T(8,128)(2,1)}, bf16[768,384]{1,0:T(8,128)(2,1)}, f32[128,384]{1,0:T(8,128)}) custom-call(s32[3,2,4]{2,1,0:T(2,128)} %bitcast.1, s32[4,3]{1,0:T(4,128)} %count_ref.1, bf16[512,384]{1,0:T(8,128)(2,1)} %charge_hbm.1, bf16[4,3,2,32,128]{4,3,2,1,0:T(8,128)(2,1)} %refs_9_.1, bf16[3,128,768]{2,1,0:T(8,128)(2,1)} %own_ref.1), custom_call_target="tpu_custom_call" | custom-call | flops 100000000 | bytes 1966080 | tf_op jit(solution)/shard_map/pieces/pallas_call | solution.py:559
  3.5 0.5 %collective-permute-start = (bf16[768,384]{1,0:T(8,128)(2,1)}, bf16[768,384]{1,0:T(8,128)(2,1)S(1)}, u32[]{:S(2)}, u32[]{:S(2)}) collective-permute-start(bf16[768,384]{1,0:T(8,128)(2,1)} %get-tuple-element.19), channel_id=1, source_target_pairs={{0,4},{4,0},{8,12},{12,8},{1,5},{5,1},{9,13},{13,9},{2,6},{6,2},{1... | collective-permute-start | bytes 1769480 | tf_op jit(solution)/shard_map/ppermute | solution.py:47
  4.0 0.7 %convert_element_type.8 = bf16[384]{0:T(512)(128)(2,1)S(1)} convert(s32[384]{0:T(512)} %param.11) | non-fusion elementwise | flops 384 | bytes 2304 | tf_op jit(solution)/shard_map/convert_element_type | solution.py:144
  4.7 1.0 %convert_element_type.9.keep_ref = f32[1,320,384]{2,1,0:T(8,128)S(1)} convert(bf16[1,320,384]{2,1,0:T(8,128)(2,1)} %get-tuple-element.18) | non-fusion elementwise | flops 122880 | bytes 737280 | tf_op jit(solution)/shard_map/convert_element_type | solution.py:761
  5.7 0.2 collective-permute-done.received_ref.refs_1_
  5.8 0.2 relay.1
  6.1 2.9 %collective-permute-start.1 = (bf16[64,384]{1,0:T(8,128)(2,1)S(1)}, bf16[64,384]{1,0:T(8,128)(2,1)S(1)}, u32[]{:S(2)}, u32[]{:S(2)}) collective-permute-start(bf16[64,384]{1,0:T(8,128)(2,1)S(1)} %get-tuple-element.23), channel_id=1, source_target_pairs={{0,8},{4,12},{8,0},{12,4},{1,9},{5,13},{9,1},{13,5},{2,10},{6,14},... | collective-permute-start | bytes 147464 | tf_op jit(solution)/shard_map/ppermute | solution.py:47
  9.0 0.1 collective-permute-start.5
  9.1 0.8 %copy-done.6 = bf16[3,21,200]{2,1,0:T(8,128)(2,1)S(1)} copy-done((bf16[3,21,200]{2,1,0:T(8,128)(2,1)S(1)}, bf16[3,21,200]{2,1,0:T(8,128)(2,1)}, u32[]{:S(2)}) %copy-start.6) | copy-done | bytes 25224
  9.8 0.9 %levels.1 = (f32[72,8,256]{2,1,0:T(8,128)S(1)}, s32[16,8,128]{2,1,0:T(8,128)S(1)}) custom-call(bf16[8,256]{1,0:T(8,128)(2,1)S(1)} %reshape.7.class_ref, bf16[3,21,200]{2,1,0:T(8,128)(2,1)S(1)} %copy-done.6, bf16[320,384]{1,0:T(8,128)(2,1)S(1)} %get-tuple-element.20._), custom_call_target="tpu_custom_call" | custom-call | flops 100000000 | bytes 1000000 | tf_op jit(solution)/shard_map/levels/pallas_call | solution.py:145
  10.8 0.0 copy-start.1
  10.8 3.1 %table.1.table_ref.refs_3_ = bf16[3,3,1408,256]{3,2,1,0:T(8,128)(2,1)S(1)} custom-call(f32[72,8,256]{2,1,0:T(8,128)S(1)} %get-tuple-element.21.level_ref, s32[16,8,128]{2,1,0:T(8,128)S(1)} %get-tuple-element.22.kind_ref), custom_call_target="tpu_custom_call" | custom-call | flops 4000000000 | bytes 6488064 | tf_op jit(solution)/shard_map/table/pallas_call | solution.py:236
  13.9 2.4 %bin_gradients.1.refs_4_.refs_0_ = bf16[3,128,128]{2,1,0:T(8,128)(2,1)S(1)} custom-call(bf16[3,3,1408,256]{3,2,1,0:T(8,128)(2,1)S(1)} %table.1.table_ref.refs_3_, bf16[3,128,768]{2,1,0:T(8,128)(2,1)S(1)} %copy-done.1, bf16[768,384]{1,0:T(8,128)(2,1)S(1)} %collective-permute-done.received_ref.refs_1_, bf16[64,384]{1,0:T(8,128)(2,1)S(1)} %collective-permute-done.1.refs_0_), custom_call_target="tpu_custom_call" | custom-call | flops 4000000000 | bytes 6488064 | tf_op jit(solution)/shard_map/bin_gradients/pallas_call | solution.py:307
  16.3 0.4 %collective-permute-done.5.refs_2_ = bf16[320,384]{1,0:T(8,128)(2,1)S(1)} collective-permute-done((bf16[320,384]{1,0:T(8,128)(2,1)S(1)}, bf16[320,384]{1,0:T(8,128)(2,1)S(1)}, u32[]{:S(2)}, u32[]{:S(2)}) %collective-permute-start.5) | collective-permute-done | bytes 245792 | tf_op jit(solution)/shard_map/ppermute | solution.py:47
  16.7 0.6 %slab_currents.1 = (bf16[448,128]{1,0:T(8,128)(2,1)S(1)}, bf16[896,128]{1,0:T(8,128)(2,1)S(1)}, bf16[448,128]{1,0:T(8,128)(2,1)S(1)}) custom-call(f32[320,384]{1,0:T(8,128)S(1)} %copy-done.2, bf16[768,384]{1,0:T(8,128)(2,1)S(1)} %collective-permute-done.received_ref.refs_1_, bf16[320,384]{1,0:T(8,128)(2,1)S(1)} %collective-permute-done.5.refs_2_, ...), custom_call_target="tpu_custom_call" | custom-call | flops 100000000 | bytes 688128 | tf_op jit(solution)/shard_map/slab_currents/pallas_call | solution.py:650
  17.3 1.8 %collective-permute-start.6 = (bf16[896,128]{1,0:T(8,128)(2,1)S(1)}, bf16[896,128]{1,0:T(8,128)(2,1)S(1)}, u32[]{:S(2)}, u32[]{:S(2)}) collective-permute-start(bf16[896,128]{1,0:T(8,128)(2,1)S(1)} %get-tuple-element.27), channel_id=1, source_target_pairs={{0,1},{1,0},{2,3},{3,2},{4,5},{5,4},{6,7},{7,6},{8,9},{9,8},{10,11... | collective-permute-start | bytes 688136 | tf_op jit(solution)/shard_map/ppermute | solution.py:47
  19.1 2.5 %collective-permute-start.4 = (bf16[3,128,128]{2,1,0:T(8,128)(2,1)S(1)}, bf16[3,128,128]{2,1,0:T(8,128)(2,1)S(1)}, u32[]{:S(2)}, u32[]{:S(2)}) collective-permute-start(bf16[3,128,128]{2,1,0:T(8,128)(2,1)S(1)} %bin_gradients.1.refs_4_.refs_0_), channel_id=1, source_target_pairs={{0,3},{1,2},{2,1},{3,0},{4,7},{5,6},{6,5},{7,4},{8,11},{9,10},{10,... | collective-permute-start | bytes 294920 | tf_op jit(solution)/shard_map/ppermute | solution.py:47
  21.6 0.1 collective-permute-start.3
  21.7 1.8 %collective-permute-start.2 = (bf16[3,128,128]{2,1,0:T(8,128)(2,1)S(1)}, bf16[3,128,128]{2,1,0:T(8,128)(2,1)S(1)}, u32[]{:S(2)}, u32[]{:S(2)}) collective-permute-start(bf16[3,128,128]{2,1,0:T(8,128)(2,1)S(1)} %bin_gradients.1.refs_4_.refs_0_), channel_id=1, source_target_pairs={{0,1},{1,0},{2,3},{3,2},{4,5},{5,4},{6,7},{7,6},{8,9},{9,8},{10,11... | collective-permute-start | bytes 294920 | tf_op jit(solution)/shard_map/ppermute | solution.py:47
  23.5 5.6 %collective-permute-done.6.refs_1_ = bf16[896,128]{1,0:T(8,128)(2,1)S(1)} collective-permute-done((bf16[896,128]{1,0:T(8,128)(2,1)S(1)}, bf16[896,128]{1,0:T(8,128)(2,1)S(1)}, u32[]{:S(2)}, u32[]{:S(2)}) %collective-permute-start.6) | collective-permute-done | bytes 229408 | tf_op jit(solution)/shard_map/ppermute | solution.py:47
  29.1 0.2 pass_on.1.refs_4_
  29.3 2.5 %collective-permute-start.13 = (bf16[448,128]{1,0:T(8,128)(2,1)S(1)}, bf16[448,128]{1,0:T(8,128)(2,1)S(1)}, u32[]{:S(2)}, u32[]{:S(2)}) collective-permute-start(bf16[448,128]{1,0:T(8,128)(2,1)S(1)} %pass_on.1.refs_4_), channel_id=1, source_target_pairs={{0,2},{1,3},{2,0},{3,1},{4,6},{5,7},{6,4},{7,5},{8,10},{9,11},{10,... | collective-permute-start | bytes 344072 | tf_op jit(solution)/shard_map/ppermute | solution.py:47
  31.8 0.2 merge_bins.1
  32.1 1.6 %collective-permute-start.9 = (bf16[128,384]{1,0:T(8,128)(2,1)S(1)}, bf16[128,384]{1,0:T(8,128)(2,1)S(1)}, u32[]{:S(2)}, u32[]{:S(2)}) collective-permute-start(bf16[128,384]{1,0:T(8,128)(2,1)S(1)} %get-tuple-element.28.refs_0_), channel_id=1, source_target_pairs={{0,8},{4,12},{8,0},{12,4},{1,9},{5,13},{9,1},{13,5},{2,10},{6,14},... | collective-permute-start | bytes 294920 | tf_op jit(solution)/shard_map/ppermute | solution.py:47
  33.7 0.5 %collective-permute-start.10 = (bf16[128,384]{1,0:T(8,128)(2,1)S(1)}, bf16[128,384]{1,0:T(8,128)(2,1)S(1)}, u32[]{:S(2)}, u32[]{:S(2)}) collective-permute-start(bf16[128,384]{1,0:T(8,128)(2,1)S(1)} %get-tuple-element.29.refs_1_), channel_id=1, source_target_pairs={{0,8},{4,12},{8,0},{12,4},{1,9},{5,13},{9,1},{13,5},{2,10},{6,14},... | collective-permute-start | bytes 294920 | tf_op jit(solution)/shard_map/ppermute | solution.py:47
  34.2 0.5 %collective-permute-start.8 = (bf16[128,384]{1,0:T(8,128)(2,1)S(1)}, bf16[128,384]{1,0:T(8,128)(2,1)S(1)}, u32[]{:S(2)}, u32[]{:S(2)}) collective-permute-start(bf16[128,384]{1,0:T(8,128)(2,1)S(1)} %get-tuple-element.29.refs_1_), channel_id=1, source_target_pairs={{0,4},{4,0},{8,12},{12,8},{1,5},{5,1},{9,13},{13,9},{2,6},{6,2},{1... | collective-permute-start | bytes 294920 | tf_op jit(solution)/shard_map/ppermute | solution.py:47
  34.7 2.1 %collective-permute-done.9.refs_4_ = bf16[128,384]{1,0:T(8,128)(2,1)S(1)} collective-permute-done((bf16[128,384]{1,0:T(8,128)(2,1)S(1)}, bf16[128,384]{1,0:T(8,128)(2,1)S(1)}, u32[]{:S(2)}, u32[]{:S(2)}) %collective-permute-start.9) | collective-permute-done | bytes 98336 | tf_op jit(solution)/shard_map/ppermute | solution.py:47
  36.7 1.6 %collective-permute-done.10.refs_5_ = bf16[128,384]{1,0:T(8,128)(2,1)S(1)} collective-permute-done((bf16[128,384]{1,0:T(8,128)(2,1)S(1)}, bf16[128,384]{1,0:T(8,128)(2,1)S(1)}, u32[]{:S(2)}, u32[]{:S(2)}) %collective-permute-start.10) | collective-permute-done | bytes 98336 | tf_op jit(solution)/shard_map/ppermute | solution.py:47
  38.3 0.0 copy-start.4
  38.3 0.0 copy-start.5
  38.3 2.0 %signal.1.refs_10_ = bf16[3,128,768]{2,1,0:T(8,128)(2,1)S(1)} custom-call(bf16[448,128]{1,0:T(8,128)(2,1)S(1)} %get-tuple-element.31.refs_0_, bf16[896,128]{1,0:T(8,128)(2,1)S(1)} %collective-permute-done.6.refs_1_, bf16[448,128]{1,0:T(8,128)(2,1)S(1)} %collective-permute-done.13.refs_2_, bf16[3,3,1408,256]{3,2,1,0:T(8,128)(2,1)S(1)} %table.1.table_ref.refs_3_), custom_call_target="tpu_custom_call" | custom-call | flops 4000000000 | bytes 6488064 | tf_op jit(solution)/shard_map/signal/pallas_call | solution.py:731
  40.4 1.9 %charge_gradient.1 = (bf16[512,384]{1,0:T(8,128)(2,1)}, bf16[3,128,768]{2,1,0:T(8,128)(2,1)}) custom-call(s32[3,2,4]{2,1,0:T(2,128)S(1)} %bitcast.2, s32[4,3]{1,0:T(4,128)S(1)} %copy-done.5, bf16[128,384]{1,0:T(8,128)(2,1)S(1)} %get-tuple-element.28.refs_0_, bf16[128,384]{1,0:T(8,128)(2,1)S(1)} %get-tuple-element.29.refs_1_, ...), custom_call_target="tpu_custom_call" | custom-call | flops 100000000 | bytes 786432 | tf_op jit(solution)/shard_map/charge_gradient/pallas_call | solution.py:408
  (24 shorter events, 0.1 us)
Async XLA Ops:
  3.5 2.4 %collective-permute-start = (bf16[768,384]{1,0:T(8,128)(2,1)}, bf16[768,384]{1,0:T(8,128)(2,1)S(1)}, u32[]{:S(2)}, u32[]{:S(2)}) collective-permute-start(bf16[768,384]{1,0:T(8,128)(2,1)} %get-tuple-element.19), channel_id=1, source_target_pairs={{0,4},{4,0},{8,12},{12,8},{1,5},{5,1},{9,13},{13,9},{2,6},{6,2},{1... | collective-permute-start | bytes 1769480 | tf_op jit(solution)/shard_map/ppermute | solution.py:47
  6.1 7.8 %collective-permute-start.1 = (bf16[64,384]{1,0:T(8,128)(2,1)S(1)}, bf16[64,384]{1,0:T(8,128)(2,1)S(1)}, u32[]{:S(2)}, u32[]{:S(2)}) collective-permute-start(bf16[64,384]{1,0:T(8,128)(2,1)S(1)} %get-tuple-element.23), channel_id=1, source_target_pairs={{0,8},{4,12},{8,0},{12,4},{1,9},{5,13},{9,1},{13,5},{2,10},{6,14},... | collective-permute-start | bytes 147464 | tf_op jit(solution)/shard_map/ppermute | solution.py:47
  9.0 7.7 %collective-permute-start.5 = (bf16[320,384]{1,0:T(8,128)(2,1)S(1)}, bf16[320,384]{1,0:T(8,128)(2,1)S(1)}, u32[]{:S(2)}, u32[]{:S(2)}) collective-permute-start(bf16[320,384]{1,0:T(8,128)(2,1)S(1)} %get-tuple-element.20._), channel_id=1, source_target_pairs={{0,8},{4,12},{8,0},{12,4},{1,9},{5,13},{9,1},{13,5},{2,10},{6,14},... | collective-permute-start | bytes 737288 | tf_op jit(solution)/shard_map/ppermute | solution.py:47
  9.1 0.8 %copy-start.6 = (bf16[3,21,200]{2,1,0:T(8,128)(2,1)S(1)}, bf16[3,21,200]{2,1,0:T(8,128)(2,1)}, u32[]{:S(2)}) copy-start(bf16[3,21,200]{2,1,0:T(8,128)(2,1)} %response_ref.1) | copy-start | bytes 75604
  10.8 3.1 %copy-start.1 = (bf16[3,128,768]{2,1,0:T(8,128)(2,1)S(1)}, bf16[3,128,768]{2,1,0:T(8,128)(2,1)}, u32[]{:S(2)}) copy-start(bf16[3,128,768]{2,1,0:T(8,128)(2,1)} %own_ref.1) | copy-start | bytes 1769476
  13.9 2.9 %copy-start.2 = (f32[320,384]{1,0:T(8,128)S(1)}, f32[320,384]{1,0:T(8,128)}, u32[]{:S(2)}) copy-start(f32[320,384]{1,0:T(8,128)} %get-tuple-element.24.refs_0_) | copy-start | bytes 1474564
  13.9 2.8 %copy-start.3 = (f32[128,384]{1,0:T(8,128)S(1)}, f32[128,384]{1,0:T(8,128)}, u32[]{:S(2)}) copy-start(f32[128,384]{1,0:T(8,128)} %get-tuple-element.25.refs_3_) | copy-start | bytes 589828
  17.3 11.8 %collective-permute-start.6 = (bf16[896,128]{1,0:T(8,128)(2,1)S(1)}, bf16[896,128]{1,0:T(8,128)(2,1)S(1)}, u32[]{:S(2)}, u32[]{:S(2)}) collective-permute-start(bf16[896,128]{1,0:T(8,128)(2,1)S(1)} %get-tuple-element.27), channel_id=1, source_target_pairs={{0,1},{1,0},{2,3},{3,2},{4,5},{5,4},{6,7},{7,6},{8,9},{9,8},{10,11... | collective-permute-start | bytes 688136 | tf_op jit(solution)/shard_map/ppermute | solution.py:47
  19.1 12.7 %collective-permute-start.4 = (bf16[3,128,128]{2,1,0:T(8,128)(2,1)S(1)}, bf16[3,128,128]{2,1,0:T(8,128)(2,1)S(1)}, u32[]{:S(2)}, u32[]{:S(2)}) collective-permute-start(bf16[3,128,128]{2,1,0:T(8,128)(2,1)S(1)} %bin_gradients.1.refs_4_.refs_0_), channel_id=1, source_target_pairs={{0,3},{1,2},{2,1},{3,0},{4,7},{5,6},{6,5},{7,4},{8,11},{9,10},{10,... | collective-permute-start | bytes 294920 | tf_op jit(solution)/shard_map/ppermute | solution.py:47
  21.6 10.3 %collective-permute-start.3 = (bf16[3,128,128]{2,1,0:T(8,128)(2,1)S(1)}, bf16[3,128,128]{2,1,0:T(8,128)(2,1)S(1)}, u32[]{:S(2)}, u32[]{:S(2)}) collective-permute-start(bf16[3,128,128]{2,1,0:T(8,128)(2,1)S(1)} %bin_gradients.1.refs_4_.refs_0_), channel_id=1, source_target_pairs={{0,2},{1,3},{2,0},{3,1},{4,6},{5,7},{6,4},{7,5},{8,10},{9,11},{10,... | collective-permute-start | bytes 294920 | tf_op jit(solution)/shard_map/ppermute | solution.py:47
  21.7 10.1 %collective-permute-start.2 = (bf16[3,128,128]{2,1,0:T(8,128)(2,1)S(1)}, bf16[3,128,128]{2,1,0:T(8,128)(2,1)S(1)}, u32[]{:S(2)}, u32[]{:S(2)}) collective-permute-start(bf16[3,128,128]{2,1,0:T(8,128)(2,1)S(1)} %bin_gradients.1.refs_4_.refs_0_), channel_id=1, source_target_pairs={{0,1},{1,0},{2,3},{3,2},{4,5},{5,4},{6,7},{7,6},{8,9},{9,8},{10,11... | collective-permute-start | bytes 294920 | tf_op jit(solution)/shard_map/ppermute | solution.py:47
  29.3 9.0 %collective-permute-start.13 = (bf16[448,128]{1,0:T(8,128)(2,1)S(1)}, bf16[448,128]{1,0:T(8,128)(2,1)S(1)}, u32[]{:S(2)}, u32[]{:S(2)}) collective-permute-start(bf16[448,128]{1,0:T(8,128)(2,1)S(1)} %pass_on.1.refs_4_), channel_id=1, source_target_pairs={{0,2},{1,3},{2,0},{3,1},{4,6},{5,7},{6,4},{7,5},{8,10},{9,11},{10,... | collective-permute-start | bytes 344072 | tf_op jit(solution)/shard_map/ppermute | solution.py:47
  32.1 4.7 %collective-permute-start.9 = (bf16[128,384]{1,0:T(8,128)(2,1)S(1)}, bf16[128,384]{1,0:T(8,128)(2,1)S(1)}, u32[]{:S(2)}, u32[]{:S(2)}) collective-permute-start(bf16[128,384]{1,0:T(8,128)(2,1)S(1)} %get-tuple-element.28.refs_0_), channel_id=1, source_target_pairs={{0,8},{4,12},{8,0},{12,4},{1,9},{5,13},{9,1},{13,5},{2,10},{6,14},... | collective-permute-start | bytes 294920 | tf_op jit(solution)/shard_map/ppermute | solution.py:47
  33.7 4.6 %collective-permute-start.10 = (bf16[128,384]{1,0:T(8,128)(2,1)S(1)}, bf16[128,384]{1,0:T(8,128)(2,1)S(1)}, u32[]{:S(2)}, u32[]{:S(2)}) collective-permute-start(bf16[128,384]{1,0:T(8,128)(2,1)S(1)} %get-tuple-element.29.refs_1_), channel_id=1, source_target_pairs={{0,8},{4,12},{8,0},{12,4},{1,9},{5,13},{9,1},{13,5},{2,10},{6,14},... | collective-permute-start | bytes 294920 | tf_op jit(solution)/shard_map/ppermute | solution.py:47
  34.1 6.2 %collective-permute-start.7 = (bf16[128,384]{1,0:T(8,128)(2,1)S(1)}, bf16[128,384]{1,0:T(8,128)(2,1)S(1)}, u32[]{:S(2)}, u32[]{:S(2)}) collective-permute-start(bf16[128,384]{1,0:T(8,128)(2,1)S(1)} %get-tuple-element.28.refs_0_), channel_id=1, source_target_pairs={{0,4},{4,0},{8,12},{12,8},{1,5},{5,1},{9,13},{13,9},{2,6},{6,2},{1... | collective-permute-start | bytes 294920 | tf_op jit(solution)/shard_map/ppermute | solution.py:47
  34.2 6.2 %collective-permute-start.8 = (bf16[128,384]{1,0:T(8,128)(2,1)S(1)}, bf16[128,384]{1,0:T(8,128)(2,1)S(1)}, u32[]{:S(2)}, u32[]{:S(2)}) collective-permute-start(bf16[128,384]{1,0:T(8,128)(2,1)S(1)} %get-tuple-element.29.refs_1_), channel_id=1, source_target_pairs={{0,4},{4,0},{8,12},{12,8},{1,5},{5,1},{9,13},{13,9},{2,6},{6,2},{1... | collective-permute-start | bytes 294920 | tf_op jit(solution)/shard_map/ppermute | solution.py:47
  36.7 3.6 %collective-permute-start.11 = (bf16[128,384]{1,0:T(8,128)(2,1)S(1)}, bf16[128,384]{1,0:T(8,128)(2,1)S(1)}, u32[]{:S(2)}, u32[]{:S(2)}) collective-permute-start(bf16[128,384]{1,0:T(8,128)(2,1)S(1)} %collective-permute-done.9.refs_4_), channel_id=1, source_target_pairs={{0,4},{4,0},{8,12},{12,8},{1,5},{5,1},{9,13},{13,9},{2,6},{6,2},{1... | collective-permute-start | bytes 294920 | tf_op jit(solution)/shard_map/ppermute | solution.py:47
  38.3 2.0 %collective-permute-start.12 = (bf16[128,384]{1,0:T(8,128)(2,1)S(1)}, bf16[128,384]{1,0:T(8,128)(2,1)S(1)}, u32[]{:S(2)}, u32[]{:S(2)}) collective-permute-start(bf16[128,384]{1,0:T(8,128)(2,1)S(1)} %collective-permute-done.10.refs_5_), channel_id=1, source_target_pairs={{0,4},{4,0},{8,12},{12,8},{1,5},{5,1},{9,13},{13,9},{2,6},{6,2},{1... | collective-permute-start | bytes 294920 | tf_op jit(solution)/shard_map/ppermute | solution.py:47
  38.3 2.0 %copy-start = (bf16[4,3,2,32,128]{4,3,2,1,0:T(8,128)(2,1)S(1)}, bf16[4,3,2,32,128]{4,3,2,1,0:T(8,128)(2,1)}, u32[]{:S(2)}) copy-start(bf16[4,3,2,32,128]{4,3,2,1,0:T(8,128)(2,1)} %refs_9_.1) | copy-start | bytes 589828
  38.3 2.1 %copy-start.4 = (s32[4,3,2]{0,2,1:T(2,128)S(1)}, s32[4,3,2]{0,2,1:T(2,128)}, u32[]{:S(2)}) copy-start(s32[4,3,2]{0,2,1:T(2,128)} %param.9) | copy-start | bytes 292
  38.3 2.0 %copy-start.5 = (s32[4,3]{1,0:T(4,128)S(1)}, s32[4,3]{1,0:T(4,128)}, u32[]{:S(2)}) copy-start(s32[4,3]{1,0:T(4,128)} %count_ref.1) | copy-start | bytes 148

commit v8 on v7

--- a/solution.py
+++ b/solution.py
@@ -246,7 +246,7 @@
 
 
 def back_kernel(table_ref, own_ref, received_ref, *refs, wire_taps):
-    others, (out_ref, cot_ref, wide_ref) = refs[:-3], refs[-3:]
+    others, (out_ref, cross_ref, cot_ref, wide_ref) = refs[:-4], refs[-4:]
     planes, blocks, _, span = table_ref.shape
     _, wires, ticks = own_ref.shape
     total = received_ref.shape[1]
@@ -297,6 +297,8 @@
             both = jnp.where(lane < WINDOW, left + pltpu.roll(right, WINDOW, 1), none)
             result += pltpu.roll(both, block * step, 1) if block else both
         out_ref[plane] = result.astype(BF16)
+        if plane < planes - 1:
+            cross_ref[plane] = result.astype(BF16)
 
 
 def backward(table, cotangent, received, others, wire_taps):
@@ -306,9 +308,12 @@
     columns = (wire_taps + 1) // 2
     return pl.pallas_call(
         functools.partial(back_kernel, wire_taps=wire_taps),
-        out_shape=jax.ShapeDtypeStruct((planes, wires, LANES), BF16),
+        out_shape=(
+            jax.ShapeDtypeStruct((planes, wires, LANES), BF16),
+            jax.ShapeDtypeStruct((planes - 1, wires, LANES), BF16),
+        ),
         in_specs=[vmem()] * (3 + len(others)),
-        out_specs=vmem(),
+        out_specs=(vmem(), vmem()),
         scratch_shapes=[
             pltpu.VMEM((planes, extent, ticks), BF16),
             pltpu.VMEM((2, columns, extent, LANES), F32),
@@ -319,56 +324,90 @@
     )(table, cotangent, received, *others)
 
 
-def merge_kernel(*refs, bins, lead):
-    planes, wires, _ = refs[0].shape
-    outs, slab_ref = refs[-planes - 1 : -1], refs[-1]
-    parts = refs[: -planes - 2]
+def join_kernel(first_ref, second_ref, out_ref):
+    count = out_ref.shape[0] // 2
+    out_ref[:count] = first_ref[first_ref.shape[0] - count :]
+    out_ref[count:] = second_ref[second_ref.shape[0] - count :]
+
+
+def join(first, second, count):
+    shape = (2 * count,) + first.shape[1:]
+    return pl.pallas_call(
+        join_kernel,
+        out_shape=jax.ShapeDtypeStruct(shape, BF16),
+        in_specs=[vmem()] * 2,
+        out_specs=vmem(),
+        compiler_params=params(),
+        cost_estimate=cost(1e6, 4 * math.prod(shape)),
+        name="join",
+    )(first, second)
+
+
+def added(slab_ref, p, bins, lead, total):
+    slabs, _, wires, _ = slab_ref.shape
+    lane = lax.broadcasted_iota(jnp.int32, (wires, LANES), 1)
+    none = jnp.zeros((wires, LANES), F32)
+    tiles = [none] * (total // LANES)
+    for source in range(slabs):
+        values = slab_ref[source, p].astype(F32)
+        tile, shift = (source * bins - lead) // LANES, (source * bins - lead) % LANES
+        if shift:
+            values = pltpu.roll(values, shift, 1)
+        for t, inside in ((tile, lane >= shift), (tile + 1, lane < shift)):
+            if 0 <= t < len(tiles):
+                tiles[t] += jnp.where(inside, values, none)
+    return [values.astype(BF16) for values in tiles]
+
+
+def merge_kernel(*refs, bins, lead, planes):
+    outs, slab_ref = refs[-planes - 2 : -1], refs[-1]
     total = outs[0].shape[1]
     slab = lax.axis_index("drift")
-    for k, part in enumerate(parts):
-        slab_ref[slab ^ k] = part[...]
-    lane = lax.broadcasted_iota(jnp.int32, (wires, LANES), 1)
-    none = jnp.zeros((wires, LANES), F32)
+    for k in range(slab_ref.shape[0]):
+        slab_ref[slab ^ k] = refs[k][:planes]
     for p in range(planes):
-        tiles = [none] * (total // LANES)
-        for source in range(len(parts)):
-            values = slab_ref[source, p].astype(F32)
-            tile, shift = (source * bins - lead) // LANES, (source * bins - lead) % LANES
-            if shift:
-                values = pltpu.roll(values, shift, 1)
-            for t, inside in ((tile, lane >= shift), (tile + 1, lane < shift)):
-                if 0 <= t < len(tiles):
-                    tiles[t] += jnp.where(inside, values, none)
-        for t, values in enumerate(tiles):
-            outs[p][:, t * LANES : (t + 1) * LANES] = values.astype(BF16)
-
-
-def merge(parts, bins, total, before):
-    planes, wires, _ = parts[0].shape
-    return pl.pallas_call(
-        functools.partial(merge_kernel, bins=bins, lead=WINDOW // 2 - HB),
-        out_shape=(jax.ShapeDtypeStruct((wires, total), BF16),) * planes,
-        in_specs=[vmem()] * len(parts) + [anywhere()],
-        out_specs=(vmem(),) * planes,
-        scratch_shapes=[pltpu.VMEM((len(parts), planes, wires, LANES), BF16)],
+        for t, values in enumerate(added(slab_ref, p, bins, lead, total)):
+            here = slice(t * LANES, (t + 1) * LANES)
+            outs[p][:, here] = values
+            outs[planes][p, :, here] = values
+
+
+def merge(arrays, bins, total, before):
+    planes, wires, _ = arrays[0].shape
+    return pl.pallas_call(
+        functools.partial(merge_kernel, bins=bins, lead=WINDOW // 2 - HB, planes=planes),
+        out_shape=(jax.ShapeDtypeStruct((wires, total), BF16),) * planes
+        + (jax.ShapeDtypeStruct((planes, wires, total), BF16),),
+        in_specs=[vmem()] * len(arrays) + [anywhere()],
+        out_specs=(vmem(),) * (planes + 1),
+        scratch_shapes=[pltpu.VMEM((len(arrays), planes, wires, LANES), BF16)],
         compiler_params=params(),
         cost_estimate=cost(1e8, 4 * planes * wires * total),
         name="merge_bins",
-    )(*parts, before)
-
-
-def charge_kernel(block_ref, count_ref, *refs):
-    sources, (local_ref, share_ref, signal_ref, out_hbm, signal_hbm) = refs[:-9], refs[-9:-4]
-    all_ref, chosen_ref, out_ref, sems = refs[-4:]
+    )(*arrays, before)
+
+
+def charge_kernel(block_ref, count_ref, *refs, places, order, bins, lead):
+    sources, refs = refs[:-12], refs[-12:]
+    held_ref, brought_ref, share_ref, signal_ref, out_hbm, signal_hbm = refs[:6]
+    all_ref, chosen_ref, out_ref, slab_ref, local_ref, sems = refs[6:]
     cells, planes, entries, wire_block, width = share_ref.shape
     owners, _, wires, total = all_ref.shape
     per_owner = wires // wire_block
     z = lax.axis_index("gz")
-    for i, source in enumerate(sources):
-        if len(sources) == planes - 1:
-            all_ref[:, i] = source[...]
+    slab = lax.axis_index("drift")
+    for i, k in enumerate(order):
+        slab_ref[slab ^ k, 0] = held_ref[i]
+        slab_ref[slab ^ k ^ 1, 0] = brought_ref[i]
+    for t, values in enumerate(added(slab_ref, 0, bins, lead, total)):
+        local_ref[:, t * LANES : (t + 1) * LANES] = values
+    for (k, p), source in zip(places, sources, strict=True):
+        if k is None:
+            all_ref[:, p] = source[...]
+        elif p is None:
+            all_ref[z ^ k] = source[...]
         else:
-            all_ref[z ^ (i // (planes - 1)), i % (planes - 1)] = source[...]
+            all_ref[z ^ k, p] = source[...]
     empty = jnp.zeros((wire_block, total), BF16)
     stores = [pltpu.make_async_copy(signal_ref, signal_hbm, sems.at[cells])]
     stores[0].start()
@@ -401,28 +440,34 @@
         store.wait()
 
 
-def charge_gradient(ovl_block, ovl_count, sources, local, intersection, owners, signal):
+def charge_gradient(
+    ovl_block, ovl_count, sources, places, ends, order, intersection, owners, signal, bins, total
+):
     cells, planes, entries, wire_block, width = intersection.shape
-    wires, total = local.shape
+    wires = ends[0].shape[1]
     shape = (owners, planes - 1, wires, total)
     return pl.pallas_call(
-        charge_kernel,
+        functools.partial(
+            charge_kernel, places=places, order=order, bins=bins, lead=WINDOW // 2 - HB
+        ),
         out_shape=(
             jax.ShapeDtypeStruct((cells * width, total), BF16),
             jax.ShapeDtypeStruct(signal.shape, BF16),
         ),
-        in_specs=[smem(), smem()] + [vmem()] * (len(sources) + 3),
+        in_specs=[smem(), smem()] + [vmem()] * (len(sources) + 4),
         out_specs=(anywhere(), anywhere()),
         scratch_shapes=[
             pltpu.VMEM(shape, BF16),
             pltpu.VMEM((cells, planes * entries * wire_block, total), BF16),
             pltpu.VMEM((cells * width, total), BF16),
+            pltpu.VMEM((2 * len(order), 1, wires, LANES), BF16),
+            pltpu.VMEM((wires, total), BF16),
             pltpu.SemaphoreType.DMA((cells + 1,)),
         ],
         compiler_params=params(),
         cost_estimate=cost(1e8, 2 * math.prod(shape)),
         name="charge_gradient",
-    )(jnp.transpose(ovl_block, (1, 2, 0)), ovl_count, *sources, local, intersection, signal)
+    )(jnp.transpose(ovl_block, (1, 2, 0)), ovl_count, *sources, *ends, intersection, signal)
 
 
 def pieces_kernel(
@@ -766,8 +811,18 @@
         diff_class, response, bins, slabs, sums[0] if sums else received
     )
     table = build_table(levels, kinds, planes, wire_taps, ticks)
-    partial = backward(table, cotangent, received, beyond, wire_taps)
-    spread = [partial] + [swap(partial, "drift", k) for k in range(1, slabs)]
+    partial, crossing = backward(table, cotangent, received, beyond, wire_taps)
+    distance = slabs // 2
+    spread = [crossing] + [
+        swap(partial if k == distance else crossing, "drift", k) for k in range(1, slabs)
+    ]
+    held, order = join(partial, spread[distance], 1), [0, distance]
+    distance //= 2
+    while distance > 1:
+        held = join(held, swap(held, "drift", distance), len(order))
+        order += [k ^ distance for k in order]
+        distance //= 2
+    ends = [held, swap(held, "drift", 1)]
 
     cuts = cut_slabs(
         currents, received, others, local_currents, bins, slabs, planes - 1, half, partial
@@ -778,16 +833,19 @@
             block = ready = pass_on(block, windows[1:], step, cuts[0].shape[0])
         windows.append(swap(block, "drift", 1 << step))
 
-    *cross, own = merge(spread, bins, total, ready)
+    count = planes - 1
+    *cross, both = merge(spread, bins, total, ready)
     if owners == 4:
         across = [swap(block, "gz", 2) for block in cross]
-        sources = [*cross, *(swap(block, "gz", 1) for block in cross)]
-        sources += [*across, *(swap(block, "gz", 1) for block in across)]
+        sources = [both, swap(both, "gz", 1), *across, *(swap(block, "gz", 1) for block in across)]
+        places = [(0, None), (1, None)]
+        places += [(2, p) for p in range(count)] + [(3, p) for p in range(count)]
     else:
         sources = [lax.all_gather(block, "gz", axis=0) for block in cross]
+        places = [(None, p) for p in range(count)]
     signal = forward(windows, table, wires, wire_taps)
     charge_grad, signal = charge_gradient(
-        ovl_block, ovl_count, sources, own, intersection, owners, signal
+        ovl_block, ovl_count, sources, places, ends, order, intersection, owners, signal, bins, total
     )
     return signal, charge_grad
 

time: 42.6 us -> 41.5 us (0.974)
  waiting for transfers between devices: 9.83 us -> 7.27 us
  starting transfers between devices: 14.8 us -> 16.3 us
    ppermute x14, waiting for transfers between devices: 9.83 us -> 7.27 us  [swap(): return lax.ppermute(block, axis, [(i, i ^ distance) for i in range(count)])]
    ppermute x14, starting transfers between devices: 14.8 us -> 16.3 us  [swap(): return lax.ppermute(block, axis, [(i, i ^ distance) for i in range(count)])]
    pallas_call x1 -> x2, Pallas kernels: 1.94 us -> 1.94 us  [the longest x1 1.94 us: charge_gradient(): pl.pallas_call(functools.partial(charge_kernel, places=places, order=orde...]
  transfers between devices with their start and end apart: 14 -> 14, of which waited for: 5 -> 6; matrix products, arithmetic and copies ran while one was open for 4% -> 4% of each run, Pallas kernels for 21% -> 21%
where the time goes in v8:
time: 41.5 us; the launch traced here: 41.2 us
  starting transfers between devices  16.3 us (39%)
  Pallas kernels  14.3 us (34%)
  waiting for transfers between devices  7.27 us (18%)
  other arithmetic  1.66 us (4%)
  between operations  0.83 us (2%)
  local copies, waits for them, and re-layouts  0.82 us (2%)
    ppermute x14, starting transfers between devices, swap(): return lax.ppermute(block, axis, [(i, i ^ distance) for i in range(count)])  16.3 us
    ppermute x14, waiting for transfers between devices, swap(): return lax.ppermute(block, axis, [(i, i ^ distance) for i in range(count)])  7.27 us
    pallas_call x1, Pallas kernels, build_table(): pl.pallas_call(functools.partial(table_kernel, wire_taps=wire_taps), out_...  3.07 us
    pallas_call x1, Pallas kernels, cut_pieces(): pl.pallas_call(functools.partial(pieces_kernel, half=half), out_shape=out...  2.81 us
    pallas_call x1, Pallas kernels, backward(): pl.pallas_call(functools.partial(back_kernel, wire_taps=wire_taps), out_s...  2.38 us
    pallas_call x1, Pallas kernels, forward(): pl.pallas_call(functools.partial(signal_kernel, wire_taps=wire_taps), out...  1.97 us
    pallas_call x1, Pallas kernels, charge_gradient(): pl.pallas_call(functools.partial(charge_kernel, places=places, order=orde...  1.94 us
    convert_element_type x1, other arithmetic, local(): sums, edges = relay(keep.astype(F32), received) if owners > 2 else ((), ())  0.98 us
  transfers between devices with their start and end apart: 14, of which 6 were waited for; matrix products, arithmetic and copies ran while one was open for 4% of the time, Pallas kernels for 21%

profile of v8, /device:TPU:0, one launch (start us, length us, event | category | flops | bytes accessed | tf_op | source)
XLA Modules:
  0.0 41.2 jit_solution(15982584496191857962)
XLA Ops:
  0.6 2.8 %pieces.1 = (f32[320,384]{1,0:T(8,128)}, bf16[1,320,384]{2,1,0:T(8,128)(2,1)}, bf16[768,384]{1,0:T(8,128)(2,1)}, f32[128,384]{1,0:T(8,128)}) custom-call(s32[3,2,4]{2,1,0:T(2,128)} %bitcast.1, s32[4,3]{1,0:T(4,128)} %count_ref.1, bf16[512,384]{1,0:T(8,128)(2,1)} %charge_hbm.1, bf16[4,3,2,32,128]{4,3,2,1,0:T(8,128)(2,1)} %refs_8_.1, bf16[3,128,768]{2,1,0:T(8,128)(2,1)} %own_ref.1), custom_call_target="tpu_custom_call" | custom-call | flops 100000000 | bytes 1966080 | tf_op jit(solution)/shard_map/pieces/pallas_call | solution.py:604
  3.4 0.5 %collective-permute-start = (bf16[768,384]{1,0:T(8,128)(2,1)}, bf16[768,384]{1,0:T(8,128)(2,1)S(1)}, u32[]{:S(2)}, u32[]{:S(2)}) collective-permute-start(bf16[768,384]{1,0:T(8,128)(2,1)} %get-tuple-element.21), channel_id=1, source_target_pairs={{0,4},{4,0},{8,12},{12,8},{1,5},{5,1},{9,13},{13,9},{2,6},{6,2},{1... | collective-permute-start | bytes 1769480 | tf_op jit(solution)/shard_map/ppermute | solution.py:47
  4.0 0.7 %convert_element_type.8 = bf16[384]{0:T(512)(128)(2,1)S(1)} convert(s32[384]{0:T(512)} %param.11) | non-fusion elementwise | flops 384 | bytes 2304 | tf_op jit(solution)/shard_map/convert_element_type | solution.py:144
  4.7 1.0 %convert_element_type.9.keep_ref = f32[1,320,384]{2,1,0:T(8,128)S(1)} convert(bf16[1,320,384]{2,1,0:T(8,128)(2,1)} %get-tuple-element.20) | non-fusion elementwise | flops 122880 | bytes 737280 | tf_op jit(solution)/shard_map/convert_element_type | solution.py:806
  5.7 0.2 collective-permute-done.received_ref.refs_1_
  5.8 0.2 relay.1
  6.1 2.9 %collective-permute-start.1 = (bf16[64,384]{1,0:T(8,128)(2,1)S(1)}, bf16[64,384]{1,0:T(8,128)(2,1)S(1)}, u32[]{:S(2)}, u32[]{:S(2)}) collective-permute-start(bf16[64,384]{1,0:T(8,128)(2,1)S(1)} %get-tuple-element.25), channel_id=1, source_target_pairs={{0,8},{4,12},{8,0},{12,4},{1,9},{5,13},{9,1},{13,5},{2,10},{6,14},... | collective-permute-start | bytes 147464 | tf_op jit(solution)/shard_map/ppermute | solution.py:47
  9.0 0.1 collective-permute-start.5
  9.1 0.8 %copy-done.6 = bf16[3,21,200]{2,1,0:T(8,128)(2,1)S(1)} copy-done((bf16[3,21,200]{2,1,0:T(8,128)(2,1)S(1)}, bf16[3,21,200]{2,1,0:T(8,128)(2,1)}, u32[]{:S(2)}) %copy-start.6) | copy-done | bytes 25224
  9.8 0.9 %levels.1 = (f32[72,8,256]{2,1,0:T(8,128)S(1)}, s32[16,8,128]{2,1,0:T(8,128)S(1)}) custom-call(bf16[8,256]{1,0:T(8,128)(2,1)S(1)} %reshape.7.class_ref, bf16[3,21,200]{2,1,0:T(8,128)(2,1)S(1)} %copy-done.6, bf16[320,384]{1,0:T(8,128)(2,1)S(1)} %get-tuple-element.22._), custom_call_target="tpu_custom_call" | custom-call | flops 100000000 | bytes 1000000 | tf_op jit(solution)/shard_map/levels/pallas_call | solution.py:145
  10.8 3.1 %table.1.table_ref.refs_3_ = bf16[3,3,1408,256]{3,2,1,0:T(8,128)(2,1)S(1)} custom-call(f32[72,8,256]{2,1,0:T(8,128)S(1)} %get-tuple-element.23.level_ref, s32[16,8,128]{2,1,0:T(8,128)S(1)} %get-tuple-element.24.kind_ref), custom_call_target="tpu_custom_call" | custom-call | flops 4000000000 | bytes 6488064 | tf_op jit(solution)/shard_map/table/pallas_call | solution.py:236
  13.9 2.4 %bin_gradients.1 = (bf16[3,128,128]{2,1,0:T(8,128)(2,1)S(1)}, bf16[2,128,128]{2,1,0:T(8,128)(2,1)S(1)}) custom-call(bf16[3,3,1408,256]{3,2,1,0:T(8,128)(2,1)S(1)} %table.1.table_ref.refs_3_, bf16[3,128,768]{2,1,0:T(8,128)(2,1)S(1)} %copy-done.1, bf16[768,384]{1,0:T(8,128)(2,1)S(1)} %collective-permute-done.received_ref.refs_1_, ...), custom_call_target="tpu_custom_call" | custom-call | flops 4000000000 | bytes 6488064 | tf_op jit(solution)/shard_map/bin_gradients/pallas_call | solution.py:309
  16.3 0.4 %collective-permute-done.5.refs_2_ = bf16[320,384]{1,0:T(8,128)(2,1)S(1)} collective-permute-done((bf16[320,384]{1,0:T(8,128)(2,1)S(1)}, bf16[320,384]{1,0:T(8,128)(2,1)S(1)}, u32[]{:S(2)}, u32[]{:S(2)}) %collective-permute-start.5) | collective-permute-done | bytes 245792 | tf_op jit(solution)/shard_map/ppermute | solution.py:47
  16.7 0.6 %slab_currents.1 = (bf16[448,128]{1,0:T(8,128)(2,1)S(1)}, bf16[896,128]{1,0:T(8,128)(2,1)S(1)}, bf16[448,128]{1,0:T(8,128)(2,1)S(1)}) custom-call(f32[320,384]{1,0:T(8,128)S(1)} %copy-done.2, bf16[768,384]{1,0:T(8,128)(2,1)S(1)} %collective-permute-done.received_ref.refs_1_, bf16[320,384]{1,0:T(8,128)(2,1)S(1)} %collective-permute-done.5.refs_2_, ...), custom_call_target="tpu_custom_call" | custom-call | flops 100000000 | bytes 688128 | tf_op jit(solution)/shard_map/slab_currents/pallas_call | solution.py:695
  17.3 1.8 %collective-permute-start.6 = (bf16[896,128]{1,0:T(8,128)(2,1)S(1)}, bf16[896,128]{1,0:T(8,128)(2,1)S(1)}, u32[]{:S(2)}, u32[]{:S(2)}) collective-permute-start(bf16[896,128]{1,0:T(8,128)(2,1)S(1)} %get-tuple-element.31), channel_id=1, source_target_pairs={{0,1},{1,0},{2,3},{3,2},{4,5},{5,4},{6,7},{7,6},{8,9},{9,8},{10,11... | collective-permute-start | bytes 688136 | tf_op jit(solution)/shard_map/ppermute | solution.py:47
  19.1 2.6 %collective-permute-start.3 = (bf16[3,128,128]{2,1,0:T(8,128)(2,1)S(1)}, bf16[3,128,128]{2,1,0:T(8,128)(2,1)S(1)}, u32[]{:S(2)}, u32[]{:S(2)}) collective-permute-start(bf16[3,128,128]{2,1,0:T(8,128)(2,1)S(1)} %get-tuple-element.27.refs_4_.first_ref), channel_id=1, source_target_pairs={{0,2},{1,3},{2,0},{3,1},{4,6},{5,7},{6,4},{7,5},{8,10},{9,11},{10,... | collective-permute-start | bytes 294920 | tf_op jit(solution)/shard_map/ppermute | solution.py:47
  21.7 0.1 collective-permute-start.4
  21.8 0.8 %collective-permute-start.2 = (bf16[2,128,128]{2,1,0:T(8,128)(2,1)S(1)}, bf16[2,128,128]{2,1,0:T(8,128)(2,1)S(1)}, u32[]{:S(2)}, u32[]{:S(2)}) collective-permute-start(bf16[2,128,128]{2,1,0:T(8,128)(2,1)S(1)} %get-tuple-element.26.refs_0_), channel_id=1, source_target_pairs={{0,1},{1,0},{2,3},{3,2},{4,5},{5,4},{6,7},{7,6},{8,9},{9,8},{10,11... | collective-permute-start | bytes 196616 | tf_op jit(solution)/shard_map/ppermute | solution.py:47
  22.6 4.6 %collective-permute-done.6.refs_1_ = bf16[896,128]{1,0:T(8,128)(2,1)S(1)} collective-permute-done((bf16[896,128]{1,0:T(8,128)(2,1)S(1)}, bf16[896,128]{1,0:T(8,128)(2,1)S(1)}, u32[]{:S(2)}, u32[]{:S(2)}) %collective-permute-start.6) | collective-permute-done | bytes 229408 | tf_op jit(solution)/shard_map/ppermute | solution.py:47
  27.2 0.2 pass_on.1.refs_4_
  27.4 2.6 %collective-permute-start.13 = (bf16[448,128]{1,0:T(8,128)(2,1)S(1)}, bf16[448,128]{1,0:T(8,128)(2,1)S(1)}, u32[]{:S(2)}, u32[]{:S(2)}) collective-permute-start(bf16[448,128]{1,0:T(8,128)(2,1)S(1)} %pass_on.1.refs_4_), channel_id=1, source_target_pairs={{0,2},{1,3},{2,0},{3,1},{4,6},{5,7},{6,4},{7,5},{8,10},{9,11},{10,... | collective-permute-start | bytes 344072 | tf_op jit(solution)/shard_map/ppermute | solution.py:47
  30.0 0.7 %collective-permute-done.4.refs_3_ = bf16[2,128,128]{2,1,0:T(8,128)(2,1)S(1)} collective-permute-done((bf16[2,128,128]{2,1,0:T(8,128)(2,1)S(1)}, bf16[2,128,128]{2,1,0:T(8,128)(2,1)S(1)}, u32[]{:S(2)}, u32[]{:S(2)}) %collective-permute-start.4) | collective-permute-done | bytes 65568 | tf_op jit(solution)/shard_map/ppermute | solution.py:47
  30.8 0.2 merge_bins.1
  30.9 1.7 %collective-permute-start.8 = (bf16[128,384]{1,0:T(8,128)(2,1)S(1)}, bf16[128,384]{1,0:T(8,128)(2,1)S(1)}, u32[]{:S(2)}, u32[]{:S(2)}) collective-permute-start(bf16[128,384]{1,0:T(8,128)(2,1)S(1)} %get-tuple-element.33), channel_id=1, source_target_pairs={{0,8},{4,12},{8,0},{12,4},{1,9},{5,13},{9,1},{13,5},{2,10},{6,14},... | collective-permute-start | bytes 294920 | tf_op jit(solution)/shard_map/ppermute | solution.py:47
  32.6 0.4 %collective-permute-start.9 = (bf16[128,384]{1,0:T(8,128)(2,1)S(1)}, bf16[128,384]{1,0:T(8,128)(2,1)S(1)}, u32[]{:S(2)}, u32[]{:S(2)}) collective-permute-start(bf16[128,384]{1,0:T(8,128)(2,1)S(1)} %get-tuple-element.34), channel_id=1, source_target_pairs={{0,8},{4,12},{8,0},{12,4},{1,9},{5,13},{9,1},{13,5},{2,10},{6,14},... | collective-permute-start | bytes 294920 | tf_op jit(solution)/shard_map/ppermute | solution.py:47
  33.0 2.4 %collective-permute-start.12 = (bf16[2,128,128]{2,1,0:T(8,128)(2,1)S(1)}, bf16[2,128,128]{2,1,0:T(8,128)(2,1)S(1)}, u32[]{:S(2)}, u32[]{:S(2)}) collective-permute-start(bf16[2,128,128]{2,1,0:T(8,128)(2,1)S(1)} %join.1.refs_6_), channel_id=1, source_target_pairs={{0,1},{1,0},{2,3},{3,2},{4,5},{5,4},{6,7},{7,6},{8,9},{9,8},{10,11... | collective-permute-start | bytes 196616 | tf_op jit(solution)/shard_map/ppermute | solution.py:47
  35.5 0.1 collective-permute-done.8.refs_2_
  35.6 0.4 collective-permute-start.10
  36.0 1.2 %collective-permute-done.9.refs_3_ = bf16[128,384]{1,0:T(8,128)(2,1)S(1)} collective-permute-done((bf16[128,384]{1,0:T(8,128)(2,1)S(1)}, bf16[128,384]{1,0:T(8,128)(2,1)S(1)}, u32[]{:S(2)}, u32[]{:S(2)}) %collective-permute-start.9) | collective-permute-done | bytes 98336 | tf_op jit(solution)/shard_map/ppermute | solution.py:47
  37.2 0.0 copy-start.4
  37.2 2.0 %signal.1.refs_9_ = bf16[3,128,768]{2,1,0:T(8,128)(2,1)S(1)} custom-call(bf16[448,128]{1,0:T(8,128)(2,1)S(1)} %get-tuple-element.35.refs_0_, bf16[896,128]{1,0:T(8,128)(2,1)S(1)} %collective-permute-done.6.refs_1_, bf16[448,128]{1,0:T(8,128)(2,1)S(1)} %collective-permute-done.13.refs_2_, bf16[3,3,1408,256]{3,2,1,0:T(8,128)(2,1)S(1)} %table.1.table_ref.refs_3_), custom_call_target="tpu_custom_call" | custom-call | flops 4000000000 | bytes 6488064 | tf_op jit(solution)/shard_map/signal/pallas_call | solution.py:776
  39.3 1.9 %charge_gradient.1 = (bf16[512,384]{1,0:T(8,128)(2,1)}, bf16[3,128,768]{2,1,0:T(8,128)(2,1)}) custom-call(s32[3,2,4]{2,1,0:T(2,128)S(1)} %bitcast.2, s32[4,3]{1,0:T(4,128)S(1)} %copy-done.5, bf16[2,128,384]{2,1,0:T(8,128)(2,1)S(1)} %get-tuple-element.32.refs_0_, bf16[2,128,384]{2,1,0:T(8,128)(2,1)S(1)} %collective-permute-done.7.refs_1_, ...), custom_call_target="tpu_custom_call" | custom-call | flops 100000000 | bytes 786432 | tf_op jit(solution)/shard_map/charge_gradient/pallas_call | solution.py:449
  (25 shorter events, 0.1 us)
Async XLA Ops:
  3.4 2.4 %collective-permute-start = (bf16[768,384]{1,0:T(8,128)(2,1)}, bf16[768,384]{1,0:T(8,128)(2,1)S(1)}, u32[]{:S(2)}, u32[]{:S(2)}) collective-permute-start(bf16[768,384]{1,0:T(8,128)(2,1)} %get-tuple-element.21), channel_id=1, source_target_pairs={{0,4},{4,0},{8,12},{12,8},{1,5},{5,1},{9,13},{13,9},{2,6},{6,2},{1... | collective-permute-start | bytes 1769480 | tf_op jit(solution)/shard_map/ppermute | solution.py:47
  6.1 7.8 %collective-permute-start.1 = (bf16[64,384]{1,0:T(8,128)(2,1)S(1)}, bf16[64,384]{1,0:T(8,128)(2,1)S(1)}, u32[]{:S(2)}, u32[]{:S(2)}) collective-permute-start(bf16[64,384]{1,0:T(8,128)(2,1)S(1)} %get-tuple-element.25), channel_id=1, source_target_pairs={{0,8},{4,12},{8,0},{12,4},{1,9},{5,13},{9,1},{13,5},{2,10},{6,14},... | collective-permute-start | bytes 147464 | tf_op jit(solution)/shard_map/ppermute | solution.py:47
  9.0 7.7 %collective-permute-start.5 = (bf16[320,384]{1,0:T(8,128)(2,1)S(1)}, bf16[320,384]{1,0:T(8,128)(2,1)S(1)}, u32[]{:S(2)}, u32[]{:S(2)}) collective-permute-start(bf16[320,384]{1,0:T(8,128)(2,1)S(1)} %get-tuple-element.22._), channel_id=1, source_target_pairs={{0,8},{4,12},{8,0},{12,4},{1,9},{5,13},{9,1},{13,5},{2,10},{6,14},... | collective-permute-start | bytes 737288 | tf_op jit(solution)/shard_map/ppermute | solution.py:47
  9.1 0.8 %copy-start.6 = (bf16[3,21,200]{2,1,0:T(8,128)(2,1)S(1)}, bf16[3,21,200]{2,1,0:T(8,128)(2,1)}, u32[]{:S(2)}) copy-start(bf16[3,21,200]{2,1,0:T(8,128)(2,1)} %response_ref.1) | copy-start | bytes 75604
  10.8 3.1 %copy-start.1 = (bf16[3,128,768]{2,1,0:T(8,128)(2,1)S(1)}, bf16[3,128,768]{2,1,0:T(8,128)(2,1)}, u32[]{:S(2)}) copy-start(bf16[3,128,768]{2,1,0:T(8,128)(2,1)} %own_ref.1) | copy-start | bytes 1769476
  13.9 2.8 %copy-start.2 = (f32[320,384]{1,0:T(8,128)S(1)}, f32[320,384]{1,0:T(8,128)}, u32[]{:S(2)}) copy-start(f32[320,384]{1,0:T(8,128)} %get-tuple-element.28.refs_0_) | copy-start | bytes 1474564
  13.9 2.8 %copy-start.3 = (f32[128,384]{1,0:T(8,128)S(1)}, f32[128,384]{1,0:T(8,128)}, u32[]{:S(2)}) copy-start(f32[128,384]{1,0:T(8,128)} %get-tuple-element.29.refs_3_) | copy-start | bytes 589828
  17.3 9.9 %collective-permute-start.6 = (bf16[896,128]{1,0:T(8,128)(2,1)S(1)}, bf16[896,128]{1,0:T(8,128)(2,1)S(1)}, u32[]{:S(2)}, u32[]{:S(2)}) collective-permute-start(bf16[896,128]{1,0:T(8,128)(2,1)S(1)} %get-tuple-element.31), channel_id=1, source_target_pairs={{0,1},{1,0},{2,3},{3,2},{4,5},{5,4},{6,7},{7,6},{8,9},{9,8},{10,11... | collective-permute-start | bytes 688136 | tf_op jit(solution)/shard_map/ppermute | solution.py:47
  19.1 11.7 %collective-permute-start.3 = (bf16[3,128,128]{2,1,0:T(8,128)(2,1)S(1)}, bf16[3,128,128]{2,1,0:T(8,128)(2,1)S(1)}, u32[]{:S(2)}, u32[]{:S(2)}) collective-permute-start(bf16[3,128,128]{2,1,0:T(8,128)(2,1)S(1)} %get-tuple-element.27.refs_4_.first_ref), channel_id=1, source_target_pairs={{0,2},{1,3},{2,0},{3,1},{4,6},{5,7},{6,4},{7,5},{8,10},{9,11},{10,... | collective-permute-start | bytes 294920 | tf_op jit(solution)/shard_map/ppermute | solution.py:47
  21.7 9.1 %collective-permute-start.4 = (bf16[2,128,128]{2,1,0:T(8,128)(2,1)S(1)}, bf16[2,128,128]{2,1,0:T(8,128)(2,1)S(1)}, u32[]{:S(2)}, u32[]{:S(2)}) collective-permute-start(bf16[2,128,128]{2,1,0:T(8,128)(2,1)S(1)} %get-tuple-element.26.refs_0_), channel_id=1, source_target_pairs={{0,3},{1,2},{2,1},{3,0},{4,7},{5,6},{6,5},{7,4},{8,11},{9,10},{10,... | collective-permute-start | bytes 196616 | tf_op jit(solution)/shard_map/ppermute | solution.py:47
  21.8 9.0 %collective-permute-start.2 = (bf16[2,128,128]{2,1,0:T(8,128)(2,1)S(1)}, bf16[2,128,128]{2,1,0:T(8,128)(2,1)S(1)}, u32[]{:S(2)}, u32[]{:S(2)}) collective-permute-start(bf16[2,128,128]{2,1,0:T(8,128)(2,1)S(1)} %get-tuple-element.26.refs_0_), channel_id=1, source_target_pairs={{0,1},{1,0},{2,3},{3,2},{4,5},{5,4},{6,7},{7,6},{8,9},{9,8},{10,11... | collective-permute-start | bytes 196616 | tf_op jit(solution)/shard_map/ppermute | solution.py:47
  27.4 9.8 %collective-permute-start.13 = (bf16[448,128]{1,0:T(8,128)(2,1)S(1)}, bf16[448,128]{1,0:T(8,128)(2,1)S(1)}, u32[]{:S(2)}, u32[]{:S(2)}) collective-permute-start(bf16[448,128]{1,0:T(8,128)(2,1)S(1)} %pass_on.1.refs_4_), channel_id=1, source_target_pairs={{0,2},{1,3},{2,0},{3,1},{4,6},{5,7},{6,4},{7,5},{8,10},{9,11},{10,... | collective-permute-start | bytes 344072 | tf_op jit(solution)/shard_map/ppermute | solution.py:47
  30.9 4.7 %collective-permute-start.8 = (bf16[128,384]{1,0:T(8,128)(2,1)S(1)}, bf16[128,384]{1,0:T(8,128)(2,1)S(1)}, u32[]{:S(2)}, u32[]{:S(2)}) collective-permute-start(bf16[128,384]{1,0:T(8,128)(2,1)S(1)} %get-tuple-element.33), channel_id=1, source_target_pairs={{0,8},{4,12},{8,0},{12,4},{1,9},{5,13},{9,1},{13,5},{2,10},{6,14},... | collective-permute-start | bytes 294920 | tf_op jit(solution)/shard_map/ppermute | solution.py:47
  32.6 4.6 %collective-permute-start.9 = (bf16[128,384]{1,0:T(8,128)(2,1)S(1)}, bf16[128,384]{1,0:T(8,128)(2,1)S(1)}, u32[]{:S(2)}, u32[]{:S(2)}) collective-permute-start(bf16[128,384]{1,0:T(8,128)(2,1)S(1)} %get-tuple-element.34), channel_id=1, source_target_pairs={{0,8},{4,12},{8,0},{12,4},{1,9},{5,13},{9,1},{13,5},{2,10},{6,14},... | collective-permute-start | bytes 294920 | tf_op jit(solution)/shard_map/ppermute | solution.py:47
  33.0 6.2 %collective-permute-start.12 = (bf16[2,128,128]{2,1,0:T(8,128)(2,1)S(1)}, bf16[2,128,128]{2,1,0:T(8,128)(2,1)S(1)}, u32[]{:S(2)}, u32[]{:S(2)}) collective-permute-start(bf16[2,128,128]{2,1,0:T(8,128)(2,1)S(1)} %join.1.refs_6_), channel_id=1, source_target_pairs={{0,1},{1,0},{2,3},{3,2},{4,5},{5,4},{6,7},{7,6},{8,9},{9,8},{10,11... | collective-permute-start | bytes 196616 | tf_op jit(solution)/shard_map/ppermute | solution.py:47
  35.5 3.8 %collective-permute-start.7 = (bf16[2,128,384]{2,1,0:T(8,128)(2,1)S(1)}, bf16[2,128,384]{2,1,0:T(8,128)(2,1)S(1)}, u32[]{:S(2)}, u32[]{:S(2)}) collective-permute-start(bf16[2,128,384]{2,1,0:T(8,128)(2,1)S(1)} %get-tuple-element.32.refs_0_), channel_id=1, source_target_pairs={{0,4},{4,0},{8,12},{12,8},{1,5},{5,1},{9,13},{13,9},{2,6},{6,2},{1... | collective-permute-start | bytes 589832 | tf_op jit(solution)/shard_map/ppermute | solution.py:47
  35.6 3.6 %collective-permute-start.10 = (bf16[128,384]{1,0:T(8,128)(2,1)S(1)}, bf16[128,384]{1,0:T(8,128)(2,1)S(1)}, u32[]{:S(2)}, u32[]{:S(2)}) collective-permute-start(bf16[128,384]{1,0:T(8,128)(2,1)S(1)} %collective-permute-done.8.refs_2_), channel_id=1, source_target_pairs={{0,4},{4,0},{8,12},{12,8},{1,5},{5,1},{9,13},{13,9},{2,6},{6,2},{1... | collective-permute-start | bytes 294920 | tf_op jit(solution)/shard_map/ppermute | solution.py:47
  37.2 2.0 %collective-permute-start.11 = (bf16[128,384]{1,0:T(8,128)(2,1)S(1)}, bf16[128,384]{1,0:T(8,128)(2,1)S(1)}, u32[]{:S(2)}, u32[]{:S(2)}) collective-permute-start(bf16[128,384]{1,0:T(8,128)(2,1)S(1)} %collective-permute-done.9.refs_3_), channel_id=1, source_target_pairs={{0,4},{4,0},{8,12},{12,8},{1,5},{5,1},{9,13},{13,9},{2,6},{6,2},{1... | collective-permute-start | bytes 294920 | tf_op jit(solution)/shard_map/ppermute | solution.py:47
  37.2 2.0 %copy-start = (bf16[4,3,2,32,128]{4,3,2,1,0:T(8,128)(2,1)S(1)}, bf16[4,3,2,32,128]{4,3,2,1,0:T(8,128)(2,1)}, u32[]{:S(2)}) copy-start(bf16[4,3,2,32,128]{4,3,2,1,0:T(8,128)(2,1)} %refs_8_.1) | copy-start | bytes 589828
  37.2 2.1 %copy-start.4 = (s32[4,3,2]{0,2,1:T(2,128)S(1)}, s32[4,3,2]{0,2,1:T(2,128)}, u32[]{:S(2)}) copy-start(s32[4,3,2]{0,2,1:T(2,128)} %param.9) | copy-start | bytes 292
  37.2 2.1 %copy-start.5 = (s32[4,3]{1,0:T(4,128)S(1)}, s32[4,3]{1,0:T(4,128)}, u32[]{:S(2)}) copy-start(s32[4,3]{1,0:T(4,128)} %count_ref.1) | copy-start | bytes 148

commit v9 on v8

--- a/solution.py
+++ b/solution.py
@@ -753,16 +753,24 @@
             at = a
             both = (lane == WINDOW + a) | (lane == WINDOW + wire_taps + a)
             levels = jnp.where(both, level_ref[p, at : at + wires], levels)
+        turned = {}
         for block in range(blocks):
             i = p * blocks + block
-            even_ref[i] = pltpu.roll(currents, (-step * block) % LANES, 1)
-            odd_ref[i] = pltpu.roll(currents, (WINDOW - step * block) % LANES, 1)
+            turns = [(-step * block) % LANES, (WINDOW - step * block) % LANES]
+            for turn in turns:
+                if turn not in turned:
+                    turned[turn] = (i, len(turned) % 2)
+                    target = odd_ref if turned[turn][1] else even_ref
+                    target[i] = pltpu.roll(currents, turn, 1) if turn else currents
+            (left_at, left_odd), (right_at, right_odd) = turned[turns[0]], turned[turns[1]]
+            left_ref = (odd_ref if left_odd else even_ref).at[left_at]
+            right_ref = (odd_ref if right_odd else even_ref).at[right_at]
             for pair in range((wire_taps + 1) // 2):
                 at = 2 * pair
                 right = levels
                 if 2 * pair + 1 < wire_taps:
-                    right = odd_ref[i, at + 1 : at + 1 + wires]
-                line = jnp.where(lane < WINDOW, even_ref[i, at : at + wires], right)
+                    right = right_ref[at + 1 : at + 1 + wires]
+                line = jnp.where(lane < WINDOW, left_ref[at : at + wires], right)
                 lines_ref[i % 2, :, pair * LANES : (pair + 1) * LANES] = line.astype(BF16)
             out_ref[p, :, block * span : (block + 1) * span] = jnp.dot(
                 lines_ref[i % 2], table_ref[p, block], preferred_element_type=F32
@@ -827,14 +835,14 @@
     cuts = cut_slabs(
         currents, received, others, local_currents, bins, slabs, planes - 1, half, partial
     )
-    windows, ready = [cuts[0]], cuts[0]
+    windows = [cuts[0]]
     for step, block in enumerate(cuts[1:]):
         if step:
-            block = ready = pass_on(block, windows[1:], step, cuts[0].shape[0])
+            block = pass_on(block, windows[1:], step, cuts[0].shape[0])
         windows.append(swap(block, "drift", 1 << step))
 
     count = planes - 1
-    *cross, both = merge(spread, bins, total, ready)
+    *cross, both = merge(spread, bins, total, cuts[0])
     if owners == 4:
         across = [swap(block, "gz", 2) for block in cross]
         sources = [both, swap(both, "gz", 1), *across, *(swap(block, "gz", 1) for block in across)]

time: 41.5 us -> 41.5 us (level)
  no operation moved by 1% of the time
where the time goes in v9:
time: 41.5 us; the launch traced here: 41.2 us
  starting transfers between devices  16.3 us (39%)
  Pallas kernels  14.3 us (34%)
  waiting for transfers between devices  7.25 us (17%)
  other arithmetic  1.66 us (4%)
  local copies, waits for them, and re-layouts  0.81 us (2%)
  between operations  0.81 us (2%)
    ppermute x14, starting transfers between devices, swap(): return lax.ppermute(block, axis, [(i, i ^ distance) for i in range(count)])  16.3 us
    ppermute x14, waiting for transfers between devices, swap(): return lax.ppermute(block, axis, [(i, i ^ distance) for i in range(count)])  7.25 us
    pallas_call x1, Pallas kernels, build_table(): pl.pallas_call(functools.partial(table_kernel, wire_taps=wire_taps), out_...  3.07 us
    pallas_call x1, Pallas kernels, cut_pieces(): pl.pallas_call(functools.partial(pieces_kernel, half=half), out_shape=out...  2.81 us
    pallas_call x1, Pallas kernels, backward(): pl.pallas_call(functools.partial(back_kernel, wire_taps=wire_taps), out_s...  2.38 us
    pallas_call x1, Pallas kernels, forward(): pl.pallas_call(functools.partial(signal_kernel, wire_taps=wire_taps), out...  2 us
    pallas_call x1, Pallas kernels, charge_gradient(): pl.pallas_call(functools.partial(charge_kernel, places=places, order=orde...  1.93 us
    convert_element_type x1, other arithmetic, local(): sums, edges = relay(keep.astype(F32), received) if owners > 2 else ((), ())  0.98 us
  transfers between devices with their start and end apart: 14, of which 6 were waited for; matrix products, arithmetic and copies ran while one was open for 4% of the time, Pallas kernels for 21%

profile of v9, /device:TPU:0, one launch (start us, length us, event | category | flops | bytes accessed | tf_op | source)
XLA Modules:
  0.0 41.2 jit_solution(14508634178342117177)
XLA Ops:
  0.6 2.8 %pieces.1 = (f32[320,384]{1,0:T(8,128)}, bf16[1,320,384]{2,1,0:T(8,128)(2,1)}, bf16[768,384]{1,0:T(8,128)(2,1)}, f32[128,384]{1,0:T(8,128)}) custom-call(s32[3,2,4]{2,1,0:T(2,128)} %bitcast.1, s32[4,3]{1,0:T(4,128)} %count_ref.1, bf16[512,384]{1,0:T(8,128)(2,1)} %charge_hbm.1, bf16[4,3,2,32,128]{4,3,2,1,0:T(8,128)(2,1)} %refs_8_.1, bf16[3,128,768]{2,1,0:T(8,128)(2,1)} %own_ref.1), custom_call_target="tpu_custom_call" | custom-call | flops 100000000 | bytes 1966080 | tf_op jit(solution)/shard_map/pieces/pallas_call | solution.py:604
  3.4 0.5 %collective-permute-start = (bf16[768,384]{1,0:T(8,128)(2,1)}, bf16[768,384]{1,0:T(8,128)(2,1)S(1)}, u32[]{:S(2)}, u32[]{:S(2)}) collective-permute-start(bf16[768,384]{1,0:T(8,128)(2,1)} %get-tuple-element.21), channel_id=1, source_target_pairs={{0,4},{4,0},{8,12},{12,8},{1,5},{5,1},{9,13},{13,9},{2,6},{6,2},{1... | collective-permute-start | bytes 1769480 | tf_op jit(solution)/shard_map/ppermute | solution.py:47
  4.0 0.7 %convert_element_type.8 = bf16[384]{0:T(512)(128)(2,1)S(1)} convert(s32[384]{0:T(512)} %param.11) | non-fusion elementwise | flops 384 | bytes 2304 | tf_op jit(solution)/shard_map/convert_element_type | solution.py:144
  4.7 1.0 %convert_element_type.9.keep_ref = f32[1,320,384]{2,1,0:T(8,128)S(1)} convert(bf16[1,320,384]{2,1,0:T(8,128)(2,1)} %get-tuple-element.20) | non-fusion elementwise | flops 122880 | bytes 737280 | tf_op jit(solution)/shard_map/convert_element_type | solution.py:814
  5.7 0.2 collective-permute-done.received_ref.refs_1_
  5.8 0.2 relay.1
  6.1 2.9 %collective-permute-start.1 = (bf16[64,384]{1,0:T(8,128)(2,1)S(1)}, bf16[64,384]{1,0:T(8,128)(2,1)S(1)}, u32[]{:S(2)}, u32[]{:S(2)}) collective-permute-start(bf16[64,384]{1,0:T(8,128)(2,1)S(1)} %get-tuple-element.25), channel_id=1, source_target_pairs={{0,8},{4,12},{8,0},{12,4},{1,9},{5,13},{9,1},{13,5},{2,10},{6,14},... | collective-permute-start | bytes 147464 | tf_op jit(solution)/shard_map/ppermute | solution.py:47
  9.0 0.1 collective-permute-start.5
  9.1 0.8 %copy-done.6 = bf16[3,21,200]{2,1,0:T(8,128)(2,1)S(1)} copy-done((bf16[3,21,200]{2,1,0:T(8,128)(2,1)S(1)}, bf16[3,21,200]{2,1,0:T(8,128)(2,1)}, u32[]{:S(2)}) %copy-start.6) | copy-done | bytes 25224
  9.8 0.9 %levels.1 = (f32[72,8,256]{2,1,0:T(8,128)S(1)}, s32[16,8,128]{2,1,0:T(8,128)S(1)}) custom-call(bf16[8,256]{1,0:T(8,128)(2,1)S(1)} %reshape.7.class_ref, bf16[3,21,200]{2,1,0:T(8,128)(2,1)S(1)} %copy-done.6, bf16[320,384]{1,0:T(8,128)(2,1)S(1)} %get-tuple-element.22._), custom_call_target="tpu_custom_call" | custom-call | flops 100000000 | bytes 1000000 | tf_op jit(solution)/shard_map/levels/pallas_call | solution.py:145
  10.8 0.0 copy-start.1
  10.8 3.1 %table.1.table_ref.refs_3_ = bf16[3,3,1408,256]{3,2,1,0:T(8,128)(2,1)S(1)} custom-call(f32[72,8,256]{2,1,0:T(8,128)S(1)} %get-tuple-element.23.level_ref, s32[16,8,128]{2,1,0:T(8,128)S(1)} %get-tuple-element.24.kind_ref), custom_call_target="tpu_custom_call" | custom-call | flops 4000000000 | bytes 6488064 | tf_op jit(solution)/shard_map/table/pallas_call | solution.py:236
  13.9 2.4 %bin_gradients.1 = (bf16[3,128,128]{2,1,0:T(8,128)(2,1)S(1)}, bf16[2,128,128]{2,1,0:T(8,128)(2,1)S(1)}) custom-call(bf16[3,3,1408,256]{3,2,1,0:T(8,128)(2,1)S(1)} %table.1.table_ref.refs_3_, bf16[3,128,768]{2,1,0:T(8,128)(2,1)S(1)} %copy-done.1, bf16[768,384]{1,0:T(8,128)(2,1)S(1)} %collective-permute-done.received_ref.refs_1_, ...), custom_call_target="tpu_custom_call" | custom-call | flops 4000000000 | bytes 6488064 | tf_op jit(solution)/shard_map/bin_gradients/pallas_call | solution.py:309
  16.3 0.4 %collective-permute-done.5.refs_2_ = bf16[320,384]{1,0:T(8,128)(2,1)S(1)} collective-permute-done((bf16[320,384]{1,0:T(8,128)(2,1)S(1)}, bf16[320,384]{1,0:T(8,128)(2,1)S(1)}, u32[]{:S(2)}, u32[]{:S(2)}) %collective-permute-start.5) | collective-permute-done | bytes 245792 | tf_op jit(solution)/shard_map/ppermute | solution.py:47
  16.7 0.6 %slab_currents.1 = (bf16[448,128]{1,0:T(8,128)(2,1)S(1)}, bf16[896,128]{1,0:T(8,128)(2,1)S(1)}, bf16[448,128]{1,0:T(8,128)(2,1)S(1)}) custom-call(f32[320,384]{1,0:T(8,128)S(1)} %copy-done.2, bf16[768,384]{1,0:T(8,128)(2,1)S(1)} %collective-permute-done.received_ref.refs_1_, bf16[320,384]{1,0:T(8,128)(2,1)S(1)} %collective-permute-done.5.refs_2_, ...), custom_call_target="tpu_custom_call" | custom-call | flops 100000000 | bytes 688128 | tf_op jit(solution)/shard_map/slab_currents/pallas_call | solution.py:695
  17.3 1.8 %collective-permute-start.12 = (bf16[896,128]{1,0:T(8,128)(2,1)S(1)}, bf16[896,128]{1,0:T(8,128)(2,1)S(1)}, u32[]{:S(2)}, u32[]{:S(2)}) collective-permute-start(bf16[896,128]{1,0:T(8,128)(2,1)S(1)} %get-tuple-element.34), channel_id=1, source_target_pairs={{0,1},{1,0},{2,3},{3,2},{4,5},{5,4},{6,7},{7,6},{8,9},{9,8},{10,11... | collective-permute-start | bytes 688136 | tf_op jit(solution)/shard_map/ppermute | solution.py:47
  19.1 2.6 %collective-permute-start.3 = (bf16[3,128,128]{2,1,0:T(8,128)(2,1)S(1)}, bf16[3,128,128]{2,1,0:T(8,128)(2,1)S(1)}, u32[]{:S(2)}, u32[]{:S(2)}) collective-permute-start(bf16[3,128,128]{2,1,0:T(8,128)(2,1)S(1)} %get-tuple-element.27.refs_4_.first_ref), channel_id=1, source_target_pairs={{0,2},{1,3},{2,0},{3,1},{4,6},{5,7},{6,4},{7,5},{8,10},{9,11},{10,... | collective-permute-start | bytes 294920 | tf_op jit(solution)/shard_map/ppermute | solution.py:47
  21.7 0.1 collective-permute-start.4
  21.8 0.8 %collective-permute-start.2 = (bf16[2,128,128]{2,1,0:T(8,128)(2,1)S(1)}, bf16[2,128,128]{2,1,0:T(8,128)(2,1)S(1)}, u32[]{:S(2)}, u32[]{:S(2)}) collective-permute-start(bf16[2,128,128]{2,1,0:T(8,128)(2,1)S(1)} %get-tuple-element.26.refs_0_), channel_id=1, source_target_pairs={{0,1},{1,0},{2,3},{3,2},{4,5},{5,4},{6,7},{7,6},{8,9},{9,8},{10,11... | collective-permute-start | bytes 196616 | tf_op jit(solution)/shard_map/ppermute | solution.py:47
  22.6 4.6 %collective-permute-done.12.refs_1_ = bf16[896,128]{1,0:T(8,128)(2,1)S(1)} collective-permute-done((bf16[896,128]{1,0:T(8,128)(2,1)S(1)}, bf16[896,128]{1,0:T(8,128)(2,1)S(1)}, u32[]{:S(2)}, u32[]{:S(2)}) %collective-permute-start.12) | collective-permute-done | bytes 229408 | tf_op jit(solution)/shard_map/ppermute | solution.py:47
  27.2 0.2 pass_on.1
  27.4 2.6 %collective-permute-start.13 = (bf16[448,128]{1,0:T(8,128)(2,1)S(1)}, bf16[448,128]{1,0:T(8,128)(2,1)S(1)}, u32[]{:S(2)}, u32[]{:S(2)}) collective-permute-start(bf16[448,128]{1,0:T(8,128)(2,1)S(1)} %pass_on.1), channel_id=1, source_target_pairs={{0,2},{1,3},{2,0},{3,1},{4,6},{5,7},{6,4},{7,5},{8,10},{9,11},{10,... | collective-permute-start | bytes 344072 | tf_op jit(solution)/shard_map/ppermute | solution.py:47
  30.0 0.7 %collective-permute-done.4.refs_3_ = bf16[2,128,128]{2,1,0:T(8,128)(2,1)S(1)} collective-permute-done((bf16[2,128,128]{2,1,0:T(8,128)(2,1)S(1)}, bf16[2,128,128]{2,1,0:T(8,128)(2,1)S(1)}, u32[]{:S(2)}, u32[]{:S(2)}) %collective-permute-start.4) | collective-permute-done | bytes 65568 | tf_op jit(solution)/shard_map/ppermute | solution.py:47
  30.8 0.2 merge_bins.1
  30.9 1.7 %collective-permute-start.7 = (bf16[128,384]{1,0:T(8,128)(2,1)S(1)}, bf16[128,384]{1,0:T(8,128)(2,1)S(1)}, u32[]{:S(2)}, u32[]{:S(2)}) collective-permute-start(bf16[128,384]{1,0:T(8,128)(2,1)S(1)} %get-tuple-element.32), channel_id=1, source_target_pairs={{0,8},{4,12},{8,0},{12,4},{1,9},{5,13},{9,1},{13,5},{2,10},{6,14},... | collective-permute-start | bytes 294920 | tf_op jit(solution)/shard_map/ppermute | solution.py:47
  32.6 0.4 %collective-permute-start.8 = (bf16[128,384]{1,0:T(8,128)(2,1)S(1)}, bf16[128,384]{1,0:T(8,128)(2,1)S(1)}, u32[]{:S(2)}, u32[]{:S(2)}) collective-permute-start(bf16[128,384]{1,0:T(8,128)(2,1)S(1)} %get-tuple-element.33), channel_id=1, source_target_pairs={{0,8},{4,12},{8,0},{12,4},{1,9},{5,13},{9,1},{13,5},{2,10},{6,14},... | collective-permute-start | bytes 294920 | tf_op jit(solution)/shard_map/ppermute | solution.py:47
  33.0 2.4 %collective-permute-start.11 = (bf16[2,128,128]{2,1,0:T(8,128)(2,1)S(1)}, bf16[2,128,128]{2,1,0:T(8,128)(2,1)S(1)}, u32[]{:S(2)}, u32[]{:S(2)}) collective-permute-start(bf16[2,128,128]{2,1,0:T(8,128)(2,1)S(1)} %join.1.refs_6_), channel_id=1, source_target_pairs={{0,1},{1,0},{2,3},{3,2},{4,5},{5,4},{6,7},{7,6},{8,9},{9,8},{10,11... | collective-permute-start | bytes 196616 | tf_op jit(solution)/shard_map/ppermute | solution.py:47
  35.5 0.1 collective-permute-done.7.refs_2_
  35.6 0.4 collective-permute-start.9
  36.0 1.2 %collective-permute-done.8.refs_3_ = bf16[128,384]{1,0:T(8,128)(2,1)S(1)} collective-permute-done((bf16[128,384]{1,0:T(8,128)(2,1)S(1)}, bf16[128,384]{1,0:T(8,128)(2,1)S(1)}, u32[]{:S(2)}, u32[]{:S(2)}) %collective-permute-start.8) | collective-permute-done | bytes 98336 | tf_op jit(solution)/shard_map/ppermute | solution.py:47
  37.2 2.0 %signal.1.refs_9_ = bf16[3,128,768]{2,1,0:T(8,128)(2,1)S(1)} custom-call(bf16[448,128]{1,0:T(8,128)(2,1)S(1)} %get-tuple-element.30.refs_4_.refs_0_, bf16[896,128]{1,0:T(8,128)(2,1)S(1)} %collective-permute-done.12.refs_1_, bf16[448,128]{1,0:T(8,128)(2,1)S(1)} %collective-permute-done.13.refs_2_, bf16[3,3,1408,256]{3,2,1,0:T(8,128)(2,1)S(1)} %table.1.table_ref.refs_3_), custom_call_target="tpu_custom_call" | custom-call | flops 4000000000 | bytes 6488064 | tf_op jit(solution)/shard_map/signal/pallas_call | solution.py:784
  39.3 1.9 %charge_gradient.1 = (bf16[512,384]{1,0:T(8,128)(2,1)}, bf16[3,128,768]{2,1,0:T(8,128)(2,1)}) custom-call(s32[3,2,4]{2,1,0:T(2,128)S(1)} %bitcast.2, s32[4,3]{1,0:T(4,128)S(1)} %copy-done.5, bf16[2,128,384]{2,1,0:T(8,128)(2,1)S(1)} %get-tuple-element.31.refs_0_, bf16[2,128,384]{2,1,0:T(8,128)(2,1)S(1)} %collective-permute-done.6.refs_1_, ...), custom_call_target="tpu_custom_call" | custom-call | flops 100000000 | bytes 786432 | tf_op jit(solution)/shard_map/charge_gradient/pallas_call | solution.py:449
  (25 shorter events, 0.1 us)
Async XLA Ops:
  3.4 2.4 %collective-permute-start = (bf16[768,384]{1,0:T(8,128)(2,1)}, bf16[768,384]{1,0:T(8,128)(2,1)S(1)}, u32[]{:S(2)}, u32[]{:S(2)}) collective-permute-start(bf16[768,384]{1,0:T(8,128)(2,1)} %get-tuple-element.21), channel_id=1, source_target_pairs={{0,4},{4,0},{8,12},{12,8},{1,5},{5,1},{9,13},{13,9},{2,6},{6,2},{1... | collective-permute-start | bytes 1769480 | tf_op jit(solution)/shard_map/ppermute | solution.py:47
  6.1 7.8 %collective-permute-start.1 = (bf16[64,384]{1,0:T(8,128)(2,1)S(1)}, bf16[64,384]{1,0:T(8,128)(2,1)S(1)}, u32[]{:S(2)}, u32[]{:S(2)}) collective-permute-start(bf16[64,384]{1,0:T(8,128)(2,1)S(1)} %get-tuple-element.25), channel_id=1, source_target_pairs={{0,8},{4,12},{8,0},{12,4},{1,9},{5,13},{9,1},{13,5},{2,10},{6,14},... | collective-permute-start | bytes 147464 | tf_op jit(solution)/shard_map/ppermute | solution.py:47
  9.0 7.7 %collective-permute-start.5 = (bf16[320,384]{1,0:T(8,128)(2,1)S(1)}, bf16[320,384]{1,0:T(8,128)(2,1)S(1)}, u32[]{:S(2)}, u32[]{:S(2)}) collective-permute-start(bf16[320,384]{1,0:T(8,128)(2,1)S(1)} %get-tuple-element.22._), channel_id=1, source_target_pairs={{0,8},{4,12},{8,0},{12,4},{1,9},{5,13},{9,1},{13,5},{2,10},{6,14},... | collective-permute-start | bytes 737288 | tf_op jit(solution)/shard_map/ppermute | solution.py:47
  9.1 0.8 %copy-start.6 = (bf16[3,21,200]{2,1,0:T(8,128)(2,1)S(1)}, bf16[3,21,200]{2,1,0:T(8,128)(2,1)}, u32[]{:S(2)}) copy-start(bf16[3,21,200]{2,1,0:T(8,128)(2,1)} %response_ref.1) | copy-start | bytes 75604
  10.8 3.1 %copy-start.1 = (bf16[3,128,768]{2,1,0:T(8,128)(2,1)S(1)}, bf16[3,128,768]{2,1,0:T(8,128)(2,1)}, u32[]{:S(2)}) copy-start(bf16[3,128,768]{2,1,0:T(8,128)(2,1)} %own_ref.1) | copy-start | bytes 1769476
  13.9 2.8 %copy-start.2 = (f32[320,384]{1,0:T(8,128)S(1)}, f32[320,384]{1,0:T(8,128)}, u32[]{:S(2)}) copy-start(f32[320,384]{1,0:T(8,128)} %get-tuple-element.28.refs_0_) | copy-start | bytes 1474564
  13.9 2.8 %copy-start.3 = (f32[128,384]{1,0:T(8,128)S(1)}, f32[128,384]{1,0:T(8,128)}, u32[]{:S(2)}) copy-start(f32[128,384]{1,0:T(8,128)} %get-tuple-element.29.refs_3_) | copy-start | bytes 589828
  17.3 9.9 %collective-permute-start.12 = (bf16[896,128]{1,0:T(8,128)(2,1)S(1)}, bf16[896,128]{1,0:T(8,128)(2,1)S(1)}, u32[]{:S(2)}, u32[]{:S(2)}) collective-permute-start(bf16[896,128]{1,0:T(8,128)(2,1)S(1)} %get-tuple-element.34), channel_id=1, source_target_pairs={{0,1},{1,0},{2,3},{3,2},{4,5},{5,4},{6,7},{7,6},{8,9},{9,8},{10,11... | collective-permute-start | bytes 688136 | tf_op jit(solution)/shard_map/ppermute | solution.py:47
  19.1 11.7 %collective-permute-start.3 = (bf16[3,128,128]{2,1,0:T(8,128)(2,1)S(1)}, bf16[3,128,128]{2,1,0:T(8,128)(2,1)S(1)}, u32[]{:S(2)}, u32[]{:S(2)}) collective-permute-start(bf16[3,128,128]{2,1,0:T(8,128)(2,1)S(1)} %get-tuple-element.27.refs_4_.first_ref), channel_id=1, source_target_pairs={{0,2},{1,3},{2,0},{3,1},{4,6},{5,7},{6,4},{7,5},{8,10},{9,11},{10,... | collective-permute-start | bytes 294920 | tf_op jit(solution)/shard_map/ppermute | solution.py:47
  21.7 9.1 %collective-permute-start.4 = (bf16[2,128,128]{2,1,0:T(8,128)(2,1)S(1)}, bf16[2,128,128]{2,1,0:T(8,128)(2,1)S(1)}, u32[]{:S(2)}, u32[]{:S(2)}) collective-permute-start(bf16[2,128,128]{2,1,0:T(8,128)(2,1)S(1)} %get-tuple-element.26.refs_0_), channel_id=1, source_target_pairs={{0,3},{1,2},{2,1},{3,0},{4,7},{5,6},{6,5},{7,4},{8,11},{9,10},{10,... | collective-permute-start | bytes 196616 | tf_op jit(solution)/shard_map/ppermute | solution.py:47
  21.8 9.0 %collective-permute-start.2 = (bf16[2,128,128]{2,1,0:T(8,128)(2,1)S(1)}, bf16[2,128,128]{2,1,0:T(8,128)(2,1)S(1)}, u32[]{:S(2)}, u32[]{:S(2)}) collective-permute-start(bf16[2,128,128]{2,1,0:T(8,128)(2,1)S(1)} %get-tuple-element.26.refs_0_), channel_id=1, source_target_pairs={{0,1},{1,0},{2,3},{3,2},{4,5},{5,4},{6,7},{7,6},{8,9},{9,8},{10,11... | collective-permute-start | bytes 196616 | tf_op jit(solution)/shard_map/ppermute | solution.py:47
  27.4 9.8 %collective-permute-start.13 = (bf16[448,128]{1,0:T(8,128)(2,1)S(1)}, bf16[448,128]{1,0:T(8,128)(2,1)S(1)}, u32[]{:S(2)}, u32[]{:S(2)}) collective-permute-start(bf16[448,128]{1,0:T(8,128)(2,1)S(1)} %pass_on.1), channel_id=1, source_target_pairs={{0,2},{1,3},{2,0},{3,1},{4,6},{5,7},{6,4},{7,5},{8,10},{9,11},{10,... | collective-permute-start | bytes 344072 | tf_op jit(solution)/shard_map/ppermute | solution.py:47
  30.9 4.7 %collective-permute-start.7 = (bf16[128,384]{1,0:T(8,128)(2,1)S(1)}, bf16[128,384]{1,0:T(8,128)(2,1)S(1)}, u32[]{:S(2)}, u32[]{:S(2)}) collective-permute-start(bf16[128,384]{1,0:T(8,128)(2,1)S(1)} %get-tuple-element.32), channel_id=1, source_target_pairs={{0,8},{4,12},{8,0},{12,4},{1,9},{5,13},{9,1},{13,5},{2,10},{6,14},... | collective-permute-start | bytes 294920 | tf_op jit(solution)/shard_map/ppermute | solution.py:47
  32.6 4.6 %collective-permute-start.8 = (bf16[128,384]{1,0:T(8,128)(2,1)S(1)}, bf16[128,384]{1,0:T(8,128)(2,1)S(1)}, u32[]{:S(2)}, u32[]{:S(2)}) collective-permute-start(bf16[128,384]{1,0:T(8,128)(2,1)S(1)} %get-tuple-element.33), channel_id=1, source_target_pairs={{0,8},{4,12},{8,0},{12,4},{1,9},{5,13},{9,1},{13,5},{2,10},{6,14},... | collective-permute-start | bytes 294920 | tf_op jit(solution)/shard_map/ppermute | solution.py:47
  33.0 6.2 %collective-permute-start.11 = (bf16[2,128,128]{2,1,0:T(8,128)(2,1)S(1)}, bf16[2,128,128]{2,1,0:T(8,128)(2,1)S(1)}, u32[]{:S(2)}, u32[]{:S(2)}) collective-permute-start(bf16[2,128,128]{2,1,0:T(8,128)(2,1)S(1)} %join.1.refs_6_), channel_id=1, source_target_pairs={{0,1},{1,0},{2,3},{3,2},{4,5},{5,4},{6,7},{7,6},{8,9},{9,8},{10,11... | collective-permute-start | bytes 196616 | tf_op jit(solution)/shard_map/ppermute | solution.py:47
  35.5 3.8 %copy-start = (bf16[4,3,2,32,128]{4,3,2,1,0:T(8,128)(2,1)S(1)}, bf16[4,3,2,32,128]{4,3,2,1,0:T(8,128)(2,1)}, u32[]{:S(2)}) copy-start(bf16[4,3,2,32,128]{4,3,2,1,0:T(8,128)(2,1)} %refs_8_.1) | copy-start | bytes 589828
  35.5 3.8 %copy-start.4 = (s32[4,3,2]{0,2,1:T(2,128)S(1)}, s32[4,3,2]{0,2,1:T(2,128)}, u32[]{:S(2)}) copy-start(s32[4,3,2]{0,2,1:T(2,128)} %param.9) | copy-start | bytes 292
  35.5 3.8 %copy-start.5 = (s32[4,3]{1,0:T(4,128)S(1)}, s32[4,3]{1,0:T(4,128)}, u32[]{:S(2)}) copy-start(s32[4,3]{1,0:T(4,128)} %count_ref.1) | copy-start | bytes 148
  35.5 3.7 %collective-permute-start.6 = (bf16[2,128,384]{2,1,0:T(8,128)(2,1)S(1)}, bf16[2,128,384]{2,1,0:T(8,128)(2,1)S(1)}, u32[]{:S(2)}, u32[]{:S(2)}) collective-permute-start(bf16[2,128,384]{2,1,0:T(8,128)(2,1)S(1)} %get-tuple-element.31.refs_0_), channel_id=1, source_target_pairs={{0,4},{4,0},{8,12},{12,8},{1,5},{5,1},{9,13},{13,9},{2,6},{6,2},{1... | collective-permute-start | bytes 589832 | tf_op jit(solution)/shard_map/ppermute | solution.py:47
  35.6 3.6 %collective-permute-start.9 = (bf16[128,384]{1,0:T(8,128)(2,1)S(1)}, bf16[128,384]{1,0:T(8,128)(2,1)S(1)}, u32[]{:S(2)}, u32[]{:S(2)}) collective-permute-start(bf16[128,384]{1,0:T(8,128)(2,1)S(1)} %collective-permute-done.7.refs_2_), channel_id=1, source_target_pairs={{0,4},{4,0},{8,12},{12,8},{1,5},{5,1},{9,13},{13,9},{2,6},{6,2},{1... | collective-permute-start | bytes 294920 | tf_op jit(solution)/shard_map/ppermute | solution.py:47
  37.2 2.0 %collective-permute-start.10 = (bf16[128,384]{1,0:T(8,128)(2,1)S(1)}, bf16[128,384]{1,0:T(8,128)(2,1)S(1)}, u32[]{:S(2)}, u32[]{:S(2)}) collective-permute-start(bf16[128,384]{1,0:T(8,128)(2,1)S(1)} %collective-permute-done.8.refs_3_), channel_id=1, source_target_pairs={{0,4},{4,0},{8,12},{12,8},{1,5},{5,1},{9,13},{13,9},{2,6},{6,2},{1... | collective-permute-start | bytes 294920 | tf_op jit(solution)/shard_map/ppermute | solution.py:47

commit v10 on v9

--- a/solution.py
+++ b/solution.py
@@ -225,7 +225,7 @@
     lax.fori_loop(0, planes, whole_plane, 0)
 
 
-UNROLL = 7
+UNROLL = 21
 LEAD_SHIFT = (TPB * HB - LEAD) % LANES
 
 

time: 41.5 us -> 41 us (0.988)
  waiting for transfers between devices: 7.25 us -> 7.96 us
  Pallas kernels: 14.3 us -> 13.6 us
  starting transfers between devices: 16.3 us -> 15.8 us
    pallas_call x1, Pallas kernels: 3.07 us -> 2.34 us  [build_table(): pl.pallas_call(functools.partial(table_kernel, wire_taps=wire_taps), out_...]
    ppermute x14, waiting for transfers between devices: 7.25 us -> 7.96 us  [swap(): return lax.ppermute(block, axis, [(i, i ^ distance) for i in range(count)])]
    ppermute x14, starting transfers between devices: 16.3 us -> 15.8 us  [swap(): return lax.ppermute(block, axis, [(i, i ^ distance) for i in range(count)])]
  transfers between devices with their start and end apart: 14 -> 14, of which waited for: 6 -> 6; matrix products, arithmetic and copies ran while one was open for 4% -> 4% of each run, Pallas kernels for 21% -> 20%
where the time goes in v10:
time: 41 us; the launch traced here: 40.6 us
  starting transfers between devices  15.8 us (39%)
  Pallas kernels  13.6 us (33%)
  waiting for transfers between devices  7.96 us (19%)
  other arithmetic  1.66 us (4%)
  local copies, waits for them, and re-layouts  0.81 us (2%)
  between operations  0.81 us (2%)
    ppermute x14, starting transfers between devices, swap(): return lax.ppermute(block, axis, [(i, i ^ distance) for i in range(count)])  15.8 us
    ppermute x14, waiting for transfers between devices, swap(): return lax.ppermute(block, axis, [(i, i ^ distance) for i in range(count)])  7.96 us
    pallas_call x1, Pallas kernels, cut_pieces(): pl.pallas_call(functools.partial(pieces_kernel, half=half), out_shape=out...  2.81 us
    pallas_call x1, Pallas kernels, backward(): pl.pallas_call(functools.partial(back_kernel, wire_taps=wire_taps), out_s...  2.38 us
    pallas_call x1, Pallas kernels, build_table(): pl.pallas_call(functools.partial(table_kernel, wire_taps=wire_taps), out_...  2.34 us
    pallas_call x1, Pallas kernels, forward(): pl.pallas_call(functools.partial(signal_kernel, wire_taps=wire_taps), out...  2 us
    pallas_call x1, Pallas kernels, charge_gradient(): pl.pallas_call(functools.partial(charge_kernel, places=places, order=orde...  1.93 us
    convert_element_type x1, other arithmetic, local(): sums, edges = relay(keep.astype(F32), received) if owners > 2 else ((), ())  0.98 us
  transfers between devices with their start and end apart: 14, of which 6 were waited for; matrix products, arithmetic and copies ran while one was open for 4% of the time, Pallas kernels for 20%

profile of v10, /device:TPU:0, one launch (start us, length us, event | category | flops | bytes accessed | tf_op | source)
XLA Modules:
  0.0 40.6 jit_solution(12268646982713633015)
XLA Ops:
  0.6 2.8 %pieces.1 = (f32[320,384]{1,0:T(8,128)}, bf16[1,320,384]{2,1,0:T(8,128)(2,1)}, bf16[768,384]{1,0:T(8,128)(2,1)}, f32[128,384]{1,0:T(8,128)}) custom-call(s32[3,2,4]{2,1,0:T(2,128)} %bitcast.1, s32[4,3]{1,0:T(4,128)} %count_ref.1, bf16[512,384]{1,0:T(8,128)(2,1)} %charge_hbm.1, bf16[4,3,2,32,128]{4,3,2,1,0:T(8,128)(2,1)} %refs_8_.1, bf16[3,128,768]{2,1,0:T(8,128)(2,1)} %own_ref.1), custom_call_target="tpu_custom_call" | custom-call | flops 100000000 | bytes 1966080 | tf_op jit(solution)/shard_map/pieces/pallas_call | solution.py:604
  3.4 0.5 %collective-permute-start = (bf16[768,384]{1,0:T(8,128)(2,1)}, bf16[768,384]{1,0:T(8,128)(2,1)S(1)}, u32[]{:S(2)}, u32[]{:S(2)}) collective-permute-start(bf16[768,384]{1,0:T(8,128)(2,1)} %get-tuple-element.21), channel_id=1, source_target_pairs={{0,4},{4,0},{8,12},{12,8},{1,5},{5,1},{9,13},{13,9},{2,6},{6,2},{1... | collective-permute-start | bytes 1769480 | tf_op jit(solution)/shard_map/ppermute | solution.py:47
  4.0 0.7 %convert_element_type.8 = bf16[384]{0:T(512)(128)(2,1)S(1)} convert(s32[384]{0:T(512)} %param.11) | non-fusion elementwise | flops 384 | bytes 2304 | tf_op jit(solution)/shard_map/convert_element_type | solution.py:144
  4.7 1.0 %convert_element_type.9.keep_ref = f32[1,320,384]{2,1,0:T(8,128)S(1)} convert(bf16[1,320,384]{2,1,0:T(8,128)(2,1)} %get-tuple-element.20) | non-fusion elementwise | flops 122880 | bytes 737280 | tf_op jit(solution)/shard_map/convert_element_type | solution.py:814
  5.7 0.2 collective-permute-done.received_ref.refs_1_
  5.8 0.2 relay.1
  6.1 2.9 %collective-permute-start.1 = (bf16[64,384]{1,0:T(8,128)(2,1)S(1)}, bf16[64,384]{1,0:T(8,128)(2,1)S(1)}, u32[]{:S(2)}, u32[]{:S(2)}) collective-permute-start(bf16[64,384]{1,0:T(8,128)(2,1)S(1)} %get-tuple-element.25), channel_id=1, source_target_pairs={{0,8},{4,12},{8,0},{12,4},{1,9},{5,13},{9,1},{13,5},{2,10},{6,14},... | collective-permute-start | bytes 147464 | tf_op jit(solution)/shard_map/ppermute | solution.py:47
  9.0 0.1 collective-permute-start.5
  9.1 0.8 %copy-done.6 = bf16[3,21,200]{2,1,0:T(8,128)(2,1)S(1)} copy-done((bf16[3,21,200]{2,1,0:T(8,128)(2,1)S(1)}, bf16[3,21,200]{2,1,0:T(8,128)(2,1)}, u32[]{:S(2)}) %copy-start.6) | copy-done | bytes 25224
  9.8 0.9 %levels.1 = (f32[72,8,256]{2,1,0:T(8,128)S(1)}, s32[16,8,128]{2,1,0:T(8,128)S(1)}) custom-call(bf16[8,256]{1,0:T(8,128)(2,1)S(1)} %reshape.7.class_ref, bf16[3,21,200]{2,1,0:T(8,128)(2,1)S(1)} %copy-done.6, bf16[320,384]{1,0:T(8,128)(2,1)S(1)} %get-tuple-element.22._), custom_call_target="tpu_custom_call" | custom-call | flops 100000000 | bytes 1000000 | tf_op jit(solution)/shard_map/levels/pallas_call | solution.py:145
  10.8 0.0 copy-start.1
  10.8 2.3 %table.1.table_ref.refs_3_ = bf16[3,3,1408,256]{3,2,1,0:T(8,128)(2,1)S(1)} custom-call(f32[72,8,256]{2,1,0:T(8,128)S(1)} %get-tuple-element.23.level_ref, s32[16,8,128]{2,1,0:T(8,128)S(1)} %get-tuple-element.24.kind_ref), custom_call_target="tpu_custom_call" | custom-call | flops 4000000000 | bytes 6488064 | tf_op jit(solution)/shard_map/table/pallas_call | solution.py:236
  13.2 2.4 %bin_gradients.1 = (bf16[3,128,128]{2,1,0:T(8,128)(2,1)S(1)}, bf16[2,128,128]{2,1,0:T(8,128)(2,1)S(1)}) custom-call(bf16[3,3,1408,256]{3,2,1,0:T(8,128)(2,1)S(1)} %table.1.table_ref.refs_3_, bf16[3,128,768]{2,1,0:T(8,128)(2,1)S(1)} %copy-done.1, bf16[768,384]{1,0:T(8,128)(2,1)S(1)} %collective-permute-done.received_ref.refs_1_, ...), custom_call_target="tpu_custom_call" | custom-call | flops 4000000000 | bytes 6488064 | tf_op jit(solution)/shard_map/bin_gradients/pallas_call | solution.py:309
  15.5 1.2 %collective-permute-done.5.refs_2_ = bf16[320,384]{1,0:T(8,128)(2,1)S(1)} collective-permute-done((bf16[320,384]{1,0:T(8,128)(2,1)S(1)}, bf16[320,384]{1,0:T(8,128)(2,1)S(1)}, u32[]{:S(2)}, u32[]{:S(2)}) %collective-permute-start.5) | collective-permute-done | bytes 245792 | tf_op jit(solution)/shard_map/ppermute | solution.py:47
  16.7 0.6 %slab_currents.1 = (bf16[448,128]{1,0:T(8,128)(2,1)S(1)}, bf16[896,128]{1,0:T(8,128)(2,1)S(1)}, bf16[448,128]{1,0:T(8,128)(2,1)S(1)}) custom-call(f32[320,384]{1,0:T(8,128)S(1)} %copy-done.2, bf16[768,384]{1,0:T(8,128)(2,1)S(1)} %collective-permute-done.received_ref.refs_1_, bf16[320,384]{1,0:T(8,128)(2,1)S(1)} %collective-permute-done.5.refs_2_, ...), custom_call_target="tpu_custom_call" | custom-call | flops 100000000 | bytes 688128 | tf_op jit(solution)/shard_map/slab_currents/pallas_call | solution.py:695
  17.3 1.8 %collective-permute-start.12 = (bf16[896,128]{1,0:T(8,128)(2,1)S(1)}, bf16[896,128]{1,0:T(8,128)(2,1)S(1)}, u32[]{:S(2)}, u32[]{:S(2)}) collective-permute-start(bf16[896,128]{1,0:T(8,128)(2,1)S(1)} %get-tuple-element.34), channel_id=1, source_target_pairs={{0,1},{1,0},{2,3},{3,2},{4,5},{5,4},{6,7},{7,6},{8,9},{9,8},{10,11... | collective-permute-start | bytes 688136 | tf_op jit(solution)/shard_map/ppermute | solution.py:47
  19.1 2.6 %collective-permute-start.3 = (bf16[3,128,128]{2,1,0:T(8,128)(2,1)S(1)}, bf16[3,128,128]{2,1,0:T(8,128)(2,1)S(1)}, u32[]{:S(2)}, u32[]{:S(2)}) collective-permute-start(bf16[3,128,128]{2,1,0:T(8,128)(2,1)S(1)} %get-tuple-element.27.refs_4_.first_ref), channel_id=1, source_target_pairs={{0,2},{1,3},{2,0},{3,1},{4,6},{5,7},{6,4},{7,5},{8,10},{9,11},{10,... | collective-permute-start | bytes 294920 | tf_op jit(solution)/shard_map/ppermute | solution.py:47
  21.7 0.1 collective-permute-start.4
  21.8 0.8 %collective-permute-start.2 = (bf16[2,128,128]{2,1,0:T(8,128)(2,1)S(1)}, bf16[2,128,128]{2,1,0:T(8,128)(2,1)S(1)}, u32[]{:S(2)}, u32[]{:S(2)}) collective-permute-start(bf16[2,128,128]{2,1,0:T(8,128)(2,1)S(1)} %get-tuple-element.26.refs_0_), channel_id=1, source_target_pairs={{0,1},{1,0},{2,3},{3,2},{4,5},{5,4},{6,7},{7,6},{8,9},{9,8},{10,11... | collective-permute-start | bytes 196616 | tf_op jit(solution)/shard_map/ppermute | solution.py:47
  22.6 4.6 %collective-permute-done.12.refs_1_ = bf16[896,128]{1,0:T(8,128)(2,1)S(1)} collective-permute-done((bf16[896,128]{1,0:T(8,128)(2,1)S(1)}, bf16[896,128]{1,0:T(8,128)(2,1)S(1)}, u32[]{:S(2)}, u32[]{:S(2)}) %collective-permute-start.12) | collective-permute-done | bytes 229408 | tf_op jit(solution)/shard_map/ppermute | solution.py:47
  27.2 0.2 pass_on.1
  27.4 2.2 %collective-permute-start.13 = (bf16[448,128]{1,0:T(8,128)(2,1)S(1)}, bf16[448,128]{1,0:T(8,128)(2,1)S(1)}, u32[]{:S(2)}, u32[]{:S(2)}) collective-permute-start(bf16[448,128]{1,0:T(8,128)(2,1)S(1)} %pass_on.1), channel_id=1, source_target_pairs={{0,2},{1,3},{2,0},{3,1},{4,6},{5,7},{6,4},{7,5},{8,10},{9,11},{10,... | collective-permute-start | bytes 344072 | tf_op jit(solution)/shard_map/ppermute | solution.py:47
  29.7 0.8 %collective-permute-done.4.refs_3_ = bf16[2,128,128]{2,1,0:T(8,128)(2,1)S(1)} collective-permute-done((bf16[2,128,128]{2,1,0:T(8,128)(2,1)S(1)}, bf16[2,128,128]{2,1,0:T(8,128)(2,1)S(1)}, u32[]{:S(2)}, u32[]{:S(2)}) %collective-permute-start.4) | collective-permute-done | bytes 65568 | tf_op jit(solution)/shard_map/ppermute | solution.py:47
  30.5 0.2 merge_bins.1
  30.6 1.3 %collective-permute-start.7 = (bf16[128,384]{1,0:T(8,128)(2,1)S(1)}, bf16[128,384]{1,0:T(8,128)(2,1)S(1)}, u32[]{:S(2)}, u32[]{:S(2)}) collective-permute-start(bf16[128,384]{1,0:T(8,128)(2,1)S(1)} %get-tuple-element.32), channel_id=1, source_target_pairs={{0,8},{4,12},{8,0},{12,4},{1,9},{5,13},{9,1},{13,5},{2,10},{6,14},... | collective-permute-start | bytes 294920 | tf_op jit(solution)/shard_map/ppermute | solution.py:47
  32.0 0.8 %collective-permute-start.8 = (bf16[128,384]{1,0:T(8,128)(2,1)S(1)}, bf16[128,384]{1,0:T(8,128)(2,1)S(1)}, u32[]{:S(2)}, u32[]{:S(2)}) collective-permute-start(bf16[128,384]{1,0:T(8,128)(2,1)S(1)} %get-tuple-element.33), channel_id=1, source_target_pairs={{0,8},{4,12},{8,0},{12,4},{1,9},{5,13},{9,1},{13,5},{2,10},{6,14},... | collective-permute-start | bytes 294920 | tf_op jit(solution)/shard_map/ppermute | solution.py:47
  32.7 2.3 %collective-permute-start.11 = (bf16[2,128,128]{2,1,0:T(8,128)(2,1)S(1)}, bf16[2,128,128]{2,1,0:T(8,128)(2,1)S(1)}, u32[]{:S(2)}, u32[]{:S(2)}) collective-permute-start(bf16[2,128,128]{2,1,0:T(8,128)(2,1)S(1)} %join.1.refs_6_), channel_id=1, source_target_pairs={{0,1},{1,0},{2,3},{3,2},{4,5},{5,4},{6,7},{7,6},{8,9},{9,8},{10,11... | collective-permute-start | bytes 196616 | tf_op jit(solution)/shard_map/ppermute | solution.py:47
  35.1 0.2 collective-permute-done.7.refs_2_
  35.3 0.3 collective-permute-start.9
  35.6 1.0 %collective-permute-done.8.refs_3_ = bf16[128,384]{1,0:T(8,128)(2,1)S(1)} collective-permute-done((bf16[128,384]{1,0:T(8,128)(2,1)S(1)}, bf16[128,384]{1,0:T(8,128)(2,1)S(1)}, u32[]{:S(2)}, u32[]{:S(2)}) %collective-permute-start.8) | collective-permute-done | bytes 98336 | tf_op jit(solution)/shard_map/ppermute | solution.py:47
  36.6 2.0 %signal.1.refs_9_ = bf16[3,128,768]{2,1,0:T(8,128)(2,1)S(1)} custom-call(bf16[448,128]{1,0:T(8,128)(2,1)S(1)} %get-tuple-element.30.refs_4_.refs_0_, bf16[896,128]{1,0:T(8,128)(2,1)S(1)} %collective-permute-done.12.refs_1_, bf16[448,128]{1,0:T(8,128)(2,1)S(1)} %collective-permute-done.13.refs_2_, bf16[3,3,1408,256]{3,2,1,0:T(8,128)(2,1)S(1)} %table.1.table_ref.refs_3_), custom_call_target="tpu_custom_call" | custom-call | flops 4000000000 | bytes 6488064 | tf_op jit(solution)/shard_map/signal/pallas_call | solution.py:784
  38.7 1.9 %charge_gradient.1 = (bf16[512,384]{1,0:T(8,128)(2,1)}, bf16[3,128,768]{2,1,0:T(8,128)(2,1)}) custom-call(s32[3,2,4]{2,1,0:T(2,128)S(1)} %bitcast.2, s32[4,3]{1,0:T(4,128)S(1)} %copy-done.5, bf16[2,128,384]{2,1,0:T(8,128)(2,1)S(1)} %get-tuple-element.31.refs_0_, bf16[2,128,384]{2,1,0:T(8,128)(2,1)S(1)} %collective-permute-done.6.refs_1_, ...), custom_call_target="tpu_custom_call" | custom-call | flops 100000000 | bytes 786432 | tf_op jit(solution)/shard_map/charge_gradient/pallas_call | solution.py:449
  (25 shorter events, 0.1 us)
Async XLA Ops:
  3.4 2.4 %collective-permute-start = (bf16[768,384]{1,0:T(8,128)(2,1)}, bf16[768,384]{1,0:T(8,128)(2,1)S(1)}, u32[]{:S(2)}, u32[]{:S(2)}) collective-permute-start(bf16[768,384]{1,0:T(8,128)(2,1)} %get-tuple-element.21), channel_id=1, source_target_pairs={{0,4},{4,0},{8,12},{12,8},{1,5},{5,1},{9,13},{13,9},{2,6},{6,2},{1... | collective-permute-start | bytes 1769480 | tf_op jit(solution)/shard_map/ppermute | solution.py:47
  6.1 7.1 %collective-permute-start.1 = (bf16[64,384]{1,0:T(8,128)(2,1)S(1)}, bf16[64,384]{1,0:T(8,128)(2,1)S(1)}, u32[]{:S(2)}, u32[]{:S(2)}) collective-permute-start(bf16[64,384]{1,0:T(8,128)(2,1)S(1)} %get-tuple-element.25), channel_id=1, source_target_pairs={{0,8},{4,12},{8,0},{12,4},{1,9},{5,13},{9,1},{13,5},{2,10},{6,14},... | collective-permute-start | bytes 147464 | tf_op jit(solution)/shard_map/ppermute | solution.py:47
  9.0 7.7 %collective-permute-start.5 = (bf16[320,384]{1,0:T(8,128)(2,1)S(1)}, bf16[320,384]{1,0:T(8,128)(2,1)S(1)}, u32[]{:S(2)}, u32[]{:S(2)}) collective-permute-start(bf16[320,384]{1,0:T(8,128)(2,1)S(1)} %get-tuple-element.22._), channel_id=1, source_target_pairs={{0,8},{4,12},{8,0},{12,4},{1,9},{5,13},{9,1},{13,5},{2,10},{6,14},... | collective-permute-start | bytes 737288 | tf_op jit(solution)/shard_map/ppermute | solution.py:47
  9.1 0.8 %copy-start.6 = (bf16[3,21,200]{2,1,0:T(8,128)(2,1)S(1)}, bf16[3,21,200]{2,1,0:T(8,128)(2,1)}, u32[]{:S(2)}) copy-start(bf16[3,21,200]{2,1,0:T(8,128)(2,1)} %response_ref.1) | copy-start | bytes 75604
  10.8 2.4 %copy-start.1 = (bf16[3,128,768]{2,1,0:T(8,128)(2,1)S(1)}, bf16[3,128,768]{2,1,0:T(8,128)(2,1)}, u32[]{:S(2)}) copy-start(bf16[3,128,768]{2,1,0:T(8,128)(2,1)} %own_ref.1) | copy-start | bytes 1769476
  13.1 3.6 %copy-start.2 = (f32[320,384]{1,0:T(8,128)S(1)}, f32[320,384]{1,0:T(8,128)}, u32[]{:S(2)}) copy-start(f32[320,384]{1,0:T(8,128)} %get-tuple-element.28.refs_0_) | copy-start | bytes 1474564
  13.1 3.6 %copy-start.3 = (f32[128,384]{1,0:T(8,128)S(1)}, f32[128,384]{1,0:T(8,128)}, u32[]{:S(2)}) copy-start(f32[128,384]{1,0:T(8,128)} %get-tuple-element.29.refs_3_) | copy-start | bytes 589828
  17.3 9.9 %collective-permute-start.12 = (bf16[896,128]{1,0:T(8,128)(2,1)S(1)}, bf16[896,128]{1,0:T(8,128)(2,1)S(1)}, u32[]{:S(2)}, u32[]{:S(2)}) collective-permute-start(bf16[896,128]{1,0:T(8,128)(2,1)S(1)} %get-tuple-element.34), channel_id=1, source_target_pairs={{0,1},{1,0},{2,3},{3,2},{4,5},{5,4},{6,7},{7,6},{8,9},{9,8},{10,11... | collective-permute-start | bytes 688136 | tf_op jit(solution)/shard_map/ppermute | solution.py:47
  19.1 11.4 %collective-permute-start.3 = (bf16[3,128,128]{2,1,0:T(8,128)(2,1)S(1)}, bf16[3,128,128]{2,1,0:T(8,128)(2,1)S(1)}, u32[]{:S(2)}, u32[]{:S(2)}) collective-permute-start(bf16[3,128,128]{2,1,0:T(8,128)(2,1)S(1)} %get-tuple-element.27.refs_4_.first_ref), channel_id=1, source_target_pairs={{0,2},{1,3},{2,0},{3,1},{4,6},{5,7},{6,4},{7,5},{8,10},{9,11},{10,... | collective-permute-start | bytes 294920 | tf_op jit(solution)/shard_map/ppermute | solution.py:47
  21.7 8.8 %collective-permute-start.4 = (bf16[2,128,128]{2,1,0:T(8,128)(2,1)S(1)}, bf16[2,128,128]{2,1,0:T(8,128)(2,1)S(1)}, u32[]{:S(2)}, u32[]{:S(2)}) collective-permute-start(bf16[2,128,128]{2,1,0:T(8,128)(2,1)S(1)} %get-tuple-element.26.refs_0_), channel_id=1, source_target_pairs={{0,3},{1,2},{2,1},{3,0},{4,7},{5,6},{6,5},{7,4},{8,11},{9,10},{10,... | collective-permute-start | bytes 196616 | tf_op jit(solution)/shard_map/ppermute | solution.py:47
  21.8 8.7 %collective-permute-start.2 = (bf16[2,128,128]{2,1,0:T(8,128)(2,1)S(1)}, bf16[2,128,128]{2,1,0:T(8,128)(2,1)S(1)}, u32[]{:S(2)}, u32[]{:S(2)}) collective-permute-start(bf16[2,128,128]{2,1,0:T(8,128)(2,1)S(1)} %get-tuple-element.26.refs_0_), channel_id=1, source_target_pairs={{0,1},{1,0},{2,3},{3,2},{4,5},{5,4},{6,7},{7,6},{8,9},{9,8},{10,11... | collective-permute-start | bytes 196616 | tf_op jit(solution)/shard_map/ppermute | solution.py:47
  27.4 9.2 %collective-permute-start.13 = (bf16[448,128]{1,0:T(8,128)(2,1)S(1)}, bf16[448,128]{1,0:T(8,128)(2,1)S(1)}, u32[]{:S(2)}, u32[]{:S(2)}) collective-permute-start(bf16[448,128]{1,0:T(8,128)(2,1)S(1)} %pass_on.1), channel_id=1, source_target_pairs={{0,2},{1,3},{2,0},{3,1},{4,6},{5,7},{6,4},{7,5},{8,10},{9,11},{10,... | collective-permute-start | bytes 344072 | tf_op jit(solution)/shard_map/ppermute | solution.py:47
  30.6 4.7 %collective-permute-start.7 = (bf16[128,384]{1,0:T(8,128)(2,1)S(1)}, bf16[128,384]{1,0:T(8,128)(2,1)S(1)}, u32[]{:S(2)}, u32[]{:S(2)}) collective-permute-start(bf16[128,384]{1,0:T(8,128)(2,1)S(1)} %get-tuple-element.32), channel_id=1, source_target_pairs={{0,8},{4,12},{8,0},{12,4},{1,9},{5,13},{9,1},{13,5},{2,10},{6,14},... | collective-permute-start | bytes 294920 | tf_op jit(solution)/shard_map/ppermute | solution.py:47
  32.0 4.6 %collective-permute-start.8 = (bf16[128,384]{1,0:T(8,128)(2,1)S(1)}, bf16[128,384]{1,0:T(8,128)(2,1)S(1)}, u32[]{:S(2)}, u32[]{:S(2)}) collective-permute-start(bf16[128,384]{1,0:T(8,128)(2,1)S(1)} %get-tuple-element.33), channel_id=1, source_target_pairs={{0,8},{4,12},{8,0},{12,4},{1,9},{5,13},{9,1},{13,5},{2,10},{6,14},... | collective-permute-start | bytes 294920 | tf_op jit(solution)/shard_map/ppermute | solution.py:47
  32.7 5.9 %collective-permute-start.11 = (bf16[2,128,128]{2,1,0:T(8,128)(2,1)S(1)}, bf16[2,128,128]{2,1,0:T(8,128)(2,1)S(1)}, u32[]{:S(2)}, u32[]{:S(2)}) collective-permute-start(bf16[2,128,128]{2,1,0:T(8,128)(2,1)S(1)} %join.1.refs_6_), channel_id=1, source_target_pairs={{0,1},{1,0},{2,3},{3,2},{4,5},{5,4},{6,7},{7,6},{8,9},{9,8},{10,11... | collective-permute-start | bytes 196616 | tf_op jit(solution)/shard_map/ppermute | solution.py:47
  35.1 3.5 %copy-start = (bf16[4,3,2,32,128]{4,3,2,1,0:T(8,128)(2,1)S(1)}, bf16[4,3,2,32,128]{4,3,2,1,0:T(8,128)(2,1)}, u32[]{:S(2)}) copy-start(bf16[4,3,2,32,128]{4,3,2,1,0:T(8,128)(2,1)} %refs_8_.1) | copy-start | bytes 589828
  35.1 3.6 %copy-start.4 = (s32[4,3,2]{0,2,1:T(2,128)S(1)}, s32[4,3,2]{0,2,1:T(2,128)}, u32[]{:S(2)}) copy-start(s32[4,3,2]{0,2,1:T(2,128)} %param.9) | copy-start | bytes 292
  35.1 3.6 %copy-start.5 = (s32[4,3]{1,0:T(4,128)S(1)}, s32[4,3]{1,0:T(4,128)}, u32[]{:S(2)}) copy-start(s32[4,3]{1,0:T(4,128)} %count_ref.1) | copy-start | bytes 148
  35.1 3.5 %collective-permute-start.6 = (bf16[2,128,384]{2,1,0:T(8,128)(2,1)S(1)}, bf16[2,128,384]{2,1,0:T(8,128)(2,1)S(1)}, u32[]{:S(2)}, u32[]{:S(2)}) collective-permute-start(bf16[2,128,384]{2,1,0:T(8,128)(2,1)S(1)} %get-tuple-element.31.refs_0_), channel_id=1, source_target_pairs={{0,4},{4,0},{8,12},{12,8},{1,5},{5,1},{9,13},{13,9},{2,6},{6,2},{1... | collective-permute-start | bytes 589832 | tf_op jit(solution)/shard_map/ppermute | solution.py:47
  35.3 3.3 %collective-permute-start.9 = (bf16[128,384]{1,0:T(8,128)(2,1)S(1)}, bf16[128,384]{1,0:T(8,128)(2,1)S(1)}, u32[]{:S(2)}, u32[]{:S(2)}) collective-permute-start(bf16[128,384]{1,0:T(8,128)(2,1)S(1)} %collective-permute-done.7.refs_2_), channel_id=1, source_target_pairs={{0,4},{4,0},{8,12},{12,8},{1,5},{5,1},{9,13},{13,9},{2,6},{6,2},{1... | collective-permute-start | bytes 294920 | tf_op jit(solution)/shard_map/ppermute | solution.py:47
  36.6 2.0 %collective-permute-start.10 = (bf16[128,384]{1,0:T(8,128)(2,1)S(1)}, bf16[128,384]{1,0:T(8,128)(2,1)S(1)}, u32[]{:S(2)}, u32[]{:S(2)}) collective-permute-start(bf16[128,384]{1,0:T(8,128)(2,1)S(1)} %collective-permute-done.8.refs_3_), channel_id=1, source_target_pairs={{0,4},{4,0},{8,12},{12,8},{1,5},{5,1},{9,13},{13,9},{2,6},{6,2},{1... | collective-permute-start | bytes 294920 | tf_op jit(solution)/shard_map/ppermute | solution.py:47
